TPU v7x, 32 devices: a whole 2x2x4 slice. The times are simulated.
32 devices in a mesh: dp: 8 (over z, y), ctx: 4 (over x, core).
Axes of the slice: x: 2, y: 2, z: 4, core: 2. Of those that a mesh axis runs over, the one named last changes fastest.
Arguments:
- tokens: bfloat16 [32, 1024, 1472], P('dp', 'ctx'), may hold values from -6 to 6
- soft_mask: bfloat16 [32, 1024], P('dp', 'ctx'), may hold values from -4 to 0
- segment_ids: int32 [32, 1024], P('dp'), may hold values from 0 to 4, as said below
- buckets: int32 [1024, 1024], P('ctx'), may hold values from 0 to 31
- gain_attn: float32 [1472], replicated, may hold values from 0.5 to 1.5
- gain_ffn: float32 [1472], replicated, may hold values from 0.5 to 1.5
- bias_table: float32 [32, 6], replicated, may hold values from -4 to 4
- w_query: bfloat16 [384, 1472], P(('dp', 'ctx')), may hold values from -0.01953125 to 0.01953125
- w_key: bfloat16 [384, 1472], P(('dp', 'ctx')), may hold values from -0.15625 to 0.15625
- w_value: bfloat16 [384, 1472], P(('dp', 'ctx')), may hold values from -0.15625 to 0.15625
- w_attn_out: bfloat16 [384, 1472], P(('dp', 'ctx')), may hold values from -0.875 to 0.875
- w_gate: bfloat16 [3584, 1472], P(('dp', 'ctx')), may hold values from -0.15625 to 0.15625
- w_up: bfloat16 [3584, 1472], P(('dp', 'ctx')), may hold values from -0.15625 to 0.15625
- w_ffn_out: bfloat16 [3584, 1472], P(('dp', 'ctx')), may hold values from -0.1875 to 0.1875
- cotangent: bfloat16 [32, 1024, 1472], P('dp', 'ctx'), may hold values from -6 to 6
Outputs:
- layer_out: bfloat16 [32, 1024, 1472], P('dp', 'ctx')
- grad_tokens: float32 [32, 1024, 1472], P('dp', 'ctx')
- grad_soft_mask: float32 [32, 1024], P('dp', 'ctx')
- grad_gain_attn: float32 [1472], replicated
- grad_gain_ffn: float32 [1472], replicated
- grad_bias_table: float32 [32, 6], replicated
- grad_query: float32 [384, 1472], P(('dp', 'ctx'))
- grad_key: float32 [384, 1472], P(('dp', 'ctx'))
- grad_value: float32 [384, 1472], P(('dp', 'ctx'))
- grad_attn_out: float32 [384, 1472], P(('dp', 'ctx'))
- grad_gate: float32 [3584, 1472], P(('dp', 'ctx'))
- grad_up: float32 [3584, 1472], P(('dp', 'ctx'))
- grad_ffn_out: float32 [3584, 1472], P(('dp', 'ctx'))
Inputs may be any that keep to these rules, and one draw needn't show every extreme that they name: `segment_ids`: each row holds up to five documents numbered from 0 in order of position; in every aligned block of 4 rows one row, drawn from the seed, is one whole document.
All inputs are finite; a program needn't handle non-finite values.
Results may differ from a plain program's by a relative error of at most 0.017.
Values may be sent and summed in bfloat16 or wider, within the bound.
No kernel may reach another device: no remote copies, remote signals or barrier semaphores. Data moves between devices by JAX's collectives and lax.ppermute only.
A program may use at most 256 MiB of HBM per device.

v0:
```python
import jax
import jax.numpy as jnp
from jax import lax
from jax.sharding import PartitionSpec as P

NORM_EPSILON = 1e-06
MASK_VALUE = -1e30


def rms_norm(values, gain):
    return (
        values * lax.rsqrt(jnp.mean(values * values, axis=-1, keepdims=True) + NORM_EPSILON) * gain
    )


def bias_lookup(table, buckets):

    def add_bucket(bucket, running):
        return running + jnp.where(buckets[None] == bucket, table[bucket][:, None, None], 0.0)

    start_value = jnp.zeros((table.shape[1],) + buckets.shape, jnp.float32)
    return lax.fori_loop(0, table.shape[0], add_bucket, start_value)


def bucket_sums(grad_bias, buckets, bucket_count):

    def sum_bucket(bucket, running):
        picked = jnp.sum(jnp.where(buckets[None] == bucket, grad_bias, 0.0), axis=(1, 2))
        return running.at[bucket].set(picked)

    return lax.fori_loop(
        0, bucket_count, sum_bucket, jnp.zeros((bucket_count, grad_bias.shape[0]), jnp.float32)
    )


def logits_of(query_heads, key_heads, mask_row, query_segs, key_segs, pos_bias):
    scores = jnp.einsum("qhe,khe->hqk", query_heads, key_heads, preferred_element_type=jnp.float32)
    logits = scores + pos_bias + mask_row.astype(jnp.float32)[None, None, :]
    allowed = query_segs[:, None] == key_segs[None, :]
    return jnp.where(allowed[None], logits, MASK_VALUE)


def per_device(
    tokens,
    soft_mask,
    segment_ids,
    buckets,
    gain_attn,
    gain_ffn,
    bias_table,
    w_query,
    w_key,
    w_value,
    w_attn_out,
    w_gate,
    w_up,
    w_ffn_out,
    cotangent,
):
    full_len = segment_ids.shape[1]
    bucket_count, head_count = bias_table.shape
    position = lax.axis_index("ctx")
    tokens_here, grad_in, mask_here = (tokens, cotangent, soft_mask)
    query_segments = lax.dynamic_slice_in_dim(
        segment_ids, position * tokens.shape[1], tokens.shape[1], 1
    )
    row_count, local_len, model_dim = tokens_here.shape
    pos_bias = bias_lookup(bias_table, buckets)
    wq_full, wk_full, wv_full, wo_full = (
        lax.all_gather(w_query, ("dp", "ctx"), axis=0, tiled=True),
        lax.all_gather(w_key, ("dp", "ctx"), axis=0, tiled=True),
        lax.all_gather(w_value, ("dp", "ctx"), axis=0, tiled=True),
        lax.all_gather(w_attn_out, ("dp", "ctx"), axis=0, tiled=True),
    )
    inner_dim = wq_full.shape[0]
    head_size = inner_dim // head_count
    inputs = tokens_here.astype(jnp.float32)
    normed = rms_norm(inputs, gain_attn).astype(jnp.bfloat16)
    queries = jnp.einsum("rld,ed->rle", normed, wq_full, preferred_element_type=jnp.float32).astype(
        jnp.bfloat16
    )
    key_local = jnp.einsum(
        "rld,ed->rle", normed, wk_full, preferred_element_type=jnp.float32
    ).astype(jnp.bfloat16)
    value_local = jnp.einsum(
        "rld,ed->rle", normed, wv_full, preferred_element_type=jnp.float32
    ).astype(jnp.bfloat16)
    key_all, value_all, mask_all = (
        lax.all_gather(key_local, "ctx", axis=1, tiled=True),
        lax.all_gather(value_local, "ctx", axis=1, tiled=True),
        lax.all_gather(mask_here, "ctx", axis=1, tiled=True),
    )

    def forward_row(pieces):
        query_row, key_row, value_row, mask_row, query_segs, key_segs = pieces
        query_heads = query_row.reshape(local_len, head_count, head_size)
        key_heads = key_row.reshape(full_len, head_count, head_size)
        logits = logits_of(query_heads, key_heads, mask_row, query_segs, key_segs, pos_bias)
        largest = jnp.max(logits, axis=-1, keepdims=True)
        expd_vals = jnp.exp(logits - largest)
        totals = jnp.sum(expd_vals, axis=-1, keepdims=True)
        probs = (expd_vals / totals).astype(jnp.bfloat16)
        value_heads = value_row.reshape(full_len, head_count, head_size)
        result = jnp.einsum("hqk,khe->qhe", probs, value_heads, preferred_element_type=jnp.float32)
        return (result.reshape(local_len, inner_dim), (largest + jnp.log(totals))[..., 0])

    attended, log_totals = lax.map(
        forward_row, (queries, key_all, value_all, mask_all, query_segments, segment_ids)
    )
    attended = attended.astype(jnp.bfloat16)
    mixed = inputs + jnp.einsum(
        "rle,ed->rld", attended, wo_full, preferred_element_type=jnp.float32
    )
    wg_full, wu_full, wf_full = (
        lax.all_gather(w_gate, ("dp", "ctx"), axis=0, tiled=True),
        lax.all_gather(w_up, ("dp", "ctx"), axis=0, tiled=True),
        lax.all_gather(w_ffn_out, ("dp", "ctx"), axis=0, tiled=True),
    )
    normed_two = rms_norm(mixed, gain_ffn).astype(jnp.bfloat16)
    gate = jnp.einsum("rld,fd->rlf", normed_two, wg_full, preferred_element_type=jnp.float32)
    upward = jnp.einsum("rld,fd->rlf", normed_two, wu_full, preferred_element_type=jnp.float32)
    activated, gelu_back = jax.vjp(lambda values: jax.nn.gelu(values, approximate=True), gate)
    hidden = (activated * upward).astype(jnp.bfloat16)
    layer_out = (
        mixed + jnp.einsum("rlf,fd->rld", hidden, wf_full, preferred_element_type=jnp.float32)
    ).astype(jnp.bfloat16)
    wg_back, wu_back, wf_back = (
        lax.all_gather(w_gate, ("dp", "ctx"), axis=0, tiled=True),
        lax.all_gather(w_up, ("dp", "ctx"), axis=0, tiled=True),
        lax.all_gather(w_ffn_out, ("dp", "ctx"), axis=0, tiled=True),
    )
    grad_out = grad_in.astype(jnp.float32)
    grad_ffn_out = jnp.einsum("rlf,rld->fd", hidden, grad_in, preferred_element_type=jnp.float32)
    grad_hidden = jnp.einsum("rld,fd->rlf", grad_in, wf_back, preferred_element_type=jnp.float32)
    grad_gate_act = gelu_back(grad_hidden * upward)[0].astype(jnp.bfloat16)
    grad_upward = (grad_hidden * activated).astype(jnp.bfloat16)
    grad_gate = jnp.einsum(
        "rlf,rld->fd", grad_gate_act, normed_two, preferred_element_type=jnp.float32
    )
    grad_up = jnp.einsum("rlf,rld->fd", grad_upward, normed_two, preferred_element_type=jnp.float32)
    grad_normed_two = jnp.einsum(
        "rlf,fd->rld", grad_gate_act, wg_back, preferred_element_type=jnp.float32
    ) + jnp.einsum("rlf,fd->rld", grad_upward, wu_back, preferred_element_type=jnp.float32)
    norm_two_back = jax.vjp(rms_norm, mixed, gain_ffn)[1]
    grad_mixed_norm, grad_gain_ffn = norm_two_back(grad_normed_two)
    grad_mixed = grad_out + grad_mixed_norm
    grad_gate, grad_up, grad_ffn_out = (
        lax.psum_scatter(grad_gate, ("dp", "ctx"), scatter_dimension=0, tiled=True),
        lax.psum_scatter(grad_up, ("dp", "ctx"), scatter_dimension=0, tiled=True),
        lax.psum_scatter(grad_ffn_out, ("dp", "ctx"), scatter_dimension=0, tiled=True),
    )
    wq_back, wk_back, wv_back, wo_back = (
        lax.all_gather(w_query, ("dp", "ctx"), axis=0, tiled=True),
        lax.all_gather(w_key, ("dp", "ctx"), axis=0, tiled=True),
        lax.all_gather(w_value, ("dp", "ctx"), axis=0, tiled=True),
        lax.all_gather(w_attn_out, ("dp", "ctx"), axis=0, tiled=True),
    )
    grad_branch = grad_mixed.astype(jnp.bfloat16)
    grad_attn_out = jnp.einsum(
        "rle,rld->ed", attended, grad_branch, preferred_element_type=jnp.float32
    )
    grad_attended = jnp.einsum(
        "rld,ed->rle", grad_branch, wo_back, preferred_element_type=jnp.float32
    ).astype(jnp.bfloat16)

    def backward_row(grad_bias, pieces):
        query_row, key_row, value_row, mask_row, query_segs, key_segs, log_row, grad_row = pieces
        query_heads = query_row.reshape(local_len, head_count, head_size)
        key_heads = key_row.reshape(full_len, head_count, head_size)
        value_heads = value_row.reshape(full_len, head_count, head_size)
        grad_heads = grad_row.reshape(local_len, head_count, head_size)
        logits = logits_of(query_heads, key_heads, mask_row, query_segs, key_segs, pos_bias)
        probs = jnp.exp(logits - log_row[..., None])
        grad_val_row = jnp.einsum(
            "hqk,qhe->khe",
            probs.astype(jnp.bfloat16),
            grad_heads,
            preferred_element_type=jnp.float32,
        )
        grad_probs = jnp.einsum(
            "qhe,khe->hqk", grad_heads, value_heads, preferred_element_type=jnp.float32
        )
        grad_logits = probs * (grad_probs - jnp.sum(probs * grad_probs, axis=-1, keepdims=True))
        low_logits = grad_logits.astype(jnp.bfloat16)
        grad_query_row = jnp.einsum(
            "hqk,khe->qhe", low_logits, key_heads, preferred_element_type=jnp.float32
        )
        grad_key_row = jnp.einsum(
            "hqk,qhe->khe", low_logits, query_heads, preferred_element_type=jnp.float32
        )
        grad_mask_row = jnp.sum(grad_logits, axis=(0, 1))
        return (
            grad_bias + grad_logits,
            (
                grad_query_row.reshape(local_len, inner_dim),
                grad_key_row.reshape(full_len, inner_dim),
                grad_val_row.reshape(full_len, inner_dim),
                grad_mask_row,
            ),
        )

    bias_start = jnp.zeros((head_count, local_len, full_len), jnp.float32)
    grad_bias_full, (grad_queries, grad_keys_all, grad_values_all, grad_mask_all) = lax.scan(
        backward_row,
        bias_start,
        (
            queries,
            key_all,
            value_all,
            mask_all,
            query_segments,
            segment_ids,
            log_totals,
            grad_attended,
        ),
    )
    grad_keys, grad_values, grad_soft_mask = (
        lax.psum_scatter(
            grad_keys_all.astype(jnp.bfloat16), "ctx", scatter_dimension=1, tiled=True
        ).astype(jnp.float32),
        lax.psum_scatter(
            grad_values_all.astype(jnp.bfloat16), "ctx", scatter_dimension=1, tiled=True
        ).astype(jnp.float32),
        lax.psum_scatter(
            grad_mask_all.astype(jnp.bfloat16), "ctx", scatter_dimension=1, tiled=True
        ).astype(jnp.float32),
    )
    grad_queries = grad_queries.astype(jnp.bfloat16)
    grad_keys = grad_keys.astype(jnp.bfloat16)
    grad_values = grad_values.astype(jnp.bfloat16)
    grad_query = jnp.einsum("rle,rld->ed", grad_queries, normed, preferred_element_type=jnp.float32)
    grad_key = jnp.einsum("rle,rld->ed", grad_keys, normed, preferred_element_type=jnp.float32)
    grad_value = jnp.einsum("rle,rld->ed", grad_values, normed, preferred_element_type=jnp.float32)
    grad_normed = (
        jnp.einsum("rle,ed->rld", grad_queries, wq_back, preferred_element_type=jnp.float32)
        + jnp.einsum("rle,ed->rld", grad_keys, wk_back, preferred_element_type=jnp.float32)
        + jnp.einsum("rle,ed->rld", grad_values, wv_back, preferred_element_type=jnp.float32)
    )
    norm_one_back = jax.vjp(rms_norm, inputs, gain_attn)[1]
    grad_input_norm, grad_gain_attn = norm_one_back(grad_normed)
    grad_tokens = grad_mixed + grad_input_norm
    grad_table = bucket_sums(grad_bias_full, buckets, bucket_count)
    grad_gain_attn, grad_gain_ffn, grad_bias_table = lax.psum(
        (grad_gain_attn, grad_gain_ffn, grad_table), ("dp", "ctx")
    )
    grad_query, grad_key, grad_value, grad_attn_out = (
        lax.psum_scatter(grad_query, ("dp", "ctx"), scatter_dimension=0, tiled=True),
        lax.psum_scatter(grad_key, ("dp", "ctx"), scatter_dimension=0, tiled=True),
        lax.psum_scatter(grad_value, ("dp", "ctx"), scatter_dimension=0, tiled=True),
        lax.psum_scatter(grad_attn_out, ("dp", "ctx"), scatter_dimension=0, tiled=True),
    )
    return (
        layer_out,
        grad_tokens,
        grad_soft_mask,
        grad_gain_attn,
        grad_gain_ffn,
        grad_bias_table,
        grad_query,
        grad_key,
        grad_value,
        grad_attn_out,
        grad_gate,
        grad_up,
        grad_ffn_out,
    )


def solution(mesh):
    in_specs = (
        P("dp", "ctx", None),
        P("dp", "ctx"),
        P("dp", None),
        P("ctx", None),
        P(),
        P(),
        P(),
        P(("dp", "ctx"), None),
        P(("dp", "ctx"), None),
        P(("dp", "ctx"), None),
        P(("dp", "ctx"), None),
        P(("dp", "ctx"), None),
        P(("dp", "ctx"), None),
        P(("dp", "ctx"), None),
        P("dp", "ctx", None),
    )
    out_specs = (
        P("dp", "ctx", None),
        P("dp", "ctx", None),
        P("dp", "ctx"),
        P(),
        P(),
        P(),
        P(("dp", "ctx"), None),
        P(("dp", "ctx"), None),
        P(("dp", "ctx"), None),
        P(("dp", "ctx"), None),
        P(("dp", "ctx"), None),
        P(("dp", "ctx"), None),
        P(("dp", "ctx"), None),
    )
    return jax.shard_map(
        per_device, mesh=mesh, in_specs=in_specs, out_specs=out_specs, check_vma=False
    )
```

profile of v0, /device:TPU:0, one launch (start us, length us, event | category | flops | bytes accessed | tf_op | source)
XLA Modules:
  0.0 1668.1 jit_solution(14250123356103758474)
XLA Ops:
  13.1 55.5 %all-gather.24.cloned.1.call-done = bf16[32,12,1472]{2,1,0:T(8,128)(2,1)} async-done(((bf16[1,12,1472]{2,1,0:T(8,128)(2,1)}), bf16[32,12,1472]{2,1,0:T(8,128)(2,1)}) %all-gather.24.cloned.1.call-update) | async-done | bytes 1130512 | tf_op jit(solution)/shard_map/all_gather | solution.py:72
  76.4 48.8 %all-gather.28.cloned.1.call-done = bf16[32,12,1472]{2,1,0:T(8,128)(2,1)} async-done(((bf16[1,12,1472]{2,1,0:T(8,128)(2,1)}), bf16[32,12,1472]{2,1,0:T(8,128)(2,1)}) %all-gather.28.cloned.1.call-update) | async-done | bytes 1130512 | tf_op jit(solution)/shard_map/all_gather | solution.py:71
  135.5 227.5 %while.61 = (s32[]{:T(128)}, f32[6,256,1024]{2,1,0:T(8,128)}, s32[256,1024]{1,0:T(8,128)S(1)}, f32[32,6]{1,0:T(8,128)S(1)}, s32[]{:T(128)}, /*index=5*/s32[]{:T(128)}) while((s32[]{:T(128)}, f32[6,256,1024]{2,1,0:T(8,128)}, s32[256,1024]{1,0:T(8,128)S(1)}, f32[32,6]{1,0:T(8,128)S(1)}, s32[]{:T(128)}, /*index=5*/s32[]{:T(128)}) %tuple.172), condition=%wide.region_2.3_spmd.clone, body=%wide.region_1.2_spmd.clone.sunk | while | flops 4980739 | bytes 14155935 | solution.py:22
  390.2 45.9 %while.59 = (s32[]{:T(128)}, bf16[4,256,384]{1,2,0:T(8,128)(2,1)}, f32[4,6,256]{2,1,0:T(8,128)}, bf16[4,1024,384]{1,2,0:T(8,128)(2,1)}, s32[4,256]{1,0:T(4,128)S...) while((s32[]{:T(128)}, bf16[4,256,384]{1,2,0:T(8,128)(2,1)}, ...), condition=%wide.region_6.7_spmd, body=%wide.region_3.6_spmd.sunk | while | flops 417070592 | bytes 31666304 | solution.py:107
  443.1 19.1 %fusion.25 = f32[4,256,3584]{2,1,0:T(8,128)} fusion(bf16[4,256,1472]{1,2,0:T(8,128)(2,1)S(1)} %multiply_convert_fusion.2, bf16[3584,1472]{1,0:T(8,128)(2,1)} %all-gather.20.cloned.1.call-done), kind=kOutput, calls=%fused_computation.69 | convolution fusion | flops 10804527104 | bytes 28246016 | tf_op jit(solution)/shard_map/rld,fd->rlf/dot_general | solution.py:121
  462.2 18.5 %all-gather.22.cloned.1.call-done = bf16[3584,1472]{1,0:T(8,128)(2,1)} async-done(((bf16[112,1472]{1,0:T(8,128)(2,1)}), bf16[3584,1472]{1,0:T(8,128)(2,1)}) %all-gather.22.cloned.1.call-update) | async-done | bytes 10551312 | tf_op jit(solution)/shard_map/all_gather | solution.py:117
  480.7 18.5 %fusion.19 = f32[4,256,3584]{2,1,0:T(8,128)} fusion(bf16[4,256,1472]{1,2,0:T(8,128)(2,1)} %param.39, bf16[3584,1472]{1,0:T(8,128)(2,1)} %all-gather.22.cloned.1.call-done), kind=kOutput, calls=%fused_computation.63 | convolution fusion | flops 10804527104 | bytes 28246016 | tf_op jit(solution)/shard_map/rld,fd->rlf/dot_general | solution.py:134
  499.2 71.8 %all-gather.18.cloned.1.call-done = bf16[3584,1472]{1,0:T(8,128)(2,1)} async-done(((bf16[112,1472]{1,0:T(8,128)(2,1)}), bf16[3584,1472]{1,0:T(8,128)(2,1)}) %all-gather.18.cloned.1.call-update) | async-done | bytes 10551312 | tf_op jit(solution)/shard_map/all_gather | solution.py:115
  571.0 30.3 %fusion.18 = (bf16[4,256,3584]{2,1,0:T(8,128)(2,1)}, bf16[4,256,3584]{2,1,0:T(8,128)(2,1)S(1)}, bf16[4,256,3584]{2,1,0:T(8,128)(2,1)}) fusion(f32[4,256,3584]{2,1,0:T(8,128)} %fusion.19, f32[4,256,3584]{2,1,0:T(8,128)} %fusion.25, bf16[4,256,1472]{1,2,0:T(8,128)(2,1)S(1)} %multiply_convert_fusion.2, bf16[3584,1472]{1,0:T(8,128)(2,1)} %all-gather.18.cloned.1.call-done), kind=kOutput, calls=%fused_computation.54 | convolution fusion | flops 10899947520 | bytes 64946176 | tf_op jit(solution)/shard_map/rld,fd->rlf/dot_general | solution.py:120
  601.3 18.0 %fusion.23 = f32[4,256,1472]{1,2,0:T(8,128)} fusion(bf16[4,256,3584]{2,1,0:T(8,128)(2,1)S(1)} %get-tuple-element.578, bf16[3584,1472]{1,0:T(8,128)(2,1)} %all-gather.20.cloned.1.call-done), kind=kOutput, calls=%fused_computation.67 | convolution fusion | flops 10804527104 | bytes 23920640 | tf_op jit(solution)/shard_map/rlf,fd->rld/dot_general | solution.py:143
  619.3 19.5 %multiply_reduce_fusion.1 = (f32[1472]{0:T(1024)}, f32[4,256]{1,0:T(4,128)S(1)}, f32[4,256,1472]{1,2,0:T(8,128)S(1)}) fusion(f32[4,256,1472]{1,2,0:T(8,128)} %copy-done.5, f32[4,256]{1,0:T(4,128)S(1)} %fusion.65, f32[1472]{0:T(1024)S(1)} %copy-done.51, f32[4,256,1472]{1,2,0:T(8,128)} %fusion.23, bf16[4,256,3584]{2,1,0:T(8,128)(2,1)} %get-tuple-element.577, ...), kind=kOutput, calls=%fused_computation.85 | convolution fusion | flops 10815076352 | bytes 35999232 | tf_op jit(solution)/shard_map/rlf,fd->rld/dot_general | solution.py:141
  649.8 148.8 %while.62 = (s32[]{:T(128)}, f32[6,256,1024]{2,1,0:T(8,128)}, bf16[4,256,384]{1,2,0:T(8,128)(2,1)}, bf16[4,1024,384]{1,2,0:T(8,128)(2,1)}, bf16[4,1024,384]{1,2,...) while((s32[]{:T(128)}, f32[6,256,1024]{2,1,0:T(8,128)}, ...), condition=%wide.region_12.13_spmd.clone, body=%wide.region_9.12_spmd.clone.sunk | while | flops 1028913664 | bytes 208408976 | solution.py:203
  711.9 9.7 select_add_fusion.5
  749.5 9.7 select_add_fusion.5
  787.1 9.7 select_add_fusion.5
  800.5 18.8 %convolution_bitcast_fusion.2 = f32[3584,1472]{1,0:T(8,128)} fusion(bf16[4,256,3584]{2,1,0:T(8,128)(2,1)} %get-tuple-element.577, bf16[4,256,1472]{1,2,0:T(8,128)(2,1)S(1)} %copy-done.18), kind=kOutput, calls=%fused_computation.47 | convolution fusion | flops 10804527104 | bytes 31457280 | tf_op jit(solution)/shard_map/rlf,rld->fd/dot_general | solution.py:137
  819.4 18.0 %convolution_bitcast_fusion.1 = f32[3584,1472]{1,0:T(8,128)} fusion(bf16[4,256,3584]{2,1,0:T(8,128)(2,1)} %copy-done.59, bf16[4,256,1472]{1,2,0:T(8,128)(2,1)S(1)} %copy-done.18), kind=kOutput, calls=%fused_computation.46 | convolution fusion | flops 10804527104 | bytes 31457280 | tf_op jit(solution)/shard_map/rlf,rld->fd/dot_general | solution.py:140
  849.9 18.1 %convolution_bitcast_fusion = f32[3584,1472]{1,0:T(8,128)} fusion(bf16[4,256,3584]{2,1,0:T(8,128)(2,1)} %get-tuple-element.579, bf16[4,256,1472]{1,2,0:T(8,128)(2,1)S(1)} %copy-done.19), kind=kOutput, calls=%fused_computation.45 | convolution fusion | flops 10804527104 | bytes 31457280 | tf_op jit(solution)/shard_map/rlf,rld->fd/dot_general | solution.py:133
  880.0 165.0 %fusion.72 = (f32[16,1472]{1,0:T(8,128)S(1)}, f32[16,1472]{1,0:T(8,128)S(1)}, f32[16,1472]{1,0:T(8,128)S(1)}, f32[16,1472]{1,0:T(8,128)S(1)}) fusion(f32[384,1472]{1,0:T(8,128)} %convolution_bitcast_fusion.6, f32[384,1472]{1,0:T(8,128)} %convolution_bitcast_fusion.5, f32[384,1472]{1,0:T(8,128)} %convolution_bitcast_fusion.4, ...), kind=kCustom, calls=%all-reduce-scatter.4 | all-reduce-scatter fusion | flops 3014657 | bytes 9420800
  1045.1 12.3 collective-permute-start.31
  1064.5 179.0 %while.60 = (s32[]{:T(128)}, f32[32,6]{1,0:T(8,128)S(1)}, s32[256,1024]{1,0:T(8,128)S(1)}, f32[6,256,1024]{2,1,0:T(8,128)}, s32[]{:T(128)}, /*index=5*/s32[2]{0:T(128)S(1)}, s32[1]{0:T(128)}, s32[]{:T(128)}) while((s32[]{:T(128)}, f32[32,6]{1,0:T(8,128)S(1)}, s32[256,1024]{1,0:T(8,128)S(1)}, f32[6,256,1024]{2,1,0:T(8,128)}, s32[]{:T(128)}, ...), condition=%wide.region_24.25_spmd, body=%wide.region_21.24_spmd.sunk | while | flops 3407883 | bytes 7864579 | solution.py:31
  1254.6 19.3 %add_convert_fusion = bf16[4,256,1472]{1,2,0:T(8,128)(2,1)} fusion(f32[4,256,1472]{1,2,0:T(8,128)} %copy-done.5, bf16[4,256,3584]{2,1,0:T(8,128)(2,1)} %get-tuple-element.579, bf16[3584,1472]{1,0:T(8,128)(2,1)} %all-gather.22.cloned.1.call-done), kind=kOutput, calls=%fused_computation.88 | convolution fusion | flops 10807541760 | bytes 26935296 | tf_op jit(solution)/shard_map/rlf,fd->rld/dot_general | solution.py:125
  1365.3 40.5 %all-reduce.8 = (f32[1472]{0:T(1024)}, f32[1472]{0:T(1024)}, f32[32,6]{0,1:T(8,128)}) all-reduce(f32[1472]{0:T(1024)S(1)} %get-tuple-element.488, f32[1472]{0:T(1024)S(1)} %copy-done.56, f32[32,6]{0,1:T(8,128)S(1)} %copy.92), channel_id=1, replica_groups=mesh['dp'=8,'ctx'=4] {'dp','ctx'}, use_global_device_ids=true, to_apply=%region_18.19 | all-reduce | flops 3136 | bytes 25088 | tf_op jit(solution)/shard_map/psum | solution.py:243
  1440.5 220.6 %reduce-scatter.25.cloned.1.call-done = f32[112,1472]{1,0:T(8,128)} async-done(((f32[3584,1472]{1,0:T(8,128)}), f32[112,1472]{1,0:T(8,128)}) %reduce-scatter.25.cloned.1.call-update) | async-done | bytes 659472 | tf_op jit(solution)/shard_map/reduce_scatter | solution.py:150
  (718 shorter events, 808.1 us)
Async XLA Ops:
  7.2 61.4 %all-gather.24.cloned.1.call-start = ((), (), s32[]{:S(2)}) async-start(), calls=%async_computation.16 | async-start | bytes 1622016 | tf_op jit(solution)/shard_map/all_gather | solution.py:72
  7.9 117.3 %all-gather.28.cloned.1.call-start = ((), (), s32[]{:S(2)}) async-start(), calls=%async_computation.18 | async-start | bytes 1622016 | tf_op jit(solution)/shard_map/all_gather | solution.py:71
  8.7 359.8 %all-gather.26.cloned.1.call-start = ((), (), s32[]{:S(2)}) async-start(), calls=%async_computation.17 | async-start | bytes 1622016 | tf_op jit(solution)/shard_map/all_gather | solution.py:70
  9.4 367.3 %all-gather.30.cloned.1.call-start = ((), (), s32[]{:S(2)}) async-start(), calls=%async_computation.19 | async-start | bytes 1622016 | tf_op jit(solution)/shard_map/all_gather | solution.py:73
  10.0 370.0 %all-gather.14.cloned.1.call-start = ((), (), s32[]{:S(2)}) async-start(), calls=%async_computation.6 | async-start | bytes 3932160 | tf_op jit(solution)/shard_map/all_gather | solution.py:90
  76.4 308.2 %all-gather.16.cloned.1.call-start = ((), (), s32[]{:S(2)}) async-start(), calls=%async_computation.7 | async-start | bytes 3932160 | tf_op jit(solution)/shard_map/all_gather | solution.py:89
  133.1 309.9 %all-gather.20.cloned.1.call-start = ((), (), s32[]{:S(2)}) async-start(), calls=%async_computation.9 | async-start | bytes 11354112 | tf_op jit(solution)/shard_map/all_gather | solution.py:116
  133.9 346.8 %all-gather.22.cloned.1.call-start = ((), (), s32[]{:S(2)}) async-start(), calls=%async_computation.10 | async-start | bytes 11354112 | tf_op jit(solution)/shard_map/all_gather | solution.py:117
  134.6 436.4 %all-gather.18.cloned.1.call-start = ((), (), s32[]{:S(2)}) async-start(), calls=%async_computation.8 | async-start | bytes 11354112 | tf_op jit(solution)/shard_map/all_gather | solution.py:115
  135.4 732.7 %reduce-scatter.19.cloned.1.call-start = ((), (), s32[]{:S(2)}) async-start(), calls=%async_computation.12 | async-start | bytes 3932160 | tf_op jit(solution)/shard_map/reduce_scatter | solution.py:221
  798.7 77.2 %reduce-scatter.17.cloned.1.call-start = ((), (), s32[]{:S(2)}) async-start(), calls=%async_computation.11 | async-start | bytes 3932160 | tf_op jit(solution)/shard_map/reduce_scatter | solution.py:218
  799.4 492.7 %reduce-scatter.27.cloned.1.call-start = ((), (), s32[]{:S(2)}) async-start(), calls=%async_computation.20 | async-start | bytes 327680
  800.3 640.2 %reduce-scatter.21.cloned.1.call-start = ((), (), s32[]{:S(2)}) async-start(), calls=%async_computation.13 | async-start | bytes 22708224 | tf_op jit(solution)/shard_map/reduce_scatter | solution.py:148
  819.3 621.2 %reduce-scatter.23.cloned.1.call-start = ((), (), s32[]{:S(2)}) async-start(), calls=%async_computation.14 | async-start | bytes 22708224 | tf_op jit(solution)/shard_map/reduce_scatter | solution.py:149
  837.4 823.7 %reduce-scatter.25.cloned.1.call-start = ((), (), s32[]{:S(2)}) async-start(), calls=%async_computation.15 | async-start | bytes 22708224 | tf_op jit(solution)/shard_map/reduce_scatter | solution.py:150
  1045.1 202.4 %collective-permute-start.31 = (f32[12,1472]{1,0:T(8,128)S(1)}, f32[12,1472]{1,0:T(8,128)S(1)}, u32[]{:S(2)}, u32[]{:S(2)}) collective-permute-start(f32[12,1472]{1,0:T(8,128)S(1)} %slice.29), channel_id=1, source_target_pairs={{0,8},{1,9},{2,10},{3,11},{4,12},{5,13},{6,14},{7,15},{8,16},{9,17... | collective-permute-start | bytes 211976
  1057.4 195.2 %collective-permute-start.23 = (f32[12,1472]{1,0:T(8,128)S(1)}, f32[12,1472]{1,0:T(8,128)S(1)}, u32[]{:S(2)}, u32[]{:S(2)}) collective-permute-start(f32[12,1472]{1,0:T(8,128)S(1)} %slice.28), channel_id=1, source_target_pairs={{0,8},{1,9},{2,10},{3,11},{4,12},{5,13},{6,14},{7,15},{8,16},{9,17... | collective-permute-start | bytes 211976
  1244.8 38.0 %collective-permute-start.25 = (f32[16,1472]{1,0:T(8,128)S(1)}, f32[16,1472]{1,0:T(8,128)S(1)}, u32[]{:S(2)}, u32[]{:S(2)}) collective-permute-start(f32[16,1472]{1,0:T(8,128)S(1)} %get-tuple-element.566), channel_id=1, source_target_pairs={{0,2},{1,3},{2,4},{3,5},{4,6},{5,7},{6,8},{7,9},{8,10},{9,11},{10,... | collective-permute-start | bytes 282632
  1246.1 39.2 %collective-permute-start.26 = (f32[16,1472]{1,0:T(8,128)S(1)}, f32[16,1472]{1,0:T(8,128)S(1)}, u32[]{:S(2)}, u32[]{:S(2)}) collective-permute-start(f32[16,1472]{1,0:T(8,128)S(1)} %get-tuple-element.566), channel_id=1, source_target_pairs={{0,3},{1,4},{2,5},{3,6},{4,7},{5,8},{6,9},{7,10},{8,11},{9,12},{10... | collective-permute-start | bytes 282632
  1349.9 79.1 %collective-permute-start.2 = (f32[16,1472]{1,0:T(8,128)S(1)}, f32[16,1472]{1,0:T(8,128)}, u32[]{:S(2)}, u32[]{:S(2)}) collective-permute-start(f32[16,1472]{1,0:T(8,128)S(1)} %get-tuple-element.563), channel_id=1, source_target_pairs={{0,3},{1,4},{2,5},{3,6},{4,7},{5,8},{6,9},{7,10},{8,11},{9,12},{10... | collective-permute-start | bytes 282632
  1353.7 75.3 %collective-permute-start.3 = (f32[16,1472]{1,0:T(8,128)S(1)}, f32[16,1472]{1,0:T(8,128)}, u32[]{:S(2)}, u32[]{:S(2)}) collective-permute-start(f32[16,1472]{1,0:T(8,128)S(1)} %get-tuple-element.563), channel_id=1, source_target_pairs={{0,4},{1,5},{2,6},{3,7},{4,8},{5,9},{6,10},{7,11},{8,12},{9,13},{1... | collective-permute-start | bytes 282632
  1355.8 73.2 %collective-permute-start.4 = (f32[16,1472]{1,0:T(8,128)S(1)}, f32[16,1472]{1,0:T(8,128)}, u32[]{:S(2)}, u32[]{:S(2)}) collective-permute-start(f32[16,1472]{1,0:T(8,128)S(1)} %get-tuple-element.563), channel_id=1, source_target_pairs={{0,5},{1,6},{2,7},{3,8},{4,9},{5,10},{6,11},{7,12},{8,13},{9,14},{... | collective-permute-start | bytes 282632
  1357.8 71.3 %collective-permute-start.5 = (f32[16,1472]{1,0:T(8,128)S(1)}, f32[16,1472]{1,0:T(8,128)}, u32[]{:S(2)}, u32[]{:S(2)}) collective-permute-start(f32[16,1472]{1,0:T(8,128)S(1)} %get-tuple-element.563), channel_id=1, source_target_pairs={{0,6},{1,7},{2,8},{3,9},{4,10},{5,11},{6,12},{7,13},{8,14},{9,15},... | collective-permute-start | bytes 282632
  1359.7 69.3 %collective-permute-start.6 = (f32[16,1472]{1,0:T(8,128)S(1)}, f32[16,1472]{1,0:T(8,128)}, u32[]{:S(2)}, u32[]{:S(2)}) collective-permute-start(f32[16,1472]{1,0:T(8,128)S(1)} %get-tuple-element.563), channel_id=1, source_target_pairs={{0,7},{1,8},{2,9},{3,10},{4,11},{5,12},{6,13},{7,14},{8,15},{9,16}... | collective-permute-start | bytes 282632
  (110 other events, 3233.9 us)
Sparse Core Ops, SparseCore 0:
  10.9 57.6 all-gather.23
  71.4 53.8 all-gather.27
  128.1 53.8 all-gather.25
  184.7 53.8 all-gather.29
  240.5 27.4 all-gather.13
  270.0 28.5 all-gather.15
  301.4 88.9 all-gather.19
  393.4 87.3 all-gather.21
  483.6 87.3 all-gather.17
  798.8 36.3 reduce-scatter.18
  837.9 37.9 reduce-scatter.16
  878.2 22.1 reduce-scatter.26
  908.5 250.7 reduce-scatter.20
  1167.3 262.2 reduce-scatter.22
  1437.5 223.5 reduce-scatter.24
where the time goes:
time: 1680 us; the launch traced here: 1670 us
  other arithmetic  484 us (29%)
  waiting for transfers between devices  425 us (25%)
  matrix products  290 us (17%)
  blocking collectives  211 us (13%)
  local copies, waits for them, and re-layouts  138 us (8%)
  starting transfers between devices  103 us (6%)
    add x32, other arithmetic, add_bucket(): running + jnp.where(buckets[None] == bucket, table[bucket][:, None, None]...  222 us
    reduce_scatter x1, waiting for transfers between devices, per_device(): lax.psum_scatter(grad_ffn_out, ('dp', 'ctx'), scatter_dimension=0, tiled=...  221 us
    unnamed x1, blocking collectives  165 us
    reduce_sum x32, other arithmetic, sum_bucket(): jnp.sum(jnp.where(buckets[None] == bucket, grad_bias, 0.0), axis=(1, 2))  129 us
    unnamed x33, starting transfers between devices  102 us
    all_gather x1, waiting for transfers between devices, per_device(): lax.all_gather(w_gate, ('dp', 'ctx'), axis=0, tiled=True)  71.8 us
    all_gather x1, waiting for transfers between devices, per_device(): lax.all_gather(w_value, ('dp', 'ctx'), axis=0, tiled=True)  55.5 us
    unnamed x137, local copies, waits for them, and re-layouts  54.8 us
  transfers between devices with their start and end apart: 47, of which 6 were waited for; matrix products, arithmetic and copies ran while one was open for 51% of the time, Pallas kernels for 0%

commit v1 on v0

v1 whole, which is shorter than its diff:
```python
import functools

import jax
import jax.numpy as jnp
import numpy as np
from jax import lax
from jax.experimental import pallas as pl
from jax.experimental.pallas import tpu as pltpu
from jax.sharding import PartitionSpec as P

NORM_EPSILON = 1e-06
MASK_VALUE = -1e30
F32, BF16 = jnp.float32, jnp.bfloat16
HEAD = 64
ROW_TILE = 16
AUG = 16
DOCS = 5
ONES = 1 + DOCS
VMEM_LIMIT = 58 * 1024 * 1024
PARAMS = pltpu.CompilerParams(vmem_limit_bytes=VMEM_LIMIT)


def dot(a, b, ca, cb):
    return lax.dot_general(a, b, (((ca,), (cb,)), ((), ())), preferred_element_type=F32)


def whole(shape):
    return pl.BlockSpec(shape, lambda t: (0,) * len(shape), pipeline_mode=pl.Buffered(1))


def cost(flops, nbytes):
    return pl.CostEstimate(flops=int(flops), bytes_accessed=int(nbytes), transcendentals=0)


def norm_body(x_ref, gain_ref, n_ref):
    x = x_ref[0].astype(F32)
    scale = lax.rsqrt(jnp.mean(x * x, axis=0, keepdims=True) + NORM_EPSILON)
    n_ref[...] = (x * scale * gain_ref[...]).astype(BF16)


def first_norm(x, gain):
    rows, width, size = x.shape
    return pl.pallas_call(
        norm_body,
        grid=(rows,),
        in_specs=[pl.BlockSpec((1, width, size), lambda r: (r, 0, 0)), whole(gain.shape)],
        out_specs=pl.BlockSpec((width, size), lambda r: (0, r)),
        out_shape=jax.ShapeDtypeStruct((width, rows * size), BF16),
        compiler_params=PARAMS,
        name="first_norm",
        cost_estimate=cost(4 * x.size, 4 * x.size),
    )(x, gain)


def key_value_body(inner, n_ref, wk_ref, wv_ref, pk_ref, pv_ref, aug_ref, out_ref):
    n = n_ref[...]
    for start, w_ref, p_ref in ((0, wk_ref, pk_ref), (inner, wv_ref, pv_ref)):
        mixed_up = dot(w_ref[...], n, 1, 0).astype(BF16)
        out_ref[0, start : start + inner] = dot(p_ref[...], mixed_up, 1, 0).astype(BF16)
    out_ref[0, 2 * inner :] = aug_ref[0]


def key_value(n, wk, wv, place_k, place_v, aug):
    rows, _, size = aug.shape
    inner = place_k.shape[0]
    width = n.shape[0]
    return pl.pallas_call(
        functools.partial(key_value_body, inner),
        grid=(rows,),
        in_specs=[
            pl.BlockSpec((width, size), lambda r: (0, r)),
            whole(wk.shape),
            whole(wv.shape),
            whole(place_k.shape),
            whole(place_v.shape),
            pl.BlockSpec((1, AUG, size), lambda r: (r, 0, 0)),
        ],
        out_specs=pl.BlockSpec((1, 2 * inner + AUG, size), lambda r: (r, 0, 0)),
        out_shape=jax.ShapeDtypeStruct((rows, 2 * inner + AUG, size), BF16),
        compiler_params=PARAMS,
        name="key_value",
        cost_estimate=cost(4 * wk.size * rows * size, 4 * wk.size + 2 * n.size),
    )(n, wk, wv, place_k, place_v, aug)


def attend_body(heads, inner, q_ref, u_ref, *refs):
    *blocks, bias_ref, o_ref, lse_ref, s_ref = refs
    for h in range(heads):
        part = slice(h * HEAD, (h + 1) * HEAD)
        q = jnp.concatenate([q_ref[part], u_ref[0]], axis=0)
        top = None
        for s, k_ref in enumerate(blocks):
            k = jnp.concatenate([k_ref[0, part], k_ref[0, 2 * inner :]], axis=0)
            logits = dot(k, q, 0, 0) + bias_ref[h, s]
            s_ref[s] = logits
            peak = jnp.max(logits, axis=0, keepdims=True)
            top = peak if top is None else jnp.maximum(top, peak)
        total, out = None, None
        for s, k_ref in enumerate(blocks):
            e = jnp.exp(s_ref[s] - top)
            part_sum = jnp.sum(e, axis=0, keepdims=True)
            total = part_sum if total is None else total + part_sum
            value = k_ref[0, slice(inner + h * HEAD, inner + (h + 1) * HEAD)]
            term = dot(value, e.astype(BF16), 1, 0)
            out = term if out is None else out + term
        o_ref[part] = (out / total).astype(BF16)
        lse_ref[0, h : h + 1] = top + jnp.log(total)
    pad = lse_ref.shape[1] - heads
    if pad:
        lse_ref[0, heads:] = jnp.zeros((pad, lse_ref.shape[2]), F32)


def attend(qt, u, kv, bias, heads):
    rows, depth, size = kv[0].shape
    inner = heads * HEAD
    pad = -(-heads // 8) * 8
    return pl.pallas_call(
        functools.partial(attend_body, heads, inner),
        grid=(rows,),
        in_specs=[
            pl.BlockSpec((inner, size), lambda r: (0, r)),
            pl.BlockSpec((1, AUG, size), lambda r: (r, 0, 0)),
        ]
        + [pl.BlockSpec((1, depth, size), lambda r: (r, 0, 0))] * len(kv)
        + [whole(bias.shape)],
        out_specs=[
            pl.BlockSpec((inner, size), lambda r: (0, r)),
            pl.BlockSpec((1, pad, size), lambda r: (r, 0, 0)),
        ],
        out_shape=[
            jax.ShapeDtypeStruct((inner, rows * size), BF16),
            jax.ShapeDtypeStruct((rows, pad, size), F32),
        ],
        scratch_shapes=[pltpu.VMEM((len(kv), size, size), F32)],
        compiler_params=PARAMS,
        name="attend",
        cost_estimate=cost(16 * rows * heads * len(kv) * size * size * HEAD, 40_000_000),
    )(qt, u, *kv, bias)


def three(x):
    a = x.astype(BF16).astype(F32)
    rest = x - a
    b = rest.astype(BF16).astype(F32)
    return a, b, rest - b


def attend_back_body(heads, inner, count, q_ref, u_ref, *refs):
    blocks = refs[:count]
    bias_ref, o_ref, do_ref, lse_ref, dq_ref = refs[count : count + 5]
    grads = refs[count + 5 : 2 * count + 5]
    gb_ref = refs[2 * count + 5]
    size = bias_ref.shape[3]
    row = pl.program_id(0)
    mask_grad = [None] * count
    extra = u_ref[0].astype(F32)
    place = lax.broadcasted_iota(jnp.int32, (AUG, size), 0)

    def pick(parts, base):
        for i, value in enumerate(parts):
            base = jnp.where(place == ONES + i, value, base)
        return base.astype(BF16)

    for h in range(heads):
        part = slice(h * HEAD, (h + 1) * HEAD)
        vpart = slice(inner + h * HEAD, inner + (h + 1) * HEAD)
        q = q_ref[part]
        do = do_ref[part]
        delta = jnp.sum(do.astype(F32) * o_ref[part].astype(F32), axis=0, keepdims=True)
        q_aug = jnp.concatenate([q, pick(three(-lse_ref[0, h : h + 1]), extra)], axis=0)
        do_aug = jnp.concatenate([do, pick(three(-delta), jnp.zeros_like(extra))], axis=0)
        dq = None
        for s, k_ref in enumerate(blocks):
            k = k_ref[0, part]
            aug = k_ref[0, 2 * inner :]
            logits = dot(jnp.concatenate([k, aug], axis=0), q_aug, 0, 0) + bias_ref[h, s]
            p = jnp.exp(logits)
            dp = dot(jnp.concatenate([k_ref[0, vpart], aug], axis=0), do_aug, 0, 0)
            ds = p * dp

            @pl.when(row == 0)
            def _():
                gb_ref[h, s] = ds

            @pl.when(row > 0)
            def _():
                gb_ref[h, s] += ds

            low = ds.astype(BF16)
            grads[s][0, vpart] = dot(do, p.astype(BF16), 1, 1).astype(BF16)
            both = dot(q_aug, low, 1, 1)
            grads[s][0, part] = both[:HEAD].astype(BF16)
            g = both[HEAD : HEAD + 1]
            mask_grad[s] = g if mask_grad[s] is None else mask_grad[s] + g
            term = dot(k, low, 1, 0)
            dq = term if dq is None else dq + term
        dq_ref[part] = dq.astype(BF16)
    for s in range(count):
        grads[s][0, 2 * inner :] = jnp.broadcast_to(mask_grad[s], (AUG, size)).astype(BF16)


def attend_back(qt, u, kv, bias, ot, dot_t, lse, heads):
    rows, depth, size = kv[0].shape
    inner = heads * HEAD
    count = len(kv)
    col = pl.BlockSpec((inner, size), lambda r: (0, r))
    block = pl.BlockSpec((1, depth, size), lambda r: (r, 0, 0))
    out = pl.pallas_call(
        functools.partial(attend_back_body, heads, inner, count),
        grid=(rows,),
        in_specs=[col, pl.BlockSpec((1, AUG, size), lambda r: (r, 0, 0))]
        + [block] * count
        + [whole(bias.shape), col, col]
        + [pl.BlockSpec((1,) + lse.shape[1:], lambda r: (r, 0, 0))],
        out_specs=[col] + [block] * count + [whole(bias.shape)],
        out_shape=[jax.ShapeDtypeStruct((inner, rows * size), BF16)]
        + [jax.ShapeDtypeStruct((rows, depth, size), BF16)] * count
        + [jax.ShapeDtypeStruct(bias.shape, F32)],
        compiler_params=PARAMS,
        name="attend_back",
        cost_estimate=cost(40 * rows * heads * count * size * size * HEAD, 60_000_000),
    )(qt, u, *kv, bias, ot, dot_t, lse)
    return out[0], out[1:-1], out[-1]


def bias_body(heads, buckets_ref, table_ref, bias_ref):
    tables = [jnp.broadcast_to(table_ref[h : h + 1], (8, 128)) for h in range(heads)]
    for i in range(buckets_ref.shape[1] // 8):
        for j in range(buckets_ref.shape[2] // 128):
            at = (slice(i * 8, (i + 1) * 8), slice(j * 128, (j + 1) * 128))
            index = buckets_ref[(0,) + at]
            for h in range(heads):
                bias_ref[(h, 0) + at] = jnp.take_along_axis(tables[h], index, axis=1)


def bias_of(table, buckets):
    heads = table.shape[0]
    blocks, size, _ = buckets.shape
    return pl.pallas_call(
        functools.partial(bias_body, heads),
        grid=(blocks,),
        in_specs=[pl.BlockSpec((1, size, size), lambda s: (s, 0, 0)), whole(table.shape)],
        out_specs=pl.BlockSpec((heads, 1, size, size), lambda s: (0, s, 0, 0)),
        out_shape=jax.ShapeDtypeStruct((heads, blocks, size, size), F32),
        compiler_params=PARAMS,
        name="bias_of",
        cost_estimate=cost(16 * buckets.size * heads, 4 * buckets.size * (heads + 1)),
    )(buckets, table)


def sums_body(heads, count, buckets_ref, g_ref, out_ref):
    @pl.when(pl.program_id(0) == 0)
    def _():
        out_ref[...] = jnp.zeros_like(out_ref)

    total = out_ref[...]
    for i in range(buckets_ref.shape[1] // 8):
        at = slice(i * 8, (i + 1) * 8)
        index = buckets_ref[0, at]
        hot = [jnp.where(index == b, 1.0, 0.0) for b in range(count)]
        hot = jnp.concatenate(hot, axis=0).astype(BF16)
        g = jnp.concatenate([g_ref[h, 0, at] for h in range(heads)], axis=0)
        high = g.astype(BF16)
        low = (g - high.astype(F32)).astype(BF16)
        total += dot(jnp.concatenate([high, low], axis=0), hot, 1, 1)
    out_ref[...] = total


def bucket_sums(grad_bias, buckets, count):
    heads, blocks, size, _ = grad_bias.shape
    shape = (2 * heads * 8, count * 8)
    raw = pl.pallas_call(
        functools.partial(sums_body, heads, count),
        grid=(blocks,),
        in_specs=[
            pl.BlockSpec((1, size, size), lambda s: (s, 0, 0)),
            pl.BlockSpec((heads, 1, size, size), lambda s: (0, s, 0, 0)),
        ],
        out_specs=pl.BlockSpec(shape, lambda s: (0, 0)),
        out_shape=jax.ShapeDtypeStruct(shape, F32),
        compiler_params=PARAMS,
        name="bucket_sums",
        cost_estimate=cost(64 * grad_bias.size, 4 * grad_bias.size),
    )(buckets, grad_bias)
    raw = raw.reshape(2, heads, 8, count, 8)
    return jnp.sum(jnp.where(jnp.eye(8, dtype=bool)[None, None, :, None, :], raw, 0.0), (0, 2, 4)).T


def mix_body(x_ref, o_ref, w_ref, place_ref, gain_ref, mixed_ref, n_ref):
    spread = dot(place_ref[...], o_ref[...], 0, 0).astype(BF16)
    mixed = x_ref[0].astype(F32) + dot(w_ref[...], spread, 0, 0)
    mixed_ref[...] = mixed
    scale = lax.rsqrt(jnp.mean(mixed * mixed, axis=0, keepdims=True) + NORM_EPSILON)
    n_ref[...] = (mixed * scale * gain_ref[...]).astype(BF16)


def mix(x, ot, w, place, gain):
    rows, width, size = x.shape
    col = pl.BlockSpec((width, size), lambda r: (0, r))
    return pl.pallas_call(
        mix_body,
        grid=(rows,),
        in_specs=[
            pl.BlockSpec((1, width, size), lambda r: (r, 0, 0)),
            pl.BlockSpec((ot.shape[0], size), lambda r: (0, r)),
            whole(w.shape),
            whole(place.shape),
            whole(gain.shape),
        ],
        out_specs=[col, col],
        out_shape=[
            jax.ShapeDtypeStruct((width, rows * size), F32),
            jax.ShapeDtypeStruct((width, rows * size), BF16),
        ],
        compiler_params=PARAMS,
        name="mix",
        cost_estimate=cost(2 * w.size * rows * size, 8 * x.size + 2 * w.size),
    )(x, ot, w, place, gain)


def mix_back_body(
    mixed_ref, d0_ref, d1_ref, dy_ref, o_ref, w_ref, place_ref, gain_ref,
    dmixed_ref, do_ref, gw_ref, gg_ref, acc,
):
    row = pl.program_id(0)
    mixed = mixed_ref[...]
    dn = d0_ref[...] + d1_ref[...].astype(F32)
    scale = lax.rsqrt(jnp.mean(mixed * mixed, axis=0, keepdims=True) + NORM_EPSILON)
    unit = mixed * scale
    scaled = dn * gain_ref[...]
    inside = jnp.mean(scaled * unit, axis=0, keepdims=True)
    dmixed = dy_ref[0].astype(F32) + scale * (scaled - unit * inside)
    dmixed_ref[...] = dmixed
    low = dmixed.astype(BF16)
    spread = dot(place_ref[...], o_ref[...], 0, 0).astype(BF16)
    mixed_up = dot(w_ref[...], low, 1, 0).astype(BF16)
    do_ref[...] = dot(place_ref[...], mixed_up, 1, 0).astype(BF16)
    both = dn * unit
    gain_part = both[:, :128]
    for j in range(1, both.shape[1] // 128):
        gain_part = gain_part + both[:, j * 128 : (j + 1) * 128]
    product = dot(spread, low, 1, 1)

    @pl.when(row == 0)
    def _():
        acc[...] = product
        gg_ref[...] = gain_part

    @pl.when(row > 0)
    def _():
        acc[...] += product
        gg_ref[...] += gain_part

    @pl.when(row == pl.num_programs(0) - 1)
    def _():
        gw_ref[...] = acc[...].astype(BF16)


def mix_back(mixed, d0, d1, dy, ot, w, place, gain):
    rows, width, size = dy.shape
    inner = ot.shape[0]
    col = pl.BlockSpec((width, size), lambda r: (0, r))
    head_col = pl.BlockSpec((inner, size), lambda r: (0, r))
    return pl.pallas_call(
        mix_back_body,
        grid=(rows,),
        in_specs=[
            col,
            col,
            col,
            pl.BlockSpec((1, width, size), lambda r: (r, 0, 0)),
            head_col,
            whole(w.shape),
            whole(place.shape),
            whole(gain.shape),
        ],
        out_specs=[col, head_col, whole(w.shape), whole((width, 128))],
        out_shape=[
            jax.ShapeDtypeStruct((width, rows * size), F32),
            jax.ShapeDtypeStruct((inner, rows * size), BF16),
            jax.ShapeDtypeStruct(w.shape, BF16),
            jax.ShapeDtypeStruct((width, 128), F32),
        ],
        scratch_shapes=[pltpu.VMEM(w.shape, F32)],
        compiler_params=PARAMS,
        name="mix_back",
        cost_estimate=cost(4 * w.size * rows * size, 16 * dy.size + 4 * w.size),
    )(mixed, d0, d1, dy, ot, w, place, gain)


def ffn_body(count, *refs):
    ws = refs[:count]
    n_ref, dy_ref, act_ref = refs[count : count + 3]
    gs = refs[count + 3 : 2 * count + 3]
    acc = refs[2 * count + 3]
    step = pl.program_id(0)
    norm = n_ref[0]
    dy = dy_ref[0]

    @pl.when(step == 0)
    def _():
        acc[...] = jnp.zeros_like(acc)

    start = 0
    for w_ref in ws:
        owners, _, rows, width = w_ref.shape
        size = owners * rows
        part = slice(start, start + size)
        start += size
        gate = dot(w_ref[:, 0].reshape(size, width), norm, 1, 0)
        up = dot(w_ref[:, 1].reshape(size, width), norm, 1, 0)
        dhid = dot(w_ref[:, 2].reshape(size, width), dy, 1, 0)
        square = gate * gate
        tanh = jnp.tanh(gate * (0.7978845608028654 + 0.035677408136300125 * square))
        half = 0.5 + 0.5 * tanh
        gelu = gate * half
        bend = 0.7978845608028654 + 0.10703222440890037 * square
        slope = half + (0.5 * gate) * (1.0 - tanh * tanh) * bend
        hidden = (gelu * up).astype(BF16)
        dgate = (dhid * up * slope).astype(BF16)
        dup = (dhid * gelu).astype(BF16)
        act_ref[0, part] = dgate
        act_ref[1, part] = dup
        act_ref[2, part] = hidden
        acc[0, part] += dot(dgate, norm, 1, 1)
        acc[1, part] += dot(dup, norm, 1, 1)
        acc[2, part] += dot(hidden, dy, 1, 1)

    @pl.when(step == pl.num_programs(0) - 1)
    def _():
        start = 0
        for g_ref in gs:
            owners, _, rows, width = g_ref.shape
            size = owners * rows
            for j in range(3):
                part = acc[j, start : start + size].astype(BF16)
                g_ref[:, j] = part.reshape(owners, rows, width)
            start += size


def ffn_piece(ws, n, dy, tile):
    halves, width, tokens = n.shape
    size = sum(w.shape[0] * w.shape[2] for w in ws)
    per = tokens // tile
    steps = halves * per
    all_tokens = halves * tokens
    column = pl.BlockSpec((1, width, tile), lambda t: (t // per, 0, t % per))
    out = pl.pallas_call(
        functools.partial(ffn_body, len(ws)),
        grid=(steps,),
        in_specs=[whole(w.shape) for w in ws] + [column, column],
        out_specs=[pl.BlockSpec((3, size, tile), lambda t: (0, 0, t))] + [whole(w.shape) for w in ws],
        out_shape=[jax.ShapeDtypeStruct((3, size, all_tokens), BF16)]
        + [jax.ShapeDtypeStruct(w.shape, BF16) for w in ws],
        scratch_shapes=[pltpu.VMEM((3, size, width), F32)],
        compiler_params=PARAMS,
        name="ffn_piece",
        cost_estimate=cost(
            16 * size * width * all_tokens,
            12 * size * width + 2 * (n.size + dy.size + 3 * size * all_tokens),
        ),
    )(*ws, n, dy)
    return out[0], out[1:]


def ffn_back_body(kinds, layout, *refs):
    count = sum(layout)
    ws, acts, out_ref = refs[:count], refs[count:-1], refs[-1]
    total, at = None, 0
    for a_ref, parts in zip(acts, layout):
        start = 0
        for w_ref in ws[at : at + parts]:
            owners, _, rows, width = w_ref.shape
            size = owners * rows
            for k in range(kinds):
                term = dot(w_ref[:, k].reshape(size, width), a_ref[k, start : start + size], 0, 0)
                total = term if total is None else total + term
            start += size
        at += parts
    out_ref[...] = total.astype(out_ref.dtype)


def ffn_back(pieces, acts, which, kinds, start, count, tile, dtype):
    ws = [w for piece in pieces for w in piece]
    width = ws[0].shape[3]
    first = start // tile
    at = which // kinds
    size = sum(a.shape[1] for a in acts)
    return pl.pallas_call(
        functools.partial(ffn_back_body, kinds, [len(piece) for piece in pieces]),
        grid=(count // tile,),
        in_specs=[
            pl.BlockSpec(
                (w.shape[0], kinds) + w.shape[2:],
                lambda t: (0, at, 0, 0),
                pipeline_mode=pl.Buffered(1),
            )
            for w in ws
        ]
        + [pl.BlockSpec((kinds, a.shape[1], tile), lambda t: (at, 0, first + t)) for a in acts],
        out_specs=pl.BlockSpec((width, tile), lambda t: (0, t)),
        out_shape=jax.ShapeDtypeStruct((width, count), dtype),
        compiler_params=PARAMS,
        name="ffn_back",
        cost_estimate=cost(
            2.6 * kinds * size * width * count, 2 * kinds * size * (width + count) + 4 * width * count
        ),
    )(*ws, *acts)


def last_body(
    x_ref, n_ref, dm_ref, dq_ref, dkv_ref, wq_ref, wk_ref, wv_ref, pq_ref, pk_ref, pv_ref,
    gain_ref, gx_ref, gq_ref, gk_ref, gv_ref, gg_ref, acc,
):
    row = pl.program_id(0)
    inner = dq_ref.shape[0]
    n = n_ref[...]
    dn = None

    @pl.when(row == 0)
    def _():
        acc[...] = jnp.zeros_like(acc)

    sources = (dq_ref[...], dkv_ref[0, :inner], dkv_ref[0, inner : 2 * inner])
    for j, (d, w_ref, p_ref) in enumerate(
        zip(sources, (wq_ref, wk_ref, wv_ref), (pq_ref, pk_ref, pv_ref))
    ):
        spread = dot(p_ref[...], d, 0, 0).astype(BF16)
        term = dot(w_ref[...], spread, 0, 0)
        dn = term if dn is None else dn + term
        acc[j] += dot(spread, n, 1, 1)
    x = x_ref[0].astype(F32)
    scale = lax.rsqrt(jnp.mean(x * x, axis=0, keepdims=True) + NORM_EPSILON)
    unit = x * scale
    scaled = dn * gain_ref[...]
    inside = jnp.mean(scaled * unit, axis=0, keepdims=True)
    gx_ref[0] = dm_ref[...] + scale * (scaled - unit * inside)
    both = dn * unit
    gain_part = both[:, :128]
    for j in range(1, both.shape[1] // 128):
        gain_part = gain_part + both[:, j * 128 : (j + 1) * 128]

    @pl.when(row == 0)
    def _():
        gg_ref[...] = gain_part

    @pl.when(row > 0)
    def _():
        gg_ref[...] += gain_part

    @pl.when(row == pl.num_programs(0) - 1)
    def _():
        for j, g_ref in enumerate((gq_ref, gk_ref, gv_ref)):
            g_ref[...] = acc[j].astype(BF16)


def last_plain(x, n, dmixed, dq, dkv, ws, places, gain):
    rows, width, size = x.shape
    inner = dq.shape[0]
    flat = lambda g: jnp.transpose(g, (1, 0, 2)).reshape(g.shape[1], rows * size)
    sources = (dq, flat(dkv[:, :inner]), flat(dkv[:, inner : 2 * inner]))
    spreads = [dot(p, d, 0, 0).astype(BF16) for p, d in zip(places, sources)]
    grads = [dot(s, n, 1, 1).astype(BF16) for s in spreads]
    dn = sum(dot(w, s, 0, 0) for w, s in zip(ws, spreads))
    values = flat(x).astype(F32)
    scale = lax.rsqrt(jnp.mean(values * values, axis=0, keepdims=True) + NORM_EPSILON)
    unit = values * scale
    scaled = dn * gain
    gx = dmixed + scale * (scaled - unit * jnp.mean(scaled * unit, axis=0, keepdims=True))
    gx = jnp.transpose(gx.reshape(width, rows, size), (1, 0, 2))
    return gx, *grads, jnp.sum(dn * unit, axis=1, keepdims=True)


def last(x, n, dmixed, dq, dkv, ws, places, gain):
    rows, width, size = x.shape
    if ws[0].shape[0] > 1024:
        return last_plain(x, n, dmixed, dq, dkv, ws, places, gain)
    inner = dq.shape[0]
    col = pl.BlockSpec((width, size), lambda r: (0, r))
    block = pl.BlockSpec((1, width, size), lambda r: (r, 0, 0))
    shape = ws[0].shape
    return pl.pallas_call(
        last_body,
        grid=(rows,),
        in_specs=[
            block,
            col,
            col,
            pl.BlockSpec((inner, size), lambda r: (0, r)),
            pl.BlockSpec((1,) + dkv.shape[1:], lambda r: (r, 0, 0)),
        ]
        + [whole(w.shape) for w in ws]
        + [whole(p.shape) for p in places]
        + [whole(gain.shape)],
        out_specs=[block] + [whole(shape)] * 3 + [whole((width, 128))],
        out_shape=[jax.ShapeDtypeStruct(x.shape, F32)]
        + [jax.ShapeDtypeStruct(shape, BF16)] * 3
        + [jax.ShapeDtypeStruct((width, 128), F32)],
        scratch_shapes=[pltpu.VMEM((3,) + shape, F32)],
        compiler_params=PARAMS,
        name="last",
        cost_estimate=cost(12 * ws[0].size * rows * size, 14 * x.size + 12 * ws[0].size),
    )(x, n, dmixed, dq, dkv, *ws, *places, gain)


def make_swap(sizes):
    def swap(x, step):
        axis, bit = step
        return lax.ppermute(x, axis, [(i, i ^ bit) for i in range(sizes[axis])])

    return swap


def pad_rows(w, rows):
    return jnp.pad(w, ((0, rows - w.shape[0]), (0, 0))) if rows > w.shape[0] else w


def per_device(
    dp, ctx,
    tokens, soft_mask, segment_ids, buckets, gain_attn, gain_ffn, bias_table,
    w_query, w_key, w_value, w_attn_out, w_gate, w_up, w_ffn_out, cotangent,
):
    sizes = {"dp": dp, "ctx": ctx}
    swap = make_swap(sizes)
    rows, size, width = tokens.shape
    here = rows * size
    count, heads = bias_table.shape
    inner = heads * HEAD
    my_dp, my_ctx = lax.axis_index("dp"), lax.axis_index("ctx")
    me = my_dp * ctx + my_ctx

    core = ("ctx", 1)
    across = [("ctx", 1 << b) for b in range(1, ctx.bit_length() - 1)]
    near = [("dp", 1)] if dp > 1 else []
    far = [("dp", 1 << b) for b in range(1, dp.bit_length() - 1)]
    order_a = far + near + across
    order_b = far + across + near

    def owners_of(order):
        found = [0]
        for axis, bit in order:
            found = found + [f ^ (bit * ctx if axis == "dp" else bit) for f in found]
        return np.array(found, np.int32)

    def spread_of(order):
        each = w_query.shape[0]
        owners = me ^ jnp.asarray(owners_of(order))
        padded = -(-each // ROW_TILE) * ROW_TILE
        inside = jnp.arange(padded)
        feature = owners[:, None] * each + inside[None, :]
        feature = jnp.where(inside[None, :] < each, feature, -1).reshape(-1)
        return (jnp.arange(inner)[:, None] == feature[None, :]).astype(BF16)

    def gather(w, order):
        for step in order:
            w = jnp.concatenate([w, swap(w, step)], axis=0)
        return w

    def reduce(g, order):
        for step in reversed(order):
            half = g.shape[0] // 2
            g = g[:half] + swap(g[half:], step)
        return g[0]

    each = -(-w_query.shape[0] // ROW_TILE) * ROW_TILE
    order_qa, order_qb = order_a + [core], order_b + [core]
    slot = lambda w: pad_rows(w, each)[None]
    wk = gather(slot(w_key), order_qa)
    wv = gather(slot(w_value), order_qb)
    wq = gather(slot(w_query), order_qa)
    wo = gather(slot(w_attn_out), order_qb)
    flat = lambda w: w.reshape(-1, width)
    place_a, place_b = spread_of(order_qa), spread_of(order_qb)

    units = -(-w_gate.shape[0] // ROW_TILE)
    owners = dp * ctx // 2
    piece_units = max(1, 512 // (owners * ROW_TILE))
    stack = jnp.stack([pad_rows(w, units * ROW_TILE) for w in (w_gate, w_up, w_ffn_out)])
    cuts = []
    at = 0
    while at < units:
        take = min(piece_units, units - at)
        cuts.append((at * ROW_TILE, (at + take) * ROW_TILE))
        at += take
    pieces, piece_orders = [], []
    for i, (low, high) in enumerate(cuts):
        order = order_a if i % 2 == 0 else order_b
        w = stack[None, :, low:high]
        w = gather(w, order[:-1])
        pieces.append([w, swap(w, order[-1])])
        piece_orders.append(order)

    x = jnp.transpose(tokens, (0, 2, 1))
    dy = jnp.transpose(cotangent, (0, 2, 1))
    gain_one, gain_two = gain_attn[:, None], gain_ffn[:, None]
    normed = first_norm(x, gain_one)
    dy_own = jnp.transpose(dy, (1, 0, 2)).reshape(width, here)
    dy_pair = jnp.stack([dy_own, swap(dy_own, core)])

    def slots_of(order):
        found = [0]
        for _, bit in order:
            found = found + [f ^ bit for f in found]
        return found

    ctx_order = across + [core]
    slots = slots_of(ctx_order)
    by_block = buckets.reshape(size, ctx, size)
    buckets_t = jnp.stack(
        [
            lax.dynamic_index_in_dim(by_block, my_ctx ^ s, 1, keepdims=False).T
            for s in slots
        ]
    )
    table = jnp.pad(bias_table.T, ((0, 0), (0, 128 - count)))
    bias = bias_of(table, buckets_t)

    segs = lax.dynamic_slice_in_dim(segment_ids, my_ctx * size, size, 1)
    same = segs[:, None, :] == jnp.arange(DOCS, dtype=segs.dtype)[None, :, None]
    ones = jnp.ones((rows, 1, size), BF16)
    rest = AUG - 1 - DOCS
    aug = jnp.concatenate(
        [soft_mask[:, None, :], same.astype(BF16)] + [ones] * 3
        + [jnp.zeros((rows, rest - 3, size), BF16)],
        axis=1,
    )
    query_aug = jnp.concatenate(
        [ones, jnp.where(same, 0.0, MASK_VALUE).astype(BF16), jnp.zeros((rows, rest, size), BF16)],
        axis=1,
    )
    kv_own = key_value(normed, flat(wk), flat(wv), place_a, place_b, aug)
    kv = [kv_own]
    for step in ctx_order:
        kv = kv + [swap(k, step) for k in kv]

    queries = dot(place_a, dot(flat(wq), normed, 1, 0).astype(BF16), 1, 0).astype(BF16)
    attended, lse = attend(queries, query_aug, kv, bias, heads)
    mixed, normed_two = mix(x, attended, flat(wo), place_b, gain_two)
    n_pair = jnp.stack([normed_two, swap(normed_two, core)])

    acts, piece_grads, act_pieces = [], [], []
    for piece, order in zip(pieces, piece_orders):
        total = sum(w.shape[0] * w.shape[2] for w in piece)
        groups = [piece] if total <= 512 else [[w] for w in piece]
        grads = []
        for group in groups:
            act, g = ffn_piece(group, n_pair, dy_pair, min(512, here))
            acts.append(act)
            act_pieces.append(group)
            grads += g
        g = grads[0] + swap(grads[1], order[-1])
        piece_grads.append(reduce(g, order[:-1]))
    tile = min(512, here)
    dn_other = ffn_back(act_pieces, acts, 0, 2, here, here, tile, BF16)
    dn_own = ffn_back(act_pieces, acts, 0, 2, 0, here, tile, F32)
    dn_got = swap(dn_other, core)
    out_other = ffn_back(act_pieces, acts, 2, 1, here, here, tile, BF16)
    out_own = ffn_back(act_pieces, acts, 2, 1, 0, here, tile, F32)
    out_got = swap(out_other, core)
    out = (mixed + out_own + out_got.astype(F32)).astype(BF16)
    layer_out = jnp.transpose(out.reshape(width, rows, size), (1, 2, 0))
    ffn_grads = jnp.concatenate([g.astype(F32) for g in piece_grads], axis=1)
    grad_gate, grad_up, grad_ffn_out = (ffn_grads[j, : w_gate.shape[0]] for j in range(3))

    dmixed, dattended, gwo, gain_two_part = mix_back(
        mixed, dn_own, dn_got, dy, attended, flat(wo), place_b, gain_two
    )
    dq, dkv, grad_bias = attend_back(
        queries, query_aug, kv, bias, attended, dattended, lse, heads
    )
    dkv = list(dkv)
    for step in reversed(ctx_order):
        half = len(dkv) // 2
        dkv = [a + swap(b, step) for a, b in zip(dkv[:half], dkv[half:])]
    dkv = dkv[0]
    grad_table = bucket_sums(grad_bias, buckets_t, count)
    gx, gwq, gwk, gwv, gain_one_part = last(
        x, normed, dmixed, dq, dkv, (flat(wq), flat(wk), flat(wv)), (place_a, place_a, place_b), gain_one
    )
    unflat = lambda g: g.reshape(-1, each, width)
    grad_attn_out = reduce(unflat(gwo), order_qb)
    grad_query = reduce(unflat(gwq), order_qa)
    grad_key = reduce(unflat(gwk), order_qa)
    grad_value = reduce(unflat(gwv), order_qb)
    real = w_query.shape[0]
    attn_grads = [g[:real].astype(F32) for g in (grad_query, grad_key, grad_value, grad_attn_out)]
    small = jnp.concatenate(
        [jnp.sum(gain_one_part, 1), jnp.sum(gain_two_part, 1), grad_table.reshape(-1)]
    )
    length = small.shape[0]
    small = jnp.pad(small, (0, -length % 1024)).reshape(-1, 128)
    for step in order_qa:
        small = small + swap(small, step)
    small = small.reshape(-1)
    return (
        layer_out,
        jnp.transpose(gx, (0, 2, 1)),
        dkv[:, 2 * inner].astype(F32),
        small[:width],
        small[width : 2 * width],
        small[2 * width : length].reshape(count, heads),
        *attn_grads,
        grad_gate,
        grad_up,
        grad_ffn_out,
    )


def solution(mesh):
    split = P(("dp", "ctx"), None)
    act = P("dp", "ctx", None)
    in_specs = (act, P("dp", "ctx"), P("dp", None), P("ctx", None), P(), P(), P()) + (split,) * 7 + (act,)
    out_specs = (act, act, P("dp", "ctx"), P(), P(), P()) + (split,) * 7
    return jax.shard_map(
        functools.partial(per_device, mesh.shape["dp"], mesh.shape["ctx"]),
        mesh=mesh,
        in_specs=in_specs,
        out_specs=out_specs,
        check_vma=False,
    )
```

time: 1680 us -> 867 us (0.52)
  other arithmetic: 484 us -> 80.9 us
  Pallas kernels: 0 us -> 320 us
  matrix products: 290 us -> 5.42 us
  blocking collectives: 211 us -> 0 us
  waiting for transfers between devices: 425 us -> 298 us
  local copies, waits for them, and re-layouts: 138 us -> 70.5 us
  starting transfers between devices: 103 us -> 84.8 us
    pallas_call x0 -> x17, Pallas kernels: none -> 320 us  [the longest x4 113 us: ffn_piece(): pl.pallas_call(functools.partial(ffn_body, len(ws)), grid=(steps,), in_sp...]
    ppermute x0 -> x87, waiting for transfers between devices: none -> 298 us  [swap(): return lax.ppermute(x, axis, [(i, i ^ bit) for i in range(sizes[axis])])]
    dot_general x49 -> x1, matrix products: 290 us -> 5.42 us  [dot(): lax.dot_general(a, b, (((ca,), (cb,)), ((), ())), preferred_element_type=...]
    add x38 -> x34, other arithmetic: 267 us -> 20.2 us  [the longest x24 10.4 us: reduce(): g = g[:half] + swap(g[half:], step)]
    reduce_scatter x5 -> x0, waiting for transfers between devices: 224 us -> none  [the longest x1 221 us: per_device(): lax.psum_scatter(grad_ffn_out, ('dp', 'ctx'), scatter_dimension=0, tiled=...]
    all_gather x9 -> x0, waiting for transfers between devices: 195 us -> none  [the longest x1 71.8 us: per_device(): lax.all_gather(w_gate, ('dp', 'ctx'), axis=0, tiled=True)]
    unnamed x1 -> x0, blocking collectives: 165 us -> none
    reduce_sum x41 -> x3, other arithmetic: 158 us -> 4.45 us  [the longest x1 1.65 us: bucket_sums(): jnp.sum(jnp.where(jnp.eye(8, dtype=bool)[None, None, :, None, :], raw, 0....]
  transfers between devices with their start and end apart: 47 -> 87, of which waited for: 6 -> 32; matrix products, arithmetic and copies ran while one was open for 51% -> 17% of each run, Pallas kernels for 0% -> 37%
where the time goes in v1:
time: 867 us; the launch traced here: 862 us
  Pallas kernels  320 us (37%)
  waiting for transfers between devices  298 us (34%)
  starting transfers between devices  84.8 us (10%)
  other arithmetic  80.9 us (9%)
  local copies, waits for them, and re-layouts  70.5 us (8%)
    ppermute x87, waiting for transfers between devices, swap(): return lax.ppermute(x, axis, [(i, i ^ bit) for i in range(sizes[axis])])  298 us
    pallas_call x4, Pallas kernels, ffn_piece(): pl.pallas_call(functools.partial(ffn_body, len(ws)), grid=(steps,), in_sp...  113 us
    ppermute x87, starting transfers between devices, swap(): return lax.ppermute(x, axis, [(i, i ^ bit) for i in range(sizes[axis])])  84.8 us
    pallas_call x4, Pallas kernels, ffn_back(): pl.pallas_call(functools.partial(ffn_back_body, kinds, [len(piece) for pi...  62.7 us
    pallas_call x1, Pallas kernels, attend_back(): pl.pallas_call(functools.partial(attend_back_body, heads, inner, count),...  41.2 us
    concatenate x24, other arithmetic, gather(): w = jnp.concatenate([w, swap(w, step)], axis=0)  29.2 us
    pallas_call x1, Pallas kernels, last(): pl.pallas_call(last_body, grid=(rows,), in_specs=[block, col, col, pl.Blo...  25.9 us
    unnamed x144, local copies, waits for them, and re-layouts  19 us
  transfers between devices with their start and end apart: 87, of which 32 were waited for; matrix products, arithmetic and copies ran while one was open for 17% of the time, Pallas kernels for 37%

profile of v1, /device:TPU:0, one launch (start us, length us, event | category | flops | bytes accessed | tf_op | source)
XLA Modules:
  0.0 862.3 jit_solution(5075468766662293747)
XLA Ops:
  87.0 12.3 %key_value.1.refs_0_ = bf16[4,784,256]{2,1,0:T(8,128)(2,1)} custom-call(bf16[1472,1024]{1,0:T(8,128)(2,1)} %first_norm.1.n_ref, bf16[512,1472]{1,0:T(8,128)(2,1)} %bitcast.165, bf16[512,1472]{1,0:T(8,128)(2,1)} %bitcast.167, bf16[384,512]{1,0:T(8,128)(2,1)} %fusion.pk_ref.pq_ref, bf16[384,512]{1,0:T(8,128)(2,1)} %fusion.1.pv_ref.place_ref, ...), custom_call_target="tpu_custom_call" | custom-call | flops 3087007744 | bytes 6029312 | tf_op jit(solution)/shard_map/key_value/pallas_call | solution.py:67
  108.1 36.9 %collective-permute-done.3 = bf16[8,16,1472]{2,1,0:T(8,128)(2,1)S(1)} collective-permute-done((bf16[8,16,1472]{2,1,0:T(8,128)(2,1)S(1)}, bf16[8,16,1472]{2,1,0:T(8,128)(2,1)S(1)}, u32[]{:S(2)}, u32[]{:S(2)}) %collective-permute-start.3) | collective-permute-done | bytes 376864 | tf_op jit(solution)/shard_map/ppermute | solution.py:609
  162.6 18.3 %attend.1 = (bf16[384,1024]{1,0:T(8,128)(2,1)}, f32[4,8,256]{2,1,0:T(8,128)}) custom-call(bf16[384,1024]{1,0:T(8,128)(2,1)} %convolution_convert_fusion.1.q_ref, bf16[4,16,256]{2,1,0:T(8,128)(2,1)} %maximum_maximum_fusion.u_ref, bf16[4,784,256]{2,1,0:T(8,128)(2,1)} %key_value.1.refs_0_, bf16[4,784,256]{2,1,0:T(8,128)(2,1)} %collective-permute-done.15.refs_1_, ...), custom_call_target="tpu_custom_call" | custom-call | flops 6442450944 | bytes 40000000 | tf_op jit(solution)/shard_map/attend/pallas_call | solution.py:117
  181.0 9.2 %mix.1 = (f32[1472,1024]{1,0:T(8,128)}, bf16[1472,1024]{1,0:T(8,128)(2,1)}) custom-call(bf16[4,1472,256]{2,1,0:T(8,128)(2,1)} %bitcast.143, bf16[384,1024]{1,0:T(8,128)(2,1)} %get-tuple-element.44.o_ref.refs_5_, bf16[512,1472]{1,0:T(8,128)(2,1)} %bitcast.22.w_ref, bf16[384,512]{1,0:T(8,128)(2,1)} %fusion.1.pv_ref.place_ref, f32[1472,1]{1,0:T(8,128)} %broadcast_in_dim.112.gain_ref), custom_call_target="tpu_custom_call" | custom-call | flops 1543503872 | bytes 13565952 | tf_op jit(solution)/shard_map/mix/pallas_call | solution.py:300
  195.8 24.7 %collective-permute-done.32 = bf16[2,3,32,1472]{3,2,1,0:T(8,128)(2,1)S(1)} collective-permute-done((bf16[2,3,32,1472]{3,2,1,0:T(8,128)(2,1)S(1)}, bf16[2,3,32,1472]{3,2,1,0:T(8,128)(2,1)S(1)}, u32[]{:S(2)}, u32[]{:S(2)}) %collective-permute-start.32) | collective-permute-done | bytes 565280 | tf_op jit(solution)/shard_map/ppermute | solution.py:609
  228.2 12.6 %copy.57 = bf16[1472,4,256]{2,1,0:T(4,128)(2,1)} copy(bf16[1472,4,256]{2,0,1:T(8,128)(2,1)S(1)} %bitcast.141) | data formatting | bytes 6029312 | tf_op jit(solution)/shard_map/transpose;transpose | solution.py:697
  266.3 33.9 %collective-permute-done.26.refs_1_ = bf16[8,3,32,1472]{3,2,1,0:T(8,128)(2,1)} collective-permute-done((bf16[8,3,32,1472]{3,2,1,0:T(8,128)(2,1)}, bf16[8,3,32,1472]{3,2,1,0:T(8,128)(2,1)}, u32[]{:S(2)}, u32[]{:S(2)}) %collective-permute-start.26) | collective-permute-done | bytes 2261024 | tf_op jit(solution)/shard_map/ppermute | solution.py:609
  300.3 30.2 %ffn_piece.4 = (bf16[3,512,2048]{2,1,0:T(8,128)(2,1)}, bf16[8,3,32,1472]{3,2,1,0:T(8,128)(2,1)}, bf16[8,3,32,1472]{3,2,1,0:T(8,128)(2,1)}) custom-call(bf16[8,3,32,1472]{3,2,1,0:T(8,128)(2,1)} %pad_maximum_fusion.2.refs_0_, bf16[8,3,32,1472]{3,2,1,0:T(8,128)(2,1)} %collective-permute-done.26.refs_1_, bf16[2,1472,1024]{2,1,0:T(8,128)(2,1)} %pad_maximum_fusion.refs_2_, ...), custom_call_target="tpu_custom_call" | custom-call | flops 24696061952 | bytes 27394048 | tf_op jit(solution)/shard_map/ffn_piece/pallas_call | solution.py:448
  331.0 29.9 %ffn_piece.5 = (bf16[3,512,2048]{2,1,0:T(8,128)(2,1)}, bf16[8,3,32,1472]{3,2,1,0:T(8,128)(2,1)}, bf16[8,3,32,1472]{3,2,1,0:T(8,128)(2,1)}) custom-call(bf16[8,3,32,1472]{3,2,1,0:T(8,128)(2,1)} %copy-done.3, bf16[8,3,32,1472]{3,2,1,0:T(8,128)(2,1)} %collective-permute-done.30.refs_1_.refs_3_, bf16[2,1472,1024]{2,1,0:T(8,128)(2,1)} %pad_maximum_fusion.refs_2_, ...), custom_call_target="tpu_custom_call" | custom-call | flops 24696061952 | bytes 27394048 | tf_op jit(solution)/shard_map/ffn_piece/pallas_call | solution.py:448
  362.0 23.1 %ffn_piece.7 = (bf16[3,256,2048]{2,1,0:T(8,128)(2,1)}, bf16[8,3,16,1472]{3,2,1,0:T(8,128)(2,1)}, bf16[8,3,16,1472]{3,2,1,0:T(8,128)(2,1)}) custom-call(bf16[8,3,16,1472]{3,2,1,0:T(8,128)(2,1)} %copy-done.6, bf16[8,3,16,1472]{3,2,1,0:T(8,128)(2,1)} %collective-permute-done.38.refs_1_.refs_7_, bf16[2,1472,1024]{2,1,0:T(8,128)(2,1)} %pad_maximum_fusion.refs_2_, ...), custom_call_target="tpu_custom_call" | custom-call | flops 12348030976 | bytes 19726336 | tf_op jit(solution)/shard_map/ffn_piece/pallas_call | solution.py:448
  386.1 29.8 %ffn_piece.6 = (bf16[3,512,2048]{2,1,0:T(8,128)(2,1)}, bf16[8,3,32,1472]{3,2,1,0:T(8,128)(2,1)}, bf16[8,3,32,1472]{3,2,1,0:T(8,128)(2,1)}) custom-call(bf16[8,3,32,1472]{3,2,1,0:T(8,128)(2,1)} %copy-done.4, bf16[8,3,32,1472]{3,2,1,0:T(8,128)(2,1)} %collective-permute-done.34.refs_1_.refs_5_, bf16[2,1472,1024]{2,1,0:T(8,128)(2,1)} %pad_maximum_fusion.refs_2_, ...), custom_call_target="tpu_custom_call" | custom-call | flops 24696061952 | bytes 27394048 | tf_op jit(solution)/shard_map/ffn_piece/pallas_call | solution.py:448
  417.4 20.2 %collective-permute-done.83 = bf16[8,3,16,1472]{3,2,1,0:T(8,128)(2,1)S(1)} collective-permute-done((bf16[8,3,16,1472]{3,2,1,0:T(8,128)(2,1)}, bf16[8,3,16,1472]{3,2,1,0:T(8,128)(2,1)S(1)}, u32[]{:S(2)}, u32[]{:S(2)}) %collective-permute-start.83) | collective-permute-done | bytes 1130528 | tf_op jit(solution)/shard_map/ppermute | solution.py:609
  439.6 19.6 %ffn_back.7 = bf16[1472,1024]{1,0:T(8,128)(2,1)} custom-call(bf16[8,3,32,1472]{3,2,1,0:T(8,128)(2,1)} %pad_maximum_fusion.2.refs_0_, bf16[8,3,32,1472]{3,2,1,0:T(8,128)(2,1)} %collective-permute-done.26.refs_1_, bf16[8,3,32,1472]{3,2,1,0:T(8,128)(2,1)} %copy-done.3, bf16[8,3,32,1472]{3,2,1,0:T(8,128)(2,1)} %collective-permute-done.30.refs_1_.refs_3_, ...), custom_call_target="tpu_custom_call" | custom-call | flops 14045885440 | bytes 23920640 | tf_op jit(solution)/shard_map/ffn_back/pallas_call | solution.py:489
  459.2 20.2 %collective-permute-done.84 = bf16[4,3,16,1472]{3,2,1,0:T(8,128)(2,1)S(1)} collective-permute-done((bf16[4,3,16,1472]{3,2,1,0:T(8,128)(2,1)S(1)}, bf16[4,3,16,1472]{3,2,1,0:T(8,128)(2,1)S(1)}, u32[]{:S(2)}, u32[]{:S(2)}) %collective-permute-start.84) | collective-permute-done | bytes 565280 | tf_op jit(solution)/shard_map/ppermute | solution.py:609
  479.6 20.0 %ffn_back.6.d0_ref = f32[1472,1024]{1,0:T(8,128)} custom-call(bf16[8,3,32,1472]{3,2,1,0:T(8,128)(2,1)} %pad_maximum_fusion.2.refs_0_, bf16[8,3,32,1472]{3,2,1,0:T(8,128)(2,1)} %collective-permute-done.26.refs_1_, bf16[8,3,32,1472]{3,2,1,0:T(8,128)(2,1)} %copy-done.3, bf16[8,3,32,1472]{3,2,1,0:T(8,128)(2,1)} %collective-permute-done.30.refs_1_.refs_3_, ...), custom_call_target="tpu_custom_call" | custom-call | flops 14045885440 | bytes 23920640 | tf_op jit(solution)/shard_map/ffn_back/pallas_call | solution.py:489
  500.0 11.4 %ffn_back.5 = bf16[1472,1024]{1,0:T(8,128)(2,1)} custom-call(bf16[8,3,32,1472]{3,2,1,0:T(8,128)(2,1)} %pad_maximum_fusion.2.refs_0_, bf16[8,3,32,1472]{3,2,1,0:T(8,128)(2,1)} %collective-permute-done.26.refs_1_, bf16[8,3,32,1472]{3,2,1,0:T(8,128)(2,1)} %copy-done.3, bf16[8,3,32,1472]{3,2,1,0:T(8,128)(2,1)} %collective-permute-done.30.refs_1_.refs_3_, ...), custom_call_target="tpu_custom_call" | custom-call | flops 7022942720 | bytes 14974976 | tf_op jit(solution)/shard_map/ffn_back/pallas_call | solution.py:489
  511.5 11.7 %ffn_back.4 = f32[1472,1024]{1,0:T(8,128)} custom-call(bf16[8,3,32,1472]{3,2,1,0:T(8,128)(2,1)} %pad_maximum_fusion.2.refs_0_, bf16[8,3,32,1472]{3,2,1,0:T(8,128)(2,1)} %collective-permute-done.26.refs_1_, bf16[8,3,32,1472]{3,2,1,0:T(8,128)(2,1)} %copy-done.3, bf16[8,3,32,1472]{3,2,1,0:T(8,128)(2,1)} %collective-permute-done.30.refs_1_.refs_3_, ...), custom_call_target="tpu_custom_call" | custom-call | flops 7022942720 | bytes 14974976 | tf_op jit(solution)/shard_map/ffn_back/pallas_call | solution.py:489
  538.8 18.3 %mix_back.1 = (f32[1472,1024]{1,0:T(8,128)}, bf16[384,1024]{1,0:T(8,128)(2,1)}, bf16[512,1472]{1,0:T(8,128)(2,1)}, f32[1472,128]{1,0:T(8,128)}) custom-call(f32[1472,1024]{1,0:T(8,128)} %get-tuple-element.45.mixed_ref, f32[1472,1024]{1,0:T(8,128)} %ffn_back.6.d0_ref, bf16[1472,1024]{1,0:T(8,128)(2,1)} %collective-permute-done.42.d1_ref, ...), custom_call_target="tpu_custom_call" | custom-call | flops 3087007744 | bytes 27131904 | tf_op jit(solution)/shard_map/mix_back/pallas_call | solution.py:364
  559.5 41.2 %attend_back.1 = (bf16[384,1024]{1,0:T(8,128)(2,1)}, bf16[4,784,256]{2,1,0:T(8,128)(2,1)}, bf16[4,784,256]{2,1,0:T(8,128)(2,1)}, bf16[4,784,256]{2,1,0:T(8,128)(...) custom-call(bf16[384,1024]{1,0:T(8,128)(2,1)} %convolution_convert_fusion.1.q_ref, ...), custom_call_target="tpu_custom_call" | custom-call | flops 16106127360 | bytes 60000000 | tf_op jit(solution)/shard_map/attend_back/pallas_call | solution.py:208
  636.9 44.7 %collective-permute-done.73 = bf16[2,3,32,1472]{3,2,1,0:T(8,128)(2,1)S(1)} collective-permute-done((bf16[2,3,32,1472]{3,2,1,0:T(8,128)(2,1)S(1)}, bf16[2,3,32,1472]{3,2,1,0:T(8,128)(2,1)S(1)}, u32[]{:S(2)}, u32[]{:S(2)}) %collective-permute-start.73) | collective-permute-done | bytes 565280 | tf_op jit(solution)/shard_map/ppermute | solution.py:609
  682.8 11.4 %collective-permute-done.77 = bf16[2,3,32,1472]{3,2,1,0:T(8,128)(2,1)S(1)} collective-permute-done((bf16[2,3,32,1472]{3,2,1,0:T(8,128)(2,1)S(1)}, bf16[2,3,32,1472]{3,2,1,0:T(8,128)(2,1)S(1)}, u32[]{:S(2)}, u32[]{:S(2)}) %collective-permute-start.77) | collective-permute-done | bytes 565280 | tf_op jit(solution)/shard_map/ppermute | solution.py:609
  694.7 12.0 %collective-permute-done.81 = bf16[2,3,32,1472]{3,2,1,0:T(8,128)(2,1)S(1)} collective-permute-done((bf16[2,3,32,1472]{3,2,1,0:T(8,128)(2,1)S(1)}, bf16[2,3,32,1472]{3,2,1,0:T(8,128)(2,1)S(1)}, u32[]{:S(2)}, u32[]{:S(2)}) %collective-permute-start.81) | collective-permute-done | bytes 565280 | tf_op jit(solution)/shard_map/ppermute | solution.py:609
  736.7 27.8 %collective-permute-done.45 = bf16[4,784,256]{2,1,0:T(8,128)(2,1)S(1)} collective-permute-done((bf16[4,784,256]{2,1,0:T(8,128)(2,1)S(1)}, bf16[4,784,256]{2,1,0:T(8,128)(2,1)S(1)}, u32[]{:S(2)}, u32[]{:S(2)}) %collective-permute-start.45) | collective-permute-done | bytes 1605664 | tf_op jit(solution)/shard_map/ppermute | solution.py:609
  765.9 25.9 %last.1 = (f32[4,1472,256]{2,1,0:T(8,128)}, bf16[512,1472]{1,0:T(8,128)(2,1)}, bf16[512,1472]{1,0:T(8,128)(2,1)}, bf16[512,1472]{1,0:T(8,128)(2,1)}, f32[1472,128]{1,0:T(8,128)}) custom-call(bf16[4,1472,256]{2,1,0:T(8,128)(2,1)} %bitcast.144, bf16[1472,1024]{1,0:T(8,128)(2,1)} %first_norm.1.n_ref, f32[1472,1024]{1,0:T(8,128)} %get-tuple-element.51.dm_ref, ...), custom_call_target="tpu_custom_call" | custom-call | flops 9261023232 | bytes 30146560 | tf_op jit(solution)/shard_map/last/pallas_call | solution.py:582
  (474 shorter events, 314.6 us)
Async XLA Ops:
  13.2 87.9 %collective-permute-start.23 = (bf16[1,3,32,1472]{3,2,1,0:T(8,128)(2,1)}, bf16[1,3,32,1472]{3,2,1,0:T(8,128)(2,1)}, u32[]{:S(2)}, u32[]{:S(2)}) collective-permute-start(bf16[1,3,32,1472]{3,2,1,0:T(8,128)(2,1)} %get-tuple-element.118), channel_id=1, source_target_pairs={{0,8},{4,12},{8,0},{12,4},{16,24},{20,28},{24,16},{28,20},{1,9},{5... | collective-permute-start | bytes 847880 | tf_op jit(solution)/shard_map/ppermute | solution.py:609
  38.7 107.8 %collective-permute-start.27 = (bf16[1,3,32,1472]{3,2,1,0:T(8,128)(2,1)S(1)}, bf16[1,3,32,1472]{3,2,1,0:T(8,128)(2,1)S(1)}, u32[]{:S(2)}, u32[]{:S(2)}) collective-permute-start(bf16[1,3,32,1472]{3,2,1,0:T(8,128)(2,1)S(1)} %copy-done.11), channel_id=1, source_target_pairs={{0,8},{4,12},{8,0},{12,4},{16,24},{20,28},{24,16},{28,20},{1,9},{5... | collective-permute-start | bytes 847880 | tf_op jit(solution)/shard_map/ppermute | solution.py:609
  147.8 107.5 %collective-permute-start.40 = (bf16[1472,1024]{1,0:T(8,128)(2,1)}, bf16[1472,1024]{1,0:T(8,128)(2,1)}, u32[]{:S(2)}, u32[]{:S(2)}) collective-permute-start(bf16[1472,1024]{1,0:T(8,128)(2,1)} %bitcast.77), channel_id=1, source_target_pairs={{0,1},{1,0},{2,3},{3,2},{4,5},{5,4},{6,7},{7,6},{8,9},{9,8},{10,11... | collective-permute-start | bytes 9043976 | tf_op jit(solution)/shard_map/ppermute | solution.py:609
  161.3 61.9 %collective-permute-start.25 = (bf16[4,3,32,1472]{3,2,1,0:T(8,128)(2,1)}, bf16[4,3,32,1472]{3,2,1,0:T(8,128)(2,1)S(1)}, u32[]{:S(2)}, u32[]{:S(2)}) collective-permute-start(bf16[4,3,32,1472]{3,2,1,0:T(8,128)(2,1)} %pad_maximum_fusion.5), channel_id=1, source_target_pairs={{0,4},{4,0},{8,12},{12,8},{16,20},{20,16},{24,28},{28,24},{1,5},{5... | collective-permute-start | bytes 3391496 | tf_op jit(solution)/shard_map/ppermute | solution.py:609
  190.2 71.2 %collective-permute-start.39 = (bf16[1472,1024]{1,0:T(8,128)(2,1)}, bf16[1472,1024]{1,0:T(8,128)(2,1)}, u32[]{:S(2)}, u32[]{:S(2)}) collective-permute-start(bf16[1472,1024]{1,0:T(8,128)(2,1)} %get-tuple-element.46), channel_id=1, source_target_pairs={{0,1},{1,0},{2,3},{3,2},{4,5},{5,4},{6,7},{7,6},{8,9},{9,8},{10,11... | collective-permute-start | bytes 9043976 | tf_op jit(solution)/shard_map/ppermute | solution.py:609
  227.0 73.3 %collective-permute-start.26 = (bf16[8,3,32,1472]{3,2,1,0:T(8,128)(2,1)}, bf16[8,3,32,1472]{3,2,1,0:T(8,128)(2,1)}, u32[]{:S(2)}, u32[]{:S(2)}) collective-permute-start(bf16[8,3,32,1472]{3,2,1,0:T(8,128)(2,1)} %pad_maximum_fusion.2.refs_0_), channel_id=1, source_target_pairs={{0,2},{1,3},{2,0},{3,1},{4,6},{5,7},{6,4},{7,5},{8,10},{9,11},{10,... | collective-permute-start | bytes 6782984 | tf_op jit(solution)/shard_map/ppermute | solution.py:609
  249.7 112.3 %collective-permute-start.38 = (bf16[8,3,16,1472]{3,2,1,0:T(8,128)(2,1)S(1)}, bf16[8,3,16,1472]{3,2,1,0:T(8,128)(2,1)}, u32[]{:S(2)}, u32[]{:S(2)}) collective-permute-start(bf16[8,3,16,1472]{3,2,1,0:T(8,128)(2,1)S(1)} %pad_maximum_fusion.8.refs_0_.refs_6_), channel_id=1, source_target_pairs={{0,4},{4,0},{8,12},{12,8},{16,20},{20,16},{24,28},{28,24},{1,5},{5... | collective-permute-start | bytes 3391496 | tf_op jit(solution)/shard_map/ppermute | solution.py:609
  252.0 79.0 %collective-permute-start.30 = (bf16[8,3,32,1472]{3,2,1,0:T(8,128)(2,1)S(1)}, bf16[8,3,32,1472]{3,2,1,0:T(8,128)(2,1)}, u32[]{:S(2)}, u32[]{:S(2)}) collective-permute-start(bf16[8,3,32,1472]{3,2,1,0:T(8,128)(2,1)S(1)} %pad_maximum_fusion.3.refs_0_.refs_2_), channel_id=1, source_target_pairs={{0,4},{4,0},{8,12},{12,8},{16,20},{20,16},{24,28},{28,24},{1,5},{5... | collective-permute-start | bytes 6782984 | tf_op jit(solution)/shard_map/ppermute | solution.py:609
  255.3 130.8 %collective-permute-start.34 = (bf16[8,3,32,1472]{3,2,1,0:T(8,128)(2,1)S(1)}, bf16[8,3,32,1472]{3,2,1,0:T(8,128)(2,1)}, u32[]{:S(2)}, u32[]{:S(2)}) collective-permute-start(bf16[8,3,32,1472]{3,2,1,0:T(8,128)(2,1)S(1)} %pad_maximum_fusion.4.refs_0_.refs_4_), channel_id=1, source_target_pairs={{0,2},{1,3},{2,0},{3,1},{4,6},{5,7},{6,4},{7,5},{8,10},{9,11},{10,... | collective-permute-start | bytes 6782984 | tf_op jit(solution)/shard_map/ppermute | solution.py:609
  330.4 192.8 %collective-permute-start.71 = (bf16[8,3,32,1472]{3,2,1,0:T(8,128)(2,1)}, bf16[8,3,32,1472]{3,2,1,0:T(8,128)(2,1)}, u32[]{:S(2)}, u32[]{:S(2)}) collective-permute-start(bf16[8,3,32,1472]{3,2,1,0:T(8,128)(2,1)} %get-tuple-element.68), channel_id=1, source_target_pairs={{0,2},{1,3},{2,0},{3,1},{4,6},{5,7},{6,4},{7,5},{8,10},{9,11},{10,... | collective-permute-start | bytes 6782984 | tf_op jit(solution)/shard_map/ppermute | solution.py:609
  360.9 166.9 %collective-permute-start.75 = (bf16[8,3,32,1472]{3,2,1,0:T(8,128)(2,1)}, bf16[8,3,32,1472]{3,2,1,0:T(8,128)(2,1)}, u32[]{:S(2)}, u32[]{:S(2)}) collective-permute-start(bf16[8,3,32,1472]{3,2,1,0:T(8,128)(2,1)} %get-tuple-element.70), channel_id=1, source_target_pairs={{0,4},{4,0},{8,12},{12,8},{16,20},{20,16},{24,28},{28,24},{1,5},{5... | collective-permute-start | bytes 6782984 | tf_op jit(solution)/shard_map/ppermute | solution.py:609
  415.9 117.1 %collective-permute-start.79 = (bf16[8,3,32,1472]{3,2,1,0:T(8,128)(2,1)}, bf16[8,3,32,1472]{3,2,1,0:T(8,128)(2,1)}, u32[]{:S(2)}, u32[]{:S(2)}) collective-permute-start(bf16[8,3,32,1472]{3,2,1,0:T(8,128)(2,1)} %get-tuple-element.72), channel_id=1, source_target_pairs={{0,2},{1,3},{2,0},{3,1},{4,6},{5,7},{6,4},{7,5},{8,10},{9,11},{10,... | collective-permute-start | bytes 6782984 | tf_op jit(solution)/shard_map/ppermute | solution.py:609
  459.2 79.6 %collective-permute-start.42 = (bf16[1472,1024]{1,0:T(8,128)(2,1)}, bf16[1472,1024]{1,0:T(8,128)(2,1)}, u32[]{:S(2)}, u32[]{:S(2)}) collective-permute-start(bf16[1472,1024]{1,0:T(8,128)(2,1)} %ffn_back.7), channel_id=1, source_target_pairs={{0,1},{1,0},{2,3},{3,2},{4,5},{5,4},{6,7},{7,6},{8,9},{9,8},{10,11... | collective-permute-start | bytes 9043976 | tf_op jit(solution)/shard_map/ppermute | solution.py:609
  511.4 103.7 %collective-permute-start.41 = (bf16[1472,1024]{1,0:T(8,128)(2,1)}, bf16[1472,1024]{1,0:T(8,128)(2,1)}, u32[]{:S(2)}, u32[]{:S(2)}) collective-permute-start(bf16[1472,1024]{1,0:T(8,128)(2,1)} %ffn_back.5), channel_id=1, source_target_pairs={{0,1},{1,0},{2,3},{3,2},{4,5},{5,4},{6,7},{7,6},{8,9},{9,8},{10,11... | collective-permute-start | bytes 9043976 | tf_op jit(solution)/shard_map/ppermute | solution.py:609
  526.9 97.8 %collective-permute-start.72 = (bf16[4,3,32,1472]{3,2,1,0:T(8,128)(2,1)}, bf16[4,3,32,1472]{3,2,1,0:T(8,128)(2,1)}, u32[]{:S(2)}, u32[]{:S(2)}) collective-permute-start(bf16[4,3,32,1472]{3,2,1,0:T(8,128)(2,1)} %slice.400), channel_id=1, source_target_pairs={{0,4},{4,0},{8,12},{12,8},{16,20},{20,16},{24,28},{28,24},{1,5},{5... | collective-permute-start | bytes 3391496 | tf_op jit(solution)/shard_map/ppermute | solution.py:609
  531.5 95.0 %collective-permute-start.76 = (bf16[4,3,32,1472]{3,2,1,0:T(8,128)(2,1)}, bf16[4,3,32,1472]{3,2,1,0:T(8,128)(2,1)}, u32[]{:S(2)}, u32[]{:S(2)}) collective-permute-start(bf16[4,3,32,1472]{3,2,1,0:T(8,128)(2,1)} %slice.406), channel_id=1, source_target_pairs={{0,2},{1,3},{2,0},{3,1},{4,6},{5,7},{6,4},{7,5},{8,10},{9,11},{10,... | collective-permute-start | bytes 3391496 | tf_op jit(solution)/shard_map/ppermute | solution.py:609
  537.7 93.2 %collective-permute-start.80 = (bf16[4,3,32,1472]{3,2,1,0:T(8,128)(2,1)}, bf16[4,3,32,1472]{3,2,1,0:T(8,128)(2,1)}, u32[]{:S(2)}, u32[]{:S(2)}) collective-permute-start(bf16[4,3,32,1472]{3,2,1,0:T(8,128)(2,1)} %slice.412), channel_id=1, source_target_pairs={{0,4},{4,0},{8,12},{12,8},{16,20},{20,16},{24,28},{28,24},{1,5},{5... | collective-permute-start | bytes 3391496 | tf_op jit(solution)/shard_map/ppermute | solution.py:609
  559.5 73.2 %collective-permute-start.66 = (bf16[16,16,1472]{2,1,0:T(8,128)(2,1)}, bf16[16,16,1472]{2,1,0:T(8,128)(2,1)}, u32[]{:S(2)}, u32[]{:S(2)}) collective-permute-start(bf16[16,16,1472]{2,1,0:T(8,128)(2,1)} %bitcast.50), channel_id=1, source_target_pairs={{0,1},{1,0},{2,3},{3,2},{4,5},{5,4},{6,7},{7,6},{8,9},{9,8},{10,11... | collective-permute-start | bytes 2261000 | tf_op jit(solution)/shard_map/ppermute | solution.py:609
  615.1 110.7 %collective-permute-start.44 = (bf16[4,784,256]{2,1,0:T(8,128)(2,1)}, bf16[4,784,256]{2,1,0:T(8,128)(2,1)S(1)}, u32[]{:S(2)}, u32[]{:S(2)}) collective-permute-start(bf16[4,784,256]{2,1,0:T(8,128)(2,1)} %get-tuple-element.58), channel_id=1, source_target_pairs={{0,1},{1,0},{2,3},{3,2},{4,5},{5,4},{6,7},{7,6},{8,9},{9,8},{10,11... | collective-permute-start | bytes 4816904 | tf_op jit(solution)/shard_map/ppermute | solution.py:609
  625.0 111.7 %collective-permute-start.43 = (bf16[4,784,256]{2,1,0:T(8,128)(2,1)S(1)}, bf16[4,784,256]{2,1,0:T(8,128)(2,1)S(1)}, u32[]{:S(2)}, u32[]{:S(2)}) collective-permute-start(bf16[4,784,256]{2,1,0:T(8,128)(2,1)S(1)} %copy-done.62), channel_id=1, source_target_pairs={{0,1},{1,0},{2,3},{3,2},{4,5},{5,4},{6,7},{7,6},{8,9},{9,8},{10,11... | collective-permute-start | bytes 4816904 | tf_op jit(solution)/shard_map/ppermute | solution.py:609
  626.6 55.0 %collective-permute-start.73 = (bf16[2,3,32,1472]{3,2,1,0:T(8,128)(2,1)S(1)}, bf16[2,3,32,1472]{3,2,1,0:T(8,128)(2,1)S(1)}, u32[]{:S(2)}, u32[]{:S(2)}) collective-permute-start(bf16[2,3,32,1472]{3,2,1,0:T(8,128)(2,1)S(1)} %slice.402), channel_id=1, source_target_pairs={{0,16},{4,20},{8,24},{12,28},{16,0},{20,4},{24,8},{28,12},{1,17},{... | collective-permute-start | bytes 1695752 | tf_op jit(solution)/shard_map/ppermute | solution.py:609
  630.9 63.3 %collective-permute-start.77 = (bf16[2,3,32,1472]{3,2,1,0:T(8,128)(2,1)S(1)}, bf16[2,3,32,1472]{3,2,1,0:T(8,128)(2,1)S(1)}, u32[]{:S(2)}, u32[]{:S(2)}) collective-permute-start(bf16[2,3,32,1472]{3,2,1,0:T(8,128)(2,1)S(1)} %slice.408), channel_id=1, source_target_pairs={{0,16},{4,20},{8,24},{12,28},{16,0},{20,4},{24,8},{28,12},{1,17},{... | collective-permute-start | bytes 1695752 | tf_op jit(solution)/shard_map/ppermute | solution.py:609
  632.8 73.9 %collective-permute-start.81 = (bf16[2,3,32,1472]{3,2,1,0:T(8,128)(2,1)S(1)}, bf16[2,3,32,1472]{3,2,1,0:T(8,128)(2,1)S(1)}, u32[]{:S(2)}, u32[]{:S(2)}) collective-permute-start(bf16[2,3,32,1472]{3,2,1,0:T(8,128)(2,1)S(1)} %slice.414), channel_id=1, source_target_pairs={{0,16},{4,20},{8,24},{12,28},{16,0},{20,4},{24,8},{28,12},{1,17},{... | collective-permute-start | bytes 1695752 | tf_op jit(solution)/shard_map/ppermute | solution.py:609
  736.6 70.4 %collective-permute-start.70 = (bf16[1,16,1472]{2,1,0:T(8,128)(2,1)S(1)}, bf16[1,16,1472]{2,1,0:T(8,128)(2,1)S(1)}, u32[]{:S(2)}, u32[]{:S(2)}) collective-permute-start(bf16[1,16,1472]{2,1,0:T(8,128)(2,1)S(1)} %get-tuple-element.136), channel_id=1, source_target_pairs={{0,8},{4,12},{8,0},{12,4},{16,24},{20,28},{24,16},{28,20},{1,9},{5... | collective-permute-start | bytes 141320 | tf_op jit(solution)/shard_map/ppermute | solution.py:609
  (126 other events, 1658.9 us)

commit v2 on v1

v2 whole, which is shorter than its diff:
```python
import functools

import jax
import jax.numpy as jnp
import numpy as np
from jax import lax
from jax.experimental import pallas as pl
from jax.experimental.pallas import tpu as pltpu
from jax.sharding import Mesh, PartitionSpec as P

NORM_EPSILON = 1e-06
MASK_VALUE = -1e30
F32, BF16 = jnp.float32, jnp.bfloat16
HEAD = 64
ROW_TILE = 16
AUG = 16
DOCS = 5
ONES = 1 + DOCS
VMEM_LIMIT = 58 * 1024 * 1024
PARAMS = pltpu.CompilerParams(vmem_limit_bytes=VMEM_LIMIT)


def dot(a, b, ca, cb):
    return lax.dot_general(a, b, (((ca,), (cb,)), ((), ())), preferred_element_type=F32)


def whole(shape):
    return pl.BlockSpec(shape, lambda t: (0,) * len(shape), pipeline_mode=pl.Buffered(1))


def cost(flops, nbytes):
    return pl.CostEstimate(flops=1, bytes_accessed=1, transcendentals=0)


ANY = pl.BlockSpec(memory_space=pl.ANY)


def join(pairs):
    return [jnp.concatenate(list(pair), axis=0) for pair in pairs]


def cut_join(parts, cuts):
    out = []
    for cut in cuts:
        at = np.s_[:, :, cut[0] : cut[0] + cut[1]] if isinstance(cut, tuple) else np.s_[:, cut]
        out.append(jnp.concatenate([p[at] for p in parts], axis=0))
    return out


def fill(pair, parts):
    start = 0
    for part in parts:
        pair = pair.at[1, start : start + part.shape[0]].set(part)
        start += part.shape[0]
    return pair


def add_halves(keep, got):
    out = []
    for k, r in zip(keep, got):
        part = k.shape[0] // 2
        out.append((k[:part] + r[:part], k[part:] + r[part:]))
    return out


def add_merge(keep, got, edges):
    part = keep[0].shape[0] // 2
    ends = [slice(None, part), slice(part, None)]
    return [jnp.concatenate([k[e] + r[e] for k, r in zip(keep, got)], axis=-2) for e in ends]


def add_last(keep, got, edges):
    total = keep[0].astype(F32) + got[0].astype(F32)
    return [total[..., a:b, :] for a, b in zip(edges, edges[1:])]


def add_pairs(pairs):
    return [a + b for a, b in pairs]


PIECES = 4


def pieces_of(shape, tile, first=0):
    rows, columns = shape
    piece = (rows // PIECES, columns)
    specs = [pl.BlockSpec((piece[0], tile), lambda t: (0, first + t)) for _ in range(PIECES)]
    return specs, [jax.ShapeDtypeStruct(piece, BF16)] * PIECES


def put_pieces(refs, value):
    step = refs[0].shape[0]
    for k, ref in enumerate(refs):
        ref[...] = value[k * step : (k + 1) * step]


def norm_body(x_ref, dy_ref, gain_ref, n_ref, pair_ref, *piece_refs):
    x = x_ref[0].astype(F32)
    scale = lax.rsqrt(jnp.mean(x * x, axis=0, keepdims=True) + NORM_EPSILON)
    n_ref[...] = (x * scale * gain_ref[...]).astype(BF16)
    pair_ref[0] = dy_ref[0]
    put_pieces(piece_refs, dy_ref[0])


def first_norm(x, dy, gain):
    rows, width, size = x.shape
    block = pl.BlockSpec((1, width, size), lambda r: (r, 0, 0))
    col = pl.BlockSpec((width, size), lambda r: (0, r))
    here = rows * size
    piece_specs, piece_shapes = pieces_of((width, here), size)
    return pl.pallas_call(
        norm_body,
        grid=(rows,),
        in_specs=[block, block, whole(gain.shape)],
        out_specs=[col, pl.BlockSpec((1, width, size), lambda r: (0, 0, r))] + piece_specs,
        out_shape=[
            jax.ShapeDtypeStruct((width, here), BF16),
            jax.ShapeDtypeStruct((2, width, here), BF16),
        ]
        + piece_shapes,
        compiler_params=PARAMS,
        name="first_norm",
        cost_estimate=cost(4 * x.size, 10 * x.size),
    )(x, dy, gain)


def key_value_body(inner, n_ref, wk_ref, wv_ref, pk_ref, pv_ref, aug_ref, out_ref):
    n = n_ref[...]
    for start, w_ref, p_ref in ((0, wk_ref, pk_ref), (inner, wv_ref, pv_ref)):
        mixed_up = dot(w_ref[...], n, 1, 0).astype(BF16)
        out_ref[0, start : start + inner] = dot(p_ref[...], mixed_up, 1, 0).astype(BF16)
    out_ref[0, 2 * inner :] = aug_ref[0]


def key_value(n, wk, wv, place_k, place_v, aug, first, rows):
    size = aug.shape[2]
    inner = place_k.shape[0]
    width = n.shape[0]
    return pl.pallas_call(
        functools.partial(key_value_body, inner),
        grid=(rows,),
        in_specs=[
            pl.BlockSpec((width, size), lambda r: (0, first + r)),
            whole(wk.shape),
            whole(wv.shape),
            whole(place_k.shape),
            whole(place_v.shape),
            pl.BlockSpec((1, AUG, size), lambda r: (first + r, 0, 0)),
        ],
        out_specs=pl.BlockSpec((1, 2 * inner + AUG, size), lambda r: (r, 0, 0)),
        out_shape=jax.ShapeDtypeStruct((rows, 2 * inner + AUG, size), BF16),
        compiler_params=PARAMS,
        name="key_value",
        cost_estimate=cost(4 * wk.size * rows * size, 4 * wk.size + 2 * n.size),
    )(n, wk, wv, place_k, place_v, aug)


def project_body(n_ref, w_ref, p_ref, out_ref):
    mixed_up = dot(w_ref[...], n_ref[...], 1, 0).astype(BF16)
    out_ref[...] = dot(p_ref[...], mixed_up, 1, 0).astype(BF16)


def project(n, w, place, tile):
    width, here = n.shape
    inner = place.shape[0]
    return pl.pallas_call(
        project_body,
        grid=(here // tile,),
        in_specs=[pl.BlockSpec((width, tile), lambda t: (0, t)), whole(w.shape), whole(place.shape)],
        out_specs=pl.BlockSpec((inner, tile), lambda t: (0, t)),
        out_shape=jax.ShapeDtypeStruct((inner, here), BF16),
        compiler_params=PARAMS,
        name="project",
        cost_estimate=cost(1, 1),
    )(n, w, place)


def attend_body(heads, inner, q_ref, u_ref, *refs):
    *blocks, bias_ref, o_ref, lse_ref, s_ref = refs
    for h in range(heads):
        part = slice(h * HEAD, (h + 1) * HEAD)
        q = jnp.concatenate([q_ref[part], u_ref[0]], axis=0)
        top = None
        for s, k_ref in enumerate(blocks):
            k = jnp.concatenate([k_ref[0, part], k_ref[0, 2 * inner :]], axis=0)
            logits = dot(k, q, 0, 0) + bias_ref[h, s]
            s_ref[s] = logits
            peak = jnp.max(logits, axis=0, keepdims=True)
            top = peak if top is None else jnp.maximum(top, peak)
        total, out = None, None
        for s, k_ref in enumerate(blocks):
            e = jnp.exp(s_ref[s] - top)
            part_sum = jnp.sum(e, axis=0, keepdims=True)
            total = part_sum if total is None else total + part_sum
            value = k_ref[0, slice(inner + h * HEAD, inner + (h + 1) * HEAD)]
            term = dot(value, e.astype(BF16), 1, 0)
            out = term if out is None else out + term
        o_ref[part] = (out / total).astype(BF16)
        lse_ref[0, h : h + 1] = top + jnp.log(total)
    pad = lse_ref.shape[1] - heads
    if pad:
        lse_ref[0, heads:] = jnp.zeros((pad, lse_ref.shape[2]), F32)


def attend(qt, u, kv, bias, heads, first):
    rows, depth, size = kv[0].shape
    inner = heads * HEAD
    pad = -(-heads // 8) * 8
    return pl.pallas_call(
        functools.partial(attend_body, heads, inner),
        grid=(rows,),
        in_specs=[
            pl.BlockSpec((inner, size), lambda r: (0, first + r)),
            pl.BlockSpec((1, AUG, size), lambda r: (first + r, 0, 0)),
        ]
        + [pl.BlockSpec((1, depth, size), lambda r: (r, 0, 0))] * len(kv)
        + [whole(bias.shape)],
        out_specs=[
            pl.BlockSpec((inner, size), lambda r: (0, r)),
            pl.BlockSpec((1, pad, size), lambda r: (r, 0, 0)),
        ],
        out_shape=[
            jax.ShapeDtypeStruct((inner, rows * size), BF16),
            jax.ShapeDtypeStruct((rows, pad, size), F32),
        ],
        scratch_shapes=[pltpu.VMEM((len(kv), size, size), F32)],
        compiler_params=PARAMS,
        name="attend",
        cost_estimate=cost(16 * rows * heads * len(kv) * size * size * HEAD, 40_000_000),
    )(qt, u, *kv, bias)


def three(x):
    a = x.astype(BF16).astype(F32)
    rest = x - a
    b = rest.astype(BF16).astype(F32)
    return a, b, rest - b


def attend_back_body(heads, inner, count, more, q_ref, u_ref, *refs):
    blocks = refs[:count]
    bias_ref, o_ref, do_ref, lse_ref = refs[count : count + 4]
    refs = refs[count + 4 :]
    before_ref, refs = (refs[0], refs[1:]) if more else (None, refs)
    dq_ref = refs[0]
    grads = refs[1 : count + 1]
    gb_ref = refs[count + 1]
    size = bias_ref.shape[3]
    row = pl.program_id(0)
    mask_grad = [None] * count
    extra = u_ref[0].astype(F32)
    place = lax.broadcasted_iota(jnp.int32, (AUG, size), 0)

    def pick(parts, base):
        for i, value in enumerate(parts):
            base = jnp.where(place == ONES + i, value, base)
        return base.astype(BF16)

    for h in range(heads):
        part = slice(h * HEAD, (h + 1) * HEAD)
        vpart = slice(inner + h * HEAD, inner + (h + 1) * HEAD)
        q = q_ref[part]
        do = do_ref[part]
        delta = jnp.sum(do.astype(F32) * o_ref[part].astype(F32), axis=0, keepdims=True)
        q_aug = jnp.concatenate([q, pick(three(-lse_ref[0, h : h + 1]), extra)], axis=0)
        do_aug = jnp.concatenate([do, pick(three(-delta), jnp.zeros_like(extra))], axis=0)
        dq = None
        for s, k_ref in enumerate(blocks):
            k = k_ref[0, part]
            aug = k_ref[0, 2 * inner :]
            logits = dot(jnp.concatenate([k, aug], axis=0), q_aug, 0, 0) + bias_ref[h, s]
            p = jnp.exp(logits)
            dp = dot(jnp.concatenate([k_ref[0, vpart], aug], axis=0), do_aug, 0, 0)
            ds = p * dp

            @pl.when(row == 0)
            def _():
                gb_ref[h, s] = before_ref[h, s] + ds if more else ds

            @pl.when(row > 0)
            def _():
                gb_ref[h, s] += ds

            low = ds.astype(BF16)
            grads[s][0, vpart] = dot(do, p.astype(BF16), 1, 1).astype(BF16)
            both = dot(q_aug, low, 1, 1)
            grads[s][0, part] = both[:HEAD].astype(BF16)
            g = both[HEAD : HEAD + 1]
            mask_grad[s] = g if mask_grad[s] is None else mask_grad[s] + g
            term = dot(k, low, 1, 0)
            dq = term if dq is None else dq + term
        dq_ref[part] = dq.astype(BF16)
    for s in range(count):
        grads[s][0, 2 * inner :] = jnp.broadcast_to(mask_grad[s], (AUG, size)).astype(BF16)


def attend_back(qt, u, kv, bias, ot, dot_t, lse, heads, first, before):
    rows, depth, size = kv[0].shape
    inner = heads * HEAD
    count = len(kv)
    own = pl.BlockSpec((inner, size), lambda r: (0, r))
    col = pl.BlockSpec((inner, size), lambda r: (0, first + r))
    block = pl.BlockSpec((1, depth, size), lambda r: (r, 0, 0))
    out = pl.pallas_call(
        functools.partial(attend_back_body, heads, inner, count, len(before)),
        grid=(rows,),
        in_specs=[col, pl.BlockSpec((1, AUG, size), lambda r: (first + r, 0, 0))]
        + [block] * count
        + [whole(bias.shape), own, col]
        + [pl.BlockSpec((1,) + lse.shape[1:], lambda r: (r, 0, 0))]
        + [whole(b.shape) for b in before],
        out_specs=[own] + [block] * count + [whole(bias.shape)],
        out_shape=[jax.ShapeDtypeStruct((inner, rows * size), BF16)]
        + [jax.ShapeDtypeStruct((rows, depth, size), BF16)] * count
        + [jax.ShapeDtypeStruct(bias.shape, F32)],
        compiler_params=PARAMS,
        name="attend_back",
        cost_estimate=cost(40 * rows * heads * count * size * size * HEAD, 60_000_000),
    )(qt, u, *kv, bias, ot, dot_t, lse, *before)
    return out[0], out[1:-1], out[-1]


def bias_body(heads, slots_ref, buckets_ref, table_ref, bias_ref, buckets_t_ref):
    tables = [jnp.broadcast_to(table_ref[h : h + 1], (8, 128)) for h in range(heads)]
    buckets_t_ref[0] = buckets_ref[...].T
    for i in range(buckets_ref.shape[1] // 8):
        for j in range(buckets_ref.shape[0] // 128):
            at = (slice(i * 8, (i + 1) * 8), slice(j * 128, (j + 1) * 128))
            index = buckets_t_ref[(0,) + at]
            for h in range(heads):
                bias_ref[(h, 0) + at] = jnp.take_along_axis(tables[h], index, axis=1)


def bias_of(slots, buckets, table):
    heads = table.shape[0]
    size, blocks = buckets.shape[0], slots.shape[0]
    spec = pltpu.PrefetchScalarGridSpec(
        num_scalar_prefetch=1,
        grid=(blocks,),
        in_specs=[
            pl.BlockSpec((size, size), lambda s, slots: (0, slots[s])),
            pl.BlockSpec(table.shape, lambda s, slots: (0, 0)),
        ],
        out_specs=[
            pl.BlockSpec((heads, 1, size, size), lambda s, slots: (0, s, 0, 0)),
            pl.BlockSpec((1, size, size), lambda s, slots: (s, 0, 0)),
        ],
    )
    return pl.pallas_call(
        functools.partial(bias_body, heads),
        grid_spec=spec,
        out_shape=[
            jax.ShapeDtypeStruct((heads, blocks, size, size), F32),
            jax.ShapeDtypeStruct((blocks, size, size), jnp.int32),
        ],
        compiler_params=PARAMS,
        name="bias_of",
        cost_estimate=cost(1, 1),
    )(slots, buckets, table)


def sums_body(heads, count, buckets_ref, g_ref, out_ref):
    @pl.when(pl.program_id(0) == 0)
    def _():
        out_ref[...] = jnp.zeros_like(out_ref)

    total = out_ref[...]
    for i in range(buckets_ref.shape[1] // 8):
        at = slice(i * 8, (i + 1) * 8)
        index = buckets_ref[0, at]
        hot = [jnp.where(index == b, 1.0, 0.0) for b in range(count)]
        hot = jnp.concatenate(hot, axis=0).astype(BF16)
        g = jnp.concatenate([g_ref[h, 0, at] for h in range(heads)], axis=0)
        high = g.astype(BF16)
        low = (g - high.astype(F32)).astype(BF16)
        total += dot(jnp.concatenate([high, low], axis=0), hot, 1, 1)
    out_ref[...] = total


def bucket_sums(grad_bias, buckets, count):
    heads, blocks, size, _ = grad_bias.shape
    shape = (2 * heads * 8, count * 8)
    raw = pl.pallas_call(
        functools.partial(sums_body, heads, count),
        grid=(blocks,),
        in_specs=[
            pl.BlockSpec((1, size, size), lambda s: (s, 0, 0)),
            pl.BlockSpec((heads, 1, size, size), lambda s: (0, s, 0, 0)),
        ],
        out_specs=pl.BlockSpec(shape, lambda s: (0, 0)),
        out_shape=jax.ShapeDtypeStruct(shape, F32),
        compiler_params=PARAMS,
        name="bucket_sums",
        cost_estimate=cost(64 * grad_bias.size, 4 * grad_bias.size),
    )(buckets, grad_bias)
    raw = raw.reshape(2, heads, 8, count, 8)
    return jnp.sum(jnp.where(jnp.eye(8, dtype=bool)[None, None, :, None, :], raw, 0.0), (0, 2, 4)).T


def mix_body(x_ref, o_ref, w_ref, place_ref, gain_ref, mixed_ref, pair_ref, *piece_refs):
    spread = dot(place_ref[...], o_ref[...], 0, 0).astype(BF16)
    mixed = x_ref[0].astype(F32) + dot(w_ref[...], spread, 0, 0)
    mixed_ref[...] = mixed
    scale = lax.rsqrt(jnp.mean(mixed * mixed, axis=0, keepdims=True) + NORM_EPSILON)
    n = (mixed * scale * gain_ref[...]).astype(BF16)
    pair_ref[0] = n
    put_pieces(piece_refs, n)


def group_specs(shape, count, per, rank):
    def place(g):
        def index(r):
            inside = jnp.clip(r - g * per, 0, per - 1)
            return (0, inside) if rank == 2 else (inside, 0, 0)

        return index

    return [pl.BlockSpec(shape, place(g)) for g in range(count)]


def mix(x, ot, w, place, gain):
    rows, width, size = x.shape
    inner = ot.shape[0]
    here = rows * size
    piece_specs, piece_shapes = pieces_of((width, here), size)
    return pl.pallas_call(
        mix_body,
        grid=(rows,),
        in_specs=[
            pl.BlockSpec((1, width, size), lambda r: (r, 0, 0)),
            pl.BlockSpec((inner, size), lambda r: (0, r)),
            whole(w.shape),
            whole(place.shape),
            whole(gain.shape),
        ],
        out_specs=[
            pl.BlockSpec((width, size), lambda r: (0, r)),
            pl.BlockSpec((1, width, size), lambda r: (0, 0, r)),
        ]
        + piece_specs,
        out_shape=[
            jax.ShapeDtypeStruct((width, here), F32),
            jax.ShapeDtypeStruct((2, width, here), BF16),
        ]
        + piece_shapes,
        compiler_params=PARAMS,
        name="mix",
        cost_estimate=cost(1, 1),
    )(x, ot, w, place, gain)


def units_of(ws):
    return sum(w.shape[0] * w.shape[2] for w in ws)


def entries_of(ws):
    return sum(w.shape[0] for w in ws)


def loads_of(refs, buf, sems, kinds):
    copies, start = [], 0
    for a, ref in enumerate(refs):
        for k, kind in enumerate(kinds):
            inside = buf.at[k, pl.ds(start, ref.shape[0])]
            copies.append(pltpu.make_async_copy(ref.at[:, kind], inside, sems.at[a, k]))
        start += ref.shape[0]
    return copies


def ffn_body(count, masks, me_ref, *refs):
    ws, (n_ref, dy_ref, act_ref), refs = refs[:count], refs[count : count + 3], refs[count + 3 :]
    gs, (buf, acc, in_sems, out_sems) = refs[:-4], refs[-4:]
    t = pl.program_id(0)
    entries, rows, width = buf.shape[1:]
    size = entries * rows
    loads = loads_of(ws, buf, in_sems, range(3))

    @pl.when(t == 0)
    def _():
        for copy in loads:
            copy.start()
        acc[...] = jnp.zeros_like(acc)
        for copy in loads:
            copy.wait()

    norm = n_ref[0]
    dy = dy_ref[0]
    gate = dot(buf[0].reshape(size, width), norm, 1, 0)
    up = dot(buf[1].reshape(size, width), norm, 1, 0)
    dhid = dot(buf[2].reshape(size, width), dy, 1, 0)
    inside = gate * (0.7978845608028654 + 0.035677408136300125 * (gate * gate))
    half = 0.5 + 0.5 * jnp.tanh(inside)
    gelu = gate * half
    slope = half * (1.0 + (1.0 - half) * (6.0 * inside - 3.1915382432114616 * gate))
    dgate = (dhid * up * slope).astype(BF16)
    dup = (dhid * gelu).astype(BF16)
    hidden = (gelu * up).astype(BF16)
    act_ref[0] = dgate
    act_ref[1] = dup
    act_ref[2] = hidden
    acc[0] += dot(dgate, norm, 1, 1)
    acc[1] += dot(dup, norm, 1, 1)
    acc[2] += dot(hidden, dy, 1, 1)

    @pl.when(t == pl.num_programs(0) - 1)
    def _():
        for k in range(3):
            buf[k] = acc[k].astype(BF16).reshape(entries, rows, width)
        stores = []
        if masks is None:
            start = 0
            for g, out in enumerate(gs):
                for k in range(3):
                    inside = buf.at[k, pl.ds(start, out.shape[0])]
                    stores.append(pltpu.make_async_copy(inside, out.at[:, k], out_sems.at[g, k]))
                start += out.shape[0]
        else:
            part = len(masks) // 2
            for s, mask in enumerate(masks):
                for k in range(3):
                    inside, out = buf.at[k, me_ref[0] ^ mask], gs[s // part].at[s % part, k]
                    stores.append(pltpu.make_async_copy(inside, out, out_sems.at[s, k]))
        for copy in stores:
            copy.start()
        for copy in stores:
            copy.wait()


def ffn_group(me, ws, n, dy, tile, masks=None):
    halves, width, tokens = n.shape
    per = tokens // tile
    all_tokens = halves * tokens
    size = units_of(ws)
    inner = (entries_of(ws),) + ws[0].shape[2:]
    column = pl.BlockSpec((1, width, tile), lambda t, me: (t // per, 0, t % per))
    stores = len(ws) if masks is None else len(masks)
    shapes = [w.shape for w in ws]
    if masks is not None:
        shapes = [(inner[0] // 2, 3) + inner[1:]] * 2
    spec = pltpu.PrefetchScalarGridSpec(
        num_scalar_prefetch=1,
        grid=(halves * per,),
        in_specs=[ANY] * len(ws) + [column, column],
        out_specs=[pl.BlockSpec((3, size, tile), lambda t, me: (0, 0, t))] + [ANY] * len(shapes),
        scratch_shapes=[
            pltpu.VMEM((3,) + inner, BF16),
            pltpu.VMEM((3, size, width), F32),
            pltpu.SemaphoreType.DMA((len(ws), 3)),
            pltpu.SemaphoreType.DMA((stores, 3)),
        ],
    )
    out = pl.pallas_call(
        functools.partial(ffn_body, len(ws), masks),
        grid_spec=spec,
        out_shape=[jax.ShapeDtypeStruct((3, size, all_tokens), BF16)]
        + [jax.ShapeDtypeStruct(shape, BF16) for shape in shapes],
        compiler_params=PARAMS,
        name="ffn_group",
        cost_estimate=cost(1, 1),
    )(me, *ws, n, dy)
    return out[0], out[1:]


def ffn_terms(layout, kinds, refs):
    count, total = len(layout), sum(layout)
    ws, acts, refs = refs[:total], refs[total : total + count], refs[total + count :]
    bufs, sems = refs[:count], refs[count]

    @pl.when(pl.program_id(0) == 0)
    def _():
        copies, start = [], 0
        for p, arrays in enumerate(layout):
            copies += loads_of(ws[start : start + arrays], bufs[p], sems.at[p], kinds)
            start += arrays
        for copy in copies:
            copy.start()
        for copy in copies:
            copy.wait()

    out = None
    for act, buf in zip(acts, bufs):
        _, entries, rows, width = buf.shape
        for k in range(len(kinds)):
            term = dot(buf[k].reshape(entries * rows, width), act[k], 0, 0)
            out = term if out is None else out + term
    return out


def layout_of(groups):
    return tuple(len(ws) for ws in groups)


def flat_of(groups):
    return [w for ws in groups for w in ws]


def ffn_specs(groups, acts, kinds, tile, first):
    at = kinds[0] // len(kinds)
    return [ANY] * len(flat_of(groups)) + [
        pl.BlockSpec((len(kinds), a.shape[1], tile), lambda t: (at, 0, first + t)) for a in acts
    ]


def ffn_scratch(groups, kinds):
    return [
        pltpu.VMEM((len(kinds), entries_of(ws)) + ws[0].shape[2:], BF16) for ws in groups
    ] + [pltpu.SemaphoreType.DMA((len(groups), max(layout_of(groups)), len(kinds)))]


def ffn_back_body(layout, kinds, *refs):
    ins = sum(layout) + len(layout)
    total = ffn_terms(layout, kinds, refs[:ins] + refs[ins + PIECES :])
    put_pieces(refs[ins : ins + PIECES], total.astype(BF16))


def ffn_back(groups, acts, kinds, start, count, tile):
    width = groups[0][0].shape[3]
    piece_specs, piece_shapes = pieces_of((width, count), tile)
    return pl.pallas_call(
        functools.partial(ffn_back_body, layout_of(groups), kinds),
        grid=(count // tile,),
        in_specs=ffn_specs(groups, acts, kinds, tile, start // tile),
        out_specs=piece_specs,
        out_shape=piece_shapes,
        scratch_shapes=ffn_scratch(groups, kinds),
        compiler_params=PARAMS,
        name="ffn_back",
        cost_estimate=cost(1, 1),
    )(*flat_of(groups), *acts)


def layer_out_body(layout, *refs):
    ins = sum(layout) + len(layout)
    mixed_ref, out_ref = refs[ins], refs[ins + 1 + PIECES]
    got = jnp.concatenate([r[...] for r in refs[ins + 1 : ins + 1 + PIECES]], axis=0)
    total = ffn_terms(layout, [2], refs[:ins] + refs[ins + 2 + PIECES :])
    out_ref[0] = (mixed_ref[...] + total + got.astype(F32)).astype(BF16)


def layer_out_of(groups, acts, mixed, got, rows):
    width, here = mixed.shape
    size = here // rows
    col = pl.BlockSpec((width, size), lambda t: (0, t))
    return pl.pallas_call(
        functools.partial(layer_out_body, layout_of(groups)),
        grid=(rows,),
        in_specs=ffn_specs(groups, acts, [2], size, 0) + [col] + pieces_of(mixed.shape, size)[0],
        out_specs=pl.BlockSpec((1, width, size), lambda t: (t, 0, 0)),
        out_shape=jax.ShapeDtypeStruct((rows, width, size), BF16),
        scratch_shapes=ffn_scratch(groups, [2]),
        compiler_params=PARAMS,
        name="layer_out_of",
        cost_estimate=cost(1, 1),
    )(*flat_of(groups), *acts, mixed, *got)


def mix_back_body(layout, *refs):
    ins = sum(layout) + len(layout)
    weights, refs = refs[:ins], refs[ins:]
    pieces, refs = refs[:PIECES], refs[PIECES:]
    mixed_ref, dy_ref, o_ref, w_ref, place_ref, gain_ref = refs[:6]
    refs = refs[6:]
    inside_grad = len(refs) == 6 + len(layout) + 1
    dmixed_ref, do_ref, gg_ref = refs[:3]
    low_ref, high_ref, acc = refs[3:6] if inside_grad else (None, None, None)
    row = pl.program_id(0)
    got = jnp.concatenate([r[...] for r in pieces], axis=0)
    dn = ffn_terms(layout, [0, 1], weights + refs[-len(layout) - 1 :]) + got.astype(F32)
    mixed = mixed_ref[...]
    scale = lax.rsqrt(jnp.mean(mixed * mixed, axis=0, keepdims=True) + NORM_EPSILON)
    unit = mixed * scale
    scaled = dn * gain_ref[...]
    inside = jnp.mean(scaled * unit, axis=0, keepdims=True)
    dmixed = dy_ref[0].astype(F32) + scale * (scaled - unit * inside)
    dmixed_ref[...] = dmixed
    low = dmixed.astype(BF16)
    spread = dot(place_ref[...], o_ref[...], 0, 0).astype(BF16)
    mixed_up = dot(w_ref[...], low, 1, 0).astype(BF16)
    do_ref[...] = dot(place_ref[...], mixed_up, 1, 0).astype(BF16)
    both = dn * unit
    gain_part = both[:, :128]
    for j in range(1, both.shape[1] // 128):
        gain_part = gain_part + both[:, j * 128 : (j + 1) * 128]

    @pl.when(row == 0)
    def _():
        gg_ref[...] = gain_part

    @pl.when(row > 0)
    def _():
        gg_ref[...] += gain_part

    if inside_grad:
        product = dot(spread, low, 1, 1)

        @pl.when(row == 0)
        def _():
            acc[...] = product

        @pl.when(row > 0)
        def _():
            acc[...] += product

        @pl.when(row == pl.num_programs(0) - 1)
        def _():
            half = low_ref.shape[0]
            low_ref[...] = acc[:half].astype(BF16)
            high_ref[...] = acc[half:].astype(BF16)


def mix_back(groups, acts, mixed, d1, dy, ot, w, place, gain):
    rows, width, size = dy.shape
    inner = ot.shape[0]
    here = rows * size
    col = pl.BlockSpec((width, size), lambda r: (0, r))
    head_col = pl.BlockSpec((inner, size), lambda r: (0, r))
    fits = w.shape[0] <= 1024
    half = (w.shape[0] // 2, width)
    out = pl.pallas_call(
        functools.partial(mix_back_body, layout_of(groups)),
        grid=(rows,),
        in_specs=ffn_specs(groups, acts, [0, 1], size, 0)
        + pieces_of(mixed.shape, size)[0]
        + [col, pl.BlockSpec((1, width, size), lambda r: (r, 0, 0)), head_col]
        + [whole(w.shape), whole(place.shape), whole(gain.shape)],
        out_specs=[col, head_col, whole((width, 128))] + [whole(half)] * (2 * fits),
        out_shape=[
            jax.ShapeDtypeStruct((width, here), F32),
            jax.ShapeDtypeStruct((inner, here), BF16),
            jax.ShapeDtypeStruct((width, 128), F32),
        ]
        + [jax.ShapeDtypeStruct(half, BF16)] * (2 * fits),
        scratch_shapes=[pltpu.VMEM(w.shape, F32)] * fits + ffn_scratch(groups, [0, 1]),
        compiler_params=PARAMS,
        name="mix_back",
        cost_estimate=cost(1, 1),
    )(*flat_of(groups), *acts, *d1, mixed, dy, ot, w, place, gain)
    if not fits:
        spread = dot(place, ot, 0, 0).astype(BF16)
        product = dot(spread, out[0].astype(BF16), 1, 1).astype(BF16)
        out = [*out, product[: half[0]], product[half[0] :]]
    return out


def grads_body(per, groups, parts, n_ref, *refs):
    d_refs, refs = refs[:groups], refs[groups:]
    places, refs = refs[: len(parts)], refs[len(parts) :]
    outs, (acc, d_scr) = refs[: 2 * len(parts)], refs[2 * len(parts) :]
    row = pl.program_id(0)
    n = n_ref[...]
    for g, d_ref in enumerate(d_refs):

        @pl.when(row // per == g)
        def _():
            d_scr[...] = d_ref[...].reshape(d_scr.shape)

    products = []
    for (start, stop), p_ref in zip(parts, places):
        spread = dot(p_ref[...], d_scr[start:stop], 0, 0).astype(BF16)
        products.append(dot(spread, n, 1, 1))

    @pl.when(row == 0)
    def _():
        for j, product in enumerate(products):
            acc[j] = product

    @pl.when(row > 0)
    def _():
        for j, product in enumerate(products):
            acc[j] += product

    @pl.when(row == pl.num_programs(0) - 1)
    def _():
        half = acc.shape[1] // 2
        for j in range(len(parts)):
            outs[2 * j][...] = acc[j, :half].astype(BF16)
            outs[2 * j + 1][...] = acc[j, half:].astype(BF16)


def projection_grads(n, groups, parts, places, rows):
    if len(parts) > 1 and places[0].shape[1] > 1024:
        return [
            half
            for part, p in zip(parts, places)
            for half in projection_grads(n, groups, [part], [p], rows)
        ]
    width, here = n.shape
    size = here // rows
    per = rows // len(groups)
    rank = groups[0].ndim
    depth = groups[0].shape[-2]
    shape = (depth, size) if rank == 2 else (1, depth, size)
    wide = (places[0].shape[1], width)
    return pl.pallas_call(
        functools.partial(grads_body, per, len(groups), parts),
        grid=(rows,),
        in_specs=[pl.BlockSpec((width, size), lambda r: (0, r))]
        + group_specs(shape, len(groups), per, rank)
        + [whole(p.shape) for p in places],
        out_specs=[whole((wide[0] // 2, width))] * (2 * len(parts)),
        out_shape=[jax.ShapeDtypeStruct((wide[0] // 2, width), BF16)] * (2 * len(parts)),
        scratch_shapes=[pltpu.VMEM((len(parts),) + wide, F32), pltpu.VMEM((depth, size), BF16)],
        compiler_params=PARAMS,
        name="projection_grads",
        cost_estimate=cost(
            2 * len(parts) * wide[0] * width * here, 2 * n.size + 2 * len(parts) * wide[0] * width
        ),
    )(n, *groups, *places)


def last_body(per, groups, x_ref, dm_ref, *refs):
    dq_refs, dkv_refs, refs = refs[:groups], refs[groups : 2 * groups], refs[2 * groups :]
    ws, places, refs = refs[:3], refs[3:6], refs[6:]
    gain_ref, gx_ref, gg_ref, d_scr = refs
    row = pl.program_id(0)
    inner = dq_refs[0].shape[0]
    for g in range(groups):

        @pl.when(row // per == g)
        def _():
            d_scr[:inner] = dq_refs[g][...]
            d_scr[inner:] = dkv_refs[g][0, : 2 * inner]

    dn = None
    for j in range(3):
        spread = dot(places[j][...], d_scr[j * inner : (j + 1) * inner], 0, 0).astype(BF16)
        term = dot(ws[j][...], spread, 0, 0)
        dn = term if dn is None else dn + term
    x = x_ref[0].astype(F32)
    scale = lax.rsqrt(jnp.mean(x * x, axis=0, keepdims=True) + NORM_EPSILON)
    unit = x * scale
    scaled = dn * gain_ref[...]
    inside = jnp.mean(scaled * unit, axis=0, keepdims=True)
    gx_ref[0] = dm_ref[...] + scale * (scaled - unit * inside)
    both = dn * unit
    gain_part = both[:, :128]
    for j in range(1, both.shape[1] // 128):
        gain_part = gain_part + both[:, j * 128 : (j + 1) * 128]

    @pl.when(row == 0)
    def _():
        gg_ref[...] = gain_part

    @pl.when(row > 0)
    def _():
        gg_ref[...] += gain_part


def last(x, dmixed, dqs, dkvs, ws, places, gain):
    rows, width, size = x.shape
    inner = dqs[0].shape[0]
    per = rows // len(dqs)
    col = pl.BlockSpec((width, size), lambda r: (0, r))
    block = pl.BlockSpec((1, width, size), lambda r: (r, 0, 0))
    return pl.pallas_call(
        functools.partial(last_body, per, len(dqs)),
        grid=(rows,),
        in_specs=[block, col]
        + group_specs((inner, size), len(dqs), per, 2)
        + group_specs((1,) + dkvs[0].shape[1:], len(dkvs), per, 3)
        + [whole(w.shape) for w in ws]
        + [whole(p.shape) for p in places]
        + [whole(gain.shape)],
        out_specs=[block, whole((width, 128))],
        out_shape=[jax.ShapeDtypeStruct(x.shape, F32), jax.ShapeDtypeStruct((width, 128), F32)],
        scratch_shapes=[pltpu.VMEM((3 * inner, size), BF16)],
        compiler_params=PARAMS,
        name="last",
        cost_estimate=cost(6 * ws[0].size * rows * size, 14 * x.size + 6 * ws[0].size),
    )(x, dmixed, *dqs, *dkvs, *ws, *places, gain)


def after(value, *markers):
    return lax.optimization_barrier((value, markers))[0]


def pad_rows(w, rows):
    return jnp.pad(w, ((0, rows - w.shape[0]), (0, 0))) if rows > w.shape[0] else w


class Links:
    def __init__(self, dp, pairs):
        self.sizes = {"dp": dp, "x": pairs, "core": 2}
        self.strides = {"dp": 2 * pairs, "x": 2, "core": 1}
        self.core = ("core", 1)
        self.across = ("x", 1)
        self.near = ("dp", 1)
        self.far_count = dp // 2

    def swap(self, x, step):
        axis, mask = step
        return lax.ppermute(x, axis, [(i, i ^ mask) for i in range(self.sizes[axis])])

    def far_steps(self):
        return [("dp", k << 1) for k in range(1, self.far_count)]

    def far_bits(self):
        return [("dp", 2 << b) for b in range(self.far_count.bit_length() - 1)]

    def masks(self, steps):
        found = [(k << 1) * self.strides["dp"] for k in range(self.far_count)]
        for axis, mask in steps:
            found = found + [f ^ (mask * self.strides[axis]) for f in found]
        return found


def per_device(
    dp, ctx,
    tokens, soft_mask, segment_ids, buckets, gain_attn, gain_ffn, bias_table,
    w_query, w_key, w_value, w_attn_out, w_gate, w_up, w_ffn_out, cotangent,
):
    links = Links(dp, ctx // 2)
    swap, core, across, near = links.swap, links.core, links.across, links.near
    far = links.far_steps()
    rows, size, width = tokens.shape
    here = rows * size
    count, heads = bias_table.shape
    inner = heads * HEAD
    my_dp, my_ctx = lax.axis_index("dp"), lax.axis_index("x") * 2 + lax.axis_index("core")
    me = my_dp * ctx + my_ctx
    tile = min(512, here)
    order_a, order_b = [near, across], [across, near]

    def spread_of(steps):
        real = w_query.shape[0]
        owners = me ^ jnp.asarray(links.masks(steps), dtype=jnp.int32)
        inside = jnp.arange(each)
        feature = owners[:, None] * real + inside[None, :]
        feature = jnp.where(inside[None, :] < real, feature, -1).reshape(-1)
        return (jnp.arange(inner)[:, None] == feature[None, :]).astype(BF16)

    token = []

    def run(work, *args):
        if token:
            args = lax.optimization_barrier((args, tuple(token)))[0]
        out = work(*args)
        token[:] = jax.tree.leaves(out)[:1]
        return out

    each = -(-w_query.shape[0] // ROW_TILE) * ROW_TILE
    slot = lambda w: pad_rows(w, each)[None]
    flat = lambda w: w.reshape(-1, width)
    far_bits = links.far_bits()
    ab, ba = (near, across), (across, near)

    def exchange(arrays, steps):
        return [(a, swap(a, step)) for a, step in zip(arrays, steps)]

    def swap_core(value):
        return [swap(v, core) for v in value]

    def close(value):
        return run(lambda v: v, value)

    class Gather:
        def __init__(self, array, cuts, direct=False, mark=None, paths=(ab, ba)):
            if mark is not None:
                array = after(array, mark)
            self.cuts, self.stage, self.paths = cuts, 0, paths
            self.hops = 1 if direct else len(far_bits)
            steps = far if direct else far_bits[:1]
            self.held = [array] + [swap(array, step) for step in steps]

        def go(self):
            self.stage += 1
            if self.stage < self.hops:
                (array,) = run(lambda *p: join([p]), *self.held)
                self.held = [array, swap(array, far_bits[self.stage])]
            elif self.stage == self.hops:
                parts = run(lambda *p: cut_join(list(p), self.cuts), *self.held)
                self.held = exchange(parts, self.paths[0])
            elif self.stage == self.hops + 1:
                self.held = exchange(run(join, self.held), self.paths[1])

        def start_of(self):
            first = self.held[0]
            return first[0] if isinstance(first, tuple) else first

        def core_go(self):
            self.held = exchange(run(join, self.held), (core, core))

        def core_end(self):
            return run(join, self.held)

    units = -(-w_gate.shape[0] // ROW_TILE)
    padded = [pad_rows(w, units * ROW_TILE) for w in (w_gate, w_up, w_ffn_out)]
    marks = [0, 3, 5, 7] if units == 7 else list(range(units + 1))
    shards = [
        jnp.stack([w[low * ROW_TILE : high * ROW_TILE] for w in padded])
        for low, high in zip(marks, marks[1:])
    ]
    attn_w = Gather(
        jnp.concatenate([slot(w) for w in (w_key, w_attn_out, w_value, w_query)], axis=1)[:, None],
        [(0, 2 * each), (2 * each, 2 * each)],
        direct=True,
    )
    same_core = ("dp", "x")
    by_hops = units == 7
    last_group = len(shards) - 1

    x = jnp.transpose(tokens, (0, 2, 1))
    dy = jnp.transpose(cotangent, (0, 2, 1))
    gain_one, gain_two = gain_attn[:, None], gain_ffn[:, None]
    place_a, place_b = spread_of(order_a + [core]), spread_of(order_b + [core])
    segs = lax.dynamic_slice_in_dim(segment_ids, my_ctx * size, size, 1)
    same = segs[:, None, :] == jnp.arange(DOCS, dtype=segs.dtype)[None, :, None]
    ones = jnp.ones((rows, 1, size), BF16)
    rest = AUG - 1 - DOCS
    aug = jnp.concatenate(
        [soft_mask[:, None, :], same.astype(BF16)] + [ones] * 3
        + [jnp.zeros((rows, rest - 3, size), BF16)],
        axis=1,
    )
    query_aug = jnp.concatenate(
        [ones, jnp.where(same, 0.0, MASK_VALUE).astype(BF16), jnp.zeros((rows, rest, size), BF16)],
        axis=1,
    )
    normed, dy_pair, *dy_own = run(first_norm, x, dy, gain_one)

    attn_w.go()
    ffn_w = [
        [lax.all_gather(after(shard, attn_w.start_of()), same_core)]
        for shard in (shards[:-1] if by_hops else shards)
    ]
    slots = jnp.array([0, 2, 1, 3], jnp.int32) ^ my_ctx
    bias, buckets_t = run(
        bias_of, slots, buckets, jnp.pad(bias_table.T, ((0, 0), (0, 128 - count)))
    )
    dy_parts = swap_core(dy_own)
    attn_w.go()
    dy_pair = run(fill, dy_pair, dy_parts)
    attn_w.core_go()
    wko, wvq = attn_w.core_end()
    pick = lambda w, k: w[:, 0, k * each : (k + 1) * each].reshape(-1, width)
    wk, wo, wv, wq = run(lambda a, b: [pick(a, 0), pick(a, 1), pick(b, 0), pick(b, 1)], wko, wvq)
    kv_own = run(lambda *a: key_value(*a, 0, rows), normed, wk, wv, place_a, place_b, aug)
    kv_across = swap(kv_own, across)
    kv_core = swap(kv_own, core)
    if by_hops:
        last_w = Gather(
            shards[-1][None], [(0, shards[-1].shape[1])], mark=kv_own, paths=((across,), (near,))
        )
    queries = run(lambda n, w, p: project(n, w, p, tile), normed, wq, place_b)
    kv_core = close(kv_core)
    if by_hops:
        last_w.go()

    kv = run(lambda *k: list(k), kv_own, kv_across, kv_core)
    kv.append(close(jnp.concatenate([swap(k, core) for k in jnp.split(kv[1], rows)])))
    attended, lse = run(lambda *a: attend(*a, heads, 0), queries, query_aug, kv, bias)
    if by_hops:
        last_w.go()
    mixed, n_pair, *normed_two = run(mix, x, attended, wo, place_a, gain_two)
    n_parts = close(swap_core(normed_two))
    if by_hops:
        last_w.go()
    n_pair = run(fill, n_pair, n_parts)

    class Sums:
        def __init__(self, grads, paths):
            self.paths = paths[: len(grads)]
            self.stage = 0
            self.send(grads)

        def send(self, halves):
            self.keep = [h[0] for h in halves]
            self.got = [swap(h[1], p[self.stage]) for h, p in zip(halves, self.paths)]

        def go(self):
            near_hops = len(self.paths[0])
            hops = near_hops + len(far_bits)
            self.stage += 1
            if self.stage > hops:
                return
            if self.stage < near_hops:
                self.send(run(add_halves, self.keep, self.got))
                return
            if self.stage == near_hops:
                rows_of = [k.shape[-2] for k in self.keep]
                self.edges = [sum(rows_of[:k]) for k in range(len(rows_of) + 1)]
                halves = run(lambda k, r: add_merge(k, r, self.edges), self.keep, self.got)
            elif self.stage < hops:
                halves = run(add_halves, self.keep, self.got)[0]
            else:
                self.out = run(lambda k, r: add_last(k[0], r[0], self.edges), self.keep, self.got)
                return
            self.keep = [halves[0]]
            self.got = [swap(halves[1], far_bits[hops - 1 - self.stage])]

    acts, sums = [], []
    me_same = (my_dp * (ctx // 2) + lax.axis_index("x")).reshape(1)
    masks = [[m >> 1 for m in links.masks(steps)] for steps in (ab, ba)]
    ffn_grads = []
    if by_hops:
        ffn_w.append(last_w.held[0])
    for i, ws in enumerate(ffn_w):
        some = tile if units_of(ws) <= 768 else tile // 2
        mask = masks[0] if by_hops and i == last_group - 1 else None
        if i == last_group and by_hops:
            ws = ffn_w[i] = close(list(ws))
        act, grads = run(
            lambda m, w, n, d: ffn_group(m, w, n, d, some, mask), me_same, ws, n_pair, dy_pair
        )
        acts.append(act)
        if by_hops and i >= last_group - 1:
            ffn_grads.append(grads)
        else:
            ffn_grads.append(lax.psum_scatter(grads[0], same_core))
    if by_hops:
        sums = [Sums(ffn_grads[-2:], [ba, ab])]

    def tick():
        for s in sums:
            s.go()

    back = run(lambda p, a: ffn_back(p, a, [0, 1], here, here, tile), ffn_w, acts)
    dn_parts = swap_core(back)
    out_other = run(lambda p, a: ffn_back(p, a, [2], here, here, tile), ffn_w, acts)
    dn_got = close(dn_parts)
    dmixed, dattended, gain_two_part, *gwo = run(
        mix_back, ffn_w, acts, mixed, dn_got, dy, attended, wo, place_a, gain_two
    )
    tick()
    dq, dkv, grad_bias = run(
        lambda *a: attend_back(*a, heads, 0, []),
        queries, query_aug, kv, bias, attended, dattended, lse,
    )
    tick()
    out_got = swap_core(out_other)
    by_core = [(dkv[0], swap(dkv[2], core)), (dkv[1], swap(dkv[3], core))]
    own, other = run(add_pairs, by_core)
    other = swap(other, across)
    entries = lambda g: tuple(v.reshape(-1, each, width) for v in g)
    home_a, home_b = (core,) + ba, (core,) + ab
    gwq = run(
        lambda n, d, p: projection_grads(n, [d], [(0, inner)], [p], rows), normed, dq, place_b
    )
    query_sum = Sums([entries(gwo), entries(gwq)], [home_a, home_b])
    grad_table = run(lambda g, b: bucket_sums(g, b, count), grad_bias, buckets_t)
    query_sum.go()
    out_got = close(out_got)
    query_sum.go()
    out = run(lambda *a: layer_out_of(*a, rows), ffn_w, acts, mixed, out_got)
    query_sum.go()
    (dkv,) = run(add_pairs, [(own, other)])
    gkv = run(
        lambda n, d, pa, pb: projection_grads(n, [d], [(0, inner), (inner, 2 * inner)], [pa, pb], rows),
        normed, dkv, place_a, place_b,
    )
    value_sum = Sums([entries(gkv[:2]), entries(gkv[2:])], [home_a, home_b])
    tick()
    value_sum.go()
    gx, gain_one_part = run(
        lambda *a: last(a[0], a[1], [a[2]], [a[3]], a[4:7], a[7:10], a[10]),
        x, dmixed, dq, dkv, wq, wk, wv, place_b, place_a, place_b, gain_one,
    )
    value_sum.go()
    query_sum.go()
    tick()
    small = jnp.concatenate(
        [jnp.sum(gain_one_part, 1), jnp.sum(gain_two_part, 1), grad_table.reshape(-1)]
    )
    length = small.shape[0]
    small = jnp.pad(small, (0, -length % 1024)).reshape(-1, 128)
    bits = [core, across] + [("dp", 1 << b) for b in range(dp.bit_length() - 1)]
    for k, one in enumerate(bits):
        got = swap(small, one)
        if k in (1, 2, 3):
            value_sum.go()
        small = run(lambda a, b: a + b, small, got)
    for _ in range(len(far_bits) + 4):
        for s in [query_sum, value_sum] + sums:
            s.go()
    small = small.reshape(-1)
    real = w_query.shape[0]
    if by_hops:
        ffn_grads[-2:] = sums[0].out
    grad_gate, grad_up, grad_ffn_out = (
        jnp.concatenate([g[j].astype(F32) for g in ffn_grads])[: w_gate.shape[0]] for j in range(3)
    )
    return (
        jnp.transpose(out, (0, 2, 1)),
        jnp.transpose(gx, (0, 2, 1)),
        dkv[:, 2 * inner].astype(F32),
        small[:width],
        small[width : 2 * width],
        small[2 * width : length].reshape(count, heads),
        query_sum.out[1][:real],
        value_sum.out[0][:real],
        value_sum.out[1][:real],
        query_sum.out[0][:real],
        grad_gate,
        grad_up,
        grad_ffn_out,
    )


def solution(mesh):
    dp, ctx = mesh.shape["dp"], mesh.shape["ctx"]
    by_core = Mesh(mesh.devices.reshape(dp, ctx // 2, 2), ("dp", "x", "core"))
    ctx_axes = ("x", "core")
    split = P(("dp", "x", "core"), None)
    act = P("dp", ctx_axes, None)
    in_specs = (
        (act, P("dp", ctx_axes), P("dp", None), P(ctx_axes, None), P(), P(), P()) + (split,) * 7 + (act,)
    )
    out_specs = (act, act, P("dp", ctx_axes), P(), P(), P()) + (split,) * 7
    return jax.shard_map(
        functools.partial(per_device, dp, ctx),
        mesh=by_core,
        in_specs=in_specs,
        out_specs=out_specs,
        check_vma=False,
    )
```

time: 867 us -> 680 us (0.78)
  waiting for transfers between devices: 298 us -> 195 us
  other arithmetic: 80.9 us -> 44.7 us
  starting transfers between devices: 84.8 us -> 48.7 us
  local copies, waits for them, and re-layouts: 70.5 us -> 39.8 us
  between operations: 2.24 us -> 15.1 us
  Pallas kernels: 320 us -> 331 us
    ppermute x87 -> x65, waiting for transfers between devices: 298 us -> 180 us  [swap(): lax.ppermute(x, axis, [(i, i ^ mask) for i in range(self.sizes[axis])])]
    ppermute x87 -> x65, starting transfers between devices: 84.8 us -> 48.4 us  [swap(): lax.ppermute(x, axis, [(i, i ^ mask) for i in range(self.sizes[axis])])]
    concatenate x25 -> x14, other arithmetic: 29.5 us -> 9.84 us  [the longest x2 3.41 us: join(): return [jnp.concatenate(list(pair), axis=0) for pair in pairs]]
    another operation x3 -> x4, local copies, waits for them, and re-layouts: 19 us -> 3.96 us  [per_device(): jnp.stack([w[low * ROW_TILE:high * ROW_TILE] for w in padded])]
    all_gather x0 -> x2, waiting for transfers between devices: none -> 14.8 us  [per_device(): lax.all_gather(after(shard, attn_w.start_of()), same_core)]
    another operation x4 -> x2, other arithmetic: 12.4 us -> 1.57 us  [per_device(): jnp.stack([w[low * ROW_TILE:high * ROW_TILE] for w in padded])]
    pallas_call x13 -> x14, Pallas kernels: 272 us -> 282 us  [the longest x3 100 us: ffn_group(): pl.pallas_call(functools.partial(ffn_body, len(ws), masks), grid_spec=spe...]
    unnamed x144 -> x99, local copies, waits for them, and re-layouts: 19 us -> 9.18 us
  transfers between devices with their start and end apart: 87 -> 68, of which waited for: 32 -> 26; matrix products, arithmetic and copies ran while one was open for 17% -> 10% of each run, Pallas kernels for 37% -> 45%
where the time goes in v2:
time: 680 us; the launch traced here: 674 us
  Pallas kernels  331 us (49%)
  waiting for transfers between devices  195 us (29%)
  starting transfers between devices  48.7 us (7%)
  other arithmetic  44.7 us (7%)
  local copies, waits for them, and re-layouts  39.8 us (6%)
  between operations  15.1 us (2%)
    ppermute x65, waiting for transfers between devices, swap(): lax.ppermute(x, axis, [(i, i ^ mask) for i in range(self.sizes[axis])])  180 us
    pallas_call x3, Pallas kernels, ffn_group(): pl.pallas_call(functools.partial(ffn_body, len(ws), masks), grid_spec=spe...  100 us
    ppermute x65, starting transfers between devices, swap(): lax.ppermute(x, axis, [(i, i ^ mask) for i in range(self.sizes[axis])])  48.4 us
    pallas_call x1, Pallas kernels, attend_back(): pl.pallas_call(functools.partial(attend_back_body, heads, inner, count, l...  41.4 us
    pallas_call x1, Pallas kernels, mix_back(): pl.pallas_call(functools.partial(mix_back_body, layout_of(groups)), grid=...  38.6 us
    pallas_call x2, Pallas kernels, ffn_back(): pl.pallas_call(functools.partial(ffn_back_body, layout_of(groups), kinds)...  30.4 us
    pallas_call x2, Pallas kernels, projection_grads(): pl.pallas_call(functools.partial(grads_body, per, len(groups), parts), gr...  20.3 us
    pallas_call x1, Pallas kernels, last(): pl.pallas_call(functools.partial(last_body, per, len(dqs)), grid=(rows,),...  18.9 us
  transfers between devices with their start and end apart: 68, of which 26 were waited for; matrix products, arithmetic and copies ran while one was open for 10% of the time, Pallas kernels for 45%

profile of v2, /device:TPU:0, one launch (start us, length us, event | category | flops | bytes accessed | tf_op | source)
XLA Modules:
  0.0 674.2 jit_solution(2318470734603481501)
XLA Ops:
  54.8 18.8 %collective-permute-done.6 = bf16[8,1,32,1472]{3,2,1,0:T(8,128)(2,1)S(1)} collective-permute-done((bf16[8,1,32,1472]{3,2,1,0:T(8,128)(2,1)S(1)}, bf16[8,1,32,1472]{3,2,1,0:T(8,128)(2,1)S(1)}, u32[]{:S(2)}, u32[]{:S(2)}) %collective-permute-start.6) | collective-permute-done | bytes 753696 | tf_op jit(solution)/shard_map/ppermute | solution.py:892
  90.7 12.3 %key_value.1.refs_0_ = bf16[4,784,256]{2,1,0:T(8,128)(2,1)} custom-call(bf16[1472,1024]{1,0:T(8,128)(2,1)} %get-tuple-element.606.n_ref, bf16[512,1472]{1,0:T(8,128)(2,1)} %bitcast.127, bf16[512,1472]{1,0:T(8,128)(2,1)} %bitcast.129, bf16[384,512]{1,0:T(8,128)(2,1)} %fusion.pk_ref.place_ref.refs_15_.refs_1_.refs_6_, ...), custom_call_target="tpu_custom_call" | custom-call | flops 1 | bytes 1 | tf_op jit(solution)/shard_map/key_value/pallas_call | solution.py:139
  110.9 12.2 %collective-permute-done.13 = bf16[1,3,32,1472]{3,2,1,0:T(8,128)(2,1)S(1)} collective-permute-done((bf16[1,3,32,1472]{3,2,1,0:T(8,128)(2,1)S(1)}, bf16[1,3,32,1472]{3,2,1,0:T(8,128)(2,1)S(1)}, u32[]{:S(2)}, u32[]{:S(2)}) %collective-permute-start.13) | collective-permute-done | bytes 282656 | tf_op jit(solution)/shard_map/ppermute | solution.py:892
  123.6 32.9 %collective-permute-done.16.refs_1_ = bf16[4,784,256]{2,1,0:T(8,128)(2,1)S(1)} collective-permute-done((bf16[4,784,256]{2,1,0:T(8,128)(2,1)}, bf16[4,784,256]{2,1,0:T(8,128)(2,1)S(1)}, u32[]{:S(2)}, u32[]{:S(2)}) %collective-permute-start.16) | collective-permute-done | bytes 1605664 | tf_op jit(solution)/shard_map/ppermute | solution.py:892
  162.6 18.3 %attend.1 = (bf16[384,1024]{1,0:T(8,128)(2,1)}, f32[4,8,256]{2,1,0:T(8,128)}) custom-call(bf16[384,1024]{1,0:T(8,128)(2,1)} %project.1.q_ref, bf16[4,16,256]{2,1,0:T(8,128)(2,1)} %maximum_maximum_fusion.1.u_ref, bf16[4,784,256]{2,1,0:T(8,128)(2,1)} %key_value.1.refs_0_, bf16[4,784,256]{2,1,0:T(8,128)(2,1)} %copy-done.3, bf16[4,784,256]{2,1,0:T(8,128)(2,1)} %copy-done.4, ...), custom_call_target="tpu_custom_call" | custom-call | flops 1 | bytes 1 | tf_op jit(solution)/shard_map/attend/pallas_call | solution.py:209
  182.7 9.7 %mix.1 = (f32[1472,1024]{1,0:T(8,128)}, bf16[2,1472,1024]{2,1,0:T(8,128)(2,1)}, bf16[368,1024]{1,0:T(8,128)(2,1)}, bf16[368,1024]{1,0:T(8,128)(2,1)}, bf16[368,1...) custom-call(bf16[4,1472,256]{2,1,0:T(8,128)(2,1)} %bitcast.123, bf16[384,1024]{1,0:T(8,128)(2,1)} %get-tuple-element.548.o_ref.refs_13_.refs_5_, ...), custom_call_target="tpu_custom_call" | custom-call | flops 1 | bytes 1 | tf_op jit(solution)/shard_map/mix/pallas_call | solution.py:426
  199.1 17.8 %collective-permute-done.21 = bf16[4,3,32,1472]{3,2,1,0:T(8,128)(2,1)} collective-permute-done((bf16[4,3,32,1472]{3,2,1,0:T(8,128)(2,1)S(1)}, bf16[4,3,32,1472]{3,2,1,0:T(8,128)(2,1)}, u32[]{:S(2)}, u32[]{:S(2)}) %collective-permute-start.21) | collective-permute-done | bytes 1130528 | tf_op jit(solution)/shard_map/ppermute | solution.py:892
  224.3 41.2 %ffn_group.3 = (bf16[3,768,2048]{2,1,0:T(8,128)(2,1)}, bf16[16,3,48,1472]{3,2,1,0:T(8,128)(2,1)}) custom-call(s32[1]{0:T(128)} %bitcast.29.me_ref, bf16[16,3,48,1472]{3,2,1,0:T(8,128)(2,1)} %bitcast.112, bf16[2,1472,1024]{2,1,0:T(8,128)(2,1)} %bitcast_dynamic-update-slice_fusion.refs_1_.refs_2_, ...), custom_call_target="tpu_custom_call" | custom-call | flops 1 | bytes 1 | tf_op jit(solution)/shard_map/ffn_group/pallas_call | solution.py:552
  265.4 14.8 %all-gather.7.cloned.1.call-done = bf16[48,32,1472]{2,1,0:T(8,128)(2,1)} async-done(((bf16[3,32,1472]{2,1,0:T(8,128)(2,1)}), bf16[48,32,1472]{2,1,0:T(8,128)(2,1)}) %all-gather.7.cloned.1.call-update) | async-done | bytes 4522000 | tf_op jit(solution)/shard_map/all_gather | solution.py:1023
  280.3 29.5 %ffn_group.4 = (bf16[3,512,2048]{2,1,0:T(8,128)(2,1)}, bf16[8,3,32,1472]{3,2,1,0:T(8,128)(2,1)}, bf16[8,3,32,1472]{3,2,1,0:T(8,128)(2,1)}) custom-call(s32[1]{0:T(128)} %bitcast.29.me_ref, bf16[16,3,32,1472]{3,2,1,0:T(8,128)(2,1)} %bitcast.117, bf16[2,1472,1024]{2,1,0:T(8,128)(2,1)} %bitcast_dynamic-update-slice_fusion.refs_1_.refs_2_, ...), custom_call_target="tpu_custom_call" | custom-call | flops 1 | bytes 1 | tf_op jit(solution)/shard_map/ffn_group/pallas_call | solution.py:552
  309.8 29.7 %ffn_group.5 = (bf16[3,512,2048]{2,1,0:T(8,128)(2,1)}, bf16[8,3,32,1472]{3,2,1,0:T(8,128)(2,1)}, bf16[8,3,32,1472]{3,2,1,0:T(8,128)(2,1)}) custom-call(s32[1]{0:T(128)} %bitcast.29.me_ref, bf16[8,3,32,1472]{3,2,1,0:T(8,128)(2,1)} %copy-done.2, bf16[8,3,32,1472]{3,2,1,0:T(8,128)(2,1)} %collective-permute-done.26.refs_1_.refs_3_, ...), custom_call_target="tpu_custom_call" | custom-call | flops 1 | bytes 1 | tf_op jit(solution)/shard_map/ffn_group/pallas_call | solution.py:552
  341.6 19.0 %ffn_back.2 = (bf16[368,1024]{1,0:T(8,128)(2,1)}, bf16[368,1024]{1,0:T(8,128)(2,1)}, bf16[368,1024]{1,0:T(8,128)(2,1)}, bf16[368,1024]{1,0:T(8,128)(2,1)}) custom-call(bf16[16,3,48,1472]{3,2,1,0:T(8,128)(2,1)} %bitcast.113, bf16[16,3,32,1472]{3,2,1,0:T(8,128)(2,1)} %bitcast.118, bf16[8,3,32,1472]{3,2,1,0:T(8,128)(2,1)} %copy-done.2, ...), custom_call_target="tpu_custom_call" | custom-call | flops 1 | bytes 1 | tf_op jit(solution)/shard_map/ffn_back/pallas_call | solution.py:619
  363.2 11.4 %ffn_back.3 = (bf16[368,1024]{1,0:T(8,128)(2,1)}, bf16[368,1024]{1,0:T(8,128)(2,1)}, bf16[368,1024]{1,0:T(8,128)(2,1)}, bf16[368,1024]{1,0:T(8,128)(2,1)}) custom-call(bf16[16,3,48,1472]{3,2,1,0:T(8,128)(2,1)} %bitcast.114, bf16[16,3,32,1472]{3,2,1,0:T(8,128)(2,1)} %bitcast.119, bf16[8,3,32,1472]{3,2,1,0:T(8,128)(2,1)} %copy-done.2, ...), custom_call_target="tpu_custom_call" | custom-call | flops 1 | bytes 1 | tf_op jit(solution)/shard_map/ffn_back/pallas_call | solution.py:619
  378.5 38.6 %mix_back.1 = (f32[1472,1024]{1,0:T(8,128)}, bf16[384,1024]{1,0:T(8,128)(2,1)}, f32[1472,128]{1,0:T(8,128)}, bf16[256,1472]{1,0:T(8,128)(2,1)}, bf16[256,1472]{1,0:T(8,128)(2,1)}) custom-call(bf16[16,3,48,1472]{3,2,1,0:T(8,128)(2,1)} %bitcast.115, bf16[16,3,32,1472]{3,2,1,0:T(8,128)(2,1)} %bitcast.120, bf16[8,3,32,1472]{3,2,1,0:T(8,128)(2,1)} %copy-done.2, ...), custom_call_target="tpu_custom_call" | custom-call | flops 1 | bytes 1 | tf_op jit(solution)/shard_map/mix_back/pallas_call | solution.py:719
  424.8 41.4 %attend_back.1 = (bf16[384,1024]{1,0:T(8,128)(2,1)}, bf16[4,784,256]{2,1,0:T(8,128)(2,1)}, bf16[4,784,256]{2,1,0:T(8,128)(2,1)}, bf16[4,784,256]{2,1,0:T(8,128)(...) custom-call(bf16[384,1024]{1,0:T(8,128)(2,1)} %project.1.q_ref, ...), custom_call_target="tpu_custom_call" | custom-call | flops 1 | bytes 1 | tf_op jit(solution)/shard_map/attend_back/pallas_call | solution.py:304
  474.5 7.9 %projection_grads.2 = (bf16[256,1472]{1,0:T(8,128)(2,1)}, bf16[256,1472]{1,0:T(8,128)(2,1)}) custom-call(bf16[1472,1024]{1,0:T(8,128)(2,1)} %get-tuple-element.606.n_ref, bf16[384,1024]{1,0:T(8,128)(2,1)} %get-tuple-element.620.refs_0_, bf16[384,512]{1,0:T(8,128)(2,1)} %fusion.1.pv_ref.p_ref.refs_1_.refs_2_.refs_5_.refs_7_), custom_call_target="tpu_custom_call" | custom-call | flops 1 | bytes 1 | tf_op jit(solution)/shard_map/projection_grads/pallas_call | solution.py:794
  483.4 8.3 %bucket_sums.1 = f32[96,256]{1,0:T(8,128)} custom-call(s32[4,256,256]{2,1,0:T(8,128)} %get-tuple-element.572.buckets_ref, f32[6,4,256,256]{3,2,1,0:T(8,128)} %get-tuple-element.573.g_ref), custom_call_target="tpu_custom_call" | custom-call | flops 1 | bytes 1 | tf_op jit(solution)/shard_map/bucket_sums/pallas_call | solution.py:383
  501.6 9.2 %collective-permute-done.43 = bf16[8,16,1472]{2,1,0:T(8,128)(2,1)S(1)} collective-permute-done((bf16[8,16,1472]{2,1,0:T(8,128)(2,1)S(1)}, bf16[8,16,1472]{2,1,0:T(8,128)(2,1)S(1)}, u32[]{:S(2)}, u32[]{:S(2)}) %collective-permute-start.43) | collective-permute-done | bytes 376864 | tf_op jit(solution)/shard_map/ppermute | solution.py:892
  517.4 13.0 %layer_out_of.1 = bf16[4,1472,256]{2,1,0:T(8,128)(2,1)} custom-call(bf16[16,3,48,1472]{3,2,1,0:T(8,128)(2,1)} %bitcast.116, bf16[16,3,32,1472]{3,2,1,0:T(8,128)(2,1)} %bitcast.121, bf16[8,3,32,1472]{3,2,1,0:T(8,128)(2,1)} %copy-done.2, bf16[8,3,32,1472]{3,2,1,0:T(8,128)(2,1)} %collective-permute-done.26.refs_1_.refs_3_, ...), custom_call_target="tpu_custom_call" | custom-call | flops 1 | bytes 1 | tf_op jit(solution)/shard_map/layer_out_of/pallas_call | solution.py:644
  530.4 23.4 %collective-permute-done.47 = bf16[4,16,1472]{2,1,0:T(8,128)(2,1)} collective-permute-done((bf16[4,16,1472]{2,1,0:T(8,128)(2,1)S(1)}, bf16[4,16,1472]{2,1,0:T(8,128)(2,1)}, u32[]{:S(2)}, u32[]{:S(2)}) %collective-permute-start.47) | collective-permute-done | bytes 188448 | tf_op jit(solution)/shard_map/ppermute | solution.py:892
  558.0 12.4 %projection_grads.3 = (bf16[256,1472]{1,0:T(8,128)(2,1)}, bf16[256,1472]{1,0:T(8,128)(2,1)}, bf16[256,1472]{1,0:T(8,128)(2,1)}, bf16[256,1472]{1,0:T(8,128)(2,1)}) custom-call(bf16[1472,1024]{1,0:T(8,128)(2,1)} %get-tuple-element.606.n_ref, bf16[4,784,256]{2,1,0:T(8,128)(2,1)} %add.258.refs_0_.refs_1_, ...), custom_call_target="tpu_custom_call" | custom-call | flops 1 | bytes 1 | tf_op jit(solution)/shard_map/projection_grads/pallas_call | solution.py:794
  583.7 18.9 %last.1 = (f32[4,1472,256]{2,1,0:T(8,128)}, f32[1472,128]{1,0:T(8,128)}) custom-call(bf16[4,1472,256]{2,1,0:T(8,128)(2,1)} %bitcast.124, f32[1472,1024]{1,0:T(8,128)} %get-tuple-element.619.dm_ref, bf16[384,1024]{1,0:T(8,128)(2,1)} %get-tuple-element.620.refs_0_, bf16[4,784,256]{2,1,0:T(8,128)(2,1)} %add.258.refs_0_.refs_1_, bf16[512,1472]{1,0:T(8,128)(2,1)} %bitcast.132, ...), custom_call_target="tpu_custom_call" | custom-call | flops 1 | bytes 1 | tf_op jit(solution)/shard_map/last/pallas_call | solution.py:855
  611.0 22.0 %collective-permute-done.64 = bf16[1,3,64,1472]{3,2,1,0:T(8,128)(2,1)S(1)} collective-permute-done((bf16[1,3,64,1472]{3,2,1,0:T(8,128)(2,1)S(1)}, bf16[1,3,64,1472]{3,2,1,0:T(8,128)(2,1)S(1)}, u32[]{:S(2)}, u32[]{:S(2)}) %collective-permute-start.64) | collective-permute-done | bytes 565280 | tf_op jit(solution)/shard_map/ppermute | solution.py:892
  637.3 14.6 %collective-permute-done.58 = bf16[2,32,1472]{2,1,0:T(8,128)(2,1)S(1)} collective-permute-done((bf16[2,32,1472]{2,1,0:T(8,128)(2,1)S(1)}, bf16[2,32,1472]{2,1,0:T(8,128)(2,1)S(1)}, u32[]{:S(2)}, u32[]{:S(2)}) %collective-permute-start.58) | collective-permute-done | bytes 188448 | tf_op jit(solution)/shard_map/ppermute | solution.py:892
  (353 shorter events, 181.9 us)
Async XLA Ops:
  7.2 217.1 %all-gather.5.cloned.1.call-start = ((), (), s32[]{:S(2)}) async-start(), calls=%async_computation.2 | async-start | bytes 7520256 | tf_op jit(solution)/shard_map/all_gather | solution.py:1023
  30.9 249.3 %all-gather.7.cloned.1.call-start = ((), (), s32[]{:S(2)}) async-start(), calls=%async_computation.3 | async-start | bytes 5013504 | tf_op jit(solution)/shard_map/all_gather | solution.py:1023
  48.9 24.7 %collective-permute-start.6 = (bf16[8,1,32,1472]{3,2,1,0:T(8,128)(2,1)S(1)}, bf16[8,1,32,1472]{3,2,1,0:T(8,128)(2,1)S(1)}, u32[]{:S(2)}, u32[]{:S(2)}) collective-permute-start(bf16[8,1,32,1472]{3,2,1,0:T(8,128)(2,1)S(1)} %constant_dynamic-update-slice_fusion.2), channel_id=1, source_target_pairs={{0,4},{4,0},{8,12},{12,8},{16,20},{20,16},{24,28},{28,24},{1,5},{5... | collective-permute-start | bytes 2261000 | tf_op jit(solution)/shard_map/ppermute | solution.py:892
  49.3 26.5 %collective-permute-start.5 = (bf16[8,1,32,1472]{3,2,1,0:T(8,128)(2,1)S(1)}, bf16[8,1,32,1472]{3,2,1,0:T(8,128)(2,1)S(1)}, u32[]{:S(2)}, u32[]{:S(2)}) collective-permute-start(bf16[8,1,32,1472]{3,2,1,0:T(8,128)(2,1)S(1)} %constant_dynamic-update-slice_fusion), channel_id=1, source_target_pairs={{0,2},{2,0},{1,3},{3,1},{4,6},{6,4},{5,7},{7,5},{8,10},{10,8},{9,1... | collective-permute-start | bytes 2261000 | tf_op jit(solution)/shard_map/ppermute | solution.py:892
  83.2 580.2 %reduce-scatter.2.cloned.1.call-start = ((), (), s32[]{:S(2)}) async-start(), calls=%async_computation.1 | async-start | bytes 7520256 | tf_op jit(solution)/shard_map/reduce_scatter | solution.py:1109
  103.0 53.4 %collective-permute-start.16 = (bf16[4,784,256]{2,1,0:T(8,128)(2,1)}, bf16[4,784,256]{2,1,0:T(8,128)(2,1)S(1)}, u32[]{:S(2)}, u32[]{:S(2)}) collective-permute-start(bf16[4,784,256]{2,1,0:T(8,128)(2,1)} %key_value.1.refs_0_), channel_id=1, source_target_pairs={{0,2},{2,0},{1,3},{3,1},{4,6},{6,4},{5,7},{7,5},{8,10},{10,8},{9,1... | collective-permute-start | bytes 4816904 | tf_op jit(solution)/shard_map/ppermute | solution.py:892
  123.2 57.7 %collective-permute-start.15 = (bf16[2,3,32,1472]{3,2,1,0:T(8,128)(2,1)S(1)}, bf16[2,3,32,1472]{3,2,1,0:T(8,128)(2,1)S(1)}, u32[]{:S(2)}, u32[]{:S(2)}) collective-permute-start(bf16[2,3,32,1472]{3,2,1,0:T(8,128)(2,1)S(1)} %constant_dynamic-update-slice_fusion.8), channel_id=1, source_target_pairs={{0,16},{4,20},{8,24},{12,28},{16,0},{20,4},{24,8},{28,12},{1,17},{... | collective-permute-start | bytes 1695752 | tf_op jit(solution)/shard_map/ppermute | solution.py:892
  181.0 35.9 %collective-permute-start.21 = (bf16[4,3,32,1472]{3,2,1,0:T(8,128)(2,1)S(1)}, bf16[4,3,32,1472]{3,2,1,0:T(8,128)(2,1)}, u32[]{:S(2)}, u32[]{:S(2)}) collective-permute-start(bf16[4,3,32,1472]{3,2,1,0:T(8,128)(2,1)S(1)} %constant_dynamic-update-slice_fusion.10), channel_id=1, source_target_pairs={{0,2},{2,0},{1,3},{3,1},{4,6},{6,4},{5,7},{7,5},{8,10},{10,8},{9,1... | collective-permute-start | bytes 3391496 | tf_op jit(solution)/shard_map/ppermute | solution.py:892
  218.4 91.4 %collective-permute-start.26 = (bf16[8,3,32,1472]{3,2,1,0:T(8,128)(2,1)S(1)}, bf16[8,3,32,1472]{3,2,1,0:T(8,128)(2,1)}, u32[]{:S(2)}, u32[]{:S(2)}) collective-permute-start(bf16[8,3,32,1472]{3,2,1,0:T(8,128)(2,1)S(1)} %constant_dynamic-update-slice_fusion.12.refs_0_.refs_2_), channel_id=1, source_target_pairs={{0,4},{4,0},{8,12},{12,8},{16,20},{20,16},{24,28},{28,24},{1,5},{5... | collective-permute-start | bytes 6782984 | tf_op jit(solution)/shard_map/ppermute | solution.py:892
  339.5 77.6 %collective-permute-start.36 = (bf16[8,3,32,1472]{3,2,1,0:T(8,128)(2,1)}, bf16[8,3,32,1472]{3,2,1,0:T(8,128)(2,1)S(1)}, u32[]{:S(2)}, u32[]{:S(2)}) collective-permute-start(bf16[8,3,32,1472]{3,2,1,0:T(8,128)(2,1)} %get-tuple-element.537), channel_id=1, source_target_pairs={{0,4},{4,0},{8,12},{12,8},{16,20},{20,16},{24,28},{28,24},{1,5},{5... | collective-permute-start | bytes 6782984 | tf_op jit(solution)/shard_map/ppermute | solution.py:892
  340.1 76.9 %collective-permute-start.35 = (bf16[8,3,32,1472]{3,2,1,0:T(8,128)(2,1)}, bf16[8,3,32,1472]{3,2,1,0:T(8,128)(2,1)}, u32[]{:S(2)}, u32[]{:S(2)}) collective-permute-start(bf16[8,3,32,1472]{3,2,1,0:T(8,128)(2,1)} %get-tuple-element.536), channel_id=1, source_target_pairs={{0,2},{2,0},{1,3},{3,1},{4,6},{6,4},{5,7},{7,5},{8,10},{10,8},{9,1... | collective-permute-start | bytes 6782984 | tf_op jit(solution)/shard_map/ppermute | solution.py:892
  421.5 45.4 %collective-permute-start.39 = (bf16[4,3,32,1472]{3,2,1,0:T(8,128)(2,1)}, bf16[4,3,32,1472]{3,2,1,0:T(8,128)(2,1)S(1)}, u32[]{:S(2)}, u32[]{:S(2)}) collective-permute-start(bf16[4,3,32,1472]{3,2,1,0:T(8,128)(2,1)} %get-tuple-element.691), channel_id=1, source_target_pairs={{0,4},{4,0},{8,12},{12,8},{16,20},{20,16},{24,28},{28,24},{1,5},{5... | collective-permute-start | bytes 3391496 | tf_op jit(solution)/shard_map/ppermute | solution.py:892
  424.3 42.7 %collective-permute-start.40 = (bf16[4,3,32,1472]{3,2,1,0:T(8,128)(2,1)}, bf16[4,3,32,1472]{3,2,1,0:T(8,128)(2,1)}, u32[]{:S(2)}, u32[]{:S(2)}) collective-permute-start(bf16[4,3,32,1472]{3,2,1,0:T(8,128)(2,1)} %get-tuple-element.689), channel_id=1, source_target_pairs={{0,2},{2,0},{1,3},{3,1},{4,6},{6,4},{5,7},{7,5},{8,10},{10,8},{9,1... | collective-permute-start | bytes 3391496 | tf_op jit(solution)/shard_map/ppermute | solution.py:892
  466.8 26.9 %collective-permute-start.41 = (bf16[16,16,1472]{2,1,0:T(8,128)(2,1)}, bf16[16,16,1472]{2,1,0:T(8,128)(2,1)}, u32[]{:S(2)}, u32[]{:S(2)}) collective-permute-start(bf16[16,16,1472]{2,1,0:T(8,128)(2,1)} %bitcast.147), channel_id=1, source_target_pairs={{0,1},{1,0},{2,3},{3,2},{4,5},{5,4},{6,7},{7,6},{8,9},{9,8},{10,11... | collective-permute-start | bytes 2261000 | tf_op jit(solution)/shard_map/ppermute | solution.py:892
  501.0 55.4 %collective-permute-start.45 = (bf16[4,784,256]{2,1,0:T(8,128)(2,1)S(1)}, bf16[4,784,256]{2,1,0:T(8,128)(2,1)S(1)}, u32[]{:S(2)}, u32[]{:S(2)}) collective-permute-start(bf16[4,784,256]{2,1,0:T(8,128)(2,1)S(1)} %add.252), channel_id=1, source_target_pairs={{0,2},{2,0},{1,3},{3,1},{4,6},{6,4},{5,7},{7,5},{8,10},{10,8},{9,1... | collective-permute-start | bytes 4816904 | tf_op jit(solution)/shard_map/ppermute | solution.py:892
  513.2 40.6 %collective-permute-start.47 = (bf16[4,16,1472]{2,1,0:T(8,128)(2,1)S(1)}, bf16[4,16,1472]{2,1,0:T(8,128)(2,1)}, u32[]{:S(2)}, u32[]{:S(2)}) collective-permute-start(bf16[4,16,1472]{2,1,0:T(8,128)(2,1)S(1)} %get-tuple-element.725), channel_id=1, source_target_pairs={{0,2},{2,0},{1,3},{3,1},{4,6},{6,4},{5,7},{7,5},{8,10},{10,8},{9,1... | collective-permute-start | bytes 565256 | tf_op jit(solution)/shard_map/ppermute | solution.py:892
  515.9 57.7 %collective-permute-start.50 = (bf16[2,3,64,1472]{3,2,1,0:T(8,128)(2,1)}, bf16[2,3,64,1472]{3,2,1,0:T(8,128)(2,1)}, u32[]{:S(2)}, u32[]{:S(2)}) collective-permute-start(bf16[2,3,64,1472]{3,2,1,0:T(8,128)(2,1)} %pad_maximum_fusion.4), channel_id=1, source_target_pairs={{0,16},{4,20},{8,24},{12,28},{16,0},{20,4},{24,8},{28,12},{1,17},{... | collective-permute-start | bytes 3391496 | tf_op jit(solution)/shard_map/ppermute | solution.py:892
  576.5 30.4 %collective-permute-start.53 = (bf16[8,16,1472]{2,1,0:T(8,128)(2,1)S(1)}, bf16[8,16,1472]{2,1,0:T(8,128)(2,1)}, u32[]{:S(2)}, u32[]{:S(2)}) collective-permute-start(bf16[8,16,1472]{2,1,0:T(8,128)(2,1)S(1)} %get-tuple-element.709), channel_id=1, source_target_pairs={{0,2},{2,0},{1,3},{3,1},{4,6},{6,4},{5,7},{7,5},{8,10},{10,8},{9,1... | collective-permute-start | bytes 1130504 | tf_op jit(solution)/shard_map/ppermute | solution.py:892
  578.9 28.0 %collective-permute-start.54 = (bf16[8,16,1472]{2,1,0:T(8,128)(2,1)S(1)}, bf16[8,16,1472]{2,1,0:T(8,128)(2,1)}, u32[]{:S(2)}, u32[]{:S(2)}) collective-permute-start(bf16[8,16,1472]{2,1,0:T(8,128)(2,1)S(1)} %get-tuple-element.707), channel_id=1, source_target_pairs={{0,4},{4,0},{8,12},{12,8},{16,20},{20,16},{24,28},{28,24},{1,5},{5... | collective-permute-start | bytes 1130504 | tf_op jit(solution)/shard_map/ppermute | solution.py:892
  580.2 27.8 %collective-permute-start.61 = (bf16[2,32,1472]{2,1,0:T(8,128)(2,1)S(1)}, bf16[2,32,1472]{2,1,0:T(8,128)(2,1)S(1)}, u32[]{:S(2)}, u32[]{:S(2)}) collective-permute-start(bf16[2,32,1472]{2,1,0:T(8,128)(2,1)S(1)} %pad_maximum_fusion.15), channel_id=1, source_target_pairs={{0,16},{4,20},{8,24},{12,28},{16,0},{20,4},{24,8},{28,12},{1,17},{... | collective-permute-start | bytes 565256 | tf_op jit(solution)/shard_map/ppermute | solution.py:892
  605.5 27.4 %collective-permute-start.64 = (bf16[1,3,64,1472]{3,2,1,0:T(8,128)(2,1)S(1)}, bf16[1,3,64,1472]{3,2,1,0:T(8,128)(2,1)S(1)}, u32[]{:S(2)}, u32[]{:S(2)}) collective-permute-start(bf16[1,3,64,1472]{3,2,1,0:T(8,128)(2,1)S(1)} %get-tuple-element.697), channel_id=1, source_target_pairs={{0,8},{4,12},{8,0},{12,4},{16,24},{20,28},{24,16},{28,20},{1,9},{5... | collective-permute-start | bytes 1695752 | tf_op jit(solution)/shard_map/ppermute | solution.py:892
  605.6 30.1 %collective-permute-start.52 = (f32[32,128]{1,0:T(8,128)S(1)}, f32[32,128]{1,0:T(8,128)S(1)}, u32[]{:S(2)}, u32[]{:S(2)}) collective-permute-start(f32[32,128]{1,0:T(8,128)S(1)} %add.263), channel_id=1, source_target_pairs={{0,2},{2,0},{1,3},{3,1},{4,6},{6,4},{5,7},{7,5},{8,10},{10,8},{9,1... | collective-permute-start | bytes 49160 | tf_op jit(solution)/shard_map/ppermute | solution.py:892
  607.9 25.0 %collective-permute-start.55 = (bf16[4,16,1472]{2,1,0:T(8,128)(2,1)S(1)}, bf16[4,16,1472]{2,1,0:T(8,128)(2,1)S(1)}, u32[]{:S(2)}, u32[]{:S(2)}) collective-permute-start(bf16[4,16,1472]{2,1,0:T(8,128)(2,1)S(1)} %get-tuple-element.723), channel_id=1, source_target_pairs={{0,4},{4,0},{8,12},{12,8},{16,20},{20,16},{24,28},{28,24},{1,5},{5... | collective-permute-start | bytes 565256 | tf_op jit(solution)/shard_map/ppermute | solution.py:892
  633.0 27.5 %collective-permute-start.62 = (bf16[1,32,1472]{2,1,0:T(8,128)(2,1)S(1)}, bf16[1,32,1472]{2,1,0:T(8,128)(2,1)S(1)}, u32[]{:S(2)}, u32[]{:S(2)}) collective-permute-start(bf16[1,32,1472]{2,1,0:T(8,128)(2,1)S(1)} %get-tuple-element.734), channel_id=1, source_target_pairs={{0,8},{4,12},{8,0},{12,4},{16,24},{20,28},{24,16},{28,20},{1,9},{5... | collective-permute-start | bytes 282632 | tf_op jit(solution)/shard_map/ppermute | solution.py:892
  (89 other events, 851.5 us)
Sparse Core Ops, SparseCore 0:
  31.1 139.2 all-gather.4
  173.7 106.4 all-gather.6
  467.0 189.1 reduce-scatter.1

commit v3 on v2

--- a/solution.py
+++ b/solution.py
@@ -69,8 +69,17 @@
     return [jnp.concatenate([k[e] + r[e] for k, r in zip(keep, got)], axis=-2) for e in ends]
 
 
+def add_piles(keep, got, edges):
+    return [
+        jnp.concatenate([k[i : i + 1] + r[i : i + 1] for k, r in zip(keep, got)], axis=-2)
+        for i in range(keep[0].shape[0])
+    ]
+
+
 def add_last(keep, got, edges):
-    total = keep[0].astype(F32) + got[0].astype(F32)
+    total = keep[0].astype(F32)
+    for r in got:
+        total = total + r[0].astype(F32)
     return [total[..., a:b, :] for a, b in zip(edges, edges[1:])]
 
 
@@ -81,11 +90,11 @@
 PIECES = 4
 
 
-def pieces_of(shape, tile, first=0):
+def pieces_of(shape, tile, pieces=PIECES):
     rows, columns = shape
-    piece = (rows // PIECES, columns)
-    specs = [pl.BlockSpec((piece[0], tile), lambda t: (0, first + t)) for _ in range(PIECES)]
-    return specs, [jax.ShapeDtypeStruct(piece, BF16)] * PIECES
+    piece = (rows // pieces, columns)
+    specs = [pl.BlockSpec((piece[0], tile), lambda t: (0, t)) for _ in range(pieces)]
+    return specs, [jax.ShapeDtypeStruct(piece, BF16)] * pieces
 
 
 def put_pieces(refs, value):
@@ -607,17 +616,17 @@
     ] + [pltpu.SemaphoreType.DMA((len(groups), max(layout_of(groups)), len(kinds)))]
 
 
-def ffn_back_body(layout, kinds, *refs):
+def ffn_back_body(layout, kinds, pieces, *refs):
     ins = sum(layout) + len(layout)
-    total = ffn_terms(layout, kinds, refs[:ins] + refs[ins + PIECES :])
-    put_pieces(refs[ins : ins + PIECES], total.astype(BF16))
-
-
-def ffn_back(groups, acts, kinds, start, count, tile):
+    total = ffn_terms(layout, kinds, refs[:ins] + refs[ins + pieces :])
+    put_pieces(refs[ins : ins + pieces], total.astype(BF16))
+
+
+def ffn_back(groups, acts, kinds, start, count, tile, pieces):
     width = groups[0][0].shape[3]
-    piece_specs, piece_shapes = pieces_of((width, count), tile)
+    piece_specs, piece_shapes = pieces_of((width, count), tile, pieces)
     return pl.pallas_call(
-        functools.partial(ffn_back_body, layout_of(groups), kinds),
+        functools.partial(ffn_back_body, layout_of(groups), kinds, pieces),
         grid=(count // tile,),
         in_specs=ffn_specs(groups, acts, kinds, tile, start // tile),
         out_specs=piece_specs,
@@ -631,10 +640,9 @@
 
 def layer_out_body(layout, *refs):
     ins = sum(layout) + len(layout)
-    mixed_ref, out_ref = refs[ins], refs[ins + 1 + PIECES]
-    got = jnp.concatenate([r[...] for r in refs[ins + 1 : ins + 1 + PIECES]], axis=0)
-    total = ffn_terms(layout, [2], refs[:ins] + refs[ins + 2 + PIECES :])
-    out_ref[0] = (mixed_ref[...] + total + got.astype(F32)).astype(BF16)
+    mixed_ref, got_ref, out_ref = refs[ins : ins + 3]
+    total = ffn_terms(layout, [2], refs[:ins] + refs[ins + 3 :])
+    out_ref[0] = (mixed_ref[...] + total + got_ref[...].astype(F32)).astype(BF16)
 
 
 def layer_out_of(groups, acts, mixed, got, rows):
@@ -644,25 +652,25 @@
     return pl.pallas_call(
         functools.partial(layer_out_body, layout_of(groups)),
         grid=(rows,),
-        in_specs=ffn_specs(groups, acts, [2], size, 0) + [col] + pieces_of(mixed.shape, size)[0],
+        in_specs=ffn_specs(groups, acts, [2], size, 0) + [col, col],
         out_specs=pl.BlockSpec((1, width, size), lambda t: (t, 0, 0)),
         out_shape=jax.ShapeDtypeStruct((rows, width, size), BF16),
         scratch_shapes=ffn_scratch(groups, [2]),
         compiler_params=PARAMS,
         name="layer_out_of",
         cost_estimate=cost(1, 1),
-    )(*flat_of(groups), *acts, mixed, *got)
+    )(*flat_of(groups), *acts, mixed, got)
 
 
 def mix_back_body(layout, *refs):
     ins = sum(layout) + len(layout)
     weights, refs = refs[:ins], refs[ins:]
     pieces, refs = refs[:PIECES], refs[PIECES:]
-    mixed_ref, dy_ref, o_ref, w_ref, place_ref, gain_ref = refs[:6]
-    refs = refs[6:]
-    inside_grad = len(refs) == 6 + len(layout) + 1
+    mixed_ref, dy_ref, o_ref, w_ref, place_ref, home_ref, gain_ref = refs[:7]
+    refs = refs[7:]
+    inside_grad = len(refs) == 5 + len(layout) + 1
     dmixed_ref, do_ref, gg_ref = refs[:3]
-    low_ref, high_ref, acc = refs[3:6] if inside_grad else (None, None, None)
+    gw_ref, acc = refs[3:5] if inside_grad else (None, None)
     row = pl.program_id(0)
     got = jnp.concatenate([r[...] for r in pieces], axis=0)
     dn = ffn_terms(layout, [0, 1], weights + refs[-len(layout) - 1 :]) + got.astype(F32)
@@ -674,7 +682,7 @@
     dmixed = dy_ref[0].astype(F32) + scale * (scaled - unit * inside)
     dmixed_ref[...] = dmixed
     low = dmixed.astype(BF16)
-    spread = dot(place_ref[...], o_ref[...], 0, 0).astype(BF16)
+    spread = dot(home_ref[...], o_ref[...], 0, 0).astype(BF16)
     mixed_up = dot(w_ref[...], low, 1, 0).astype(BF16)
     do_ref[...] = dot(place_ref[...], mixed_up, 1, 0).astype(BF16)
     both = dn * unit
@@ -703,42 +711,38 @@
 
         @pl.when(row == pl.num_programs(0) - 1)
         def _():
-            half = low_ref.shape[0]
-            low_ref[...] = acc[:half].astype(BF16)
-            high_ref[...] = acc[half:].astype(BF16)
-
-
-def mix_back(groups, acts, mixed, d1, dy, ot, w, place, gain):
+            gw_ref[...] = acc[...].astype(BF16)
+
+
+def mix_back(groups, acts, mixed, d1, dy, ot, w, place, home, gain):
     rows, width, size = dy.shape
     inner = ot.shape[0]
     here = rows * size
     col = pl.BlockSpec((width, size), lambda r: (0, r))
     head_col = pl.BlockSpec((inner, size), lambda r: (0, r))
     fits = w.shape[0] <= 1024
-    half = (w.shape[0] // 2, width)
     out = pl.pallas_call(
         functools.partial(mix_back_body, layout_of(groups)),
         grid=(rows,),
         in_specs=ffn_specs(groups, acts, [0, 1], size, 0)
         + pieces_of(mixed.shape, size)[0]
         + [col, pl.BlockSpec((1, width, size), lambda r: (r, 0, 0)), head_col]
-        + [whole(w.shape), whole(place.shape), whole(gain.shape)],
-        out_specs=[col, head_col, whole((width, 128))] + [whole(half)] * (2 * fits),
+        + [whole(w.shape), whole(place.shape), whole(home.shape), whole(gain.shape)],
+        out_specs=[col, head_col, whole((width, 128))] + [whole(w.shape)] * fits,
         out_shape=[
             jax.ShapeDtypeStruct((width, here), F32),
             jax.ShapeDtypeStruct((inner, here), BF16),
             jax.ShapeDtypeStruct((width, 128), F32),
         ]
-        + [jax.ShapeDtypeStruct(half, BF16)] * (2 * fits),
+        + [jax.ShapeDtypeStruct(w.shape, BF16)] * fits,
         scratch_shapes=[pltpu.VMEM(w.shape, F32)] * fits + ffn_scratch(groups, [0, 1]),
         compiler_params=PARAMS,
         name="mix_back",
         cost_estimate=cost(1, 1),
-    )(*flat_of(groups), *acts, *d1, mixed, dy, ot, w, place, gain)
+    )(*flat_of(groups), *acts, *d1, mixed, dy, ot, w, place, home, gain)
     if not fits:
-        spread = dot(place, ot, 0, 0).astype(BF16)
-        product = dot(spread, out[0].astype(BF16), 1, 1).astype(BF16)
-        out = [*out, product[: half[0]], product[half[0] :]]
+        spread = dot(home, ot, 0, 0).astype(BF16)
+        out = [*out, dot(spread, out[0].astype(BF16), 1, 1).astype(BF16)]
     return out
 
 
@@ -935,7 +939,7 @@
         if token:
             args = lax.optimization_barrier((args, tuple(token)))[0]
         out = work(*args)
-        token[:] = jax.tree.leaves(out)[:1]
+        token[:] = jax.tree.leaves(out)
         return out
 
     each = -(-w_query.shape[0] // ROW_TILE) * ROW_TILE
@@ -1003,6 +1007,9 @@
     dy = jnp.transpose(cotangent, (0, 2, 1))
     gain_one, gain_two = gain_attn[:, None], gain_ffn[:, None]
     place_a, place_b = spread_of(order_a + [core]), spread_of(order_b + [core])
+    real = w_query.shape[0]
+    home_row = jnp.arange(inner) // real * each + jnp.arange(inner) % real
+    home = (home_row[:, None] == jnp.arange(inner // real * each)[None, :]).astype(BF16)
     segs = lax.dynamic_slice_in_dim(segment_ids, my_ctx * size, size, 1)
     same = segs[:, None, :] == jnp.arange(DOCS, dtype=segs.dtype)[None, :, None]
     ones = jnp.ones((rows, 1, size), BF16)
@@ -1030,27 +1037,27 @@
     dy_parts = swap_core(dy_own)
     attn_w.go()
     dy_pair = run(fill, dy_pair, dy_parts)
+    if by_hops:
+        last_w = Gather(
+            shards[-1][None], [(0, shards[-1].shape[1])], mark=dy_pair, paths=((across,), (near,))
+        )
     attn_w.core_go()
     wko, wvq = attn_w.core_end()
     pick = lambda w, k: w[:, 0, k * each : (k + 1) * each].reshape(-1, width)
+    if by_hops:
+        last_w.go()
     wk, wo, wv, wq = run(lambda a, b: [pick(a, 0), pick(a, 1), pick(b, 0), pick(b, 1)], wko, wvq)
     kv_own = run(lambda *a: key_value(*a, 0, rows), normed, wk, wv, place_a, place_b, aug)
     kv_across = swap(kv_own, across)
     kv_core = swap(kv_own, core)
-    if by_hops:
-        last_w = Gather(
-            shards[-1][None], [(0, shards[-1].shape[1])], mark=kv_own, paths=((across,), (near,))
-        )
     queries = run(lambda n, w, p: project(n, w, p, tile), normed, wq, place_b)
     kv_core = close(kv_core)
+
+    kv = run(lambda *k: list(k), kv_own, kv_across, kv_core)
+    kv.append(close(jnp.concatenate([swap(k, core) for k in jnp.split(kv[1], rows)])))
     if by_hops:
         last_w.go()
-
-    kv = run(lambda *k: list(k), kv_own, kv_across, kv_core)
-    kv.append(close(jnp.concatenate([swap(k, core) for k in jnp.split(kv[1], rows)])))
     attended, lse = run(lambda *a: attend(*a, heads, 0), queries, query_aug, kv, bias)
-    if by_hops:
-        last_w.go()
     mixed, n_pair, *normed_two = run(mix, x, attended, wo, place_a, gain_two)
     n_parts = close(swap_core(normed_two))
     if by_hops:
@@ -1058,8 +1065,8 @@
     n_pair = run(fill, n_pair, n_parts)
 
     class Sums:
-        def __init__(self, grads, paths):
-            self.paths = paths[: len(grads)]
+        def __init__(self, grads, paths, direct=False):
+            self.paths, self.direct = paths[: len(grads)], direct
             self.stage = 0
             self.send(grads)
 
@@ -1069,7 +1076,7 @@
 
         def go(self):
             near_hops = len(self.paths[0])
-            hops = near_hops + len(far_bits)
+            hops = near_hops + (1 if self.direct else len(far_bits))
             self.stage += 1
             if self.stage > hops:
                 return
@@ -1079,11 +1086,16 @@
             if self.stage == near_hops:
                 rows_of = [k.shape[-2] for k in self.keep]
                 self.edges = [sum(rows_of[:k]) for k in range(len(rows_of) + 1)]
+                if self.direct:
+                    piles = run(lambda k, r: add_piles(k, r, self.edges), self.keep, self.got)
+                    self.keep = [piles[0]]
+                    self.got = [swap(pile, step) for pile, step in zip(piles[1:], far)]
+                    return
                 halves = run(lambda k, r: add_merge(k, r, self.edges), self.keep, self.got)
             elif self.stage < hops:
                 halves = run(add_halves, self.keep, self.got)[0]
             else:
-                self.out = run(lambda k, r: add_last(k[0], r[0], self.edges), self.keep, self.got)
+                self.out = run(lambda k, r: add_last(k[0], r, self.edges), self.keep, self.got)
                 return
             self.keep = [halves[0]]
             self.got = [swap(halves[1], far_bits[hops - 1 - self.stage])]
@@ -1093,12 +1105,12 @@
     masks = [[m >> 1 for m in links.masks(steps)] for steps in (ab, ba)]
     ffn_grads = []
     if by_hops:
-        ffn_w.append(last_w.held[0])
+        ffn_w.append(None)
     for i, ws in enumerate(ffn_w):
+        if i == last_group and by_hops:
+            ws = ffn_w[i] = close(list(last_w.held[0]))
         some = tile if units_of(ws) <= 768 else tile // 2
         mask = masks[0] if by_hops and i == last_group - 1 else None
-        if i == last_group and by_hops:
-            ws = ffn_w[i] = close(list(ws))
         act, grads = run(
             lambda m, w, n, d: ffn_group(m, w, n, d, some, mask), me_same, ws, n_pair, dy_pair
         )
@@ -1114,49 +1126,51 @@
         for s in sums:
             s.go()
 
-    back = run(lambda p, a: ffn_back(p, a, [0, 1], here, here, tile), ffn_w, acts)
-    dn_parts = swap_core(back)
-    out_other = run(lambda p, a: ffn_back(p, a, [2], here, here, tile), ffn_w, acts)
-    dn_got = close(dn_parts)
-    dmixed, dattended, gain_two_part, *gwo = run(
-        mix_back, ffn_w, acts, mixed, dn_got, dy, attended, wo, place_a, gain_two
-    )
+    back = run(lambda p, a: ffn_back(p, a, [0, 1], here, here, tile, PIECES), ffn_w, acts)
+    dn_got = swap_core(back)
+    (out_other,) = run(lambda p, a: ffn_back(p, a, [2], here, here, tile, 1), ffn_w, acts)
+    dn_got = close(dn_got)
+    out_got = swap(out_other, core)
+
+    dmixed, dattended, gain_two_part, gwo = run(
+        mix_back, ffn_w, acts, mixed, dn_got, dy, attended, wo, place_a, home, gain_two
+    )
+    everywhere = ("dp", "x", "core")
+    scatter = lambda g: lax.psum_scatter(g.reshape(-1, each, width), everywhere, tiled=False)
+    grad_attn_out = scatter(gwo)
     tick()
     dq, dkv, grad_bias = run(
         lambda *a: attend_back(*a, heads, 0, []),
         queries, query_aug, kv, bias, attended, dattended, lse,
     )
+    by_core = [(dkv[0], swap(dkv[2], core)), (dkv[1], swap(dkv[3], core))]
     tick()
-    out_got = swap_core(out_other)
-    by_core = [(dkv[0], swap(dkv[2], core)), (dkv[1], swap(dkv[3], core))]
+    if by_hops:
+        ffn_grads[0] = close(ffn_grads[0])
+    gwq = run(
+        lambda n, d, p: projection_grads(n, [d], [(0, inner)], [p], rows), normed, dq, home
+    )
+    grad_query = scatter(jnp.concatenate(gwq))
     own, other = run(add_pairs, by_core)
     other = swap(other, across)
-    entries = lambda g: tuple(v.reshape(-1, each, width) for v in g)
-    home_a, home_b = (core,) + ba, (core,) + ab
-    gwq = run(
-        lambda n, d, p: projection_grads(n, [d], [(0, inner)], [p], rows), normed, dq, place_b
-    )
-    query_sum = Sums([entries(gwo), entries(gwq)], [home_a, home_b])
     grad_table = run(lambda g, b: bucket_sums(g, b, count), grad_bias, buckets_t)
-    query_sum.go()
-    out_got = close(out_got)
-    query_sum.go()
     out = run(lambda *a: layer_out_of(*a, rows), ffn_w, acts, mixed, out_got)
-    query_sum.go()
+    tick()
+    grad_attn_out = close(grad_attn_out)
     (dkv,) = run(add_pairs, [(own, other)])
     gkv = run(
         lambda n, d, pa, pb: projection_grads(n, [d], [(0, inner), (inner, 2 * inner)], [pa, pb], rows),
         normed, dkv, place_a, place_b,
     )
-    value_sum = Sums([entries(gkv[:2]), entries(gkv[2:])], [home_a, home_b])
-    tick()
+    entries = lambda g: tuple(v.reshape(-1, each, width) for v in g)
+    home_a, home_b = (core,) + ba, (core,) + ab
+    value_sum = Sums([entries(gkv[:2]), entries(gkv[2:])], [home_a, home_b], direct=dp <= 8)
     value_sum.go()
     gx, gain_one_part = run(
         lambda *a: last(a[0], a[1], [a[2]], [a[3]], a[4:7], a[7:10], a[10]),
         x, dmixed, dq, dkv, wq, wk, wv, place_b, place_a, place_b, gain_one,
     )
     value_sum.go()
-    query_sum.go()
     tick()
     small = jnp.concatenate(
         [jnp.sum(gain_one_part, 1), jnp.sum(gain_two_part, 1), grad_table.reshape(-1)]
@@ -1166,14 +1180,13 @@
     bits = [core, across] + [("dp", 1 << b) for b in range(dp.bit_length() - 1)]
     for k, one in enumerate(bits):
         got = swap(small, one)
-        if k in (1, 2, 3):
+        if k in (1, 3):
             value_sum.go()
         small = run(lambda a, b: a + b, small, got)
     for _ in range(len(far_bits) + 4):
-        for s in [query_sum, value_sum] + sums:
+        for s in [value_sum] + sums:
             s.go()
     small = small.reshape(-1)
-    real = w_query.shape[0]
     if by_hops:
         ffn_grads[-2:] = sums[0].out
     grad_gate, grad_up, grad_ffn_out = (
@@ -1186,10 +1199,10 @@
         small[:width],
         small[width : 2 * width],
         small[2 * width : length].reshape(count, heads),
-        query_sum.out[1][:real],
+        grad_query[:real].astype(F32),
         value_sum.out[0][:real],
         value_sum.out[1][:real],
-        query_sum.out[0][:real],
+        grad_attn_out[:real].astype(F32),
         grad_gate,
         grad_up,
         grad_ffn_out,

time: 680 us -> 709 us (1.043)
  waiting for transfers between devices: 195 us -> 228 us
    reduce_scatter x0 -> x2, waiting for transfers between devices: none -> 71.2 us  [per_device(): lax.psum_scatter(g.reshape(-1, each, width), everywhere, tiled=False)]
    ppermute x65 -> x55, waiting for transfers between devices: 180 us -> 156 us  [swap(): lax.ppermute(x, axis, [(i, i ^ mask) for i in range(self.sizes[axis])])]
    all_gather x2, waiting for transfers between devices: 14.8 us -> 0.01 us  [per_device(): lax.all_gather(after(shard, attn_w.start_of()), same_core)]
    ppermute x65 -> x55, starting transfers between devices: 48.4 us -> 47.2 us  [swap(): lax.ppermute(x, axis, [(i, i ^ mask) for i in range(self.sizes[axis])])]
  transfers between devices with their start and end apart: 68 -> 60, of which waited for: 26 -> 25; matrix products, arithmetic and copies ran while one was open for 10% -> 11% of each run, Pallas kernels for 45% -> 47%
where the time goes in v3:
time: 709 us; the launch traced here: 705 us
  Pallas kernels  332 us (47%)
  waiting for transfers between devices  228 us (32%)
  starting transfers between devices  47.5 us (7%)
  other arithmetic  42.2 us (6%)
  local copies, waits for them, and re-layouts  40.8 us (6%)
  between operations  14.9 us (2%)
    ppermute x55, waiting for transfers between devices, swap(): lax.ppermute(x, axis, [(i, i ^ mask) for i in range(self.sizes[axis])])  156 us
    pallas_call x3, Pallas kernels, ffn_group(): pl.pallas_call(functools.partial(ffn_body, len(ws), masks), grid_spec=spe...  100 us
    reduce_scatter x2, waiting for transfers between devices, per_device(): lax.psum_scatter(g.reshape(-1, each, width), everywhere, tiled=False)  71.2 us
    ppermute x55, starting transfers between devices, swap(): lax.ppermute(x, axis, [(i, i ^ mask) for i in range(self.sizes[axis])])  47.2 us
    pallas_call x1, Pallas kernels, attend_back(): pl.pallas_call(functools.partial(attend_back_body, heads, inner, count, l...  41.4 us
    pallas_call x1, Pallas kernels, mix_back(): pl.pallas_call(functools.partial(mix_back_body, layout_of(groups)), grid=...  39.2 us
    pallas_call x2, Pallas kernels, ffn_back(): pl.pallas_call(functools.partial(ffn_back_body, layout_of(groups), kinds,...  30.8 us
    pallas_call x2, Pallas kernels, projection_grads(): pl.pallas_call(functools.partial(grads_body, per, len(groups), parts), gr...  20.1 us
  transfers between devices with their start and end apart: 60, of which 25 were waited for; matrix products, arithmetic and copies ran while one was open for 11% of the time, Pallas kernels for 47%

profile of v3, /device:TPU:0, one launch (start us, length us, event | category | flops | bytes accessed | tf_op | source)
XLA Modules:
  0.0 704.8 jit_solution(9064391004254571980)
XLA Ops:
  18.5 7.2 %first_norm.1 = (bf16[1472,1024]{1,0:T(8,128)(2,1)}, bf16[2,1472,1024]{2,1,0:T(8,128)(2,1)}, bf16[368,1024]{1,0:T(8,128)(2,1)}, bf16[368,1024]{1,0:T(8,128)(2,1)...) custom-call(bf16[4,1472,256]{2,1,0:T(8,128)(2,1)} %bitcast.118, bf16[4,1472,256]{2,1,0:T(8,128)(2,1)} %bitcast.129, ...), custom_call_target="tpu_custom_call" | custom-call | flops 1 | bytes 1 | tf_op jit(solution)/shard_map/first_norm/pallas_call | solution.py:120
  36.9 6.8 bias_of.1
  55.0 18.8 %collective-permute-done.11 = bf16[8,1,32,1472]{3,2,1,0:T(8,128)(2,1)S(1)} collective-permute-done((bf16[8,1,32,1472]{3,2,1,0:T(8,128)(2,1)S(1)}, bf16[8,1,32,1472]{3,2,1,0:T(8,128)(2,1)S(1)}, u32[]{:S(2)}, u32[]{:S(2)}) %collective-permute-start.11) | collective-permute-done | bytes 753696 | tf_op jit(solution)/shard_map/ppermute | solution.py:896
  86.0 9.4 %collective-permute-done.9 = bf16[1,3,32,1472]{3,2,1,0:T(8,128)(2,1)S(1)} collective-permute-done((bf16[1,3,32,1472]{3,2,1,0:T(8,128)(2,1)S(1)}, bf16[1,3,32,1472]{3,2,1,0:T(8,128)(2,1)S(1)}, u32[]{:S(2)}, u32[]{:S(2)}) %collective-permute-start.9) | collective-permute-done | bytes 282656 | tf_op jit(solution)/shard_map/ppermute | solution.py:896
  99.2 12.6 %key_value.1.refs_0_ = bf16[4,784,256]{2,1,0:T(8,128)(2,1)} custom-call(bf16[1472,1024]{1,0:T(8,128)(2,1)} %get-tuple-element.564.n_ref, bf16[512,1472]{1,0:T(8,128)(2,1)} %bitcast.123, bf16[512,1472]{1,0:T(8,128)(2,1)} %bitcast.125, bf16[384,512]{1,0:T(8,128)(2,1)} %fusion.pk_ref.place_ref.refs_15_.refs_1_.refs_6_, ...), custom_call_target="tpu_custom_call" | custom-call | flops 1 | bytes 1 | tf_op jit(solution)/shard_map/key_value/pallas_call | solution.py:148
  121.1 41.7 %collective-permute-done.15.refs_1_ = bf16[4,784,256]{2,1,0:T(8,128)(2,1)S(1)} collective-permute-done((bf16[4,784,256]{2,1,0:T(8,128)(2,1)}, bf16[4,784,256]{2,1,0:T(8,128)(2,1)S(1)}, u32[]{:S(2)}, u32[]{:S(2)}) %collective-permute-start.15) | collective-permute-done | bytes 1605664 | tf_op jit(solution)/shard_map/ppermute | solution.py:896
  170.2 18.3 %attend.1 = (bf16[384,1024]{1,0:T(8,128)(2,1)}, f32[4,8,256]{2,1,0:T(8,128)}) custom-call(bf16[384,1024]{1,0:T(8,128)(2,1)} %project.1.q_ref, bf16[4,16,256]{2,1,0:T(8,128)(2,1)} %maximum_maximum_fusion.1.u_ref, bf16[4,784,256]{2,1,0:T(8,128)(2,1)} %key_value.1.refs_0_, bf16[4,784,256]{2,1,0:T(8,128)(2,1)} %copy-done.3, bf16[4,784,256]{2,1,0:T(8,128)(2,1)} %copy-done.4, ...), custom_call_target="tpu_custom_call" | custom-call | flops 1 | bytes 1 | tf_op jit(solution)/shard_map/attend/pallas_call | solution.py:218
  189.7 9.6 %mix.1 = (f32[1472,1024]{1,0:T(8,128)}, bf16[2,1472,1024]{2,1,0:T(8,128)(2,1)}, bf16[368,1024]{1,0:T(8,128)(2,1)}, bf16[368,1024]{1,0:T(8,128)(2,1)}, bf16[368,1...) custom-call(bf16[4,1472,256]{2,1,0:T(8,128)(2,1)} %bitcast.119, bf16[384,1024]{1,0:T(8,128)(2,1)} %get-tuple-element.525.o_ref.refs_13_.refs_5_, ...), custom_call_target="tpu_custom_call" | custom-call | flops 1 | bytes 1 | tf_op jit(solution)/shard_map/mix/pallas_call | solution.py:435
  212.5 41.1 %ffn_group.3 = (bf16[3,768,2048]{2,1,0:T(8,128)(2,1)}, bf16[16,3,48,1472]{3,2,1,0:T(8,128)(2,1)}) custom-call(s32[1]{0:T(128)} %bitcast.29.me_ref, bf16[16,3,48,1472]{3,2,1,0:T(8,128)(2,1)} %bitcast.108, bf16[2,1472,1024]{2,1,0:T(8,128)(2,1)} %bitcast_dynamic-update-slice_fusion.refs_1_.refs_2_, ...), custom_call_target="tpu_custom_call" | custom-call | flops 1 | bytes 1 | tf_op jit(solution)/shard_map/ffn_group/pallas_call | solution.py:561
  255.3 29.9 %ffn_group.4 = (bf16[3,512,2048]{2,1,0:T(8,128)(2,1)}, bf16[8,3,32,1472]{3,2,1,0:T(8,128)(2,1)}, bf16[8,3,32,1472]{3,2,1,0:T(8,128)(2,1)}) custom-call(s32[1]{0:T(128)} %bitcast.29.me_ref, bf16[16,3,32,1472]{3,2,1,0:T(8,128)(2,1)} %bitcast.113, bf16[2,1472,1024]{2,1,0:T(8,128)(2,1)} %bitcast_dynamic-update-slice_fusion.refs_1_.refs_2_, ...), custom_call_target="tpu_custom_call" | custom-call | flops 1 | bytes 1 | tf_op jit(solution)/shard_map/ffn_group/pallas_call | solution.py:561
  285.3 35.8 %collective-permute-done.26.refs_1_.refs_3_ = bf16[8,3,32,1472]{3,2,1,0:T(8,128)(2,1)} collective-permute-done((bf16[8,3,32,1472]{3,2,1,0:T(8,128)(2,1)S(1)}, bf16[8,3,32,1472]{3,2,1,0:T(8,128)(2,1)}, u32[]{:S(2)}, u32[]{:S(2)}) %collective-permute-start.26) | collective-permute-done | bytes 2261024 | tf_op jit(solution)/shard_map/ppermute | solution.py:896
  321.1 29.2 %ffn_group.5 = (bf16[3,512,2048]{2,1,0:T(8,128)(2,1)}, bf16[8,3,32,1472]{3,2,1,0:T(8,128)(2,1)}, bf16[8,3,32,1472]{3,2,1,0:T(8,128)(2,1)}) custom-call(s32[1]{0:T(128)} %bitcast.29.me_ref, bf16[8,3,32,1472]{3,2,1,0:T(8,128)(2,1)} %copy-done.2, bf16[8,3,32,1472]{3,2,1,0:T(8,128)(2,1)} %collective-permute-done.26.refs_1_.refs_3_, ...), custom_call_target="tpu_custom_call" | custom-call | flops 1 | bytes 1 | tf_op jit(solution)/shard_map/ffn_group/pallas_call | solution.py:561
  353.9 19.5 %ffn_back.2 = (bf16[368,1024]{1,0:T(8,128)(2,1)}, bf16[368,1024]{1,0:T(8,128)(2,1)}, bf16[368,1024]{1,0:T(8,128)(2,1)}, bf16[368,1024]{1,0:T(8,128)(2,1)}) custom-call(bf16[16,3,48,1472]{3,2,1,0:T(8,128)(2,1)} %bitcast.109, bf16[16,3,32,1472]{3,2,1,0:T(8,128)(2,1)} %bitcast.114, bf16[8,3,32,1472]{3,2,1,0:T(8,128)(2,1)} %copy-done.2, ...), custom_call_target="tpu_custom_call" | custom-call | flops 1 | bytes 1 | tf_op jit(solution)/shard_map/ffn_back/pallas_call | solution.py:628
  377.0 11.2 %ffn_back.3 = bf16[1472,1024]{1,0:T(8,128)(2,1)} custom-call(bf16[16,3,48,1472]{3,2,1,0:T(8,128)(2,1)} %bitcast.110, bf16[16,3,32,1472]{3,2,1,0:T(8,128)(2,1)} %bitcast.115, bf16[8,3,32,1472]{3,2,1,0:T(8,128)(2,1)} %copy-done.2, bf16[8,3,32,1472]{3,2,1,0:T(8,128)(2,1)} %collective-permute-done.26.refs_1_.refs_3_, ...), custom_call_target="tpu_custom_call" | custom-call | flops 1 | bytes 1 | tf_op jit(solution)/shard_map/ffn_back/pallas_call | solution.py:628
  391.2 39.2 %mix_back.1 = (f32[1472,1024]{1,0:T(8,128)}, bf16[384,1024]{1,0:T(8,128)(2,1)}, f32[1472,128]{1,0:T(8,128)}, bf16[512,1472]{1,0:T(8,128)(2,1)}) custom-call(bf16[16,3,48,1472]{3,2,1,0:T(8,128)(2,1)} %bitcast.111, bf16[16,3,32,1472]{3,2,1,0:T(8,128)(2,1)} %bitcast.116, bf16[8,3,32,1472]{3,2,1,0:T(8,128)(2,1)} %copy-done.2, ...), custom_call_target="tpu_custom_call" | custom-call | flops 1 | bytes 1 | tf_op jit(solution)/shard_map/mix_back/pallas_call | solution.py:724
  437.1 41.4 %attend_back.1 = (bf16[384,1024]{1,0:T(8,128)(2,1)}, bf16[4,784,256]{2,1,0:T(8,128)(2,1)}, bf16[4,784,256]{2,1,0:T(8,128)(2,1)}, bf16[4,784,256]{2,1,0:T(8,128)(...) custom-call(bf16[384,1024]{1,0:T(8,128)(2,1)} %project.1.q_ref, ...), custom_call_target="tpu_custom_call" | custom-call | flops 1 | bytes 1 | tf_op jit(solution)/shard_map/attend_back/pallas_call | solution.py:313
  485.8 8.0 %projection_grads.2 = (bf16[256,1472]{1,0:T(8,128)(2,1)}, bf16[256,1472]{1,0:T(8,128)(2,1)}) custom-call(bf16[1472,1024]{1,0:T(8,128)(2,1)} %get-tuple-element.564.n_ref, bf16[384,1024]{1,0:T(8,128)(2,1)} %get-tuple-element.578.refs_0_, bf16[384,512]{1,0:T(8,128)(2,1)} %fusion.2.refs_16_.refs_1_), custom_call_target="tpu_custom_call" | custom-call | flops 1 | bytes 1 | tf_op jit(solution)/shard_map/projection_grads/pallas_call | solution.py:798
  500.6 8.0 %bucket_sums.1 = f32[96,256]{1,0:T(8,128)} custom-call(s32[4,256,256]{2,1,0:T(8,128)} %get-tuple-element.548.buckets_ref, f32[6,4,256,256]{3,2,1,0:T(8,128)} %get-tuple-element.549.g_ref), custom_call_target="tpu_custom_call" | custom-call | flops 1 | bytes 1 | tf_op jit(solution)/shard_map/bucket_sums/pallas_call | solution.py:392
  510.6 13.3 %layer_out_of.1 = bf16[4,1472,256]{2,1,0:T(8,128)(2,1)} custom-call(bf16[16,3,48,1472]{3,2,1,0:T(8,128)(2,1)} %bitcast.112, bf16[16,3,32,1472]{3,2,1,0:T(8,128)(2,1)} %bitcast.117, bf16[8,3,32,1472]{3,2,1,0:T(8,128)(2,1)} %copy-done.2, bf16[8,3,32,1472]{3,2,1,0:T(8,128)(2,1)} %collective-permute-done.26.refs_1_.refs_3_, ...), custom_call_target="tpu_custom_call" | custom-call | flops 1 | bytes 1 | tf_op jit(solution)/shard_map/layer_out_of/pallas_call | solution.py:652
  523.9 18.9 %collective-permute-done.39 = bf16[2,3,64,1472]{3,2,1,0:T(8,128)(2,1)} collective-permute-done((bf16[2,3,64,1472]{3,2,1,0:T(8,128)(2,1)}, bf16[2,3,64,1472]{3,2,1,0:T(8,128)(2,1)}, u32[]{:S(2)}, u32[]{:S(2)}) %collective-permute-start.39) | collective-permute-done | bytes 1130528 | tf_op jit(solution)/shard_map/ppermute | solution.py:896
  546.3 17.7 %reduce-scatter.6.cloned.1.call-done = bf16[1,16,1472]{2,1,0:T(8,128)(2,1)} async-done(((bf16[32,16,1472]{2,1,0:T(8,128)(2,1)}), bf16[1,16,1472]{2,1,0:T(8,128)(2,1)}) %reduce-scatter.6.cloned.1.call-update) | async-done | bytes 47120 | tf_op jit(solution)/shard_map/reduce_scatter | solution.py:1139
  567.0 12.1 %projection_grads.3 = (bf16[256,1472]{1,0:T(8,128)(2,1)}, bf16[256,1472]{1,0:T(8,128)(2,1)}, bf16[256,1472]{1,0:T(8,128)(2,1)}, bf16[256,1472]{1,0:T(8,128)(2,1)}) custom-call(bf16[1472,1024]{1,0:T(8,128)(2,1)} %get-tuple-element.564.n_ref, bf16[4,784,256]{2,1,0:T(8,128)(2,1)} %add.252.refs_0_.refs_1_, ...), custom_call_target="tpu_custom_call" | custom-call | flops 1 | bytes 1 | tf_op jit(solution)/shard_map/projection_grads/pallas_call | solution.py:798
  592.4 19.0 %last.1 = (f32[4,1472,256]{2,1,0:T(8,128)}, f32[1472,128]{1,0:T(8,128)}) custom-call(bf16[4,1472,256]{2,1,0:T(8,128)(2,1)} %bitcast.120, f32[1472,1024]{1,0:T(8,128)} %get-tuple-element.577.dm_ref, bf16[384,1024]{1,0:T(8,128)(2,1)} %get-tuple-element.578.refs_0_, bf16[4,784,256]{2,1,0:T(8,128)(2,1)} %add.252.refs_0_.refs_1_, bf16[512,1472]{1,0:T(8,128)(2,1)} %bitcast.128, ...), custom_call_target="tpu_custom_call" | custom-call | flops 1 | bytes 1 | tf_op jit(solution)/shard_map/last/pallas_call | solution.py:859
  612.9 53.5 %reduce-scatter.8.cloned.1.call-done = bf16[1,16,1472]{2,1,0:T(8,128)(2,1)} async-done(((bf16[32,16,1472]{2,1,0:T(8,128)(2,1)}), bf16[1,16,1472]{2,1,0:T(8,128)(2,1)}) %reduce-scatter.8.cloned.1.call-update) | async-done | bytes 47120 | tf_op jit(solution)/shard_map/reduce_scatter | solution.py:1139
  (328 shorter events, 167.6 us)
Async XLA Ops:
  7.2 205.3 %all-gather.5.cloned.1.call-start = ((), (), s32[]{:S(2)}) async-start(), calls=%async_computation.6 | async-start | bytes 7520256 | tf_op jit(solution)/shard_map/all_gather | solution.py:1030
  30.9 224.4 %all-gather.7.cloned.1.call-start = ((), (), s32[]{:S(2)}) async-start(), calls=%async_computation.7 | async-start | bytes 5013504 | tf_op jit(solution)/shard_map/all_gather | solution.py:1030
  31.1 20.3 %collective-permute-start.4 = (bf16[368,1024]{1,0:T(8,128)(2,1)}, bf16[368,1024]{1,0:T(8,128)(2,1)S(1)}, u32[]{:S(2)}, u32[]{:S(2)}) collective-permute-start(bf16[368,1024]{1,0:T(8,128)(2,1)} %get-tuple-element.364), channel_id=1, source_target_pairs={{0,1},{1,0},{2,3},{3,2},{4,5},{5,4},{6,7},{7,6},{8,9},{9,8},{10,11... | collective-permute-start | bytes 2261000 | tf_op jit(solution)/shard_map/ppermute | solution.py:896
  31.6 19.8 %collective-permute-start.5 = (bf16[368,1024]{1,0:T(8,128)(2,1)}, bf16[368,1024]{1,0:T(8,128)(2,1)S(1)}, u32[]{:S(2)}, u32[]{:S(2)}) collective-permute-start(bf16[368,1024]{1,0:T(8,128)(2,1)} %get-tuple-element.365), channel_id=1, source_target_pairs={{0,1},{1,0},{2,3},{3,2},{4,5},{5,4},{6,7},{7,6},{8,9},{9,8},{10,11... | collective-permute-start | bytes 2261000 | tf_op jit(solution)/shard_map/ppermute | solution.py:896
  49.1 24.7 %collective-permute-start.11 = (bf16[8,1,32,1472]{3,2,1,0:T(8,128)(2,1)S(1)}, bf16[8,1,32,1472]{3,2,1,0:T(8,128)(2,1)S(1)}, u32[]{:S(2)}, u32[]{:S(2)}) collective-permute-start(bf16[8,1,32,1472]{3,2,1,0:T(8,128)(2,1)S(1)} %constant_dynamic-update-slice_fusion.2), channel_id=1, source_target_pairs={{0,4},{4,0},{8,12},{12,8},{16,20},{20,16},{24,28},{28,24},{1,5},{5... | collective-permute-start | bytes 2261000 | tf_op jit(solution)/shard_map/ppermute | solution.py:896
  49.7 26.4 %collective-permute-start.10 = (bf16[8,1,32,1472]{3,2,1,0:T(8,128)(2,1)S(1)}, bf16[8,1,32,1472]{3,2,1,0:T(8,128)(2,1)S(1)}, u32[]{:S(2)}, u32[]{:S(2)}) collective-permute-start(bf16[8,1,32,1472]{3,2,1,0:T(8,128)(2,1)S(1)} %constant_dynamic-update-slice_fusion), channel_id=1, source_target_pairs={{0,2},{2,0},{1,3},{3,1},{4,6},{6,4},{5,7},{7,5},{8,10},{10,8},{9,1... | collective-permute-start | bytes 2261000 | tf_op jit(solution)/shard_map/ppermute | solution.py:896
  82.4 403.4 %reduce-scatter.4.cloned.1.call-start = ((), (), s32[]{:S(2)}) async-start(), calls=%async_computation.3 | async-start | bytes 7520256 | tf_op jit(solution)/shard_map/reduce_scatter | solution.py:1121
  111.8 51.1 %collective-permute-start.15 = (bf16[4,784,256]{2,1,0:T(8,128)(2,1)}, bf16[4,784,256]{2,1,0:T(8,128)(2,1)S(1)}, u32[]{:S(2)}, u32[]{:S(2)}) collective-permute-start(bf16[4,784,256]{2,1,0:T(8,128)(2,1)} %key_value.1.refs_0_), channel_id=1, source_target_pairs={{0,2},{2,0},{1,3},{3,1},{4,6},{6,4},{5,7},{7,5},{8,10},{10,8},{9,1... | collective-permute-start | bytes 4816904 | tf_op jit(solution)/shard_map/ppermute | solution.py:896
  113.0 55.9 %collective-permute-start.14 = (bf16[2,3,32,1472]{3,2,1,0:T(8,128)(2,1)S(1)}, bf16[2,3,32,1472]{3,2,1,0:T(8,128)(2,1)S(1)}, u32[]{:S(2)}, u32[]{:S(2)}) collective-permute-start(bf16[2,3,32,1472]{3,2,1,0:T(8,128)(2,1)S(1)} %constant_dynamic-update-slice_fusion.12), channel_id=1, source_target_pairs={{0,16},{4,20},{8,24},{12,28},{16,0},{20,4},{24,8},{28,12},{1,17},{... | collective-permute-start | bytes 1695752 | tf_op jit(solution)/shard_map/ppermute | solution.py:896
  169.0 37.0 %collective-permute-start.21 = (bf16[4,3,32,1472]{3,2,1,0:T(8,128)(2,1)S(1)}, bf16[4,3,32,1472]{3,2,1,0:T(8,128)(2,1)}, u32[]{:S(2)}, u32[]{:S(2)}) collective-permute-start(bf16[4,3,32,1472]{3,2,1,0:T(8,128)(2,1)S(1)} %constant_dynamic-update-slice_fusion.14), channel_id=1, source_target_pairs={{0,2},{2,0},{1,3},{3,1},{4,6},{6,4},{5,7},{7,5},{8,10},{10,8},{9,1... | collective-permute-start | bytes 3391496 | tf_op jit(solution)/shard_map/ppermute | solution.py:896
  253.6 310.3 %reduce-scatter.6.cloned.1.call-start = ((), (), s32[]{:S(2)}) async-start(), calls=%async_computation.4 | async-start | bytes 1622016 | tf_op jit(solution)/shard_map/reduce_scatter | solution.py:1139
  253.7 67.4 %collective-permute-start.26 = (bf16[8,3,32,1472]{3,2,1,0:T(8,128)(2,1)S(1)}, bf16[8,3,32,1472]{3,2,1,0:T(8,128)(2,1)}, u32[]{:S(2)}, u32[]{:S(2)}) collective-permute-start(bf16[8,3,32,1472]{3,2,1,0:T(8,128)(2,1)S(1)} %constant_dynamic-update-slice_fusion.16.refs_0_.refs_2_), channel_id=1, source_target_pairs={{0,4},{4,0},{8,12},{12,8},{16,20},{20,16},{24,28},{28,24},{1,5},{5... | collective-permute-start | bytes 6782984 | tf_op jit(solution)/shard_map/ppermute | solution.py:896
  350.3 80.1 %collective-permute-start.33 = (bf16[8,3,32,1472]{3,2,1,0:T(8,128)(2,1)}, bf16[8,3,32,1472]{3,2,1,0:T(8,128)(2,1)S(1)}, u32[]{:S(2)}, u32[]{:S(2)}) collective-permute-start(bf16[8,3,32,1472]{3,2,1,0:T(8,128)(2,1)} %get-tuple-element.469), channel_id=1, source_target_pairs={{0,4},{4,0},{8,12},{12,8},{16,20},{20,16},{24,28},{28,24},{1,5},{5... | collective-permute-start | bytes 6782984 | tf_op jit(solution)/shard_map/ppermute | solution.py:896
  352.5 78.0 %collective-permute-start.32 = (bf16[8,3,32,1472]{3,2,1,0:T(8,128)(2,1)}, bf16[8,3,32,1472]{3,2,1,0:T(8,128)(2,1)}, u32[]{:S(2)}, u32[]{:S(2)}) collective-permute-start(bf16[8,3,32,1472]{3,2,1,0:T(8,128)(2,1)} %get-tuple-element.459), channel_id=1, source_target_pairs={{0,2},{2,0},{1,3},{3,1},{4,6},{6,4},{5,7},{7,5},{8,10},{10,8},{9,1... | collective-permute-start | bytes 6782984 | tf_op jit(solution)/shard_map/ppermute | solution.py:896
  434.9 44.2 %collective-permute-start.36 = (bf16[4,3,32,1472]{3,2,1,0:T(8,128)(2,1)}, bf16[4,3,32,1472]{3,2,1,0:T(8,128)(2,1)S(1)}, u32[]{:S(2)}, u32[]{:S(2)}) collective-permute-start(bf16[4,3,32,1472]{3,2,1,0:T(8,128)(2,1)} %get-tuple-element.641), channel_id=1, source_target_pairs={{0,4},{4,0},{8,12},{12,8},{16,20},{20,16},{24,28},{28,24},{1,5},{5... | collective-permute-start | bytes 3391496 | tf_op jit(solution)/shard_map/ppermute | solution.py:896
  436.4 42.7 %collective-permute-start.37 = (bf16[4,3,32,1472]{3,2,1,0:T(8,128)(2,1)}, bf16[4,3,32,1472]{3,2,1,0:T(8,128)(2,1)}, u32[]{:S(2)}, u32[]{:S(2)}) collective-permute-start(bf16[4,3,32,1472]{3,2,1,0:T(8,128)(2,1)} %get-tuple-element.639), channel_id=1, source_target_pairs={{0,2},{2,0},{1,3},{3,1},{4,6},{6,4},{5,7},{7,5},{8,10},{10,8},{9,1... | collective-permute-start | bytes 3391496 | tf_op jit(solution)/shard_map/ppermute | solution.py:896
  436.9 73.7 %collective-permute-start.27 = (bf16[1472,1024]{1,0:T(8,128)(2,1)}, bf16[1472,1024]{1,0:T(8,128)(2,1)}, u32[]{:S(2)}, u32[]{:S(2)}) collective-permute-start(bf16[1472,1024]{1,0:T(8,128)(2,1)} %ffn_back.3), channel_id=1, source_target_pairs={{0,1},{1,0},{2,3},{3,2},{4,5},{5,4},{6,7},{7,6},{8,9},{9,8},{10,11... | collective-permute-start | bytes 9043976 | tf_op jit(solution)/shard_map/ppermute | solution.py:896
  437.0 229.4 %reduce-scatter.8.cloned.1.call-start = ((), (), s32[]{:S(2)}) async-start(), calls=%async_computation.5 | async-start | bytes 1622016 | tf_op jit(solution)/shard_map/reduce_scatter | solution.py:1139
  481.7 61.1 %collective-permute-start.39 = (bf16[2,3,64,1472]{3,2,1,0:T(8,128)(2,1)}, bf16[2,3,64,1472]{3,2,1,0:T(8,128)(2,1)}, u32[]{:S(2)}, u32[]{:S(2)}) collective-permute-start(bf16[2,3,64,1472]{3,2,1,0:T(8,128)(2,1)} %pad_maximum_fusion.3), channel_id=1, source_target_pairs={{0,16},{4,20},{8,24},{12,28},{16,0},{20,4},{24,8},{28,12},{1,17},{... | collective-permute-start | bytes 3391496 | tf_op jit(solution)/shard_map/ppermute | solution.py:896
  497.0 67.0 %collective-permute-start.38 = (bf16[4,784,256]{2,1,0:T(8,128)(2,1)}, bf16[4,784,256]{2,1,0:T(8,128)(2,1)}, u32[]{:S(2)}, u32[]{:S(2)}) collective-permute-start(bf16[4,784,256]{2,1,0:T(8,128)(2,1)} %add.249), channel_id=1, source_target_pairs={{0,2},{2,0},{1,3},{3,1},{4,6},{6,4},{5,7},{7,5},{8,10},{10,8},{9,1... | collective-permute-start | bytes 4816904 | tf_op jit(solution)/shard_map/ppermute | solution.py:896
  580.3 92.3 %collective-permute-start.54 = (bf16[1,3,64,1472]{3,2,1,0:T(8,128)(2,1)}, bf16[1,3,64,1472]{3,2,1,0:T(8,128)(2,1)}, u32[]{:S(2)}, u32[]{:S(2)}) collective-permute-start(bf16[1,3,64,1472]{3,2,1,0:T(8,128)(2,1)} %get-tuple-element.647), channel_id=1, source_target_pairs={{0,8},{4,12},{8,0},{12,4},{16,24},{20,28},{24,16},{28,20},{1,9},{5... | collective-permute-start | bytes 1695752 | tf_op jit(solution)/shard_map/ppermute | solution.py:896
  587.4 81.9 %collective-permute-start.44 = (bf16[8,16,1472]{2,1,0:T(8,128)(2,1)}, bf16[8,16,1472]{2,1,0:T(8,128)(2,1)}, u32[]{:S(2)}, u32[]{:S(2)}) collective-permute-start(bf16[8,16,1472]{2,1,0:T(8,128)(2,1)} %get-tuple-element.659), channel_id=1, source_target_pairs={{0,2},{2,0},{1,3},{3,1},{4,6},{6,4},{5,7},{7,5},{8,10},{10,8},{9,1... | collective-permute-start | bytes 1130504 | tf_op jit(solution)/shard_map/ppermute | solution.py:896
  589.7 79.6 %collective-permute-start.45 = (bf16[8,16,1472]{2,1,0:T(8,128)(2,1)}, bf16[8,16,1472]{2,1,0:T(8,128)(2,1)S(1)}, u32[]{:S(2)}, u32[]{:S(2)}) collective-permute-start(bf16[8,16,1472]{2,1,0:T(8,128)(2,1)} %get-tuple-element.657), channel_id=1, source_target_pairs={{0,4},{4,0},{8,12},{12,8},{16,20},{20,16},{24,28},{28,24},{1,5},{5... | collective-permute-start | bytes 1130504 | tf_op jit(solution)/shard_map/ppermute | solution.py:896
  612.8 55.0 %collective-permute-start.42 = (f32[32,128]{1,0:T(8,128)S(1)}, f32[32,128]{1,0:T(8,128)S(1)}, u32[]{:S(2)}, u32[]{:S(2)}) collective-permute-start(f32[32,128]{1,0:T(8,128)S(1)} %pad_bitcast_fusion.4), channel_id=1, source_target_pairs={{0,1},{1,0},{2,3},{3,2},{4,5},{5,4},{6,7},{7,6},{8,9},{9,8},{10,11... | collective-permute-start | bytes 49160 | tf_op jit(solution)/shard_map/ppermute | solution.py:896
  (77 other events, 766.9 us)
Sparse Core Ops, SparseCore 0:
  31.1 136.9 all-gather.4
  170.9 81.0 all-gather.6
  257.3 172.2 reduce-scatter.3
  437.1 126.7 reduce-scatter.5
  569.1 97.2 reduce-scatter.7

commit v4 on v3

--- a/solution.py
+++ b/solution.py
@@ -133,10 +133,23 @@
     )(x, dy, gain)
 
 
+def picked(w, index):
+    entries, _, _, width = w.shape
+    each = w.shape[2] // 2
+    return pl.BlockSpec(
+        (entries, 1, each, width), lambda t: (0, 0, index, 0), pipeline_mode=pl.Buffered(1)
+    )
+
+
+def flat_rows(w_ref):
+    entries, _, each, width = w_ref.shape
+    return w_ref[...].reshape(entries * each, width)
+
+
 def key_value_body(inner, n_ref, wk_ref, wv_ref, pk_ref, pv_ref, aug_ref, out_ref):
     n = n_ref[...]
     for start, w_ref, p_ref in ((0, wk_ref, pk_ref), (inner, wv_ref, pv_ref)):
-        mixed_up = dot(w_ref[...], n, 1, 0).astype(BF16)
+        mixed_up = dot(flat_rows(w_ref), n, 1, 0).astype(BF16)
         out_ref[0, start : start + inner] = dot(p_ref[...], mixed_up, 1, 0).astype(BF16)
     out_ref[0, 2 * inner :] = aug_ref[0]
 
@@ -150,8 +163,8 @@
         grid=(rows,),
         in_specs=[
             pl.BlockSpec((width, size), lambda r: (0, first + r)),
-            whole(wk.shape),
-            whole(wv.shape),
+            picked(wk, 0),
+            picked(wv, 0),
             whole(place_k.shape),
             whole(place_v.shape),
             pl.BlockSpec((1, AUG, size), lambda r: (first + r, 0, 0)),
@@ -165,7 +178,7 @@
 
 
 def project_body(n_ref, w_ref, p_ref, out_ref):
-    mixed_up = dot(w_ref[...], n_ref[...], 1, 0).astype(BF16)
+    mixed_up = dot(flat_rows(w_ref), n_ref[...], 1, 0).astype(BF16)
     out_ref[...] = dot(p_ref[...], mixed_up, 1, 0).astype(BF16)
 
 
@@ -175,7 +188,7 @@
     return pl.pallas_call(
         project_body,
         grid=(here // tile,),
-        in_specs=[pl.BlockSpec((width, tile), lambda t: (0, t)), whole(w.shape), whole(place.shape)],
+        in_specs=[pl.BlockSpec((width, tile), lambda t: (0, t)), picked(w, 1), whole(place.shape)],
         out_specs=pl.BlockSpec((inner, tile), lambda t: (0, t)),
         out_shape=jax.ShapeDtypeStruct((inner, here), BF16),
         compiler_params=PARAMS,
@@ -408,7 +421,7 @@
 
 def mix_body(x_ref, o_ref, w_ref, place_ref, gain_ref, mixed_ref, pair_ref, *piece_refs):
     spread = dot(place_ref[...], o_ref[...], 0, 0).astype(BF16)
-    mixed = x_ref[0].astype(F32) + dot(w_ref[...], spread, 0, 0)
+    mixed = x_ref[0].astype(F32) + dot(flat_rows(w_ref), spread, 0, 0)
     mixed_ref[...] = mixed
     scale = lax.rsqrt(jnp.mean(mixed * mixed, axis=0, keepdims=True) + NORM_EPSILON)
     n = (mixed * scale * gain_ref[...]).astype(BF16)
@@ -438,7 +451,7 @@
         in_specs=[
             pl.BlockSpec((1, width, size), lambda r: (r, 0, 0)),
             pl.BlockSpec((inner, size), lambda r: (0, r)),
-            whole(w.shape),
+            picked(w, 1),
             whole(place.shape),
             whole(gain.shape),
         ],
@@ -683,7 +696,7 @@
     dmixed_ref[...] = dmixed
     low = dmixed.astype(BF16)
     spread = dot(home_ref[...], o_ref[...], 0, 0).astype(BF16)
-    mixed_up = dot(w_ref[...], low, 1, 0).astype(BF16)
+    mixed_up = dot(flat_rows(w_ref), low, 1, 0).astype(BF16)
     do_ref[...] = dot(place_ref[...], mixed_up, 1, 0).astype(BF16)
     both = dn * unit
     gain_part = both[:, :128]
@@ -720,22 +733,23 @@
     here = rows * size
     col = pl.BlockSpec((width, size), lambda r: (0, r))
     head_col = pl.BlockSpec((inner, size), lambda r: (0, r))
-    fits = w.shape[0] <= 1024
+    grad = (home.shape[1], width)
+    fits = grad[0] <= 1024
     out = pl.pallas_call(
         functools.partial(mix_back_body, layout_of(groups)),
         grid=(rows,),
         in_specs=ffn_specs(groups, acts, [0, 1], size, 0)
         + pieces_of(mixed.shape, size)[0]
         + [col, pl.BlockSpec((1, width, size), lambda r: (r, 0, 0)), head_col]
-        + [whole(w.shape), whole(place.shape), whole(home.shape), whole(gain.shape)],
-        out_specs=[col, head_col, whole((width, 128))] + [whole(w.shape)] * fits,
+        + [picked(w, 1), whole(place.shape), whole(home.shape), whole(gain.shape)],
+        out_specs=[col, head_col, whole((width, 128))] + [whole(grad)] * fits,
         out_shape=[
             jax.ShapeDtypeStruct((width, here), F32),
             jax.ShapeDtypeStruct((inner, here), BF16),
             jax.ShapeDtypeStruct((width, 128), F32),
         ]
-        + [jax.ShapeDtypeStruct(w.shape, BF16)] * fits,
-        scratch_shapes=[pltpu.VMEM(w.shape, F32)] * fits + ffn_scratch(groups, [0, 1]),
+        + [jax.ShapeDtypeStruct(grad, BF16)] * fits,
+        scratch_shapes=[pltpu.VMEM(grad, F32)] * fits + ffn_scratch(groups, [0, 1]),
         compiler_params=PARAMS,
         name="mix_back",
         cost_estimate=cost(1, 1),
@@ -828,7 +842,7 @@
     dn = None
     for j in range(3):
         spread = dot(places[j][...], d_scr[j * inner : (j + 1) * inner], 0, 0).astype(BF16)
-        term = dot(ws[j][...], spread, 0, 0)
+        term = dot(flat_rows(ws[j]), spread, 0, 0)
         dn = term if dn is None else dn + term
     x = x_ref[0].astype(F32)
     scale = lax.rsqrt(jnp.mean(x * x, axis=0, keepdims=True) + NORM_EPSILON)
@@ -862,7 +876,7 @@
         in_specs=[block, col]
         + group_specs((inner, size), len(dqs), per, 2)
         + group_specs((1,) + dkvs[0].shape[1:], len(dkvs), per, 3)
-        + [whole(w.shape) for w in ws]
+        + [picked(w, index) for w, index in zip(ws, (1, 0, 0))]
         + [whole(p.shape) for p in places]
         + [whole(gain.shape)],
         out_specs=[block, whole((width, 128))],
@@ -987,18 +1001,19 @@
         def core_end(self):
             return run(join, self.held)
 
+    attn_w = Gather(
+        jnp.concatenate([slot(w) for w in (w_key, w_attn_out, w_value, w_query)], axis=1)[:, None],
+        [(0, 2 * each), (2 * each, 2 * each)],
+        direct=True,
+    )
     units = -(-w_gate.shape[0] // ROW_TILE)
-    padded = [pad_rows(w, units * ROW_TILE) for w in (w_gate, w_up, w_ffn_out)]
+    ffn_own = after((w_gate, w_up, w_ffn_out), attn_w.held[0])
+    padded = [pad_rows(w, units * ROW_TILE) for w in ffn_own]
     marks = [0, 3, 5, 7] if units == 7 else list(range(units + 1))
     shards = [
         jnp.stack([w[low * ROW_TILE : high * ROW_TILE] for w in padded])
         for low, high in zip(marks, marks[1:])
     ]
-    attn_w = Gather(
-        jnp.concatenate([slot(w) for w in (w_key, w_attn_out, w_value, w_query)], axis=1)[:, None],
-        [(0, 2 * each), (2 * each, 2 * each)],
-        direct=True,
-    )
     same_core = ("dp", "x")
     by_hops = units == 7
     last_group = len(shards) - 1
@@ -1008,8 +1023,6 @@
     gain_one, gain_two = gain_attn[:, None], gain_ffn[:, None]
     place_a, place_b = spread_of(order_a + [core]), spread_of(order_b + [core])
     real = w_query.shape[0]
-    home_row = jnp.arange(inner) // real * each + jnp.arange(inner) % real
-    home = (home_row[:, None] == jnp.arange(inner // real * each)[None, :]).astype(BF16)
     segs = lax.dynamic_slice_in_dim(segment_ids, my_ctx * size, size, 1)
     same = segs[:, None, :] == jnp.arange(DOCS, dtype=segs.dtype)[None, :, None]
     ones = jnp.ones((rows, 1, size), BF16)
@@ -1024,6 +1037,7 @@
         axis=1,
     )
     normed, dy_pair, *dy_own = run(first_norm, x, dy, gain_one)
+    place_a, place_b, aug, query_aug, shards = close((place_a, place_b, aug, query_aug, shards))
 
     attn_w.go()
     ffn_w = [
@@ -1036,21 +1050,22 @@
     )
     dy_parts = swap_core(dy_own)
     attn_w.go()
+    if by_hops:
+        last_w = Gather(
+            shards[-1][None],
+            [(0, shards[-1].shape[1])],
+            mark=attn_w.start_of(),
+            paths=((across,), (near,)),
+        )
     dy_pair = run(fill, dy_pair, dy_parts)
     if by_hops:
-        last_w = Gather(
-            shards[-1][None], [(0, shards[-1].shape[1])], mark=dy_pair, paths=((across,), (near,))
-        )
+        last_w.go()
     attn_w.core_go()
     wko, wvq = attn_w.core_end()
-    pick = lambda w, k: w[:, 0, k * each : (k + 1) * each].reshape(-1, width)
-    if by_hops:
-        last_w.go()
-    wk, wo, wv, wq = run(lambda a, b: [pick(a, 0), pick(a, 1), pick(b, 0), pick(b, 1)], wko, wvq)
-    kv_own = run(lambda *a: key_value(*a, 0, rows), normed, wk, wv, place_a, place_b, aug)
+    kv_own = run(lambda *a: key_value(*a, 0, rows), normed, wko, wvq, place_a, place_b, aug)
     kv_across = swap(kv_own, across)
     kv_core = swap(kv_own, core)
-    queries = run(lambda n, w, p: project(n, w, p, tile), normed, wq, place_b)
+    queries = run(lambda n, w, p: project(n, w, p, tile), normed, wvq, place_b)
     kv_core = close(kv_core)
 
     kv = run(lambda *k: list(k), kv_own, kv_across, kv_core)
@@ -1058,7 +1073,7 @@
     if by_hops:
         last_w.go()
     attended, lse = run(lambda *a: attend(*a, heads, 0), queries, query_aug, kv, bias)
-    mixed, n_pair, *normed_two = run(mix, x, attended, wo, place_a, gain_two)
+    mixed, n_pair, *normed_two = run(mix, x, attended, wko, place_a, gain_two)
     n_parts = close(swap_core(normed_two))
     if by_hops:
         last_w.go()
@@ -1095,7 +1110,8 @@
             elif self.stage < hops:
                 halves = run(add_halves, self.keep, self.got)[0]
             else:
-                self.out = run(lambda k, r: add_last(k[0], r, self.edges), self.keep, self.got)
+                got = after(self.got, *token)
+                self.out = add_last(self.keep[0], got, self.edges)
                 return
             self.keep = [halves[0]]
             self.got = [swap(halves[1], far_bits[hops - 1 - self.stage])]
@@ -1108,13 +1124,16 @@
         ffn_w.append(None)
     for i, ws in enumerate(ffn_w):
         if i == last_group and by_hops:
-            ws = ffn_w[i] = close(list(last_w.held[0]))
+            ws = ffn_w[i] = last_ws
         some = tile if units_of(ws) <= 768 else tile // 2
         mask = masks[0] if by_hops and i == last_group - 1 else None
         act, grads = run(
             lambda m, w, n, d: ffn_group(m, w, n, d, some, mask), me_same, ws, n_pair, dy_pair
         )
         acts.append(act)
+        if by_hops and i == 0:
+            last_ws = close(list(last_w.held[0]))
+            grads = [after(g, last_ws) for g in grads]
         if by_hops and i >= last_group - 1:
             ffn_grads.append(grads)
         else:
@@ -1133,12 +1152,10 @@
     out_got = swap(out_other, core)
 
     dmixed, dattended, gain_two_part, gwo = run(
-        mix_back, ffn_w, acts, mixed, dn_got, dy, attended, wo, place_a, home, gain_two
-    )
-    everywhere = ("dp", "x", "core")
-    scatter = lambda g: lax.psum_scatter(g.reshape(-1, each, width), everywhere, tiled=False)
-    grad_attn_out = scatter(gwo)
+        mix_back, ffn_w, acts, mixed, dn_got, dy, attended, wko, place_a, place_a, gain_two
+    )
     tick()
+    out_got = close(out_got)
     dq, dkv, grad_bias = run(
         lambda *a: attend_back(*a, heads, 0, []),
         queries, query_aug, kv, bias, attended, dattended, lse,
@@ -1147,31 +1164,35 @@
     tick()
     if by_hops:
         ffn_grads[0] = close(ffn_grads[0])
+    entries = lambda g: tuple(v.reshape(-1, each, width) for v in g)
+    home_a, home_b = (core,) + ba, (core,) + ab
     gwq = run(
-        lambda n, d, p: projection_grads(n, [d], [(0, inner)], [p], rows), normed, dq, home
-    )
-    grad_query = scatter(jnp.concatenate(gwq))
+        lambda n, d, p: projection_grads(n, [d], [(0, inner)], [p], rows), normed, dq, place_b
+    )
     own, other = run(add_pairs, by_core)
     other = swap(other, across)
+    part = gwo.shape[0] // 2
+    query_sum = Sums([entries((gwo[:part], gwo[part:])), entries(gwq)], [home_a, home_b])
     grad_table = run(lambda g, b: bucket_sums(g, b, count), grad_bias, buckets_t)
+    query_sum.go()
     out = run(lambda *a: layer_out_of(*a, rows), ffn_w, acts, mixed, out_got)
-    tick()
-    grad_attn_out = close(grad_attn_out)
+    query_sum.go()
     (dkv,) = run(add_pairs, [(own, other)])
     gkv = run(
         lambda n, d, pa, pb: projection_grads(n, [d], [(0, inner), (inner, 2 * inner)], [pa, pb], rows),
         normed, dkv, place_a, place_b,
     )
-    entries = lambda g: tuple(v.reshape(-1, each, width) for v in g)
-    home_a, home_b = (core,) + ba, (core,) + ab
     value_sum = Sums([entries(gkv[:2]), entries(gkv[2:])], [home_a, home_b], direct=dp <= 8)
+    tick()
+    query_sum.go()
     value_sum.go()
     gx, gain_one_part = run(
         lambda *a: last(a[0], a[1], [a[2]], [a[3]], a[4:7], a[7:10], a[10]),
-        x, dmixed, dq, dkv, wq, wk, wv, place_b, place_a, place_b, gain_one,
+        x, dmixed, dq, dkv, wvq, wko, wvq, place_b, place_a, place_b, gain_one,
     )
     value_sum.go()
     tick()
+    query_sum.go()
     small = jnp.concatenate(
         [jnp.sum(gain_one_part, 1), jnp.sum(gain_two_part, 1), grad_table.reshape(-1)]
     )
@@ -1184,7 +1205,7 @@
             value_sum.go()
         small = run(lambda a, b: a + b, small, got)
     for _ in range(len(far_bits) + 4):
-        for s in [value_sum] + sums:
+        for s in [query_sum, value_sum] + sums:
             s.go()
     small = small.reshape(-1)
     if by_hops:
@@ -1199,10 +1220,10 @@
         small[:width],
         small[width : 2 * width],
         small[2 * width : length].reshape(count, heads),
-        grad_query[:real].astype(F32),
+        query_sum.out[1][:real],
         value_sum.out[0][:real],
         value_sum.out[1][:real],
-        grad_attn_out[:real].astype(F32),
+        query_sum.out[0][:real],
         grad_gate,
         grad_up,
         grad_ffn_out,

time: 709 us -> 621 us (0.88)
  waiting for transfers between devices: 228 us -> 133 us
    reduce_scatter x2 -> x0, waiting for transfers between devices: 71.2 us -> none  [per_device(): lax.psum_scatter(g.reshape(-1, each, width), everywhere, tiled=False)]
    ppermute x55 -> x63, waiting for transfers between devices: 156 us -> 133 us  [swap(): lax.ppermute(x, axis, [(i, i ^ mask) for i in range(self.sizes[axis])])]
    add x7 -> x12, other arithmetic: 10.7 us -> 17.5 us  [add_halves(): out.append((k[:part] + r[:part], k[part:] + r[part:]))]
    ppermute x55 -> x63, starting transfers between devices: 47.2 us -> 53.7 us  [swap(): lax.ppermute(x, axis, [(i, i ^ mask) for i in range(self.sizes[axis])])]
  transfers between devices with their start and end apart: 60 -> 66, of which waited for: 25 -> 28; matrix products, arithmetic and copies ran while one was open for 11% -> 12% of each run, Pallas kernels for 47% -> 54%
where the time goes in v4:
time: 621 us; the launch traced here: 616 us
  Pallas kernels  332 us (53%)
  waiting for transfers between devices  133 us (21%)
  starting transfers between devices  53.9 us (9%)
  other arithmetic  42.5 us (7%)
  local copies, waits for them, and re-layouts  38.9 us (6%)
  between operations  15.2 us (2%)
    ppermute x63, waiting for transfers between devices, swap(): lax.ppermute(x, axis, [(i, i ^ mask) for i in range(self.sizes[axis])])  133 us
    pallas_call x3, Pallas kernels, ffn_group(): pl.pallas_call(functools.partial(ffn_body, len(ws), masks), grid_spec=spe...  101 us
    ppermute x63, starting transfers between devices, swap(): lax.ppermute(x, axis, [(i, i ^ mask) for i in range(self.sizes[axis])])  53.7 us
    pallas_call x1, Pallas kernels, attend_back(): pl.pallas_call(functools.partial(attend_back_body, heads, inner, count, l...  42.2 us
    pallas_call x1, Pallas kernels, mix_back(): pl.pallas_call(functools.partial(mix_back_body, layout_of(groups)), grid=...  39 us
    pallas_call x2, Pallas kernels, ffn_back(): pl.pallas_call(functools.partial(ffn_back_body, layout_of(groups), kinds,...  30.4 us
    pallas_call x2, Pallas kernels, projection_grads(): pl.pallas_call(functools.partial(grads_body, per, len(groups), parts), gr...  20.2 us
    pallas_call x1, Pallas kernels, last(): pl.pallas_call(functools.partial(last_body, per, len(dqs)), grid=(rows,),...  19.2 us
  transfers between devices with their start and end apart: 66, of which 28 were waited for; matrix products, arithmetic and copies ran while one was open for 12% of the time, Pallas kernels for 54%

profile of v4, /device:TPU:0, one launch (start us, length us, event | category | flops | bytes accessed | tf_op | source)
XLA Modules:
  0.0 616.2 jit_solution(3133122131371365499)
XLA Ops:
  9.1 5.1 collective-permute-start.2
  21.9 7.2 %first_norm.1 = (bf16[1472,1024]{1,0:T(8,128)(2,1)}, bf16[2,1472,1024]{2,1,0:T(8,128)(2,1)}, bf16[368,1024]{1,0:T(8,128)(2,1)}, bf16[368,1024]{1,0:T(8,128)(2,1)...) custom-call(bf16[4,1472,256]{2,1,0:T(8,128)(2,1)} %bitcast.112, bf16[4,1472,256]{2,1,0:T(8,128)(2,1)} %bitcast.115, ...), custom_call_target="tpu_custom_call" | custom-call | flops 1 | bytes 1 | tf_op jit(solution)/shard_map/first_norm/pallas_call | solution.py:120
  36.0 6.9 %bias_of.1 = (f32[6,4,256,256]{3,2,1,0:T(8,128)}, s32[4,256,256]{2,1,0:T(8,128)}) custom-call(s32[4]{0:T(128)} %broadcast_xor_fusion.slots_ref, s32[256,1024]{1,0:T(8,128)} %buckets_ref, f32[6,128]{1,0:T(8,128)} %pad.57.table_ref), custom_call_target="tpu_custom_call" | custom-call | flops 1 | bytes 1 | tf_op jit(solution)/shard_map/bias_of/pallas_call | solution.py:371
  50.3 9.0 %collective-permute-done.5 = bf16[1,3,32,1472]{3,2,1,0:T(8,128)(2,1)S(1)} collective-permute-done((bf16[1,3,32,1472]{3,2,1,0:T(8,128)(2,1)S(1)}, bf16[1,3,32,1472]{3,2,1,0:T(8,128)(2,1)S(1)}, u32[]{:S(2)}, u32[]{:S(2)}) %collective-permute-start.5) | collective-permute-done | bytes 282656 | tf_op jit(solution)/shard_map/ppermute | solution.py:910
  77.9 12.4 %key_value.1.refs_0_ = bf16[4,784,256]{2,1,0:T(8,128)(2,1)} custom-call(bf16[1472,1024]{1,0:T(8,128)(2,1)} %get-tuple-element.601.n_ref, bf16[32,1,32,1472]{3,2,1,0:T(8,128)(2,1)} %copy-done.3, bf16[32,1,32,1472]{3,2,1,0:T(8,128)(2,1)} %constant_dynamic-update-slice_fusion.12.wv_ref.w_ref.refs_2_.refs_4_, ...), custom_call_target="tpu_custom_call" | custom-call | flops 1 | bytes 1 | tf_op jit(solution)/shard_map/key_value/pallas_call | solution.py:161
  94.9 5.3 project.1.q_ref
  100.2 53.0 %collective-permute-done.15.refs_1_ = bf16[4,784,256]{2,1,0:T(8,128)(2,1)S(1)} collective-permute-done((bf16[4,784,256]{2,1,0:T(8,128)(2,1)}, bf16[4,784,256]{2,1,0:T(8,128)(2,1)S(1)}, u32[]{:S(2)}, u32[]{:S(2)}) %collective-permute-start.15) | collective-permute-done | bytes 1605664 | tf_op jit(solution)/shard_map/ppermute | solution.py:910
  161.1 18.3 %attend.1 = (bf16[384,1024]{1,0:T(8,128)(2,1)}, f32[4,8,256]{2,1,0:T(8,128)}) custom-call(bf16[384,1024]{1,0:T(8,128)(2,1)} %project.1.q_ref, bf16[4,16,256]{2,1,0:T(8,128)(2,1)} %get-tuple-element.550.u_ref, bf16[4,784,256]{2,1,0:T(8,128)(2,1)} %key_value.1.refs_0_, bf16[4,784,256]{2,1,0:T(8,128)(2,1)} %copy-done.4, bf16[4,784,256]{2,1,0:T(8,128)(2,1)} %copy-done.5, ...), custom_call_target="tpu_custom_call" | custom-call | flops 1 | bytes 1 | tf_op jit(solution)/shard_map/attend/pallas_call | solution.py:231
  180.6 9.6 %mix.1 = (f32[1472,1024]{1,0:T(8,128)}, bf16[2,1472,1024]{2,1,0:T(8,128)(2,1)}, bf16[368,1024]{1,0:T(8,128)(2,1)}, bf16[368,1024]{1,0:T(8,128)(2,1)}, bf16[368,1...) custom-call(bf16[4,1472,256]{2,1,0:T(8,128)(2,1)} %bitcast.113, bf16[384,1024]{1,0:T(8,128)(2,1)} %get-tuple-element.556.o_ref.refs_13_.refs_5_, ...), custom_call_target="tpu_custom_call" | custom-call | flops 1 | bytes 1 | tf_op jit(solution)/shard_map/mix/pallas_call | solution.py:448
  203.3 41.3 %ffn_group.3 = (bf16[3,768,2048]{2,1,0:T(8,128)(2,1)}, bf16[16,3,48,1472]{3,2,1,0:T(8,128)(2,1)}) custom-call(s32[1]{0:T(128)} %bitcast.25.me_ref, bf16[16,3,48,1472]{3,2,1,0:T(8,128)(2,1)} %bitcast.102, bf16[2,1472,1024]{2,1,0:T(8,128)(2,1)} %bitcast_dynamic-update-slice_fusion.refs_1_.refs_2_, ...), custom_call_target="tpu_custom_call" | custom-call | flops 1 | bytes 1 | tf_op jit(solution)/shard_map/ffn_group/pallas_call | solution.py:574
  244.6 24.0 %collective-permute-done.26.refs_1_.refs_3_ = bf16[8,3,32,1472]{3,2,1,0:T(8,128)(2,1)} collective-permute-done((bf16[8,3,32,1472]{3,2,1,0:T(8,128)(2,1)S(1)}, bf16[8,3,32,1472]{3,2,1,0:T(8,128)(2,1)}, u32[]{:S(2)}, u32[]{:S(2)}) %collective-permute-start.26) | collective-permute-done | bytes 2261024 | tf_op jit(solution)/shard_map/ppermute | solution.py:910
  268.6 29.6 %ffn_group.4 = (bf16[3,512,2048]{2,1,0:T(8,128)(2,1)}, bf16[8,3,32,1472]{3,2,1,0:T(8,128)(2,1)}, bf16[8,3,32,1472]{3,2,1,0:T(8,128)(2,1)}) custom-call(s32[1]{0:T(128)} %bitcast.25.me_ref, bf16[16,3,32,1472]{3,2,1,0:T(8,128)(2,1)} %bitcast.107, bf16[2,1472,1024]{2,1,0:T(8,128)(2,1)} %bitcast_dynamic-update-slice_fusion.refs_1_.refs_2_, ...), custom_call_target="tpu_custom_call" | custom-call | flops 1 | bytes 1 | tf_op jit(solution)/shard_map/ffn_group/pallas_call | solution.py:574
  298.3 29.7 %ffn_group.5 = (bf16[3,512,2048]{2,1,0:T(8,128)(2,1)}, bf16[8,3,32,1472]{3,2,1,0:T(8,128)(2,1)}, bf16[8,3,32,1472]{3,2,1,0:T(8,128)(2,1)}) custom-call(s32[1]{0:T(128)} %bitcast.25.me_ref, bf16[8,3,32,1472]{3,2,1,0:T(8,128)(2,1)} %copy-done.2, bf16[8,3,32,1472]{3,2,1,0:T(8,128)(2,1)} %collective-permute-done.26.refs_1_.refs_3_, ...), custom_call_target="tpu_custom_call" | custom-call | flops 1 | bytes 1 | tf_op jit(solution)/shard_map/ffn_group/pallas_call | solution.py:574
  329.7 19.1 %ffn_back.2 = (bf16[368,1024]{1,0:T(8,128)(2,1)}, bf16[368,1024]{1,0:T(8,128)(2,1)}, bf16[368,1024]{1,0:T(8,128)(2,1)}, bf16[368,1024]{1,0:T(8,128)(2,1)}) custom-call(bf16[16,3,48,1472]{3,2,1,0:T(8,128)(2,1)} %bitcast.103, bf16[16,3,32,1472]{3,2,1,0:T(8,128)(2,1)} %bitcast.108, bf16[8,3,32,1472]{3,2,1,0:T(8,128)(2,1)} %copy-done.2, ...), custom_call_target="tpu_custom_call" | custom-call | flops 1 | bytes 1 | tf_op jit(solution)/shard_map/ffn_back/pallas_call | solution.py:641
  351.5 11.4 %ffn_back.3 = bf16[1472,1024]{1,0:T(8,128)(2,1)} custom-call(bf16[16,3,48,1472]{3,2,1,0:T(8,128)(2,1)} %bitcast.104, bf16[16,3,32,1472]{3,2,1,0:T(8,128)(2,1)} %bitcast.109, bf16[8,3,32,1472]{3,2,1,0:T(8,128)(2,1)} %copy-done.2, bf16[8,3,32,1472]{3,2,1,0:T(8,128)(2,1)} %collective-permute-done.26.refs_1_.refs_3_, ...), custom_call_target="tpu_custom_call" | custom-call | flops 1 | bytes 1 | tf_op jit(solution)/shard_map/ffn_back/pallas_call | solution.py:641
  364.7 39.0 %mix_back.1 = (f32[1472,1024]{1,0:T(8,128)}, bf16[384,1024]{1,0:T(8,128)(2,1)}, f32[1472,128]{1,0:T(8,128)}, bf16[512,1472]{1,0:T(8,128)(2,1)}) custom-call(bf16[16,3,48,1472]{3,2,1,0:T(8,128)(2,1)} %bitcast.105, bf16[16,3,32,1472]{3,2,1,0:T(8,128)(2,1)} %bitcast.110, bf16[8,3,32,1472]{3,2,1,0:T(8,128)(2,1)} %copy-done.2, ...), custom_call_target="tpu_custom_call" | custom-call | flops 1 | bytes 1 | tf_op jit(solution)/shard_map/mix_back/pallas_call | solution.py:738
  414.3 42.2 %attend_back.1 = (bf16[384,1024]{1,0:T(8,128)(2,1)}, bf16[4,784,256]{2,1,0:T(8,128)(2,1)}, bf16[4,784,256]{2,1,0:T(8,128)(2,1)}, bf16[4,784,256]{2,1,0:T(8,128)(...) custom-call(bf16[384,1024]{1,0:T(8,128)(2,1)} %project.1.q_ref, ...), custom_call_target="tpu_custom_call" | custom-call | flops 1 | bytes 1 | tf_op jit(solution)/shard_map/attend_back/pallas_call | solution.py:326
  462.1 8.0 %projection_grads.2 = (bf16[256,1472]{1,0:T(8,128)(2,1)}, bf16[256,1472]{1,0:T(8,128)(2,1)}) custom-call(bf16[1472,1024]{1,0:T(8,128)(2,1)} %get-tuple-element.601.n_ref, bf16[384,1024]{1,0:T(8,128)(2,1)} %get-tuple-element.621.refs_0_, bf16[384,512]{1,0:T(8,128)(2,1)} %fusion.1.pv_ref.p_ref.refs_1_.refs_2_.refs_5_.refs_7_), custom_call_target="tpu_custom_call" | custom-call | flops 1 | bytes 1 | tf_op jit(solution)/shard_map/projection_grads/pallas_call | solution.py:812
  473.1 8.0 %bucket_sums.1 = f32[96,256]{1,0:T(8,128)} custom-call(s32[4,256,256]{2,1,0:T(8,128)} %get-tuple-element.580.buckets_ref, f32[6,4,256,256]{3,2,1,0:T(8,128)} %get-tuple-element.581.g_ref), custom_call_target="tpu_custom_call" | custom-call | flops 1 | bytes 1 | tf_op jit(solution)/shard_map/bucket_sums/pallas_call | solution.py:405
  493.1 13.1 %layer_out_of.1 = bf16[4,1472,256]{2,1,0:T(8,128)(2,1)} custom-call(bf16[16,3,48,1472]{3,2,1,0:T(8,128)(2,1)} %bitcast.106, bf16[16,3,32,1472]{3,2,1,0:T(8,128)(2,1)} %bitcast.111, bf16[8,3,32,1472]{3,2,1,0:T(8,128)(2,1)} %copy-done.2, bf16[8,3,32,1472]{3,2,1,0:T(8,128)(2,1)} %collective-permute-done.26.refs_1_.refs_3_, ...), custom_call_target="tpu_custom_call" | custom-call | flops 1 | bytes 1 | tf_op jit(solution)/shard_map/layer_out_of/pallas_call | solution.py:665
  506.2 11.7 %collective-permute-done.41 = bf16[8,16,1472]{2,1,0:T(8,128)(2,1)} collective-permute-done((bf16[8,16,1472]{2,1,0:T(8,128)(2,1)S(1)}, bf16[8,16,1472]{2,1,0:T(8,128)(2,1)}, u32[]{:S(2)}, u32[]{:S(2)}) %collective-permute-start.41) | collective-permute-done | bytes 376864 | tf_op jit(solution)/shard_map/ppermute | solution.py:910
  524.8 12.3 %projection_grads.3 = (bf16[256,1472]{1,0:T(8,128)(2,1)}, bf16[256,1472]{1,0:T(8,128)(2,1)}, bf16[256,1472]{1,0:T(8,128)(2,1)}, bf16[256,1472]{1,0:T(8,128)(2,1)}) custom-call(bf16[1472,1024]{1,0:T(8,128)(2,1)} %get-tuple-element.601.n_ref, bf16[4,784,256]{2,1,0:T(8,128)(2,1)} %add.272.refs_0_.refs_1_, ...), custom_call_target="tpu_custom_call" | custom-call | flops 1 | bytes 1 | tf_op jit(solution)/shard_map/projection_grads/pallas_call | solution.py:812
  537.0 6.2 %collective-permute-done.47 = bf16[2,3,64,1472]{3,2,1,0:T(8,128)(2,1)} collective-permute-done((bf16[2,3,64,1472]{3,2,1,0:T(8,128)(2,1)}, bf16[2,3,64,1472]{3,2,1,0:T(8,128)(2,1)}, u32[]{:S(2)}, u32[]{:S(2)}) %collective-permute-start.47) | collective-permute-done | bytes 1130528 | tf_op jit(solution)/shard_map/ppermute | solution.py:910
  557.4 19.2 %last.1 = (f32[4,1472,256]{2,1,0:T(8,128)}, f32[1472,128]{1,0:T(8,128)}) custom-call(bf16[4,1472,256]{2,1,0:T(8,128)(2,1)} %bitcast.114, f32[1472,1024]{1,0:T(8,128)} %get-tuple-element.620.dm_ref, bf16[384,1024]{1,0:T(8,128)(2,1)} %get-tuple-element.621.refs_0_, bf16[4,784,256]{2,1,0:T(8,128)(2,1)} %add.272.refs_0_.refs_1_, ...), custom_call_target="tpu_custom_call" | custom-call | flops 1 | bytes 1 | tf_op jit(solution)/shard_map/last/pallas_call | solution.py:873
  (347 shorter events, 159.5 us)
Async XLA Ops:
  7.3 196.0 %all-gather.5.cloned.1.call-start = ((), (), s32[]{:S(2)}) async-start(), calls=%async_computation.2 | async-start | bytes 7520256 | tf_op jit(solution)/shard_map/all_gather | solution.py:1044
  9.1 20.8 %collective-permute-start.2 = (bf16[1,1,64,1472]{3,2,1,0:T(8,128)(2,1)S(1)}, bf16[1,1,64,1472]{3,2,1,0:T(8,128)(2,1)S(1)}, u32[]{:S(2)}, u32[]{:S(2)}) collective-permute-start(bf16[1,1,64,1472]{3,2,1,0:T(8,128)(2,1)S(1)} %maximum_bitcast_fusion), channel_id=1, source_target_pairs={{0,24},{4,28},{8,16},{12,20},{16,8},{20,12},{24,0},{28,4},{1,25},{... | collective-permute-start | bytes 565256 | tf_op jit(solution)/shard_map/ppermute | solution.py:910
  31.1 237.5 %all-gather.7.cloned.1.call-start = ((), (), s32[]{:S(2)}) async-start(), calls=%async_computation.3 | async-start | bytes 5013504 | tf_op jit(solution)/shard_map/all_gather | solution.py:1044
  66.0 396.1 %reduce-scatter.2.cloned.1.call-start = ((), (), s32[]{:S(2)}) async-start(), calls=%async_computation.1 | async-start | bytes 7520256 | tf_op jit(solution)/shard_map/reduce_scatter | solution.py:1140
  90.4 62.9 %collective-permute-start.15 = (bf16[4,784,256]{2,1,0:T(8,128)(2,1)}, bf16[4,784,256]{2,1,0:T(8,128)(2,1)S(1)}, u32[]{:S(2)}, u32[]{:S(2)}) collective-permute-start(bf16[4,784,256]{2,1,0:T(8,128)(2,1)} %key_value.1.refs_0_), channel_id=1, source_target_pairs={{0,2},{2,0},{1,3},{3,1},{4,6},{6,4},{5,7},{7,5},{8,10},{10,8},{9,1... | collective-permute-start | bytes 4816904 | tf_op jit(solution)/shard_map/ppermute | solution.py:910
  92.0 67.4 %collective-permute-start.10 = (bf16[2,3,32,1472]{3,2,1,0:T(8,128)(2,1)S(1)}, bf16[2,3,32,1472]{3,2,1,0:T(8,128)(2,1)S(1)}, u32[]{:S(2)}, u32[]{:S(2)}) collective-permute-start(bf16[2,3,32,1472]{3,2,1,0:T(8,128)(2,1)S(1)} %constant_dynamic-update-slice_fusion.4), channel_id=1, source_target_pairs={{0,16},{4,20},{8,24},{12,28},{16,0},{20,4},{24,8},{28,12},{1,17},{... | collective-permute-start | bytes 1695752 | tf_op jit(solution)/shard_map/ppermute | solution.py:910
  159.5 37.3 %collective-permute-start.21 = (bf16[4,3,32,1472]{3,2,1,0:T(8,128)(2,1)S(1)}, bf16[4,3,32,1472]{3,2,1,0:T(8,128)(2,1)}, u32[]{:S(2)}, u32[]{:S(2)}) collective-permute-start(bf16[4,3,32,1472]{3,2,1,0:T(8,128)(2,1)S(1)} %constant_dynamic-update-slice_fusion.14), channel_id=1, source_target_pairs={{0,2},{2,0},{1,3},{3,1},{4,6},{6,4},{5,7},{7,5},{8,10},{10,8},{9,1... | collective-permute-start | bytes 3391496 | tf_op jit(solution)/shard_map/ppermute | solution.py:910
  198.3 70.3 %collective-permute-start.26 = (bf16[8,3,32,1472]{3,2,1,0:T(8,128)(2,1)S(1)}, bf16[8,3,32,1472]{3,2,1,0:T(8,128)(2,1)}, u32[]{:S(2)}, u32[]{:S(2)}) collective-permute-start(bf16[8,3,32,1472]{3,2,1,0:T(8,128)(2,1)S(1)} %constant_dynamic-update-slice_fusion.16.refs_0_.refs_2_), channel_id=1, source_target_pairs={{0,4},{4,0},{8,12},{12,8},{16,20},{20,16},{24,28},{28,24},{1,5},{5... | collective-permute-start | bytes 6782984 | tf_op jit(solution)/shard_map/ppermute | solution.py:910
  328.0 75.7 %collective-permute-start.29 = (bf16[8,3,32,1472]{3,2,1,0:T(8,128)(2,1)}, bf16[8,3,32,1472]{3,2,1,0:T(8,128)(2,1)}, u32[]{:S(2)}, u32[]{:S(2)}) collective-permute-start(bf16[8,3,32,1472]{3,2,1,0:T(8,128)(2,1)} %get-tuple-element.499), channel_id=1, source_target_pairs={{0,4},{4,0},{8,12},{12,8},{16,20},{20,16},{24,28},{28,24},{1,5},{5... | collective-permute-start | bytes 6782984 | tf_op jit(solution)/shard_map/ppermute | solution.py:910
  328.5 75.2 %collective-permute-start.28 = (bf16[8,3,32,1472]{3,2,1,0:T(8,128)(2,1)}, bf16[8,3,32,1472]{3,2,1,0:T(8,128)(2,1)}, u32[]{:S(2)}, u32[]{:S(2)}) collective-permute-start(bf16[8,3,32,1472]{3,2,1,0:T(8,128)(2,1)} %get-tuple-element.491), channel_id=1, source_target_pairs={{0,2},{2,0},{1,3},{3,1},{4,6},{6,4},{5,7},{7,5},{8,10},{10,8},{9,1... | collective-permute-start | bytes 6782984 | tf_op jit(solution)/shard_map/ppermute | solution.py:910
  362.9 51.4 %collective-permute-start.27 = (bf16[1472,1024]{1,0:T(8,128)(2,1)}, bf16[1472,1024]{1,0:T(8,128)(2,1)S(1)}, u32[]{:S(2)}, u32[]{:S(2)}) collective-permute-start(bf16[1472,1024]{1,0:T(8,128)(2,1)} %ffn_back.3), channel_id=1, source_target_pairs={{0,1},{1,0},{2,3},{3,2},{4,5},{5,4},{6,7},{7,6},{8,9},{9,8},{10,11... | collective-permute-start | bytes 9043976 | tf_op jit(solution)/shard_map/ppermute | solution.py:910
  407.6 49.6 %collective-permute-start.34 = (bf16[4,3,32,1472]{3,2,1,0:T(8,128)(2,1)}, bf16[4,3,32,1472]{3,2,1,0:T(8,128)(2,1)}, u32[]{:S(2)}, u32[]{:S(2)}) collective-permute-start(bf16[4,3,32,1472]{3,2,1,0:T(8,128)(2,1)} %get-tuple-element.685), channel_id=1, source_target_pairs={{0,4},{4,0},{8,12},{12,8},{16,20},{20,16},{24,28},{28,24},{1,5},{5... | collective-permute-start | bytes 3391496 | tf_op jit(solution)/shard_map/ppermute | solution.py:910
  411.4 45.7 %collective-permute-start.35 = (bf16[4,3,32,1472]{3,2,1,0:T(8,128)(2,1)}, bf16[4,3,32,1472]{3,2,1,0:T(8,128)(2,1)}, u32[]{:S(2)}, u32[]{:S(2)}) collective-permute-start(bf16[4,3,32,1472]{3,2,1,0:T(8,128)(2,1)} %get-tuple-element.683), channel_id=1, source_target_pairs={{0,2},{2,0},{1,3},{3,1},{4,6},{6,4},{5,7},{7,5},{8,10},{10,8},{9,1... | collective-permute-start | bytes 3391496 | tf_op jit(solution)/shard_map/ppermute | solution.py:910
  414.3 69.4 %collective-permute-start.36 = (bf16[16,16,1472]{2,1,0:T(8,128)(2,1)}, bf16[16,16,1472]{2,1,0:T(8,128)(2,1)}, u32[]{:S(2)}, u32[]{:S(2)}) collective-permute-start(bf16[16,16,1472]{2,1,0:T(8,128)(2,1)} %bitcast.33), channel_id=1, source_target_pairs={{0,1},{1,0},{2,3},{3,2},{4,5},{5,4},{6,7},{7,6},{8,9},{9,8},{10,11... | collective-permute-start | bytes 2261000 | tf_op jit(solution)/shard_map/ppermute | solution.py:910
  472.1 49.6 %collective-permute-start.40 = (bf16[4,784,256]{2,1,0:T(8,128)(2,1)}, bf16[4,784,256]{2,1,0:T(8,128)(2,1)}, u32[]{:S(2)}, u32[]{:S(2)}) collective-permute-start(bf16[4,784,256]{2,1,0:T(8,128)(2,1)} %add.263), channel_id=1, source_target_pairs={{0,2},{2,0},{1,3},{3,1},{4,6},{6,4},{5,7},{7,5},{8,10},{10,8},{9,1... | collective-permute-start | bytes 4816904 | tf_op jit(solution)/shard_map/ppermute | solution.py:910
  485.2 32.8 %collective-permute-start.41 = (bf16[8,16,1472]{2,1,0:T(8,128)(2,1)S(1)}, bf16[8,16,1472]{2,1,0:T(8,128)(2,1)}, u32[]{:S(2)}, u32[]{:S(2)}) collective-permute-start(bf16[8,16,1472]{2,1,0:T(8,128)(2,1)S(1)} %get-tuple-element.703), channel_id=1, source_target_pairs={{0,2},{2,0},{1,3},{3,1},{4,6},{6,4},{5,7},{7,5},{8,10},{10,8},{9,1... | collective-permute-start | bytes 1130504 | tf_op jit(solution)/shard_map/ppermute | solution.py:910
  488.7 29.2 %collective-permute-start.42 = (bf16[8,16,1472]{2,1,0:T(8,128)(2,1)}, bf16[8,16,1472]{2,1,0:T(8,128)(2,1)}, u32[]{:S(2)}, u32[]{:S(2)}) collective-permute-start(bf16[8,16,1472]{2,1,0:T(8,128)(2,1)} %get-tuple-element.701), channel_id=1, source_target_pairs={{0,4},{4,0},{8,12},{12,8},{16,20},{20,16},{24,28},{28,24},{1,5},{5... | collective-permute-start | bytes 1130504 | tf_op jit(solution)/shard_map/ppermute | solution.py:910
  489.2 54.0 %collective-permute-start.47 = (bf16[2,3,64,1472]{3,2,1,0:T(8,128)(2,1)}, bf16[2,3,64,1472]{3,2,1,0:T(8,128)(2,1)}, u32[]{:S(2)}, u32[]{:S(2)}) collective-permute-start(bf16[2,3,64,1472]{3,2,1,0:T(8,128)(2,1)} %pad_maximum_fusion.2), channel_id=1, source_target_pairs={{0,16},{4,20},{8,24},{12,28},{16,0},{20,4},{24,8},{28,12},{1,17},{... | collective-permute-start | bytes 3391496 | tf_op jit(solution)/shard_map/ppermute | solution.py:910
  519.0 25.7 %collective-permute-start.45 = (bf16[4,16,1472]{2,1,0:T(8,128)(2,1)S(1)}, bf16[4,16,1472]{2,1,0:T(8,128)(2,1)S(1)}, u32[]{:S(2)}, u32[]{:S(2)}) collective-permute-start(bf16[4,16,1472]{2,1,0:T(8,128)(2,1)S(1)} %get-tuple-element.719), channel_id=1, source_target_pairs={{0,4},{4,0},{8,12},{12,8},{16,20},{20,16},{24,28},{28,24},{1,5},{5... | collective-permute-start | bytes 565256 | tf_op jit(solution)/shard_map/ppermute | solution.py:910
  520.6 24.1 %collective-permute-start.46 = (bf16[4,16,1472]{2,1,0:T(8,128)(2,1)S(1)}, bf16[4,16,1472]{2,1,0:T(8,128)(2,1)S(1)}, u32[]{:S(2)}, u32[]{:S(2)}) collective-permute-start(bf16[4,16,1472]{2,1,0:T(8,128)(2,1)S(1)} %get-tuple-element.717), channel_id=1, source_target_pairs={{0,2},{2,0},{1,3},{3,1},{4,6},{6,4},{5,7},{7,5},{8,10},{10,8},{9,1... | collective-permute-start | bytes 565256 | tf_op jit(solution)/shard_map/ppermute | solution.py:910
  548.4 29.9 %collective-permute-start.50 = (bf16[8,16,1472]{2,1,0:T(8,128)(2,1)S(1)}, bf16[8,16,1472]{2,1,0:T(8,128)(2,1)}, u32[]{:S(2)}, u32[]{:S(2)}) collective-permute-start(bf16[8,16,1472]{2,1,0:T(8,128)(2,1)S(1)} %get-tuple-element.699), channel_id=1, source_target_pairs={{0,2},{2,0},{1,3},{3,1},{4,6},{6,4},{5,7},{7,5},{8,10},{10,8},{9,1... | collective-permute-start | bytes 1130504 | tf_op jit(solution)/shard_map/ppermute | solution.py:910
  550.0 28.2 %collective-permute-start.51 = (bf16[8,16,1472]{2,1,0:T(8,128)(2,1)}, bf16[8,16,1472]{2,1,0:T(8,128)(2,1)}, u32[]{:S(2)}, u32[]{:S(2)}) collective-permute-start(bf16[8,16,1472]{2,1,0:T(8,128)(2,1)} %get-tuple-element.697), channel_id=1, source_target_pairs={{0,4},{4,0},{8,12},{12,8},{16,20},{20,16},{24,28},{28,24},{1,5},{5... | collective-permute-start | bytes 1130504 | tf_op jit(solution)/shard_map/ppermute | solution.py:910
  551.6 32.2 %collective-permute-start.49 = (bf16[2,32,1472]{2,1,0:T(8,128)(2,1)}, bf16[2,32,1472]{2,1,0:T(8,128)(2,1)}, u32[]{:S(2)}, u32[]{:S(2)}) collective-permute-start(bf16[2,32,1472]{2,1,0:T(8,128)(2,1)} %pad_maximum_fusion.12), channel_id=1, source_target_pairs={{0,16},{4,20},{8,24},{12,28},{16,0},{20,4},{24,8},{28,12},{1,17},{... | collective-permute-start | bytes 565256 | tf_op jit(solution)/shard_map/ppermute | solution.py:910
  551.7 30.8 %collective-permute-start.62 = (bf16[1,3,64,1472]{3,2,1,0:T(8,128)(2,1)S(1)}, bf16[1,3,64,1472]{3,2,1,0:T(8,128)(2,1)}, u32[]{:S(2)}, u32[]{:S(2)}) collective-permute-start(bf16[1,3,64,1472]{3,2,1,0:T(8,128)(2,1)S(1)} %get-tuple-element.687), channel_id=1, source_target_pairs={{0,8},{4,12},{8,0},{12,4},{16,24},{20,28},{24,16},{28,20},{1,9},{5... | collective-permute-start | bytes 1695752 | tf_op jit(solution)/shard_map/ppermute | solution.py:910
  (85 other events, 700.4 us)
Sparse Core Ops, SparseCore 0:
  31.2 132.1 all-gather.4
  166.2 97.7 all-gather.6
  269.3 169.1 reduce-scatter.1

commit v5 on v4

--- a/solution.py
+++ b/solution.py
@@ -1055,7 +1055,7 @@
             shards[-1][None],
             [(0, shards[-1].shape[1])],
             mark=attn_w.start_of(),
-            paths=((across,), (near,)),
+            paths=((near,), (across,)),
         )
     dy_pair = run(fill, dy_pair, dy_parts)
     if by_hops:
@@ -1067,16 +1067,16 @@
     kv_core = swap(kv_own, core)
     queries = run(lambda n, w, p: project(n, w, p, tile), normed, wvq, place_b)
     kv_core = close(kv_core)
-
-    kv = run(lambda *k: list(k), kv_own, kv_across, kv_core)
-    kv.append(close(jnp.concatenate([swap(k, core) for k in jnp.split(kv[1], rows)])))
     if by_hops:
         last_w.go()
+
+    kv = run(lambda *k: list(k), kv_own, kv_across, kv_core)
+    kv.append(close(jnp.concatenate([swap(k, core) for k in jnp.split(kv[1], min(2, rows))])))
     attended, lse = run(lambda *a: attend(*a, heads, 0), queries, query_aug, kv, bias)
+    if by_hops:
+        last_w.go()
     mixed, n_pair, *normed_two = run(mix, x, attended, wko, place_a, gain_two)
     n_parts = close(swap_core(normed_two))
-    if by_hops:
-        last_w.go()
     n_pair = run(fill, n_pair, n_parts)
 
     class Sums:
@@ -1126,7 +1126,7 @@
         if i == last_group and by_hops:
             ws = ffn_w[i] = last_ws
         some = tile if units_of(ws) <= 768 else tile // 2
-        mask = masks[0] if by_hops and i == last_group - 1 else None
+        mask = masks[1] if by_hops and i == last_group - 1 else None
         act, grads = run(
             lambda m, w, n, d: ffn_group(m, w, n, d, some, mask), me_same, ws, n_pair, dy_pair
         )
@@ -1139,7 +1139,7 @@
         else:
             ffn_grads.append(lax.psum_scatter(grads[0], same_core))
     if by_hops:
-        sums = [Sums(ffn_grads[-2:], [ba, ab])]
+        sums = [Sums(ffn_grads[-2:], [ab, ba])]
 
     def tick():
         for s in sums:
@@ -1152,7 +1152,7 @@
     out_got = swap(out_other, core)
 
     dmixed, dattended, gain_two_part, gwo = run(
-        mix_back, ffn_w, acts, mixed, dn_got, dy, attended, wko, place_a, place_a, gain_two
+        mix_back, ffn_w, acts, mixed, dn_got, dy, attended, wko, place_a, place_b, gain_two
     )
     tick()
     out_got = close(out_got)
@@ -1172,7 +1172,7 @@
     own, other = run(add_pairs, by_core)
     other = swap(other, across)
     part = gwo.shape[0] // 2
-    query_sum = Sums([entries((gwo[:part], gwo[part:])), entries(gwq)], [home_a, home_b])
+    query_sum = Sums([entries((gwo[:part], gwo[part:])), entries(gwq)], [home_b, home_b])
     grad_table = run(lambda g, b: bucket_sums(g, b, count), grad_bias, buckets_t)
     query_sum.go()
     out = run(lambda *a: layer_out_of(*a, rows), ffn_w, acts, mixed, out_got)
@@ -1201,8 +1201,10 @@
     bits = [core, across] + [("dp", 1 << b) for b in range(dp.bit_length() - 1)]
     for k, one in enumerate(bits):
         got = swap(small, one)
-        if k in (1, 3):
+        if k == 1:
             value_sum.go()
+        if k == 3:
+            value_sum.got = close(value_sum.got)
         small = run(lambda a, b: a + b, small, got)
     for _ in range(len(far_bits) + 4):
         for s in [query_sum, value_sum] + sums:

time: 621 us -> 622 us (level)
    all_gather x2, waiting for transfers between devices: 0.02 us -> 12.6 us  [per_device(): lax.all_gather(after(shard, attn_w.start_of()), same_core)]
    ppermute x63 -> x61, waiting for transfers between devices: 133 us -> 122 us  [swap(): lax.ppermute(x, axis, [(i, i ^ mask) for i in range(self.sizes[axis])])]
    ppermute x63 -> x61, starting transfers between devices: 53.7 us -> 51.5 us  [swap(): lax.ppermute(x, axis, [(i, i ^ mask) for i in range(self.sizes[axis])])]
  transfers between devices with their start and end apart: 66 -> 64, of which waited for: 28 -> 26; matrix products, arithmetic and copies ran while one was open for 12% -> 12% of each run, Pallas kernels for 54% -> 54%
where the time goes in v5:
time: 622 us; the launch traced here: 617 us
  Pallas kernels  332 us (53%)
  waiting for transfers between devices  134 us (22%)
  starting transfers between devices  51.8 us (8%)
  other arithmetic  42.4 us (7%)
  local copies, waits for them, and re-layouts  41.6 us (7%)
  between operations  15.3 us (2%)
    ppermute x61, waiting for transfers between devices, swap(): lax.ppermute(x, axis, [(i, i ^ mask) for i in range(self.sizes[axis])])  122 us
    pallas_call x3, Pallas kernels, ffn_group(): pl.pallas_call(functools.partial(ffn_body, len(ws), masks), grid_spec=spe...  100 us
    ppermute x61, starting transfers between devices, swap(): lax.ppermute(x, axis, [(i, i ^ mask) for i in range(self.sizes[axis])])  51.5 us
    pallas_call x1, Pallas kernels, attend_back(): pl.pallas_call(functools.partial(attend_back_body, heads, inner, count, l...  42.2 us
    pallas_call x1, Pallas kernels, mix_back(): pl.pallas_call(functools.partial(mix_back_body, layout_of(groups)), grid=...  38.5 us
    pallas_call x2, Pallas kernels, ffn_back(): pl.pallas_call(functools.partial(ffn_back_body, layout_of(groups), kinds,...  30.6 us
    pallas_call x2, Pallas kernels, projection_grads(): pl.pallas_call(functools.partial(grads_body, per, len(groups), parts), gr...  20.3 us
    pallas_call x1, Pallas kernels, last(): pl.pallas_call(functools.partial(last_body, per, len(dqs)), grid=(rows,),...  19.2 us
  transfers between devices with their start and end apart: 64, of which 26 were waited for; matrix products, arithmetic and copies ran while one was open for 12% of the time, Pallas kernels for 54%

profile of v5, /device:TPU:0, one launch (start us, length us, event | category | flops | bytes accessed | tf_op | source)
XLA Modules:
  0.0 617.1 jit_solution(10408223851206113053)
XLA Ops:
  22.0 7.2 %first_norm.1 = (bf16[1472,1024]{1,0:T(8,128)(2,1)}, bf16[2,1472,1024]{2,1,0:T(8,128)(2,1)}, bf16[368,1024]{1,0:T(8,128)(2,1)}, bf16[368,1024]{1,0:T(8,128)(2,1)...) custom-call(bf16[4,1472,256]{2,1,0:T(8,128)(2,1)} %bitcast.112, bf16[4,1472,256]{2,1,0:T(8,128)(2,1)} %bitcast.115, ...), custom_call_target="tpu_custom_call" | custom-call | flops 1 | bytes 1 | tf_op jit(solution)/shard_map/first_norm/pallas_call | solution.py:120
  36.0 6.8 %bias_of.1 = (f32[6,4,256,256]{3,2,1,0:T(8,128)}, s32[4,256,256]{2,1,0:T(8,128)}) custom-call(s32[4]{0:T(128)} %broadcast_xor_fusion.slots_ref, s32[256,1024]{1,0:T(8,128)} %buckets_ref, f32[6,128]{1,0:T(8,128)} %pad.57.table_ref), custom_call_target="tpu_custom_call" | custom-call | flops 1 | bytes 1 | tf_op jit(solution)/shard_map/bias_of/pallas_call | solution.py:371
  50.3 8.9 %collective-permute-done.5 = bf16[1,3,32,1472]{3,2,1,0:T(8,128)(2,1)S(1)} collective-permute-done((bf16[1,3,32,1472]{3,2,1,0:T(8,128)(2,1)S(1)}, bf16[1,3,32,1472]{3,2,1,0:T(8,128)(2,1)S(1)}, u32[]{:S(2)}, u32[]{:S(2)}) %collective-permute-start.5) | collective-permute-done | bytes 282656 | tf_op jit(solution)/shard_map/ppermute | solution.py:910
  77.9 12.3 %key_value.1.refs_0_ = bf16[4,784,256]{2,1,0:T(8,128)(2,1)} custom-call(bf16[1472,1024]{1,0:T(8,128)(2,1)} %get-tuple-element.604.n_ref, bf16[32,1,32,1472]{3,2,1,0:T(8,128)(2,1)} %copy-done.3, bf16[32,1,32,1472]{3,2,1,0:T(8,128)(2,1)} %constant_dynamic-update-slice_fusion.12.wv_ref.w_ref.refs_2_.refs_4_, ...), custom_call_target="tpu_custom_call" | custom-call | flops 1 | bytes 1 | tf_op jit(solution)/shard_map/key_value/pallas_call | solution.py:161
  94.8 5.3 project.1.q_ref
  100.1 46.0 %collective-permute-done.10 = bf16[2,3,32,1472]{3,2,1,0:T(8,128)(2,1)S(1)} collective-permute-done((bf16[2,3,32,1472]{3,2,1,0:T(8,128)(2,1)S(1)}, bf16[2,3,32,1472]{3,2,1,0:T(8,128)(2,1)S(1)}, u32[]{:S(2)}, u32[]{:S(2)}) %collective-permute-start.10) | collective-permute-done | bytes 565280 | tf_op jit(solution)/shard_map/ppermute | solution.py:910
  146.6 6.6 %collective-permute-done.17.refs_1_ = bf16[4,784,256]{2,1,0:T(8,128)(2,1)S(1)} collective-permute-done((bf16[4,784,256]{2,1,0:T(8,128)(2,1)}, bf16[4,784,256]{2,1,0:T(8,128)(2,1)S(1)}, u32[]{:S(2)}, u32[]{:S(2)}) %collective-permute-start.17) | collective-permute-done | bytes 1605664 | tf_op jit(solution)/shard_map/ppermute | solution.py:910
  159.2 18.3 %attend.1 = (bf16[384,1024]{1,0:T(8,128)(2,1)}, f32[4,8,256]{2,1,0:T(8,128)}) custom-call(bf16[384,1024]{1,0:T(8,128)(2,1)} %project.1.q_ref, bf16[4,16,256]{2,1,0:T(8,128)(2,1)} %get-tuple-element.553.u_ref, bf16[4,784,256]{2,1,0:T(8,128)(2,1)} %key_value.1.refs_0_, bf16[4,784,256]{2,1,0:T(8,128)(2,1)} %copy-done.4, bf16[4,784,256]{2,1,0:T(8,128)(2,1)} %copy-done.5, ...), custom_call_target="tpu_custom_call" | custom-call | flops 1 | bytes 1 | tf_op jit(solution)/shard_map/attend/pallas_call | solution.py:231
  182.7 9.6 %mix.1 = (f32[1472,1024]{1,0:T(8,128)}, bf16[2,1472,1024]{2,1,0:T(8,128)(2,1)}, bf16[368,1024]{1,0:T(8,128)(2,1)}, bf16[368,1024]{1,0:T(8,128)(2,1)}, bf16[368,1...) custom-call(bf16[4,1472,256]{2,1,0:T(8,128)(2,1)} %bitcast.113, bf16[384,1024]{1,0:T(8,128)(2,1)} %get-tuple-element.559.o_ref.refs_13_.refs_5_, ...), custom_call_target="tpu_custom_call" | custom-call | flops 1 | bytes 1 | tf_op jit(solution)/shard_map/mix/pallas_call | solution.py:448
  205.4 41.2 %ffn_group.3 = (bf16[3,768,2048]{2,1,0:T(8,128)(2,1)}, bf16[16,3,48,1472]{3,2,1,0:T(8,128)(2,1)}) custom-call(s32[1]{0:T(128)} %bitcast.25.me_ref, bf16[16,3,48,1472]{3,2,1,0:T(8,128)(2,1)} %bitcast.102, bf16[2,1472,1024]{2,1,0:T(8,128)(2,1)} %bitcast_dynamic-update-slice_fusion.refs_1_.refs_2_, ...), custom_call_target="tpu_custom_call" | custom-call | flops 1 | bytes 1 | tf_op jit(solution)/shard_map/ffn_group/pallas_call | solution.py:574
  246.6 12.1 %collective-permute-done.20.refs_1_.refs_3_ = bf16[8,3,32,1472]{3,2,1,0:T(8,128)(2,1)} collective-permute-done((bf16[8,3,32,1472]{3,2,1,0:T(8,128)(2,1)S(1)}, bf16[8,3,32,1472]{3,2,1,0:T(8,128)(2,1)}, u32[]{:S(2)}, u32[]{:S(2)}) %collective-permute-start.20) | collective-permute-done | bytes 2261024 | tf_op jit(solution)/shard_map/ppermute | solution.py:910
  258.7 12.6 %all-gather.7.cloned.1.call-done = bf16[48,32,1472]{2,1,0:T(8,128)(2,1)} async-done(((bf16[3,32,1472]{2,1,0:T(8,128)(2,1)}), bf16[48,32,1472]{2,1,0:T(8,128)(2,1)}) %all-gather.7.cloned.1.call-update) | async-done | bytes 4522000 | tf_op jit(solution)/shard_map/all_gather | solution.py:1044
  271.3 29.6 %ffn_group.4 = (bf16[3,512,2048]{2,1,0:T(8,128)(2,1)}, bf16[8,3,32,1472]{3,2,1,0:T(8,128)(2,1)}, bf16[8,3,32,1472]{3,2,1,0:T(8,128)(2,1)}) custom-call(s32[1]{0:T(128)} %bitcast.25.me_ref, bf16[16,3,32,1472]{3,2,1,0:T(8,128)(2,1)} %bitcast.107, bf16[2,1472,1024]{2,1,0:T(8,128)(2,1)} %bitcast_dynamic-update-slice_fusion.refs_1_.refs_2_, ...), custom_call_target="tpu_custom_call" | custom-call | flops 1 | bytes 1 | tf_op jit(solution)/shard_map/ffn_group/pallas_call | solution.py:574
  300.9 29.7 %ffn_group.5 = (bf16[3,512,2048]{2,1,0:T(8,128)(2,1)}, bf16[8,3,32,1472]{3,2,1,0:T(8,128)(2,1)}, bf16[8,3,32,1472]{3,2,1,0:T(8,128)(2,1)}) custom-call(s32[1]{0:T(128)} %bitcast.25.me_ref, bf16[8,3,32,1472]{3,2,1,0:T(8,128)(2,1)} %copy-done.2, bf16[8,3,32,1472]{3,2,1,0:T(8,128)(2,1)} %collective-permute-done.20.refs_1_.refs_3_, ...), custom_call_target="tpu_custom_call" | custom-call | flops 1 | bytes 1 | tf_op jit(solution)/shard_map/ffn_group/pallas_call | solution.py:574
  332.6 19.2 %ffn_back.2 = (bf16[368,1024]{1,0:T(8,128)(2,1)}, bf16[368,1024]{1,0:T(8,128)(2,1)}, bf16[368,1024]{1,0:T(8,128)(2,1)}, bf16[368,1024]{1,0:T(8,128)(2,1)}) custom-call(bf16[16,3,48,1472]{3,2,1,0:T(8,128)(2,1)} %bitcast.103, bf16[16,3,32,1472]{3,2,1,0:T(8,128)(2,1)} %bitcast.108, bf16[8,3,32,1472]{3,2,1,0:T(8,128)(2,1)} %copy-done.2, ...), custom_call_target="tpu_custom_call" | custom-call | flops 1 | bytes 1 | tf_op jit(solution)/shard_map/ffn_back/pallas_call | solution.py:641
  354.6 11.5 %ffn_back.3 = bf16[1472,1024]{1,0:T(8,128)(2,1)} custom-call(bf16[16,3,48,1472]{3,2,1,0:T(8,128)(2,1)} %bitcast.104, bf16[16,3,32,1472]{3,2,1,0:T(8,128)(2,1)} %bitcast.109, bf16[8,3,32,1472]{3,2,1,0:T(8,128)(2,1)} %copy-done.2, bf16[8,3,32,1472]{3,2,1,0:T(8,128)(2,1)} %collective-permute-done.20.refs_1_.refs_3_, ...), custom_call_target="tpu_custom_call" | custom-call | flops 1 | bytes 1 | tf_op jit(solution)/shard_map/ffn_back/pallas_call | solution.py:641
  367.6 38.5 %mix_back.1 = (f32[1472,1024]{1,0:T(8,128)}, bf16[384,1024]{1,0:T(8,128)(2,1)}, f32[1472,128]{1,0:T(8,128)}, bf16[512,1472]{1,0:T(8,128)(2,1)}) custom-call(bf16[16,3,48,1472]{3,2,1,0:T(8,128)(2,1)} %bitcast.105, bf16[16,3,32,1472]{3,2,1,0:T(8,128)(2,1)} %bitcast.110, bf16[8,3,32,1472]{3,2,1,0:T(8,128)(2,1)} %copy-done.2, ...), custom_call_target="tpu_custom_call" | custom-call | flops 1 | bytes 1 | tf_op jit(solution)/shard_map/mix_back/pallas_call | solution.py:738
  416.3 42.2 %attend_back.1 = (bf16[384,1024]{1,0:T(8,128)(2,1)}, bf16[4,784,256]{2,1,0:T(8,128)(2,1)}, bf16[4,784,256]{2,1,0:T(8,128)(2,1)}, bf16[4,784,256]{2,1,0:T(8,128)(...) custom-call(bf16[384,1024]{1,0:T(8,128)(2,1)} %project.1.q_ref, ...), custom_call_target="tpu_custom_call" | custom-call | flops 1 | bytes 1 | tf_op jit(solution)/shard_map/attend_back/pallas_call | solution.py:326
  464.1 8.0 %projection_grads.2 = (bf16[256,1472]{1,0:T(8,128)(2,1)}, bf16[256,1472]{1,0:T(8,128)(2,1)}) custom-call(bf16[1472,1024]{1,0:T(8,128)(2,1)} %get-tuple-element.604.n_ref, bf16[384,1024]{1,0:T(8,128)(2,1)} %get-tuple-element.624.refs_0_, bf16[384,512]{1,0:T(8,128)(2,1)} %fusion.1.pv_ref.p_ref.refs_16_.refs_1_.refs_2_.refs_5_.refs_7_), custom_call_target="tpu_custom_call" | custom-call | flops 1 | bytes 1 | tf_op jit(solution)/shard_map/projection_grads/pallas_call | solution.py:812
  475.2 8.0 %bucket_sums.1 = f32[96,256]{1,0:T(8,128)} custom-call(s32[4,256,256]{2,1,0:T(8,128)} %get-tuple-element.583.buckets_ref, f32[6,4,256,256]{3,2,1,0:T(8,128)} %get-tuple-element.584.g_ref), custom_call_target="tpu_custom_call" | custom-call | flops 1 | bytes 1 | tf_op jit(solution)/shard_map/bucket_sums/pallas_call | solution.py:405
  493.7 13.1 %layer_out_of.1 = bf16[4,1472,256]{2,1,0:T(8,128)(2,1)} custom-call(bf16[16,3,48,1472]{3,2,1,0:T(8,128)(2,1)} %bitcast.106, bf16[16,3,32,1472]{3,2,1,0:T(8,128)(2,1)} %bitcast.111, bf16[8,3,32,1472]{3,2,1,0:T(8,128)(2,1)} %copy-done.2, bf16[8,3,32,1472]{3,2,1,0:T(8,128)(2,1)} %collective-permute-done.20.refs_1_.refs_3_, ...), custom_call_target="tpu_custom_call" | custom-call | flops 1 | bytes 1 | tf_op jit(solution)/shard_map/layer_out_of/pallas_call | solution.py:665
  515.4 12.3 %projection_grads.3 = (bf16[256,1472]{1,0:T(8,128)(2,1)}, bf16[256,1472]{1,0:T(8,128)(2,1)}, bf16[256,1472]{1,0:T(8,128)(2,1)}, bf16[256,1472]{1,0:T(8,128)(2,1)}) custom-call(bf16[1472,1024]{1,0:T(8,128)(2,1)} %get-tuple-element.604.n_ref, bf16[4,784,256]{2,1,0:T(8,128)(2,1)} %add.272.refs_0_.refs_1_, ...), custom_call_target="tpu_custom_call" | custom-call | flops 1 | bytes 1 | tf_op jit(solution)/shard_map/projection_grads/pallas_call | solution.py:812
  527.7 17.2 %collective-permute-done.45 = bf16[2,3,64,1472]{3,2,1,0:T(8,128)(2,1)} collective-permute-done((bf16[2,3,64,1472]{3,2,1,0:T(8,128)(2,1)}, bf16[2,3,64,1472]{3,2,1,0:T(8,128)(2,1)}, u32[]{:S(2)}, u32[]{:S(2)}) %collective-permute-start.45) | collective-permute-done | bytes 1130528 | tf_op jit(solution)/shard_map/ppermute | solution.py:910
  558.5 19.2 %last.1 = (f32[4,1472,256]{2,1,0:T(8,128)}, f32[1472,128]{1,0:T(8,128)}) custom-call(bf16[4,1472,256]{2,1,0:T(8,128)(2,1)} %bitcast.114, f32[1472,1024]{1,0:T(8,128)} %get-tuple-element.623.dm_ref, bf16[384,1024]{1,0:T(8,128)(2,1)} %get-tuple-element.624.refs_0_, bf16[4,784,256]{2,1,0:T(8,128)(2,1)} %add.272.refs_0_.refs_1_, ...), custom_call_target="tpu_custom_call" | custom-call | flops 1 | bytes 1 | tf_op jit(solution)/shard_map/last/pallas_call | solution.py:873
  (331 shorter events, 166.5 us)
Async XLA Ops:
  7.3 198.1 %all-gather.5.cloned.1.call-start = ((), (), s32[]{:S(2)}) async-start(), calls=%async_computation.2 | async-start | bytes 7520256 | tf_op jit(solution)/shard_map/all_gather | solution.py:1044
  9.1 20.7 %collective-permute-start.2 = (bf16[1,1,64,1472]{3,2,1,0:T(8,128)(2,1)S(1)}, bf16[1,1,64,1472]{3,2,1,0:T(8,128)(2,1)S(1)}, u32[]{:S(2)}, u32[]{:S(2)}) collective-permute-start(bf16[1,1,64,1472]{3,2,1,0:T(8,128)(2,1)S(1)} %maximum_bitcast_fusion), channel_id=1, source_target_pairs={{0,24},{4,28},{8,16},{12,20},{16,8},{20,12},{24,0},{28,4},{1,25},{... | collective-permute-start | bytes 565256 | tf_op jit(solution)/shard_map/ppermute | solution.py:910
  31.1 240.2 %all-gather.7.cloned.1.call-start = ((), (), s32[]{:S(2)}) async-start(), calls=%async_computation.3 | async-start | bytes 5013504 | tf_op jit(solution)/shard_map/all_gather | solution.py:1044
  43.8 19.6 %collective-permute-start.11 = (bf16[8,1,32,1472]{3,2,1,0:T(8,128)(2,1)S(1)}, bf16[8,1,32,1472]{3,2,1,0:T(8,128)(2,1)S(1)}, u32[]{:S(2)}, u32[]{:S(2)}) collective-permute-start(bf16[8,1,32,1472]{3,2,1,0:T(8,128)(2,1)S(1)} %constant_dynamic-update-slice_fusion), channel_id=1, source_target_pairs={{0,2},{2,0},{1,3},{3,1},{4,6},{6,4},{5,7},{7,5},{8,10},{10,8},{9,1... | collective-permute-start | bytes 2261000 | tf_op jit(solution)/shard_map/ppermute | solution.py:910
  66.0 398.1 %reduce-scatter.2.cloned.1.call-start = ((), (), s32[]{:S(2)}) async-start(), calls=%async_computation.1 | async-start | bytes 7520256 | tf_op jit(solution)/shard_map/reduce_scatter | solution.py:1140
  90.3 62.9 %collective-permute-start.17 = (bf16[4,784,256]{2,1,0:T(8,128)(2,1)}, bf16[4,784,256]{2,1,0:T(8,128)(2,1)S(1)}, u32[]{:S(2)}, u32[]{:S(2)}) collective-permute-start(bf16[4,784,256]{2,1,0:T(8,128)(2,1)} %key_value.1.refs_0_), channel_id=1, source_target_pairs={{0,2},{2,0},{1,3},{3,1},{4,6},{6,4},{5,7},{7,5},{8,10},{10,8},{9,1... | collective-permute-start | bytes 4816904 | tf_op jit(solution)/shard_map/ppermute | solution.py:910
  91.9 54.2 %collective-permute-start.10 = (bf16[2,3,32,1472]{3,2,1,0:T(8,128)(2,1)S(1)}, bf16[2,3,32,1472]{3,2,1,0:T(8,128)(2,1)S(1)}, u32[]{:S(2)}, u32[]{:S(2)}) collective-permute-start(bf16[2,3,32,1472]{3,2,1,0:T(8,128)(2,1)S(1)} %constant_dynamic-update-slice_fusion.4), channel_id=1, source_target_pairs={{0,16},{4,20},{8,24},{12,28},{16,0},{20,4},{24,8},{28,12},{1,17},{... | collective-permute-start | bytes 1695752 | tf_op jit(solution)/shard_map/ppermute | solution.py:910
  146.2 31.3 %collective-permute-start.16 = (bf16[4,3,32,1472]{3,2,1,0:T(8,128)(2,1)S(1)}, bf16[4,3,32,1472]{3,2,1,0:T(8,128)(2,1)S(1)}, u32[]{:S(2)}, u32[]{:S(2)}) collective-permute-start(bf16[4,3,32,1472]{3,2,1,0:T(8,128)(2,1)S(1)} %constant_dynamic-update-slice_fusion.14), channel_id=1, source_target_pairs={{0,4},{4,0},{8,12},{12,8},{16,20},{20,16},{24,28},{28,24},{1,5},{5... | collective-permute-start | bytes 3391496 | tf_op jit(solution)/shard_map/ppermute | solution.py:910
  179.9 78.7 %collective-permute-start.20 = (bf16[8,3,32,1472]{3,2,1,0:T(8,128)(2,1)S(1)}, bf16[8,3,32,1472]{3,2,1,0:T(8,128)(2,1)}, u32[]{:S(2)}, u32[]{:S(2)}) collective-permute-start(bf16[8,3,32,1472]{3,2,1,0:T(8,128)(2,1)S(1)} %constant_dynamic-update-slice_fusion.16.refs_0_.refs_2_), channel_id=1, source_target_pairs={{0,2},{2,0},{1,3},{3,1},{4,6},{6,4},{5,7},{7,5},{8,10},{10,8},{9,1... | collective-permute-start | bytes 6782984 | tf_op jit(solution)/shard_map/ppermute | solution.py:910
  330.5 75.6 %collective-permute-start.27 = (bf16[8,3,32,1472]{3,2,1,0:T(8,128)(2,1)}, bf16[8,3,32,1472]{3,2,1,0:T(8,128)(2,1)}, u32[]{:S(2)}, u32[]{:S(2)}) collective-permute-start(bf16[8,3,32,1472]{3,2,1,0:T(8,128)(2,1)} %get-tuple-element.502), channel_id=1, source_target_pairs={{0,2},{2,0},{1,3},{3,1},{4,6},{6,4},{5,7},{7,5},{8,10},{10,8},{9,1... | collective-permute-start | bytes 6782984 | tf_op jit(solution)/shard_map/ppermute | solution.py:910
  331.1 75.0 %collective-permute-start.26 = (bf16[8,3,32,1472]{3,2,1,0:T(8,128)(2,1)}, bf16[8,3,32,1472]{3,2,1,0:T(8,128)(2,1)}, u32[]{:S(2)}, u32[]{:S(2)}) collective-permute-start(bf16[8,3,32,1472]{3,2,1,0:T(8,128)(2,1)} %get-tuple-element.494), channel_id=1, source_target_pairs={{0,4},{4,0},{8,12},{12,8},{16,20},{20,16},{24,28},{28,24},{1,5},{5... | collective-permute-start | bytes 6782984 | tf_op jit(solution)/shard_map/ppermute | solution.py:910
  366.0 50.2 %collective-permute-start.25 = (bf16[1472,1024]{1,0:T(8,128)(2,1)}, bf16[1472,1024]{1,0:T(8,128)(2,1)S(1)}, u32[]{:S(2)}, u32[]{:S(2)}) collective-permute-start(bf16[1472,1024]{1,0:T(8,128)(2,1)} %ffn_back.3), channel_id=1, source_target_pairs={{0,1},{1,0},{2,3},{3,2},{4,5},{5,4},{6,7},{7,6},{8,9},{9,8},{10,11... | collective-permute-start | bytes 9043976 | tf_op jit(solution)/shard_map/ppermute | solution.py:910
  409.9 49.2 %collective-permute-start.32 = (bf16[4,3,32,1472]{3,2,1,0:T(8,128)(2,1)}, bf16[4,3,32,1472]{3,2,1,0:T(8,128)(2,1)}, u32[]{:S(2)}, u32[]{:S(2)}) collective-permute-start(bf16[4,3,32,1472]{3,2,1,0:T(8,128)(2,1)} %get-tuple-element.691), channel_id=1, source_target_pairs={{0,2},{2,0},{1,3},{3,1},{4,6},{6,4},{5,7},{7,5},{8,10},{10,8},{9,1... | collective-permute-start | bytes 3391496 | tf_op jit(solution)/shard_map/ppermute | solution.py:910
  414.0 45.1 %collective-permute-start.33 = (bf16[4,3,32,1472]{3,2,1,0:T(8,128)(2,1)}, bf16[4,3,32,1472]{3,2,1,0:T(8,128)(2,1)}, u32[]{:S(2)}, u32[]{:S(2)}) collective-permute-start(bf16[4,3,32,1472]{3,2,1,0:T(8,128)(2,1)} %get-tuple-element.689), channel_id=1, source_target_pairs={{0,4},{4,0},{8,12},{12,8},{16,20},{20,16},{24,28},{28,24},{1,5},{5... | collective-permute-start | bytes 3391496 | tf_op jit(solution)/shard_map/ppermute | solution.py:910
  416.2 69.5 %collective-permute-start.34 = (bf16[16,16,1472]{2,1,0:T(8,128)(2,1)}, bf16[16,16,1472]{2,1,0:T(8,128)(2,1)}, u32[]{:S(2)}, u32[]{:S(2)}) collective-permute-start(bf16[16,16,1472]{2,1,0:T(8,128)(2,1)} %bitcast.33), channel_id=1, source_target_pairs={{0,1},{1,0},{2,3},{3,2},{4,5},{5,4},{6,7},{7,6},{8,9},{9,8},{10,11... | collective-permute-start | bytes 2261000 | tf_op jit(solution)/shard_map/ppermute | solution.py:910
  474.1 38.3 %collective-permute-start.38 = (bf16[4,784,256]{2,1,0:T(8,128)(2,1)}, bf16[4,784,256]{2,1,0:T(8,128)(2,1)}, u32[]{:S(2)}, u32[]{:S(2)}) collective-permute-start(bf16[4,784,256]{2,1,0:T(8,128)(2,1)} %add.263), channel_id=1, source_target_pairs={{0,2},{2,0},{1,3},{3,1},{4,6},{6,4},{5,7},{7,5},{8,10},{10,8},{9,1... | collective-permute-start | bytes 4816904 | tf_op jit(solution)/shard_map/ppermute | solution.py:910
  491.3 53.6 %collective-permute-start.45 = (bf16[2,3,64,1472]{3,2,1,0:T(8,128)(2,1)}, bf16[2,3,64,1472]{3,2,1,0:T(8,128)(2,1)}, u32[]{:S(2)}, u32[]{:S(2)}) collective-permute-start(bf16[2,3,64,1472]{3,2,1,0:T(8,128)(2,1)} %pad_maximum_fusion.2), channel_id=1, source_target_pairs={{0,16},{4,20},{8,24},{12,28},{16,0},{20,4},{24,8},{28,12},{1,17},{... | collective-permute-start | bytes 3391496 | tf_op jit(solution)/shard_map/ppermute | solution.py:910
  507.9 38.5 %collective-permute-start.43 = (bf16[4,16,1472]{2,1,0:T(8,128)(2,1)S(1)}, bf16[4,16,1472]{2,1,0:T(8,128)(2,1)S(1)}, u32[]{:S(2)}, u32[]{:S(2)}) collective-permute-start(bf16[4,16,1472]{2,1,0:T(8,128)(2,1)S(1)} %get-tuple-element.723), channel_id=1, source_target_pairs={{0,2},{2,0},{1,3},{3,1},{4,6},{6,4},{5,7},{7,5},{8,10},{10,8},{9,1... | collective-permute-start | bytes 565256 | tf_op jit(solution)/shard_map/ppermute | solution.py:910
  510.3 36.1 %collective-permute-start.44 = (bf16[4,16,1472]{2,1,0:T(8,128)(2,1)S(1)}, bf16[4,16,1472]{2,1,0:T(8,128)(2,1)S(1)}, u32[]{:S(2)}, u32[]{:S(2)}) collective-permute-start(bf16[4,16,1472]{2,1,0:T(8,128)(2,1)S(1)} %get-tuple-element.721), channel_id=1, source_target_pairs={{0,2},{2,0},{1,3},{3,1},{4,6},{6,4},{5,7},{7,5},{8,10},{10,8},{9,1... | collective-permute-start | bytes 565256 | tf_op jit(solution)/shard_map/ppermute | solution.py:910
  550.0 29.2 %collective-permute-start.48 = (bf16[8,16,1472]{2,1,0:T(8,128)(2,1)S(1)}, bf16[8,16,1472]{2,1,0:T(8,128)(2,1)}, u32[]{:S(2)}, u32[]{:S(2)}) collective-permute-start(bf16[8,16,1472]{2,1,0:T(8,128)(2,1)S(1)} %get-tuple-element.703), channel_id=1, source_target_pairs={{0,2},{2,0},{1,3},{3,1},{4,6},{6,4},{5,7},{7,5},{8,10},{10,8},{9,1... | collective-permute-start | bytes 1130504 | tf_op jit(solution)/shard_map/ppermute | solution.py:910
  552.3 26.9 %collective-permute-start.49 = (bf16[8,16,1472]{2,1,0:T(8,128)(2,1)}, bf16[8,16,1472]{2,1,0:T(8,128)(2,1)}, u32[]{:S(2)}, u32[]{:S(2)}) collective-permute-start(bf16[8,16,1472]{2,1,0:T(8,128)(2,1)} %get-tuple-element.701), channel_id=1, source_target_pairs={{0,4},{4,0},{8,12},{12,8},{16,20},{20,16},{24,28},{28,24},{1,5},{5... | collective-permute-start | bytes 1130504 | tf_op jit(solution)/shard_map/ppermute | solution.py:910
  553.8 30.7 %collective-permute-start.47 = (bf16[2,32,1472]{2,1,0:T(8,128)(2,1)}, bf16[2,32,1472]{2,1,0:T(8,128)(2,1)}, u32[]{:S(2)}, u32[]{:S(2)}) collective-permute-start(bf16[2,32,1472]{2,1,0:T(8,128)(2,1)} %pad_maximum_fusion.12), channel_id=1, source_target_pairs={{0,16},{4,20},{8,24},{12,28},{16,0},{20,4},{24,8},{28,12},{1,17},{... | collective-permute-start | bytes 565256 | tf_op jit(solution)/shard_map/ppermute | solution.py:910
  553.8 29.3 %collective-permute-start.60 = (bf16[1,3,64,1472]{3,2,1,0:T(8,128)(2,1)S(1)}, bf16[1,3,64,1472]{3,2,1,0:T(8,128)(2,1)}, u32[]{:S(2)}, u32[]{:S(2)}) collective-permute-start(bf16[1,3,64,1472]{3,2,1,0:T(8,128)(2,1)S(1)} %get-tuple-element.693), channel_id=1, source_target_pairs={{0,8},{4,12},{8,0},{12,4},{16,24},{20,28},{24,16},{28,20},{1,9},{5... | collective-permute-start | bytes 1695752 | tf_op jit(solution)/shard_map/ppermute | solution.py:910
  585.4 23.2 %collective-permute-start.59 = (bf16[1,32,1472]{2,1,0:T(8,128)(2,1)S(1)}, bf16[1,32,1472]{2,1,0:T(8,128)(2,1)S(1)}, u32[]{:S(2)}, u32[]{:S(2)}) collective-permute-start(bf16[1,32,1472]{2,1,0:T(8,128)(2,1)S(1)} %get-tuple-element.736), channel_id=1, source_target_pairs={{0,8},{4,12},{8,0},{12,4},{16,24},{20,28},{24,16},{28,20},{1,9},{5... | collective-permute-start | bytes 282632 | tf_op jit(solution)/shard_map/ppermute | solution.py:910
  (77 other events, 747.5 us)
Sparse Core Ops, SparseCore 0:
  31.2 132.1 all-gather.4
  166.2 105.0 all-gather.6
  276.6 165.9 reduce-scatter.1

commit v6 on v5

--- a/solution.py
+++ b/solution.py
@@ -87,7 +87,7 @@
     return [a + b for a, b in pairs]
 
 
-PIECES = 4
+PIECES = 2
 
 
 def pieces_of(shape, tile, pieces=PIECES):
@@ -133,12 +133,15 @@
     )(x, dy, gain)
 
 
-def picked(w, index):
-    entries, _, _, width = w.shape
-    each = w.shape[2] // 2
-    return pl.BlockSpec(
-        (entries, 1, each, width), lambda t: (0, 0, index, 0), pipeline_mode=pl.Buffered(1)
-    )
+def picked(pair, index):
+    return [
+        pl.BlockSpec(
+            (w.shape[0], 1, w.shape[2] // 2, w.shape[3]),
+            lambda t: (0, 0, index, 0),
+            pipeline_mode=pl.Buffered(1),
+        )
+        for w in pair
+    ]
 
 
 def flat_rows(w_ref):
@@ -146,11 +149,19 @@
     return w_ref[...].reshape(entries * each, width)
 
 
-def key_value_body(inner, n_ref, wk_ref, wv_ref, pk_ref, pv_ref, aug_ref, out_ref):
+def forth(refs, x):
+    return jnp.concatenate([dot(flat_rows(w), x, 1, 0).astype(BF16) for w in refs], axis=0)
+
+
+def back(refs, x):
+    part = x.shape[0] // 2
+    return dot(flat_rows(refs[0]), x[:part], 0, 0) + dot(flat_rows(refs[1]), x[part:], 0, 0)
+
+
+def key_value_body(inner, n_ref, wk0, wk1, wv0, wv1, pk_ref, pv_ref, aug_ref, out_ref):
     n = n_ref[...]
-    for start, w_ref, p_ref in ((0, wk_ref, pk_ref), (inner, wv_ref, pv_ref)):
-        mixed_up = dot(flat_rows(w_ref), n, 1, 0).astype(BF16)
-        out_ref[0, start : start + inner] = dot(p_ref[...], mixed_up, 1, 0).astype(BF16)
+    for start, refs, p_ref in ((0, (wk0, wk1), pk_ref), (inner, (wv0, wv1), pv_ref)):
+        out_ref[0, start : start + inner] = dot(p_ref[...], forth(refs, n), 1, 0).astype(BF16)
     out_ref[0, 2 * inner :] = aug_ref[0]
 
 
@@ -161,10 +172,10 @@
     return pl.pallas_call(
         functools.partial(key_value_body, inner),
         grid=(rows,),
-        in_specs=[
-            pl.BlockSpec((width, size), lambda r: (0, first + r)),
-            picked(wk, 0),
-            picked(wv, 0),
+        in_specs=[pl.BlockSpec((width, size), lambda r: (0, first + r))]
+        + picked(wk, 0)
+        + picked(wv, 0)
+        + [
             whole(place_k.shape),
             whole(place_v.shape),
             pl.BlockSpec((1, AUG, size), lambda r: (first + r, 0, 0)),
@@ -173,13 +184,12 @@
         out_shape=jax.ShapeDtypeStruct((rows, 2 * inner + AUG, size), BF16),
         compiler_params=PARAMS,
         name="key_value",
-        cost_estimate=cost(4 * wk.size * rows * size, 4 * wk.size + 2 * n.size),
-    )(n, wk, wv, place_k, place_v, aug)
-
-
-def project_body(n_ref, w_ref, p_ref, out_ref):
-    mixed_up = dot(flat_rows(w_ref), n_ref[...], 1, 0).astype(BF16)
-    out_ref[...] = dot(p_ref[...], mixed_up, 1, 0).astype(BF16)
+        cost_estimate=cost(1, 1),
+    )(n, *wk, *wv, place_k, place_v, aug)
+
+
+def project_body(n_ref, w0, w1, p_ref, out_ref):
+    out_ref[...] = dot(p_ref[...], forth((w0, w1), n_ref[...]), 1, 0).astype(BF16)
 
 
 def project(n, w, place, tile):
@@ -188,13 +198,13 @@
     return pl.pallas_call(
         project_body,
         grid=(here // tile,),
-        in_specs=[pl.BlockSpec((width, tile), lambda t: (0, t)), picked(w, 1), whole(place.shape)],
+        in_specs=[pl.BlockSpec((width, tile), lambda t: (0, t))] + picked(w, 1) + [whole(place.shape)],
         out_specs=pl.BlockSpec((inner, tile), lambda t: (0, t)),
         out_shape=jax.ShapeDtypeStruct((inner, here), BF16),
         compiler_params=PARAMS,
         name="project",
         cost_estimate=cost(1, 1),
-    )(n, w, place)
+    )(n, *w, place)
 
 
 def attend_body(heads, inner, q_ref, u_ref, *refs):
@@ -419,9 +429,9 @@
     return jnp.sum(jnp.where(jnp.eye(8, dtype=bool)[None, None, :, None, :], raw, 0.0), (0, 2, 4)).T
 
 
-def mix_body(x_ref, o_ref, w_ref, place_ref, gain_ref, mixed_ref, pair_ref, *piece_refs):
+def mix_body(x_ref, o_ref, w0, w1, place_ref, gain_ref, mixed_ref, pair_ref, *piece_refs):
     spread = dot(place_ref[...], o_ref[...], 0, 0).astype(BF16)
-    mixed = x_ref[0].astype(F32) + dot(flat_rows(w_ref), spread, 0, 0)
+    mixed = x_ref[0].astype(F32) + back((w0, w1), spread)
     mixed_ref[...] = mixed
     scale = lax.rsqrt(jnp.mean(mixed * mixed, axis=0, keepdims=True) + NORM_EPSILON)
     n = (mixed * scale * gain_ref[...]).astype(BF16)
@@ -451,10 +461,9 @@
         in_specs=[
             pl.BlockSpec((1, width, size), lambda r: (r, 0, 0)),
             pl.BlockSpec((inner, size), lambda r: (0, r)),
-            picked(w, 1),
-            whole(place.shape),
-            whole(gain.shape),
-        ],
+        ]
+        + picked(w, 1)
+        + [whole(place.shape), whole(gain.shape)],
         out_specs=[
             pl.BlockSpec((width, size), lambda r: (0, r)),
             pl.BlockSpec((1, width, size), lambda r: (0, 0, r)),
@@ -468,7 +477,7 @@
         compiler_params=PARAMS,
         name="mix",
         cost_estimate=cost(1, 1),
-    )(x, ot, w, place, gain)
+    )(x, ot, *w, place, gain)
 
 
 def units_of(ws):
@@ -679,8 +688,8 @@
     ins = sum(layout) + len(layout)
     weights, refs = refs[:ins], refs[ins:]
     pieces, refs = refs[:PIECES], refs[PIECES:]
-    mixed_ref, dy_ref, o_ref, w_ref, place_ref, home_ref, gain_ref = refs[:7]
-    refs = refs[7:]
+    mixed_ref, dy_ref, o_ref, w0, w1, place_ref, home_ref, gain_ref = refs[:8]
+    refs = refs[8:]
     inside_grad = len(refs) == 5 + len(layout) + 1
     dmixed_ref, do_ref, gg_ref = refs[:3]
     gw_ref, acc = refs[3:5] if inside_grad else (None, None)
@@ -696,8 +705,7 @@
     dmixed_ref[...] = dmixed
     low = dmixed.astype(BF16)
     spread = dot(home_ref[...], o_ref[...], 0, 0).astype(BF16)
-    mixed_up = dot(flat_rows(w_ref), low, 1, 0).astype(BF16)
-    do_ref[...] = dot(place_ref[...], mixed_up, 1, 0).astype(BF16)
+    do_ref[...] = dot(place_ref[...], forth((w0, w1), low), 1, 0).astype(BF16)
     both = dn * unit
     gain_part = both[:, :128]
     for j in range(1, both.shape[1] // 128):
@@ -741,7 +749,8 @@
         in_specs=ffn_specs(groups, acts, [0, 1], size, 0)
         + pieces_of(mixed.shape, size)[0]
         + [col, pl.BlockSpec((1, width, size), lambda r: (r, 0, 0)), head_col]
-        + [picked(w, 1), whole(place.shape), whole(home.shape), whole(gain.shape)],
+        + picked(w, 1)
+        + [whole(place.shape), whole(home.shape), whole(gain.shape)],
         out_specs=[col, head_col, whole((width, 128))] + [whole(grad)] * fits,
         out_shape=[
             jax.ShapeDtypeStruct((width, here), F32),
@@ -753,7 +762,7 @@
         compiler_params=PARAMS,
         name="mix_back",
         cost_estimate=cost(1, 1),
-    )(*flat_of(groups), *acts, *d1, mixed, dy, ot, w, place, home, gain)
+    )(*flat_of(groups), *acts, *d1, mixed, dy, ot, *w, place, home, gain)
     if not fits:
         spread = dot(home, ot, 0, 0).astype(BF16)
         out = [*out, dot(spread, out[0].astype(BF16), 1, 1).astype(BF16)]
@@ -828,7 +837,7 @@
 
 def last_body(per, groups, x_ref, dm_ref, *refs):
     dq_refs, dkv_refs, refs = refs[:groups], refs[groups : 2 * groups], refs[2 * groups :]
-    ws, places, refs = refs[:3], refs[3:6], refs[6:]
+    ws, places, refs = (refs[:2], refs[2:4], refs[4:6]), refs[6:9], refs[9:]
     gain_ref, gx_ref, gg_ref, d_scr = refs
     row = pl.program_id(0)
     inner = dq_refs[0].shape[0]
@@ -842,7 +851,7 @@
     dn = None
     for j in range(3):
         spread = dot(places[j][...], d_scr[j * inner : (j + 1) * inner], 0, 0).astype(BF16)
-        term = dot(flat_rows(ws[j]), spread, 0, 0)
+        term = back(ws[j], spread)
         dn = term if dn is None else dn + term
     x = x_ref[0].astype(F32)
     scale = lax.rsqrt(jnp.mean(x * x, axis=0, keepdims=True) + NORM_EPSILON)
@@ -876,7 +885,7 @@
         in_specs=[block, col]
         + group_specs((inner, size), len(dqs), per, 2)
         + group_specs((1,) + dkvs[0].shape[1:], len(dkvs), per, 3)
-        + [picked(w, index) for w, index in zip(ws, (1, 0, 0))]
+        + [spec for w, index in zip(ws, (1, 0, 0)) for spec in picked(w, index)]
         + [whole(p.shape) for p in places]
         + [whole(gain.shape)],
         out_specs=[block, whole((width, 128))],
@@ -884,8 +893,8 @@
         scratch_shapes=[pltpu.VMEM((3 * inner, size), BF16)],
         compiler_params=PARAMS,
         name="last",
-        cost_estimate=cost(6 * ws[0].size * rows * size, 14 * x.size + 6 * ws[0].size),
-    )(x, dmixed, *dqs, *dkvs, *ws, *places, gain)
+        cost_estimate=cost(1, 1),
+    )(x, dmixed, *dqs, *dkvs, *[w for pair in ws for w in pair], *places, gain)
 
 
 def after(value, *markers):
@@ -999,7 +1008,7 @@
             self.held = exchange(run(join, self.held), (core, core))
 
         def core_end(self):
-            return run(join, self.held)
+            return close([list(pair) for pair in self.held])
 
     attn_w = Gather(
         jnp.concatenate([slot(w) for w in (w_key, w_attn_out, w_value, w_query)], axis=1)[:, None],
@@ -1119,10 +1128,13 @@
     acts, sums = [], []
     me_same = (my_dp * (ctx // 2) + lax.axis_index("x")).reshape(1)
     masks = [[m >> 1 for m in links.masks(steps)] for steps in (ab, ba)]
-    ffn_grads = []
+    ffn_grads = {}
     if by_hops:
         ffn_w.append(None)
-    for i, ws in enumerate(ffn_w):
+    sequence = [0, 2, 1] if by_hops else range(len(ffn_w))
+    by_group = {}
+    for i in sequence:
+        ws = ffn_w[i]
         if i == last_group and by_hops:
             ws = ffn_w[i] = last_ws
         some = tile if units_of(ws) <= 768 else tile // 2
@@ -1130,14 +1142,13 @@
         act, grads = run(
             lambda m, w, n, d: ffn_group(m, w, n, d, some, mask), me_same, ws, n_pair, dy_pair
         )
-        acts.append(act)
+        by_group[i] = act
         if by_hops and i == 0:
             last_ws = close(list(last_w.held[0]))
             grads = [after(g, last_ws) for g in grads]
-        if by_hops and i >= last_group - 1:
-            ffn_grads.append(grads)
-        else:
-            ffn_grads.append(lax.psum_scatter(grads[0], same_core))
+        ffn_grads[i] = grads if by_hops and i else lax.psum_scatter(grads[0], same_core)
+    ffn_grads = [ffn_grads[i] for i in range(len(ffn_w))]
+    acts = [by_group[i] for i in range(len(ffn_w))]
     if by_hops:
         sums = [Sums(ffn_grads[-2:], [ab, ba])]
 
@@ -1176,6 +1187,7 @@
     grad_table = run(lambda g, b: bucket_sums(g, b, count), grad_bias, buckets_t)
     query_sum.go()
     out = run(lambda *a: layer_out_of(*a, rows), ffn_w, acts, mixed, out_got)
+    tick()
     query_sum.go()
     (dkv,) = run(add_pairs, [(own, other)])
     gkv = run(
@@ -1183,7 +1195,6 @@
         normed, dkv, place_a, place_b,
     )
     value_sum = Sums([entries(gkv[:2]), entries(gkv[2:])], [home_a, home_b], direct=dp <= 8)
-    tick()
     query_sum.go()
     value_sum.go()
     gx, gain_one_part = run(

time: 622 us -> 595 us (0.957)
  waiting for transfers between devices: 134 us -> 120 us
  local copies, waits for them, and re-layouts: 41.6 us -> 33.1 us
    ppermute x61 -> x55, waiting for transfers between devices: 122 us -> 106 us  [swap(): lax.ppermute(x, axis, [(i, i ^ mask) for i in range(self.sizes[axis])])]
    reduce_scatter x1, waiting for transfers between devices: 0.01 us -> 13.3 us  [per_device(): lax.psum_scatter(grads[0], same_core)]
    all_gather x2, waiting for transfers between devices: 12.6 us -> 1.37 us  [per_device(): lax.all_gather(after(shard, attn_w.start_of()), same_core)]
    concatenate x8 -> x6, local copies, waits for them, and re-layouts: 6.52 us -> 0.26 us  [join(): return [jnp.concatenate(list(pair), axis=0) for pair in pairs]]
    ppermute x61 -> x55, starting transfers between devices: 51.5 us -> 48.6 us  [swap(): lax.ppermute(x, axis, [(i, i ^ mask) for i in range(self.sizes[axis])])]
  transfers between devices with their start and end apart: 64 -> 58, of which waited for: 26 -> 23; matrix products, arithmetic and copies ran while one was open for 12% -> 11% of each run, Pallas kernels for 54% -> 56%
where the time goes in v6:
time: 595 us; the launch traced here: 591 us
  Pallas kernels  329 us (55%)
  waiting for transfers between devices  120 us (20%)
  starting transfers between devices  48.9 us (8%)
  other arithmetic  45 us (8%)
  local copies, waits for them, and re-layouts  33.1 us (6%)
  between operations  15 us (3%)
    ppermute x55, waiting for transfers between devices, swap(): lax.ppermute(x, axis, [(i, i ^ mask) for i in range(self.sizes[axis])])  106 us
    pallas_call x3, Pallas kernels, ffn_group(): pl.pallas_call(functools.partial(ffn_body, len(ws), masks), grid_spec=spe...  100 us
    ppermute x55, starting transfers between devices, swap(): lax.ppermute(x, axis, [(i, i ^ mask) for i in range(self.sizes[axis])])  48.6 us
    pallas_call x1, Pallas kernels, attend_back(): pl.pallas_call(functools.partial(attend_back_body, heads, inner, count, l...  42.7 us
    pallas_call x1, Pallas kernels, mix_back(): pl.pallas_call(functools.partial(mix_back_body, layout_of(groups)), grid=...  38.4 us
    pallas_call x2, Pallas kernels, ffn_back(): pl.pallas_call(functools.partial(ffn_back_body, layout_of(groups), kinds,...  30.8 us
    pallas_call x2, Pallas kernels, projection_grads(): pl.pallas_call(functools.partial(grads_body, per, len(groups), parts), gr...  20.2 us
    pallas_call x1, Pallas kernels, last(): pl.pallas_call(functools.partial(last_body, per, len(dqs)), grid=(rows,),...  18.9 us
  transfers between devices with their start and end apart: 58, of which 23 were waited for; matrix products, arithmetic and copies ran while one was open for 11% of the time, Pallas kernels for 56%

profile of v6, /device:TPU:0, one launch (start us, length us, event | category | flops | bytes accessed | tf_op | source)
XLA Modules:
  0.0 591.2 jit_solution(12358187438979008196)
XLA Ops:
  9.1 5.1 collective-permute-start.2
  21.9 7.2 %first_norm.1 = (bf16[1472,1024]{1,0:T(8,128)(2,1)}, bf16[2,1472,1024]{2,1,0:T(8,128)(2,1)}, bf16[736,1024]{1,0:T(8,128)(2,1)}, bf16[736,1024]{1,0:T(8,128)(2,1)}) custom-call(bf16[4,1472,256]{2,1,0:T(8,128)(2,1)} %bitcast.104, bf16[4,1472,256]{2,1,0:T(8,128)(2,1)} %bitcast.107, f32[1472,1]{1,0:T(8,128)} %copy.38.gain_ref), custom_call_target="tpu_custom_call" | custom-call | flops 1 | bytes 1 | tf_op jit(solution)/shard_map/first_norm/pallas_call | solution.py:120
  36.2 6.8 %bias_of.1 = (f32[6,4,256,256]{3,2,1,0:T(8,128)}, s32[4,256,256]{2,1,0:T(8,128)}) custom-call(s32[4]{0:T(128)} %broadcast_xor_fusion.slots_ref, s32[256,1024]{1,0:T(8,128)} %buckets_ref, f32[6,128]{1,0:T(8,128)} %pad.41.table_ref), custom_call_target="tpu_custom_call" | custom-call | flops 1 | bytes 1 | tf_op jit(solution)/shard_map/bias_of/pallas_call | solution.py:381
  53.2 6.9 %collective-permute-done.5 = bf16[1,3,32,1472]{3,2,1,0:T(8,128)(2,1)S(1)} collective-permute-done((bf16[1,3,32,1472]{3,2,1,0:T(8,128)(2,1)S(1)}, bf16[1,3,32,1472]{3,2,1,0:T(8,128)(2,1)S(1)}, u32[]{:S(2)}, u32[]{:S(2)}) %collective-permute-start.5) | collective-permute-done | bytes 282656 | tf_op jit(solution)/shard_map/ppermute | solution.py:919
  72.3 9.3 %key_value.1.refs_0_ = bf16[4,784,256]{2,1,0:T(8,128)(2,1)} custom-call(bf16[1472,1024]{1,0:T(8,128)(2,1)} %get-tuple-element.539.n_ref, bf16[16,1,32,1472]{3,2,1,0:T(8,128)(2,1)} %copy-done.3, bf16[16,1,32,1472]{3,2,1,0:T(8,128)(2,1)} %copy-done.5, bf16[16,1,32,1472]{3,2,1,0:T(8,128)(2,1)} %copy-done.4, bf16[16,1,32,1472]{3,2,1,0:T(8,128)(2,1)} %copy-done.6, ...), custom_call_target="tpu_custom_call" | custom-call | flops 1 | bytes 1 | tf_op jit(solution)/shard_map/key_value/pallas_call | solution.py:172
  84.3 5.1 project.1.q_ref
  89.5 35.7 %collective-permute-done.8 = bf16[2,3,32,1472]{3,2,1,0:T(8,128)(2,1)S(1)} collective-permute-done((bf16[2,3,32,1472]{3,2,1,0:T(8,128)(2,1)S(1)}, bf16[2,3,32,1472]{3,2,1,0:T(8,128)(2,1)S(1)}, u32[]{:S(2)}, u32[]{:S(2)}) %collective-permute-start.8) | collective-permute-done | bytes 565280 | tf_op jit(solution)/shard_map/ppermute | solution.py:919
  134.7 18.3 %attend.1 = (bf16[384,1024]{1,0:T(8,128)(2,1)}, f32[4,8,256]{2,1,0:T(8,128)}) custom-call(bf16[384,1024]{1,0:T(8,128)(2,1)} %project.1.q_ref, bf16[4,16,256]{2,1,0:T(8,128)(2,1)} %get-tuple-element.486.u_ref, bf16[4,784,256]{2,1,0:T(8,128)(2,1)} %key_value.1.refs_0_, bf16[4,784,256]{2,1,0:T(8,128)(2,1)} %copy-done.7, bf16[4,784,256]{2,1,0:T(8,128)(2,1)} %copy-done.8, ...), custom_call_target="tpu_custom_call" | custom-call | flops 1 | bytes 1 | tf_op jit(solution)/shard_map/attend/pallas_call | solution.py:241
  153.0 7.9 %collective-permute-done.14 = bf16[4,3,32,1472]{3,2,1,0:T(8,128)(2,1)S(1)} collective-permute-done((bf16[4,3,32,1472]{3,2,1,0:T(8,128)(2,1)S(1)}, bf16[4,3,32,1472]{3,2,1,0:T(8,128)(2,1)S(1)}, u32[]{:S(2)}, u32[]{:S(2)}) %collective-permute-start.14) | collective-permute-done | bytes 1130528 | tf_op jit(solution)/shard_map/ppermute | solution.py:919
  166.1 9.6 %mix.1 = (f32[1472,1024]{1,0:T(8,128)}, bf16[2,1472,1024]{2,1,0:T(8,128)(2,1)}, bf16[736,1024]{1,0:T(8,128)(2,1)}, bf16[736,1024]{1,0:T(8,128)(2,1)}) custom-call(bf16[4,1472,256]{2,1,0:T(8,128)(2,1)} %bitcast.105, bf16[384,1024]{1,0:T(8,128)(2,1)} %get-tuple-element.492.o_ref.refs_11_.refs_5_, bf16[16,1,32,1472]{3,2,1,0:T(8,128)(2,1)} %copy-done.3, ...), custom_call_target="tpu_custom_call" | custom-call | flops 1 | bytes 1 | tf_op jit(solution)/shard_map/mix/pallas_call | solution.py:458
  186.9 41.2 %ffn_group.3 = (bf16[3,768,2048]{2,1,0:T(8,128)(2,1)}, bf16[16,3,48,1472]{3,2,1,0:T(8,128)(2,1)}) custom-call(s32[1]{0:T(128)} %bitcast.23.me_ref, bf16[16,3,48,1472]{3,2,1,0:T(8,128)(2,1)} %bitcast.94, bf16[2,1472,1024]{2,1,0:T(8,128)(2,1)} %bitcast_dynamic-update-slice_fusion.refs_1_.refs_2_, ...), custom_call_target="tpu_custom_call" | custom-call | flops 1 | bytes 1 | tf_op jit(solution)/shard_map/ffn_group/pallas_call | solution.py:583
  228.2 29.1 %ffn_group.4 = (bf16[3,512,2048]{2,1,0:T(8,128)(2,1)}, bf16[8,3,32,1472]{3,2,1,0:T(8,128)(2,1)}, bf16[8,3,32,1472]{3,2,1,0:T(8,128)(2,1)}) custom-call(s32[1]{0:T(128)} %bitcast.23.me_ref, bf16[8,3,32,1472]{3,2,1,0:T(8,128)(2,1)} %copy-done.2, bf16[8,3,32,1472]{3,2,1,0:T(8,128)(2,1)} %collective-permute-done.18.refs_1_.refs_3_, ...), custom_call_target="tpu_custom_call" | custom-call | flops 1 | bytes 1 | tf_op jit(solution)/shard_map/ffn_group/pallas_call | solution.py:583
  258.6 30.0 %ffn_group.5 = (bf16[3,512,2048]{2,1,0:T(8,128)(2,1)}, bf16[8,3,32,1472]{3,2,1,0:T(8,128)(2,1)}, bf16[8,3,32,1472]{3,2,1,0:T(8,128)(2,1)}) custom-call(s32[1]{0:T(128)} %bitcast.23.me_ref, bf16[16,3,32,1472]{3,2,1,0:T(8,128)(2,1)} %bitcast.99, bf16[2,1472,1024]{2,1,0:T(8,128)(2,1)} %bitcast_dynamic-update-slice_fusion.refs_1_.refs_2_, ...), custom_call_target="tpu_custom_call" | custom-call | flops 1 | bytes 1 | tf_op jit(solution)/shard_map/ffn_group/pallas_call | solution.py:583
  290.8 19.3 %ffn_back.2 = (bf16[736,1024]{1,0:T(8,128)(2,1)}, bf16[736,1024]{1,0:T(8,128)(2,1)}) custom-call(bf16[16,3,48,1472]{3,2,1,0:T(8,128)(2,1)} %bitcast.95, bf16[16,3,32,1472]{3,2,1,0:T(8,128)(2,1)} %bitcast.100, bf16[8,3,32,1472]{3,2,1,0:T(8,128)(2,1)} %copy-done.2, bf16[8,3,32,1472]{3,2,1,0:T(8,128)(2,1)} %collective-permute-done.18.refs_1_.refs_3_, ...), custom_call_target="tpu_custom_call" | custom-call | flops 1 | bytes 1 | tf_op jit(solution)/shard_map/ffn_back/pallas_call | solution.py:650
  310.7 11.5 %ffn_back.3 = bf16[1472,1024]{1,0:T(8,128)(2,1)} custom-call(bf16[16,3,48,1472]{3,2,1,0:T(8,128)(2,1)} %bitcast.96, bf16[16,3,32,1472]{3,2,1,0:T(8,128)(2,1)} %bitcast.101, bf16[8,3,32,1472]{3,2,1,0:T(8,128)(2,1)} %copy-done.2, bf16[8,3,32,1472]{3,2,1,0:T(8,128)(2,1)} %collective-permute-done.18.refs_1_.refs_3_, ...), custom_call_target="tpu_custom_call" | custom-call | flops 1 | bytes 1 | tf_op jit(solution)/shard_map/ffn_back/pallas_call | solution.py:650
  323.5 38.4 %mix_back.1 = (f32[1472,1024]{1,0:T(8,128)}, bf16[384,1024]{1,0:T(8,128)(2,1)}, f32[1472,128]{1,0:T(8,128)}, bf16[512,1472]{1,0:T(8,128)(2,1)}) custom-call(bf16[16,3,48,1472]{3,2,1,0:T(8,128)(2,1)} %bitcast.97, bf16[16,3,32,1472]{3,2,1,0:T(8,128)(2,1)} %bitcast.102, bf16[8,3,32,1472]{3,2,1,0:T(8,128)(2,1)} %copy-done.2, ...), custom_call_target="tpu_custom_call" | custom-call | flops 1 | bytes 1 | tf_op jit(solution)/shard_map/mix_back/pallas_call | solution.py:746
  372.0 42.7 %attend_back.1 = (bf16[384,1024]{1,0:T(8,128)(2,1)}, bf16[4,784,256]{2,1,0:T(8,128)(2,1)}, bf16[4,784,256]{2,1,0:T(8,128)(2,1)}, bf16[4,784,256]{2,1,0:T(8,128)(...) custom-call(bf16[384,1024]{1,0:T(8,128)(2,1)} %project.1.q_ref, ...), custom_call_target="tpu_custom_call" | custom-call | flops 1 | bytes 1 | tf_op jit(solution)/shard_map/attend_back/pallas_call | solution.py:336
  420.3 13.3 %reduce-scatter.2.cloned.1.call-done = bf16[1,3,48,1472]{3,2,1,0:T(8,128)(2,1)} async-done(((bf16[16,3,48,1472]{3,2,1,0:T(8,128)(2,1)}), bf16[1,3,48,1472]{3,2,1,0:T(8,128)(2,1)}) %reduce-scatter.2.cloned.1.call-update) | async-done | bytes 423952 | tf_op jit(solution)/shard_map/reduce_scatter | solution.py:1149
  433.6 8.1 %projection_grads.2 = (bf16[256,1472]{1,0:T(8,128)(2,1)}, bf16[256,1472]{1,0:T(8,128)(2,1)}) custom-call(bf16[1472,1024]{1,0:T(8,128)(2,1)} %get-tuple-element.539.n_ref, bf16[384,1024]{1,0:T(8,128)(2,1)} %get-tuple-element.557.refs_0_, bf16[384,512]{1,0:T(8,128)(2,1)} %fusion.1.pv_ref.p_ref.refs_15_.refs_1_.refs_2_.refs_8_.refs_10_), custom_call_target="tpu_custom_call" | custom-call | flops 1 | bytes 1 | tf_op jit(solution)/shard_map/projection_grads/pallas_call | solution.py:821
  446.4 8.0 %bucket_sums.1 = f32[96,256]{1,0:T(8,128)} custom-call(s32[4,256,256]{2,1,0:T(8,128)} %get-tuple-element.516.buckets_ref, f32[6,4,256,256]{3,2,1,0:T(8,128)} %get-tuple-element.517.g_ref), custom_call_target="tpu_custom_call" | custom-call | flops 1 | bytes 1 | tf_op jit(solution)/shard_map/bucket_sums/pallas_call | solution.py:415
  461.8 13.2 %layer_out_of.1 = bf16[4,1472,256]{2,1,0:T(8,128)(2,1)} custom-call(bf16[16,3,48,1472]{3,2,1,0:T(8,128)(2,1)} %bitcast.98, bf16[16,3,32,1472]{3,2,1,0:T(8,128)(2,1)} %bitcast.103, bf16[8,3,32,1472]{3,2,1,0:T(8,128)(2,1)} %copy-done.2, bf16[8,3,32,1472]{3,2,1,0:T(8,128)(2,1)} %collective-permute-done.18.refs_1_.refs_3_, ...), custom_call_target="tpu_custom_call" | custom-call | flops 1 | bytes 1 | tf_op jit(solution)/shard_map/layer_out_of/pallas_call | solution.py:674
  475.0 21.5 %collective-permute-done.35 = bf16[2,3,64,1472]{3,2,1,0:T(8,128)(2,1)} collective-permute-done((bf16[2,3,64,1472]{3,2,1,0:T(8,128)(2,1)}, bf16[2,3,64,1472]{3,2,1,0:T(8,128)(2,1)}, u32[]{:S(2)}, u32[]{:S(2)}) %collective-permute-start.35) | collective-permute-done | bytes 1130528 | tf_op jit(solution)/shard_map/ppermute | solution.py:919
  507.6 12.1 %projection_grads.3 = (bf16[256,1472]{1,0:T(8,128)(2,1)}, bf16[256,1472]{1,0:T(8,128)(2,1)}, bf16[256,1472]{1,0:T(8,128)(2,1)}, bf16[256,1472]{1,0:T(8,128)(2,1)}) custom-call(bf16[1472,1024]{1,0:T(8,128)(2,1)} %get-tuple-element.539.n_ref, bf16[4,784,256]{2,1,0:T(8,128)(2,1)} %add.266.refs_0_.refs_1_, ...), custom_call_target="tpu_custom_call" | custom-call | flops 1 | bytes 1 | tf_op jit(solution)/shard_map/projection_grads/pallas_call | solution.py:821
  532.8 18.9 %last.1 = (f32[4,1472,256]{2,1,0:T(8,128)}, f32[1472,128]{1,0:T(8,128)}) custom-call(bf16[4,1472,256]{2,1,0:T(8,128)(2,1)} %bitcast.106, f32[1472,1024]{1,0:T(8,128)} %get-tuple-element.556.dm_ref, bf16[384,1024]{1,0:T(8,128)(2,1)} %get-tuple-element.557.refs_0_, bf16[4,784,256]{2,1,0:T(8,128)(2,1)} %add.266.refs_0_.refs_1_, ...), custom_call_target="tpu_custom_call" | custom-call | flops 1 | bytes 1 | tf_op jit(solution)/shard_map/last/pallas_call | solution.py:882
  (311 shorter events, 156.8 us)
Async XLA Ops:
  7.3 179.6 %all-gather.5.cloned.1.call-start = ((), (), s32[]{:S(2)}) async-start(), calls=%async_computation.2 | async-start | bytes 7520256 | tf_op jit(solution)/shard_map/all_gather | solution.py:1053
  31.1 227.5 %all-gather.7.cloned.1.call-start = ((), (), s32[]{:S(2)}) async-start(), calls=%async_computation.3 | async-start | bytes 5013504 | tf_op jit(solution)/shard_map/all_gather | solution.py:1053
  36.0 397.6 %reduce-scatter.2.cloned.1.call-start = ((), (), s32[]{:S(2)}) async-start(), calls=%async_computation.1 | async-start | bytes 7520256 | tf_op jit(solution)/shard_map/reduce_scatter | solution.py:1149
  81.8 47.0 %collective-permute-start.15 = (bf16[4,784,256]{2,1,0:T(8,128)(2,1)}, bf16[4,784,256]{2,1,0:T(8,128)(2,1)S(1)}, u32[]{:S(2)}, u32[]{:S(2)}) collective-permute-start(bf16[4,784,256]{2,1,0:T(8,128)(2,1)} %key_value.1.refs_0_), channel_id=1, source_target_pairs={{0,2},{2,0},{1,3},{3,1},{4,6},{6,4},{5,7},{7,5},{8,10},{10,8},{9,1... | collective-permute-start | bytes 4816904 | tf_op jit(solution)/shard_map/ppermute | solution.py:919
  82.2 42.9 %collective-permute-start.8 = (bf16[2,3,32,1472]{3,2,1,0:T(8,128)(2,1)S(1)}, bf16[2,3,32,1472]{3,2,1,0:T(8,128)(2,1)S(1)}, u32[]{:S(2)}, u32[]{:S(2)}) collective-permute-start(bf16[2,3,32,1472]{3,2,1,0:T(8,128)(2,1)S(1)} %constant_dynamic-update-slice_fusion.4), channel_id=1, source_target_pairs={{0,16},{4,20},{8,24},{12,28},{16,0},{20,4},{24,8},{28,12},{1,17},{... | collective-permute-start | bytes 1695752 | tf_op jit(solution)/shard_map/ppermute | solution.py:919
  125.2 35.7 %collective-permute-start.14 = (bf16[4,3,32,1472]{3,2,1,0:T(8,128)(2,1)S(1)}, bf16[4,3,32,1472]{3,2,1,0:T(8,128)(2,1)S(1)}, u32[]{:S(2)}, u32[]{:S(2)}) collective-permute-start(bf16[4,3,32,1472]{3,2,1,0:T(8,128)(2,1)S(1)} %constant_dynamic-update-slice_fusion.10), channel_id=1, source_target_pairs={{0,4},{4,0},{8,12},{12,8},{16,20},{20,16},{24,28},{28,24},{1,5},{5... | collective-permute-start | bytes 3391496 | tf_op jit(solution)/shard_map/ppermute | solution.py:919
  163.3 64.8 %collective-permute-start.18 = (bf16[8,3,32,1472]{3,2,1,0:T(8,128)(2,1)S(1)}, bf16[8,3,32,1472]{3,2,1,0:T(8,128)(2,1)}, u32[]{:S(2)}, u32[]{:S(2)}) collective-permute-start(bf16[8,3,32,1472]{3,2,1,0:T(8,128)(2,1)S(1)} %constant_dynamic-update-slice_fusion.12.refs_0_.refs_2_), channel_id=1, source_target_pairs={{0,2},{2,0},{1,3},{3,1},{4,6},{6,4},{5,7},{7,5},{8,10},{10,8},{9,1... | collective-permute-start | bytes 6782984 | tf_op jit(solution)/shard_map/ppermute | solution.py:919
  288.7 73.2 %collective-permute-start.22 = (bf16[8,3,32,1472]{3,2,1,0:T(8,128)(2,1)}, bf16[8,3,32,1472]{3,2,1,0:T(8,128)(2,1)}, u32[]{:S(2)}, u32[]{:S(2)}) collective-permute-start(bf16[8,3,32,1472]{3,2,1,0:T(8,128)(2,1)} %get-tuple-element.440), channel_id=1, source_target_pairs={{0,4},{4,0},{8,12},{12,8},{16,20},{20,16},{24,28},{28,24},{1,5},{5... | collective-permute-start | bytes 6782984 | tf_op jit(solution)/shard_map/ppermute | solution.py:919
  290.2 71.6 %collective-permute-start.23 = (bf16[8,3,32,1472]{3,2,1,0:T(8,128)(2,1)}, bf16[8,3,32,1472]{3,2,1,0:T(8,128)(2,1)}, u32[]{:S(2)}, u32[]{:S(2)}) collective-permute-start(bf16[8,3,32,1472]{3,2,1,0:T(8,128)(2,1)} %get-tuple-element.433), channel_id=1, source_target_pairs={{0,2},{2,0},{1,3},{3,1},{4,6},{6,4},{5,7},{7,5},{8,10},{10,8},{9,1... | collective-permute-start | bytes 6782984 | tf_op jit(solution)/shard_map/ppermute | solution.py:919
  322.2 49.8 %collective-permute-start.21 = (bf16[1472,1024]{1,0:T(8,128)(2,1)}, bf16[1472,1024]{1,0:T(8,128)(2,1)S(1)}, u32[]{:S(2)}, u32[]{:S(2)}) collective-permute-start(bf16[1472,1024]{1,0:T(8,128)(2,1)} %ffn_back.3), channel_id=1, source_target_pairs={{0,1},{1,0},{2,3},{3,2},{4,5},{5,4},{6,7},{7,6},{8,9},{9,8},{10,11... | collective-permute-start | bytes 9043976 | tf_op jit(solution)/shard_map/ppermute | solution.py:919
  365.7 49.6 %collective-permute-start.26 = (bf16[4,3,32,1472]{3,2,1,0:T(8,128)(2,1)}, bf16[4,3,32,1472]{3,2,1,0:T(8,128)(2,1)}, u32[]{:S(2)}, u32[]{:S(2)}) collective-permute-start(bf16[4,3,32,1472]{3,2,1,0:T(8,128)(2,1)} %get-tuple-element.627), channel_id=1, source_target_pairs={{0,2},{2,0},{1,3},{3,1},{4,6},{6,4},{5,7},{7,5},{8,10},{10,8},{9,1... | collective-permute-start | bytes 3391496 | tf_op jit(solution)/shard_map/ppermute | solution.py:919
  369.9 45.3 %collective-permute-start.27 = (bf16[4,3,32,1472]{3,2,1,0:T(8,128)(2,1)}, bf16[4,3,32,1472]{3,2,1,0:T(8,128)(2,1)}, u32[]{:S(2)}, u32[]{:S(2)}) collective-permute-start(bf16[4,3,32,1472]{3,2,1,0:T(8,128)(2,1)} %get-tuple-element.625), channel_id=1, source_target_pairs={{0,4},{4,0},{8,12},{12,8},{16,20},{20,16},{24,28},{28,24},{1,5},{5... | collective-permute-start | bytes 3391496 | tf_op jit(solution)/shard_map/ppermute | solution.py:919
  371.8 85.2 %collective-permute-start.28 = (bf16[16,16,1472]{2,1,0:T(8,128)(2,1)}, bf16[16,16,1472]{2,1,0:T(8,128)(2,1)}, u32[]{:S(2)}, u32[]{:S(2)}) collective-permute-start(bf16[16,16,1472]{2,1,0:T(8,128)(2,1)} %bitcast.29), channel_id=1, source_target_pairs={{0,1},{1,0},{2,3},{3,2},{4,5},{5,4},{6,7},{7,6},{8,9},{9,8},{10,11... | collective-permute-start | bytes 2261000 | tf_op jit(solution)/shard_map/ppermute | solution.py:919
  414.7 28.2 %collective-permute-start.30 = (bf16[4,784,256]{2,1,0:T(8,128)(2,1)}, bf16[4,784,256]{2,1,0:T(8,128)(2,1)S(1)}, u32[]{:S(2)}, u32[]{:S(2)}) collective-permute-start(bf16[4,784,256]{2,1,0:T(8,128)(2,1)} %get-tuple-element.499), channel_id=1, source_target_pairs={{0,1},{1,0},{2,3},{3,2},{4,5},{5,4},{6,7},{7,6},{8,9},{9,8},{10,11... | collective-permute-start | bytes 4816904 | tf_op jit(solution)/shard_map/ppermute | solution.py:919
  415.1 27.8 %collective-permute-start.31 = (bf16[4,784,256]{2,1,0:T(8,128)(2,1)}, bf16[4,784,256]{2,1,0:T(8,128)(2,1)S(1)}, u32[]{:S(2)}, u32[]{:S(2)}) collective-permute-start(bf16[4,784,256]{2,1,0:T(8,128)(2,1)} %get-tuple-element.500), channel_id=1, source_target_pairs={{0,1},{1,0},{2,3},{3,2},{4,5},{5,4},{6,7},{7,6},{8,9},{9,8},{10,11... | collective-permute-start | bytes 4816904 | tf_op jit(solution)/shard_map/ppermute | solution.py:919
  441.6 54.9 %collective-permute-start.35 = (bf16[2,3,64,1472]{3,2,1,0:T(8,128)(2,1)}, bf16[2,3,64,1472]{3,2,1,0:T(8,128)(2,1)}, u32[]{:S(2)}, u32[]{:S(2)}) collective-permute-start(bf16[2,3,64,1472]{3,2,1,0:T(8,128)(2,1)} %pad_maximum_fusion.2), channel_id=1, source_target_pairs={{0,16},{4,20},{8,24},{12,28},{16,0},{20,4},{24,8},{28,12},{1,17},{... | collective-permute-start | bytes 3391496 | tf_op jit(solution)/shard_map/ppermute | solution.py:919
  444.5 60.1 %collective-permute-start.32 = (bf16[4,784,256]{2,1,0:T(8,128)(2,1)}, bf16[4,784,256]{2,1,0:T(8,128)(2,1)}, u32[]{:S(2)}, u32[]{:S(2)}) collective-permute-start(bf16[4,784,256]{2,1,0:T(8,128)(2,1)} %add.255), channel_id=1, source_target_pairs={{0,2},{2,0},{1,3},{3,1},{4,6},{6,4},{5,7},{7,5},{8,10},{10,8},{9,1... | collective-permute-start | bytes 4816904 | tf_op jit(solution)/shard_map/ppermute | solution.py:919
  458.4 40.3 %collective-permute-start.33 = (bf16[8,16,1472]{2,1,0:T(8,128)(2,1)S(1)}, bf16[8,16,1472]{2,1,0:T(8,128)(2,1)}, u32[]{:S(2)}, u32[]{:S(2)}) collective-permute-start(bf16[8,16,1472]{2,1,0:T(8,128)(2,1)S(1)} %get-tuple-element.643), channel_id=1, source_target_pairs={{0,4},{4,0},{8,12},{12,8},{16,20},{20,16},{24,28},{28,24},{1,5},{5... | collective-permute-start | bytes 1130504 | tf_op jit(solution)/shard_map/ppermute | solution.py:919
  461.2 37.5 %collective-permute-start.34 = (bf16[8,16,1472]{2,1,0:T(8,128)(2,1)S(1)}, bf16[8,16,1472]{2,1,0:T(8,128)(2,1)}, u32[]{:S(2)}, u32[]{:S(2)}) collective-permute-start(bf16[8,16,1472]{2,1,0:T(8,128)(2,1)S(1)} %get-tuple-element.641), channel_id=1, source_target_pairs={{0,4},{4,0},{8,12},{12,8},{16,20},{20,16},{24,28},{28,24},{1,5},{5... | collective-permute-start | bytes 1130504 | tf_op jit(solution)/shard_map/ppermute | solution.py:919
  524.3 29.0 %collective-permute-start.42 = (bf16[8,16,1472]{2,1,0:T(8,128)(2,1)}, bf16[8,16,1472]{2,1,0:T(8,128)(2,1)}, u32[]{:S(2)}, u32[]{:S(2)}) collective-permute-start(bf16[8,16,1472]{2,1,0:T(8,128)(2,1)} %get-tuple-element.639), channel_id=1, source_target_pairs={{0,2},{2,0},{1,3},{3,1},{4,6},{6,4},{5,7},{7,5},{8,10},{10,8},{9,1... | collective-permute-start | bytes 1130504 | tf_op jit(solution)/shard_map/ppermute | solution.py:919
  526.6 26.7 %collective-permute-start.43 = (bf16[8,16,1472]{2,1,0:T(8,128)(2,1)}, bf16[8,16,1472]{2,1,0:T(8,128)(2,1)}, u32[]{:S(2)}, u32[]{:S(2)}) collective-permute-start(bf16[8,16,1472]{2,1,0:T(8,128)(2,1)} %get-tuple-element.637), channel_id=1, source_target_pairs={{0,4},{4,0},{8,12},{12,8},{16,20},{20,16},{24,28},{28,24},{1,5},{5... | collective-permute-start | bytes 1130504 | tf_op jit(solution)/shard_map/ppermute | solution.py:919
  527.7 29.4 %collective-permute-start.54 = (bf16[1,3,64,1472]{3,2,1,0:T(8,128)(2,1)S(1)}, bf16[1,3,64,1472]{3,2,1,0:T(8,128)(2,1)}, u32[]{:S(2)}, u32[]{:S(2)}) collective-permute-start(bf16[1,3,64,1472]{3,2,1,0:T(8,128)(2,1)S(1)} %copy-done.22), channel_id=1, source_target_pairs={{0,8},{4,12},{8,0},{12,4},{16,24},{20,28},{24,16},{28,20},{1,9},{5... | collective-permute-start | bytes 1695752 | tf_op jit(solution)/shard_map/ppermute | solution.py:919
  527.8 30.6 %collective-permute-start.41 = (bf16[2,32,1472]{2,1,0:T(8,128)(2,1)S(1)}, bf16[2,32,1472]{2,1,0:T(8,128)(2,1)}, u32[]{:S(2)}, u32[]{:S(2)}) collective-permute-start(bf16[2,32,1472]{2,1,0:T(8,128)(2,1)S(1)} %pad_maximum_fusion.12), channel_id=1, source_target_pairs={{0,16},{4,20},{8,24},{12,28},{16,0},{20,4},{24,8},{28,12},{1,17},{... | collective-permute-start | bytes 565256 | tf_op jit(solution)/shard_map/ppermute | solution.py:919
  559.4 23.5 %collective-permute-start.53 = (bf16[1,32,1472]{2,1,0:T(8,128)(2,1)S(1)}, bf16[1,32,1472]{2,1,0:T(8,128)(2,1)S(1)}, u32[]{:S(2)}, u32[]{:S(2)}) collective-permute-start(bf16[1,32,1472]{2,1,0:T(8,128)(2,1)S(1)} %get-tuple-element.672), channel_id=1, source_target_pairs={{0,8},{4,12},{8,0},{12,4},{16,24},{20,28},{24,16},{28,20},{1,9},{5... | collective-permute-start | bytes 282632 | tf_op jit(solution)/shard_map/ppermute | solution.py:919
  (71 other events, 644.9 us)
Sparse Core Ops, SparseCore 0:
  31.2 130.8 all-gather.4
  164.9 93.7 all-gather.6
  264.0 169.5 reduce-scatter.1

commit v7 on v6

--- a/solution.py
+++ b/solution.py
@@ -1173,21 +1173,20 @@
     )
     by_core = [(dkv[0], swap(dkv[2], core)), (dkv[1], swap(dkv[3], core))]
     tick()
+    entries = lambda g: tuple(v.reshape(-1, each, width) for v in g)
+    home_a, home_b = (core,) + ba, (core,) + ab
+    own, other = run(add_pairs, by_core)
+    other = swap(other, across)
+    gwq = run(
+        lambda n, d, p: projection_grads(n, [d], [(0, inner)], [p], rows), normed, dq, place_b
+    )
     if by_hops:
         ffn_grads[0] = close(ffn_grads[0])
-    entries = lambda g: tuple(v.reshape(-1, each, width) for v in g)
-    home_a, home_b = (core,) + ba, (core,) + ab
-    gwq = run(
-        lambda n, d, p: projection_grads(n, [d], [(0, inner)], [p], rows), normed, dq, place_b
-    )
-    own, other = run(add_pairs, by_core)
-    other = swap(other, across)
     part = gwo.shape[0] // 2
     query_sum = Sums([entries((gwo[:part], gwo[part:])), entries(gwq)], [home_b, home_b])
     grad_table = run(lambda g, b: bucket_sums(g, b, count), grad_bias, buckets_t)
     query_sum.go()
     out = run(lambda *a: layer_out_of(*a, rows), ffn_w, acts, mixed, out_got)
-    tick()
     query_sum.go()
     (dkv,) = run(add_pairs, [(own, other)])
     gkv = run(
@@ -1195,6 +1194,7 @@
         normed, dkv, place_a, place_b,
     )
     value_sum = Sums([entries(gkv[:2]), entries(gkv[2:])], [home_a, home_b], direct=dp <= 8)
+    tick()
     query_sum.go()
     value_sum.go()
     gx, gain_one_part = run(

time: 595 us -> 578 us (0.971)
  waiting for transfers between devices: 120 us -> 104 us
    reduce_scatter x1, waiting for transfers between devices: 13.3 us -> 0.01 us  [per_device(): lax.psum_scatter(grads[0], same_core)]
  transfers between devices with their start and end apart: 58 -> 58, of which waited for: 23 -> 23; matrix products, arithmetic and copies ran while one was open for 11% -> 12% of each run, Pallas kernels for 56% -> 57%
where the time goes in v7:
time: 578 us; the launch traced here: 574 us
  Pallas kernels  329 us (57%)
  waiting for transfers between devices  104 us (18%)
  starting transfers between devices  47.9 us (8%)
  other arithmetic  42.4 us (7%)
  local copies, waits for them, and re-layouts  35.6 us (6%)
  between operations  15 us (3%)
    ppermute x55, waiting for transfers between devices, swap(): lax.ppermute(x, axis, [(i, i ^ mask) for i in range(self.sizes[axis])])  103 us
    pallas_call x3, Pallas kernels, ffn_group(): pl.pallas_call(functools.partial(ffn_body, len(ws), masks), grid_spec=spe...  100 us
    ppermute x55, starting transfers between devices, swap(): lax.ppermute(x, axis, [(i, i ^ mask) for i in range(self.sizes[axis])])  47.6 us
    pallas_call x1, Pallas kernels, attend_back(): pl.pallas_call(functools.partial(attend_back_body, heads, inner, count, l...  43 us
    pallas_call x1, Pallas kernels, mix_back(): pl.pallas_call(functools.partial(mix_back_body, layout_of(groups)), grid=...  38.5 us
    pallas_call x2, Pallas kernels, ffn_back(): pl.pallas_call(functools.partial(ffn_back_body, layout_of(groups), kinds,...  30.7 us
    pallas_call x2, Pallas kernels, projection_grads(): pl.pallas_call(functools.partial(grads_body, per, len(groups), parts), gr...  20.1 us
    pallas_call x1, Pallas kernels, last(): pl.pallas_call(functools.partial(last_body, per, len(dqs)), grid=(rows,),...  19.2 us
  transfers between devices with their start and end apart: 58, of which 23 were waited for; matrix products, arithmetic and copies ran while one was open for 12% of the time, Pallas kernels for 57%

profile of v7, /device:TPU:0, one launch (start us, length us, event | category | flops | bytes accessed | tf_op | source)
XLA Modules:
  0.0 574.0 jit_solution(5383400808902818590)
XLA Ops:
  9.1 5.1 collective-permute-start.2
  21.9 7.2 %first_norm.1 = (bf16[1472,1024]{1,0:T(8,128)(2,1)}, bf16[2,1472,1024]{2,1,0:T(8,128)(2,1)}, bf16[736,1024]{1,0:T(8,128)(2,1)}, bf16[736,1024]{1,0:T(8,128)(2,1)}) custom-call(bf16[4,1472,256]{2,1,0:T(8,128)(2,1)} %bitcast.104, bf16[4,1472,256]{2,1,0:T(8,128)(2,1)} %bitcast.107, f32[1472,1]{1,0:T(8,128)} %copy.38.gain_ref), custom_call_target="tpu_custom_call" | custom-call | flops 1 | bytes 1 | tf_op jit(solution)/shard_map/first_norm/pallas_call | solution.py:120
  36.2 6.8 %bias_of.1 = (f32[6,4,256,256]{3,2,1,0:T(8,128)}, s32[4,256,256]{2,1,0:T(8,128)}) custom-call(s32[4]{0:T(128)} %broadcast_xor_fusion.slots_ref, s32[256,1024]{1,0:T(8,128)} %buckets_ref, f32[6,128]{1,0:T(8,128)} %pad.41.table_ref), custom_call_target="tpu_custom_call" | custom-call | flops 1 | bytes 1 | tf_op jit(solution)/shard_map/bias_of/pallas_call | solution.py:381
  53.2 7.0 %collective-permute-done.5 = bf16[1,3,32,1472]{3,2,1,0:T(8,128)(2,1)S(1)} collective-permute-done((bf16[1,3,32,1472]{3,2,1,0:T(8,128)(2,1)S(1)}, bf16[1,3,32,1472]{3,2,1,0:T(8,128)(2,1)S(1)}, u32[]{:S(2)}, u32[]{:S(2)}) %collective-permute-start.5) | collective-permute-done | bytes 282656 | tf_op jit(solution)/shard_map/ppermute | solution.py:919
  60.2 5.0 collective-permute-done.10
  72.4 9.3 %key_value.1.refs_0_ = bf16[4,784,256]{2,1,0:T(8,128)(2,1)} custom-call(bf16[1472,1024]{1,0:T(8,128)(2,1)} %get-tuple-element.537.n_ref, bf16[16,1,32,1472]{3,2,1,0:T(8,128)(2,1)} %copy-done.3, bf16[16,1,32,1472]{3,2,1,0:T(8,128)(2,1)} %copy-done.5, bf16[16,1,32,1472]{3,2,1,0:T(8,128)(2,1)} %copy-done.4, bf16[16,1,32,1472]{3,2,1,0:T(8,128)(2,1)} %copy-done.6, ...), custom_call_target="tpu_custom_call" | custom-call | flops 1 | bytes 1 | tf_op jit(solution)/shard_map/key_value/pallas_call | solution.py:172
  84.4 5.1 project.1.q_ref
  89.5 37.0 %collective-permute-done.8 = bf16[2,3,32,1472]{3,2,1,0:T(8,128)(2,1)S(1)} collective-permute-done((bf16[2,3,32,1472]{3,2,1,0:T(8,128)(2,1)S(1)}, bf16[2,3,32,1472]{3,2,1,0:T(8,128)(2,1)S(1)}, u32[]{:S(2)}, u32[]{:S(2)}) %collective-permute-start.8) | collective-permute-done | bytes 565280 | tf_op jit(solution)/shard_map/ppermute | solution.py:919
  134.9 18.3 %attend.1 = (bf16[384,1024]{1,0:T(8,128)(2,1)}, f32[4,8,256]{2,1,0:T(8,128)}) custom-call(bf16[384,1024]{1,0:T(8,128)(2,1)} %project.1.q_ref, bf16[4,16,256]{2,1,0:T(8,128)(2,1)} %get-tuple-element.486.u_ref, bf16[4,784,256]{2,1,0:T(8,128)(2,1)} %key_value.1.refs_0_, bf16[4,784,256]{2,1,0:T(8,128)(2,1)} %copy-done.7, bf16[4,784,256]{2,1,0:T(8,128)(2,1)} %copy-done.8, ...), custom_call_target="tpu_custom_call" | custom-call | flops 1 | bytes 1 | tf_op jit(solution)/shard_map/attend/pallas_call | solution.py:241
  153.3 7.6 %collective-permute-done.14 = bf16[4,3,32,1472]{3,2,1,0:T(8,128)(2,1)S(1)} collective-permute-done((bf16[4,3,32,1472]{3,2,1,0:T(8,128)(2,1)S(1)}, bf16[4,3,32,1472]{3,2,1,0:T(8,128)(2,1)S(1)}, u32[]{:S(2)}, u32[]{:S(2)}) %collective-permute-start.14) | collective-permute-done | bytes 1130528 | tf_op jit(solution)/shard_map/ppermute | solution.py:919
  166.0 9.6 %mix.1 = (f32[1472,1024]{1,0:T(8,128)}, bf16[2,1472,1024]{2,1,0:T(8,128)(2,1)}, bf16[736,1024]{1,0:T(8,128)(2,1)}, bf16[736,1024]{1,0:T(8,128)(2,1)}) custom-call(bf16[4,1472,256]{2,1,0:T(8,128)(2,1)} %bitcast.105, bf16[384,1024]{1,0:T(8,128)(2,1)} %get-tuple-element.492.o_ref.refs_11_.refs_5_, bf16[16,1,32,1472]{3,2,1,0:T(8,128)(2,1)} %copy-done.3, ...), custom_call_target="tpu_custom_call" | custom-call | flops 1 | bytes 1 | tf_op jit(solution)/shard_map/mix/pallas_call | solution.py:458
  186.8 41.2 %ffn_group.3 = (bf16[3,768,2048]{2,1,0:T(8,128)(2,1)}, bf16[16,3,48,1472]{3,2,1,0:T(8,128)(2,1)}) custom-call(s32[1]{0:T(128)} %bitcast.23.me_ref, bf16[16,3,48,1472]{3,2,1,0:T(8,128)(2,1)} %bitcast.94, bf16[2,1472,1024]{2,1,0:T(8,128)(2,1)} %bitcast_dynamic-update-slice_fusion.refs_1_.refs_2_, ...), custom_call_target="tpu_custom_call" | custom-call | flops 1 | bytes 1 | tf_op jit(solution)/shard_map/ffn_group/pallas_call | solution.py:583
  228.0 29.2 %ffn_group.4 = (bf16[3,512,2048]{2,1,0:T(8,128)(2,1)}, bf16[8,3,32,1472]{3,2,1,0:T(8,128)(2,1)}, bf16[8,3,32,1472]{3,2,1,0:T(8,128)(2,1)}) custom-call(s32[1]{0:T(128)} %bitcast.23.me_ref, bf16[8,3,32,1472]{3,2,1,0:T(8,128)(2,1)} %copy-done.2, bf16[8,3,32,1472]{3,2,1,0:T(8,128)(2,1)} %collective-permute-done.18.refs_1_.refs_3_, ...), custom_call_target="tpu_custom_call" | custom-call | flops 1 | bytes 1 | tf_op jit(solution)/shard_map/ffn_group/pallas_call | solution.py:583
  258.2 30.0 %ffn_group.5 = (bf16[3,512,2048]{2,1,0:T(8,128)(2,1)}, bf16[8,3,32,1472]{3,2,1,0:T(8,128)(2,1)}, bf16[8,3,32,1472]{3,2,1,0:T(8,128)(2,1)}) custom-call(s32[1]{0:T(128)} %bitcast.23.me_ref, bf16[16,3,32,1472]{3,2,1,0:T(8,128)(2,1)} %bitcast.99, bf16[2,1472,1024]{2,1,0:T(8,128)(2,1)} %bitcast_dynamic-update-slice_fusion.refs_1_.refs_2_, ...), custom_call_target="tpu_custom_call" | custom-call | flops 1 | bytes 1 | tf_op jit(solution)/shard_map/ffn_group/pallas_call | solution.py:583
  290.2 19.3 %ffn_back.2 = (bf16[736,1024]{1,0:T(8,128)(2,1)}, bf16[736,1024]{1,0:T(8,128)(2,1)}) custom-call(bf16[16,3,48,1472]{3,2,1,0:T(8,128)(2,1)} %bitcast.95, bf16[16,3,32,1472]{3,2,1,0:T(8,128)(2,1)} %bitcast.100, bf16[8,3,32,1472]{3,2,1,0:T(8,128)(2,1)} %copy-done.2, bf16[8,3,32,1472]{3,2,1,0:T(8,128)(2,1)} %collective-permute-done.18.refs_1_.refs_3_, ...), custom_call_target="tpu_custom_call" | custom-call | flops 1 | bytes 1 | tf_op jit(solution)/shard_map/ffn_back/pallas_call | solution.py:650
  310.1 11.5 %ffn_back.3 = bf16[1472,1024]{1,0:T(8,128)(2,1)} custom-call(bf16[16,3,48,1472]{3,2,1,0:T(8,128)(2,1)} %bitcast.96, bf16[16,3,32,1472]{3,2,1,0:T(8,128)(2,1)} %bitcast.101, bf16[8,3,32,1472]{3,2,1,0:T(8,128)(2,1)} %copy-done.2, bf16[8,3,32,1472]{3,2,1,0:T(8,128)(2,1)} %collective-permute-done.18.refs_1_.refs_3_, ...), custom_call_target="tpu_custom_call" | custom-call | flops 1 | bytes 1 | tf_op jit(solution)/shard_map/ffn_back/pallas_call | solution.py:650
  322.8 38.5 %mix_back.1 = (f32[1472,1024]{1,0:T(8,128)}, bf16[384,1024]{1,0:T(8,128)(2,1)}, f32[1472,128]{1,0:T(8,128)}, bf16[512,1472]{1,0:T(8,128)(2,1)}) custom-call(bf16[16,3,48,1472]{3,2,1,0:T(8,128)(2,1)} %bitcast.97, bf16[16,3,32,1472]{3,2,1,0:T(8,128)(2,1)} %bitcast.102, bf16[8,3,32,1472]{3,2,1,0:T(8,128)(2,1)} %copy-done.2, ...), custom_call_target="tpu_custom_call" | custom-call | flops 1 | bytes 1 | tf_op jit(solution)/shard_map/mix_back/pallas_call | solution.py:746
  370.0 43.0 %attend_back.1 = (bf16[384,1024]{1,0:T(8,128)(2,1)}, bf16[4,784,256]{2,1,0:T(8,128)(2,1)}, bf16[4,784,256]{2,1,0:T(8,128)(2,1)}, bf16[4,784,256]{2,1,0:T(8,128)(...) custom-call(bf16[384,1024]{1,0:T(8,128)(2,1)} %project.1.q_ref, ...), custom_call_target="tpu_custom_call" | custom-call | flops 1 | bytes 1 | tf_op jit(solution)/shard_map/attend_back/pallas_call | solution.py:336
  424.7 7.9 %projection_grads.2 = (bf16[256,1472]{1,0:T(8,128)(2,1)}, bf16[256,1472]{1,0:T(8,128)(2,1)}) custom-call(bf16[1472,1024]{1,0:T(8,128)(2,1)} %get-tuple-element.537.n_ref, bf16[384,1024]{1,0:T(8,128)(2,1)} %get-tuple-element.557.refs_0_, bf16[384,512]{1,0:T(8,128)(2,1)} %fusion.1.pv_ref.p_ref.refs_15_.refs_1_.refs_2_.refs_8_.refs_10_), custom_call_target="tpu_custom_call" | custom-call | flops 1 | bytes 1 | tf_op jit(solution)/shard_map/projection_grads/pallas_call | solution.py:821
  434.4 8.2 %bucket_sums.1 = f32[96,256]{1,0:T(8,128)} custom-call(s32[4,256,256]{2,1,0:T(8,128)} %get-tuple-element.516.buckets_ref, f32[6,4,256,256]{3,2,1,0:T(8,128)} %get-tuple-element.517.g_ref), custom_call_target="tpu_custom_call" | custom-call | flops 1 | bytes 1 | tf_op jit(solution)/shard_map/bucket_sums/pallas_call | solution.py:415
  453.6 12.8 %layer_out_of.1 = bf16[4,1472,256]{2,1,0:T(8,128)(2,1)} custom-call(bf16[16,3,48,1472]{3,2,1,0:T(8,128)(2,1)} %bitcast.98, bf16[16,3,32,1472]{3,2,1,0:T(8,128)(2,1)} %bitcast.103, bf16[8,3,32,1472]{3,2,1,0:T(8,128)(2,1)} %copy-done.2, bf16[8,3,32,1472]{3,2,1,0:T(8,128)(2,1)} %collective-permute-done.18.refs_1_.refs_3_, ...), custom_call_target="tpu_custom_call" | custom-call | flops 1 | bytes 1 | tf_op jit(solution)/shard_map/layer_out_of/pallas_call | solution.py:674
  474.4 12.2 %projection_grads.3 = (bf16[256,1472]{1,0:T(8,128)(2,1)}, bf16[256,1472]{1,0:T(8,128)(2,1)}, bf16[256,1472]{1,0:T(8,128)(2,1)}, bf16[256,1472]{1,0:T(8,128)(2,1)}) custom-call(bf16[1472,1024]{1,0:T(8,128)(2,1)} %get-tuple-element.537.n_ref, bf16[4,784,256]{2,1,0:T(8,128)(2,1)} %add.264.refs_0_.refs_1_, ...), custom_call_target="tpu_custom_call" | custom-call | flops 1 | bytes 1 | tf_op jit(solution)/shard_map/projection_grads/pallas_call | solution.py:821
  486.6 17.7 %collective-permute-done.39 = bf16[2,3,64,1472]{3,2,1,0:T(8,128)(2,1)} collective-permute-done((bf16[2,3,64,1472]{3,2,1,0:T(8,128)(2,1)}, bf16[2,3,64,1472]{3,2,1,0:T(8,128)(2,1)}, u32[]{:S(2)}, u32[]{:S(2)}) %collective-permute-start.39) | collective-permute-done | bytes 1130528 | tf_op jit(solution)/shard_map/ppermute | solution.py:919
  515.6 19.2 %last.1 = (f32[4,1472,256]{2,1,0:T(8,128)}, f32[1472,128]{1,0:T(8,128)}) custom-call(bf16[4,1472,256]{2,1,0:T(8,128)(2,1)} %bitcast.106, f32[1472,1024]{1,0:T(8,128)} %get-tuple-element.556.dm_ref, bf16[384,1024]{1,0:T(8,128)(2,1)} %get-tuple-element.557.refs_0_, bf16[4,784,256]{2,1,0:T(8,128)(2,1)} %add.264.refs_0_.refs_1_, ...), custom_call_target="tpu_custom_call" | custom-call | flops 1 | bytes 1 | tf_op jit(solution)/shard_map/last/pallas_call | solution.py:882
  (307 shorter events, 150.4 us)
Async XLA Ops:
  7.3 179.5 %all-gather.5.cloned.1.call-start = ((), (), s32[]{:S(2)}) async-start(), calls=%async_computation.2 | async-start | bytes 7520256 | tf_op jit(solution)/shard_map/all_gather | solution.py:1053
  9.1 20.8 %collective-permute-start.2 = (bf16[1,1,64,1472]{3,2,1,0:T(8,128)(2,1)S(1)}, bf16[1,1,64,1472]{3,2,1,0:T(8,128)(2,1)S(1)}, u32[]{:S(2)}, u32[]{:S(2)}) collective-permute-start(bf16[1,1,64,1472]{3,2,1,0:T(8,128)(2,1)S(1)} %maximum_bitcast_fusion), channel_id=1, source_target_pairs={{0,24},{4,28},{8,16},{12,20},{16,8},{20,12},{24,0},{28,4},{1,25},{... | collective-permute-start | bytes 565256 | tf_op jit(solution)/shard_map/ppermute | solution.py:919
  31.1 227.0 %all-gather.7.cloned.1.call-start = ((), (), s32[]{:S(2)}) async-start(), calls=%async_computation.3 | async-start | bytes 5013504 | tf_op jit(solution)/shard_map/all_gather | solution.py:1053
  36.0 398.4 %reduce-scatter.2.cloned.1.call-start = ((), (), s32[]{:S(2)}) async-start(), calls=%async_computation.1 | async-start | bytes 7520256 | tf_op jit(solution)/shard_map/reduce_scatter | solution.py:1149
  81.9 47.1 %collective-permute-start.15 = (bf16[4,784,256]{2,1,0:T(8,128)(2,1)}, bf16[4,784,256]{2,1,0:T(8,128)(2,1)S(1)}, u32[]{:S(2)}, u32[]{:S(2)}) collective-permute-start(bf16[4,784,256]{2,1,0:T(8,128)(2,1)} %key_value.1.refs_0_), channel_id=1, source_target_pairs={{0,2},{2,0},{1,3},{3,1},{4,6},{6,4},{5,7},{7,5},{8,10},{10,8},{9,1... | collective-permute-start | bytes 4816904 | tf_op jit(solution)/shard_map/ppermute | solution.py:919
  82.3 44.2 %collective-permute-start.8 = (bf16[2,3,32,1472]{3,2,1,0:T(8,128)(2,1)S(1)}, bf16[2,3,32,1472]{3,2,1,0:T(8,128)(2,1)S(1)}, u32[]{:S(2)}, u32[]{:S(2)}) collective-permute-start(bf16[2,3,32,1472]{3,2,1,0:T(8,128)(2,1)S(1)} %constant_dynamic-update-slice_fusion.4), channel_id=1, source_target_pairs={{0,16},{4,20},{8,24},{12,28},{16,0},{20,4},{24,8},{28,12},{1,17},{... | collective-permute-start | bytes 1695752 | tf_op jit(solution)/shard_map/ppermute | solution.py:919
  126.6 34.2 %collective-permute-start.14 = (bf16[4,3,32,1472]{3,2,1,0:T(8,128)(2,1)S(1)}, bf16[4,3,32,1472]{3,2,1,0:T(8,128)(2,1)S(1)}, u32[]{:S(2)}, u32[]{:S(2)}) collective-permute-start(bf16[4,3,32,1472]{3,2,1,0:T(8,128)(2,1)S(1)} %constant_dynamic-update-slice_fusion.10), channel_id=1, source_target_pairs={{0,4},{4,0},{8,12},{12,8},{16,20},{20,16},{24,28},{28,24},{1,5},{5... | collective-permute-start | bytes 3391496 | tf_op jit(solution)/shard_map/ppermute | solution.py:919
  163.3 64.7 %collective-permute-start.18 = (bf16[8,3,32,1472]{3,2,1,0:T(8,128)(2,1)S(1)}, bf16[8,3,32,1472]{3,2,1,0:T(8,128)(2,1)}, u32[]{:S(2)}, u32[]{:S(2)}) collective-permute-start(bf16[8,3,32,1472]{3,2,1,0:T(8,128)(2,1)S(1)} %constant_dynamic-update-slice_fusion.12.refs_0_.refs_2_), channel_id=1, source_target_pairs={{0,2},{2,0},{1,3},{3,1},{4,6},{6,4},{5,7},{7,5},{8,10},{10,8},{9,1... | collective-permute-start | bytes 6782984 | tf_op jit(solution)/shard_map/ppermute | solution.py:919
  288.1 73.1 %collective-permute-start.22 = (bf16[8,3,32,1472]{3,2,1,0:T(8,128)(2,1)}, bf16[8,3,32,1472]{3,2,1,0:T(8,128)(2,1)}, u32[]{:S(2)}, u32[]{:S(2)}) collective-permute-start(bf16[8,3,32,1472]{3,2,1,0:T(8,128)(2,1)} %get-tuple-element.440), channel_id=1, source_target_pairs={{0,4},{4,0},{8,12},{12,8},{16,20},{20,16},{24,28},{28,24},{1,5},{5... | collective-permute-start | bytes 6782984 | tf_op jit(solution)/shard_map/ppermute | solution.py:919
  289.7 71.6 %collective-permute-start.23 = (bf16[8,3,32,1472]{3,2,1,0:T(8,128)(2,1)}, bf16[8,3,32,1472]{3,2,1,0:T(8,128)(2,1)}, u32[]{:S(2)}, u32[]{:S(2)}) collective-permute-start(bf16[8,3,32,1472]{3,2,1,0:T(8,128)(2,1)} %get-tuple-element.433), channel_id=1, source_target_pairs={{0,2},{2,0},{1,3},{3,1},{4,6},{6,4},{5,7},{7,5},{8,10},{10,8},{9,1... | collective-permute-start | bytes 6782984 | tf_op jit(solution)/shard_map/ppermute | solution.py:919
  321.5 48.4 %collective-permute-start.21 = (bf16[1472,1024]{1,0:T(8,128)(2,1)}, bf16[1472,1024]{1,0:T(8,128)(2,1)S(1)}, u32[]{:S(2)}, u32[]{:S(2)}) collective-permute-start(bf16[1472,1024]{1,0:T(8,128)(2,1)} %ffn_back.3), channel_id=1, source_target_pairs={{0,1},{1,0},{2,3},{3,2},{4,5},{5,4},{6,7},{7,6},{8,9},{9,8},{10,11... | collective-permute-start | bytes 9043976 | tf_op jit(solution)/shard_map/ppermute | solution.py:919
  365.0 51.3 %collective-permute-start.28 = (bf16[4,3,32,1472]{3,2,1,0:T(8,128)(2,1)}, bf16[4,3,32,1472]{3,2,1,0:T(8,128)(2,1)}, u32[]{:S(2)}, u32[]{:S(2)}) collective-permute-start(bf16[4,3,32,1472]{3,2,1,0:T(8,128)(2,1)} %get-tuple-element.627), channel_id=1, source_target_pairs={{0,2},{2,0},{1,3},{3,1},{4,6},{6,4},{5,7},{7,5},{8,10},{10,8},{9,1... | collective-permute-start | bytes 3391496 | tf_op jit(solution)/shard_map/ppermute | solution.py:919
  369.4 47.0 %collective-permute-start.29 = (bf16[4,3,32,1472]{3,2,1,0:T(8,128)(2,1)}, bf16[4,3,32,1472]{3,2,1,0:T(8,128)(2,1)}, u32[]{:S(2)}, u32[]{:S(2)}) collective-permute-start(bf16[4,3,32,1472]{3,2,1,0:T(8,128)(2,1)} %get-tuple-element.625), channel_id=1, source_target_pairs={{0,4},{4,0},{8,12},{12,8},{16,20},{20,16},{24,28},{28,24},{1,5},{5... | collective-permute-start | bytes 3391496 | tf_op jit(solution)/shard_map/ppermute | solution.py:919
  416.3 28.9 %collective-permute-start.30 = (bf16[16,16,1472]{2,1,0:T(8,128)(2,1)}, bf16[16,16,1472]{2,1,0:T(8,128)(2,1)}, u32[]{:S(2)}, u32[]{:S(2)}) collective-permute-start(bf16[16,16,1472]{2,1,0:T(8,128)(2,1)} %bitcast.28), channel_id=1, source_target_pairs={{0,1},{1,0},{2,3},{3,2},{4,5},{5,4},{6,7},{7,6},{8,9},{9,8},{10,11... | collective-permute-start | bytes 2261000 | tf_op jit(solution)/shard_map/ppermute | solution.py:919
  433.1 38.3 %collective-permute-start.32 = (bf16[4,784,256]{2,1,0:T(8,128)(2,1)}, bf16[4,784,256]{2,1,0:T(8,128)(2,1)}, u32[]{:S(2)}, u32[]{:S(2)}) collective-permute-start(bf16[4,784,256]{2,1,0:T(8,128)(2,1)} %add.255), channel_id=1, source_target_pairs={{0,2},{2,0},{1,3},{3,1},{4,6},{6,4},{5,7},{7,5},{8,10},{10,8},{9,1... | collective-permute-start | bytes 4816904 | tf_op jit(solution)/shard_map/ppermute | solution.py:919
  446.7 19.7 %collective-permute-start.33 = (bf16[8,16,1472]{2,1,0:T(8,128)(2,1)S(1)}, bf16[8,16,1472]{2,1,0:T(8,128)(2,1)}, u32[]{:S(2)}, u32[]{:S(2)}) collective-permute-start(bf16[8,16,1472]{2,1,0:T(8,128)(2,1)S(1)} %get-tuple-element.643), channel_id=1, source_target_pairs={{0,4},{4,0},{8,12},{12,8},{16,20},{20,16},{24,28},{28,24},{1,5},{5... | collective-permute-start | bytes 1130504 | tf_op jit(solution)/shard_map/ppermute | solution.py:919
  450.7 53.6 %collective-permute-start.39 = (bf16[2,3,64,1472]{3,2,1,0:T(8,128)(2,1)}, bf16[2,3,64,1472]{3,2,1,0:T(8,128)(2,1)}, u32[]{:S(2)}, u32[]{:S(2)}) collective-permute-start(bf16[2,3,64,1472]{3,2,1,0:T(8,128)(2,1)} %pad_maximum_fusion.2), channel_id=1, source_target_pairs={{0,16},{4,20},{8,24},{12,28},{16,0},{20,4},{24,8},{28,12},{1,17},{... | collective-permute-start | bytes 3391496 | tf_op jit(solution)/shard_map/ppermute | solution.py:919
  467.5 38.7 %collective-permute-start.37 = (bf16[4,16,1472]{2,1,0:T(8,128)(2,1)S(1)}, bf16[4,16,1472]{2,1,0:T(8,128)(2,1)S(1)}, u32[]{:S(2)}, u32[]{:S(2)}) collective-permute-start(bf16[4,16,1472]{2,1,0:T(8,128)(2,1)S(1)} %get-tuple-element.659), channel_id=1, source_target_pairs={{0,2},{2,0},{1,3},{3,1},{4,6},{6,4},{5,7},{7,5},{8,10},{10,8},{9,1... | collective-permute-start | bytes 565256 | tf_op jit(solution)/shard_map/ppermute | solution.py:919
  469.2 37.0 %collective-permute-start.38 = (bf16[4,16,1472]{2,1,0:T(8,128)(2,1)S(1)}, bf16[4,16,1472]{2,1,0:T(8,128)(2,1)S(1)}, u32[]{:S(2)}, u32[]{:S(2)}) collective-permute-start(bf16[4,16,1472]{2,1,0:T(8,128)(2,1)S(1)} %get-tuple-element.657), channel_id=1, source_target_pairs={{0,2},{2,0},{1,3},{3,1},{4,6},{6,4},{5,7},{7,5},{8,10},{10,8},{9,1... | collective-permute-start | bytes 565256 | tf_op jit(solution)/shard_map/ppermute | solution.py:919
  508.1 28.3 %collective-permute-start.42 = (bf16[8,16,1472]{2,1,0:T(8,128)(2,1)S(1)}, bf16[8,16,1472]{2,1,0:T(8,128)(2,1)}, u32[]{:S(2)}, u32[]{:S(2)}) collective-permute-start(bf16[8,16,1472]{2,1,0:T(8,128)(2,1)S(1)} %get-tuple-element.639), channel_id=1, source_target_pairs={{0,2},{2,0},{1,3},{3,1},{4,6},{6,4},{5,7},{7,5},{8,10},{10,8},{9,1... | collective-permute-start | bytes 1130504 | tf_op jit(solution)/shard_map/ppermute | solution.py:919
  509.7 26.7 %collective-permute-start.43 = (bf16[8,16,1472]{2,1,0:T(8,128)(2,1)}, bf16[8,16,1472]{2,1,0:T(8,128)(2,1)}, u32[]{:S(2)}, u32[]{:S(2)}) collective-permute-start(bf16[8,16,1472]{2,1,0:T(8,128)(2,1)} %get-tuple-element.637), channel_id=1, source_target_pairs={{0,4},{4,0},{8,12},{12,8},{16,20},{20,16},{24,28},{28,24},{1,5},{5... | collective-permute-start | bytes 1130504 | tf_op jit(solution)/shard_map/ppermute | solution.py:919
  511.3 29.4 %collective-permute-start.54 = (bf16[1,3,64,1472]{3,2,1,0:T(8,128)(2,1)S(1)}, bf16[1,3,64,1472]{3,2,1,0:T(8,128)(2,1)}, u32[]{:S(2)}, u32[]{:S(2)}) collective-permute-start(bf16[1,3,64,1472]{3,2,1,0:T(8,128)(2,1)S(1)} %get-tuple-element.629), channel_id=1, source_target_pairs={{0,8},{4,12},{8,0},{12,4},{16,24},{20,28},{24,16},{28,20},{1,9},{5... | collective-permute-start | bytes 1695752 | tf_op jit(solution)/shard_map/ppermute | solution.py:919
  512.7 29.3 %collective-permute-start.41 = (bf16[2,32,1472]{2,1,0:T(8,128)(2,1)}, bf16[2,32,1472]{2,1,0:T(8,128)(2,1)}, u32[]{:S(2)}, u32[]{:S(2)}) collective-permute-start(bf16[2,32,1472]{2,1,0:T(8,128)(2,1)} %pad_maximum_fusion.12), channel_id=1, source_target_pairs={{0,16},{4,20},{8,24},{12,28},{16,0},{20,4},{24,8},{28,12},{1,17},{... | collective-permute-start | bytes 565256 | tf_op jit(solution)/shard_map/ppermute | solution.py:919
  543.0 22.7 %collective-permute-start.53 = (bf16[1,32,1472]{2,1,0:T(8,128)(2,1)S(1)}, bf16[1,32,1472]{2,1,0:T(8,128)(2,1)S(1)}, u32[]{:S(2)}, u32[]{:S(2)}) collective-permute-start(bf16[1,32,1472]{2,1,0:T(8,128)(2,1)S(1)} %get-tuple-element.672), channel_id=1, source_target_pairs={{0,8},{4,12},{8,0},{12,4},{16,24},{20,28},{24,16},{28,20},{1,9},{5... | collective-permute-start | bytes 282632 | tf_op jit(solution)/shard_map/ppermute | solution.py:919
  (69 other events, 592.1 us)
Sparse Core Ops, SparseCore 0:
  31.2 130.6 all-gather.4
  164.7 93.3 all-gather.6
  263.5 169.5 reduce-scatter.1

commit v8 on v7

--- a/solution.py
+++ b/solution.py
@@ -1185,8 +1185,8 @@
     part = gwo.shape[0] // 2
     query_sum = Sums([entries((gwo[:part], gwo[part:])), entries(gwq)], [home_b, home_b])
     grad_table = run(lambda g, b: bucket_sums(g, b, count), grad_bias, buckets_t)
-    query_sum.go()
     out = run(lambda *a: layer_out_of(*a, rows), ffn_w, acts, mixed, out_got)
+    tick()
     query_sum.go()
     (dkv,) = run(add_pairs, [(own, other)])
     gkv = run(
@@ -1194,7 +1194,6 @@
         normed, dkv, place_a, place_b,
     )
     value_sum = Sums([entries(gkv[:2]), entries(gkv[2:])], [home_a, home_b], direct=dp <= 8)
-    tick()
     query_sum.go()
     value_sum.go()
     gx, gain_one_part = run(
@@ -1214,6 +1213,7 @@
         got = swap(small, one)
         if k == 1:
             value_sum.go()
+            query_sum.go()
         if k == 3:
             value_sum.got = close(value_sum.got)
         small = run(lambda a, b: a + b, small, got)

time: 578 us -> 593 us (1.026)
  waiting for transfers between devices: 104 us -> 117 us
    reduce_scatter x1, waiting for transfers between devices: 0.01 us -> 26.3 us  [per_device(): lax.psum_scatter(grads[0], same_core)]
    ppermute x55, waiting for transfers between devices: 103 us -> 89.5 us  [swap(): lax.ppermute(x, axis, [(i, i ^ mask) for i in range(self.sizes[axis])])]
  transfers between devices with their start and end apart: 58 -> 58, of which waited for: 23 -> 21; matrix products, arithmetic and copies ran while one was open for 12% -> 11% of each run, Pallas kernels for 57% -> 56%
where the time goes in v8:
time: 593 us; the launch traced here: 589 us
  Pallas kernels  329 us (55%)
  waiting for transfers between devices  117 us (20%)
  starting transfers between devices  49.1 us (8%)
  other arithmetic  44.9 us (8%)
  local copies, waits for them, and re-layouts  33.9 us (6%)
  between operations  15 us (3%)
    pallas_call x3, Pallas kernels, ffn_group(): pl.pallas_call(functools.partial(ffn_body, len(ws), masks), grid_spec=spe...  100 us
    ppermute x55, waiting for transfers between devices, swap(): lax.ppermute(x, axis, [(i, i ^ mask) for i in range(self.sizes[axis])])  89.5 us
    ppermute x55, starting transfers between devices, swap(): lax.ppermute(x, axis, [(i, i ^ mask) for i in range(self.sizes[axis])])  48.8 us
    pallas_call x1, Pallas kernels, attend_back(): pl.pallas_call(functools.partial(attend_back_body, heads, inner, count, l...  43 us
    pallas_call x1, Pallas kernels, mix_back(): pl.pallas_call(functools.partial(mix_back_body, layout_of(groups)), grid=...  38.4 us
    pallas_call x2, Pallas kernels, ffn_back(): pl.pallas_call(functools.partial(ffn_back_body, layout_of(groups), kinds,...  30.7 us
    reduce_scatter x1, waiting for transfers between devices, per_device(): lax.psum_scatter(grads[0], same_core)  26.3 us
    pallas_call x2, Pallas kernels, projection_grads(): pl.pallas_call(functools.partial(grads_body, per, len(groups), parts), gr...  20 us
  transfers between devices with their start and end apart: 58, of which 21 were waited for; matrix products, arithmetic and copies ran while one was open for 11% of the time, Pallas kernels for 56%

profile of v8, /device:TPU:0, one launch (start us, length us, event | category | flops | bytes accessed | tf_op | source)
XLA Modules:
  0.0 589.3 jit_solution(1892888197469939147)
XLA Ops:
  9.1 5.1 collective-permute-start.2
  21.9 7.2 %first_norm.1 = (bf16[1472,1024]{1,0:T(8,128)(2,1)}, bf16[2,1472,1024]{2,1,0:T(8,128)(2,1)}, bf16[736,1024]{1,0:T(8,128)(2,1)}, bf16[736,1024]{1,0:T(8,128)(2,1)}) custom-call(bf16[4,1472,256]{2,1,0:T(8,128)(2,1)} %bitcast.104, bf16[4,1472,256]{2,1,0:T(8,128)(2,1)} %bitcast.107, f32[1472,1]{1,0:T(8,128)} %copy.38.gain_ref), custom_call_target="tpu_custom_call" | custom-call | flops 1 | bytes 1 | tf_op jit(solution)/shard_map/first_norm/pallas_call | solution.py:120
  36.2 6.9 %bias_of.1 = (f32[6,4,256,256]{3,2,1,0:T(8,128)}, s32[4,256,256]{2,1,0:T(8,128)}) custom-call(s32[4]{0:T(128)} %broadcast_xor_fusion.slots_ref, s32[256,1024]{1,0:T(8,128)} %buckets_ref, f32[6,128]{1,0:T(8,128)} %pad.41.table_ref), custom_call_target="tpu_custom_call" | custom-call | flops 1 | bytes 1 | tf_op jit(solution)/shard_map/bias_of/pallas_call | solution.py:381
  53.2 6.9 %collective-permute-done.5 = bf16[1,3,32,1472]{3,2,1,0:T(8,128)(2,1)S(1)} collective-permute-done((bf16[1,3,32,1472]{3,2,1,0:T(8,128)(2,1)S(1)}, bf16[1,3,32,1472]{3,2,1,0:T(8,128)(2,1)S(1)}, u32[]{:S(2)}, u32[]{:S(2)}) %collective-permute-start.5) | collective-permute-done | bytes 282656 | tf_op jit(solution)/shard_map/ppermute | solution.py:919
  72.4 9.3 %key_value.1.refs_0_ = bf16[4,784,256]{2,1,0:T(8,128)(2,1)} custom-call(bf16[1472,1024]{1,0:T(8,128)(2,1)} %get-tuple-element.535.n_ref, bf16[16,1,32,1472]{3,2,1,0:T(8,128)(2,1)} %copy-done.3, bf16[16,1,32,1472]{3,2,1,0:T(8,128)(2,1)} %copy-done.5, bf16[16,1,32,1472]{3,2,1,0:T(8,128)(2,1)} %copy-done.4, bf16[16,1,32,1472]{3,2,1,0:T(8,128)(2,1)} %copy-done.6, ...), custom_call_target="tpu_custom_call" | custom-call | flops 1 | bytes 1 | tf_op jit(solution)/shard_map/key_value/pallas_call | solution.py:172
  84.4 5.1 project.1.q_ref
  89.5 35.7 %collective-permute-done.8 = bf16[2,3,32,1472]{3,2,1,0:T(8,128)(2,1)S(1)} collective-permute-done((bf16[2,3,32,1472]{3,2,1,0:T(8,128)(2,1)S(1)}, bf16[2,3,32,1472]{3,2,1,0:T(8,128)(2,1)S(1)}, u32[]{:S(2)}, u32[]{:S(2)}) %collective-permute-start.8) | collective-permute-done | bytes 565280 | tf_op jit(solution)/shard_map/ppermute | solution.py:919
  134.9 18.3 %attend.1 = (bf16[384,1024]{1,0:T(8,128)(2,1)}, f32[4,8,256]{2,1,0:T(8,128)}) custom-call(bf16[384,1024]{1,0:T(8,128)(2,1)} %project.1.q_ref, bf16[4,16,256]{2,1,0:T(8,128)(2,1)} %get-tuple-element.486.u_ref, bf16[4,784,256]{2,1,0:T(8,128)(2,1)} %key_value.1.refs_0_, bf16[4,784,256]{2,1,0:T(8,128)(2,1)} %copy-done.7, bf16[4,784,256]{2,1,0:T(8,128)(2,1)} %copy-done.8, ...), custom_call_target="tpu_custom_call" | custom-call | flops 1 | bytes 1 | tf_op jit(solution)/shard_map/attend/pallas_call | solution.py:241
  153.3 7.7 %collective-permute-done.14 = bf16[4,3,32,1472]{3,2,1,0:T(8,128)(2,1)S(1)} collective-permute-done((bf16[4,3,32,1472]{3,2,1,0:T(8,128)(2,1)S(1)}, bf16[4,3,32,1472]{3,2,1,0:T(8,128)(2,1)S(1)}, u32[]{:S(2)}, u32[]{:S(2)}) %collective-permute-start.14) | collective-permute-done | bytes 1130528 | tf_op jit(solution)/shard_map/ppermute | solution.py:919
  166.0 9.6 %mix.1 = (f32[1472,1024]{1,0:T(8,128)}, bf16[2,1472,1024]{2,1,0:T(8,128)(2,1)}, bf16[736,1024]{1,0:T(8,128)(2,1)}, bf16[736,1024]{1,0:T(8,128)(2,1)}) custom-call(bf16[4,1472,256]{2,1,0:T(8,128)(2,1)} %bitcast.105, bf16[384,1024]{1,0:T(8,128)(2,1)} %get-tuple-element.492.o_ref.refs_11_.refs_5_, bf16[16,1,32,1472]{3,2,1,0:T(8,128)(2,1)} %copy-done.3, ...), custom_call_target="tpu_custom_call" | custom-call | flops 1 | bytes 1 | tf_op jit(solution)/shard_map/mix/pallas_call | solution.py:458
  186.8 41.2 %ffn_group.3 = (bf16[3,768,2048]{2,1,0:T(8,128)(2,1)}, bf16[16,3,48,1472]{3,2,1,0:T(8,128)(2,1)}) custom-call(s32[1]{0:T(128)} %bitcast.23.me_ref, bf16[16,3,48,1472]{3,2,1,0:T(8,128)(2,1)} %bitcast.94, bf16[2,1472,1024]{2,1,0:T(8,128)(2,1)} %bitcast_dynamic-update-slice_fusion.refs_1_.refs_2_, ...), custom_call_target="tpu_custom_call" | custom-call | flops 1 | bytes 1 | tf_op jit(solution)/shard_map/ffn_group/pallas_call | solution.py:583
  228.0 29.2 %ffn_group.4 = (bf16[3,512,2048]{2,1,0:T(8,128)(2,1)}, bf16[8,3,32,1472]{3,2,1,0:T(8,128)(2,1)}, bf16[8,3,32,1472]{3,2,1,0:T(8,128)(2,1)}) custom-call(s32[1]{0:T(128)} %bitcast.23.me_ref, bf16[8,3,32,1472]{3,2,1,0:T(8,128)(2,1)} %copy-done.2, bf16[8,3,32,1472]{3,2,1,0:T(8,128)(2,1)} %collective-permute-done.18.refs_1_.refs_3_, ...), custom_call_target="tpu_custom_call" | custom-call | flops 1 | bytes 1 | tf_op jit(solution)/shard_map/ffn_group/pallas_call | solution.py:583
  258.6 29.9 %ffn_group.5 = (bf16[3,512,2048]{2,1,0:T(8,128)(2,1)}, bf16[8,3,32,1472]{3,2,1,0:T(8,128)(2,1)}, bf16[8,3,32,1472]{3,2,1,0:T(8,128)(2,1)}) custom-call(s32[1]{0:T(128)} %bitcast.23.me_ref, bf16[16,3,32,1472]{3,2,1,0:T(8,128)(2,1)} %bitcast.99, bf16[2,1472,1024]{2,1,0:T(8,128)(2,1)} %bitcast_dynamic-update-slice_fusion.refs_1_.refs_2_, ...), custom_call_target="tpu_custom_call" | custom-call | flops 1 | bytes 1 | tf_op jit(solution)/shard_map/ffn_group/pallas_call | solution.py:583
  290.7 19.3 %ffn_back.2 = (bf16[736,1024]{1,0:T(8,128)(2,1)}, bf16[736,1024]{1,0:T(8,128)(2,1)}) custom-call(bf16[16,3,48,1472]{3,2,1,0:T(8,128)(2,1)} %bitcast.95, bf16[16,3,32,1472]{3,2,1,0:T(8,128)(2,1)} %bitcast.100, bf16[8,3,32,1472]{3,2,1,0:T(8,128)(2,1)} %copy-done.2, bf16[8,3,32,1472]{3,2,1,0:T(8,128)(2,1)} %collective-permute-done.18.refs_1_.refs_3_, ...), custom_call_target="tpu_custom_call" | custom-call | flops 1 | bytes 1 | tf_op jit(solution)/shard_map/ffn_back/pallas_call | solution.py:650
  310.5 11.5 %ffn_back.3 = bf16[1472,1024]{1,0:T(8,128)(2,1)} custom-call(bf16[16,3,48,1472]{3,2,1,0:T(8,128)(2,1)} %bitcast.96, bf16[16,3,32,1472]{3,2,1,0:T(8,128)(2,1)} %bitcast.101, bf16[8,3,32,1472]{3,2,1,0:T(8,128)(2,1)} %copy-done.2, bf16[8,3,32,1472]{3,2,1,0:T(8,128)(2,1)} %collective-permute-done.18.refs_1_.refs_3_, ...), custom_call_target="tpu_custom_call" | custom-call | flops 1 | bytes 1 | tf_op jit(solution)/shard_map/ffn_back/pallas_call | solution.py:650
  323.3 38.4 %mix_back.1 = (f32[1472,1024]{1,0:T(8,128)}, bf16[384,1024]{1,0:T(8,128)(2,1)}, f32[1472,128]{1,0:T(8,128)}, bf16[512,1472]{1,0:T(8,128)(2,1)}) custom-call(bf16[16,3,48,1472]{3,2,1,0:T(8,128)(2,1)} %bitcast.97, bf16[16,3,32,1472]{3,2,1,0:T(8,128)(2,1)} %bitcast.102, bf16[8,3,32,1472]{3,2,1,0:T(8,128)(2,1)} %copy-done.2, ...), custom_call_target="tpu_custom_call" | custom-call | flops 1 | bytes 1 | tf_op jit(solution)/shard_map/mix_back/pallas_call | solution.py:746
  370.4 43.0 %attend_back.1 = (bf16[384,1024]{1,0:T(8,128)(2,1)}, bf16[4,784,256]{2,1,0:T(8,128)(2,1)}, bf16[4,784,256]{2,1,0:T(8,128)(2,1)}, bf16[4,784,256]{2,1,0:T(8,128)(...) custom-call(bf16[384,1024]{1,0:T(8,128)(2,1)} %project.1.q_ref, ...), custom_call_target="tpu_custom_call" | custom-call | flops 1 | bytes 1 | tf_op jit(solution)/shard_map/attend_back/pallas_call | solution.py:336
  425.2 7.9 %projection_grads.2 = (bf16[256,1472]{1,0:T(8,128)(2,1)}, bf16[256,1472]{1,0:T(8,128)(2,1)}) custom-call(bf16[1472,1024]{1,0:T(8,128)(2,1)} %get-tuple-element.535.n_ref, bf16[384,1024]{1,0:T(8,128)(2,1)} %get-tuple-element.553.refs_0_, bf16[384,512]{1,0:T(8,128)(2,1)} %fusion.1.pv_ref.p_ref.refs_15_.refs_1_.refs_2_.refs_8_.refs_10_), custom_call_target="tpu_custom_call" | custom-call | flops 1 | bytes 1 | tf_op jit(solution)/shard_map/projection_grads/pallas_call | solution.py:821
  435.1 26.3 %reduce-scatter.2.cloned.1.call-done = bf16[1,3,48,1472]{3,2,1,0:T(8,128)(2,1)} async-done(((bf16[16,3,48,1472]{3,2,1,0:T(8,128)(2,1)}), bf16[1,3,48,1472]{3,2,1,0:T(8,128)(2,1)}) %reduce-scatter.2.cloned.1.call-update) | async-done | bytes 423952 | tf_op jit(solution)/shard_map/reduce_scatter | solution.py:1149
  461.4 8.0 %bucket_sums.1 = f32[96,256]{1,0:T(8,128)} custom-call(s32[4,256,256]{2,1,0:T(8,128)} %get-tuple-element.516.buckets_ref, f32[6,4,256,256]{3,2,1,0:T(8,128)} %get-tuple-element.517.g_ref), custom_call_target="tpu_custom_call" | custom-call | flops 1 | bytes 1 | tf_op jit(solution)/shard_map/bucket_sums/pallas_call | solution.py:415
  471.3 13.2 %layer_out_of.1 = bf16[4,1472,256]{2,1,0:T(8,128)(2,1)} custom-call(bf16[16,3,48,1472]{3,2,1,0:T(8,128)(2,1)} %bitcast.98, bf16[16,3,32,1472]{3,2,1,0:T(8,128)(2,1)} %bitcast.103, bf16[8,3,32,1472]{3,2,1,0:T(8,128)(2,1)} %copy-done.2, bf16[8,3,32,1472]{3,2,1,0:T(8,128)(2,1)} %collective-permute-done.18.refs_1_.refs_3_, ...), custom_call_target="tpu_custom_call" | custom-call | flops 1 | bytes 1 | tf_op jit(solution)/shard_map/layer_out_of/pallas_call | solution.py:674
  496.6 12.1 %projection_grads.3 = (bf16[256,1472]{1,0:T(8,128)(2,1)}, bf16[256,1472]{1,0:T(8,128)(2,1)}, bf16[256,1472]{1,0:T(8,128)(2,1)}, bf16[256,1472]{1,0:T(8,128)(2,1)}) custom-call(bf16[1472,1024]{1,0:T(8,128)(2,1)} %get-tuple-element.535.n_ref, bf16[4,784,256]{2,1,0:T(8,128)(2,1)} %add.262.refs_0_.refs_1_, ...), custom_call_target="tpu_custom_call" | custom-call | flops 1 | bytes 1 | tf_op jit(solution)/shard_map/projection_grads/pallas_call | solution.py:821
  522.1 19.2 %last.1 = (f32[4,1472,256]{2,1,0:T(8,128)}, f32[1472,128]{1,0:T(8,128)}) custom-call(bf16[4,1472,256]{2,1,0:T(8,128)(2,1)} %bitcast.106, f32[1472,1024]{1,0:T(8,128)} %get-tuple-element.552.dm_ref, bf16[384,1024]{1,0:T(8,128)(2,1)} %get-tuple-element.553.refs_0_, bf16[4,784,256]{2,1,0:T(8,128)(2,1)} %add.262.refs_0_.refs_1_, ...), custom_call_target="tpu_custom_call" | custom-call | flops 1 | bytes 1 | tf_op jit(solution)/shard_map/last/pallas_call | solution.py:882
  553.1 8.1 %collective-permute-done.44 = bf16[2,32,1472]{2,1,0:T(8,128)(2,1)S(1)} collective-permute-done((bf16[2,32,1472]{2,1,0:T(8,128)(2,1)S(1)}, bf16[2,32,1472]{2,1,0:T(8,128)(2,1)S(1)}, u32[]{:S(2)}, u32[]{:S(2)}) %collective-permute-start.44) | collective-permute-done | bytes 188448 | tf_op jit(solution)/shard_map/ppermute | solution.py:919
  (303 shorter events, 155.2 us)
Async XLA Ops:
  7.3 179.6 %all-gather.5.cloned.1.call-start = ((), (), s32[]{:S(2)}) async-start(), calls=%async_computation.2 | async-start | bytes 7520256 | tf_op jit(solution)/shard_map/all_gather | solution.py:1053
  9.1 20.8 %collective-permute-start.2 = (bf16[1,1,64,1472]{3,2,1,0:T(8,128)(2,1)S(1)}, bf16[1,1,64,1472]{3,2,1,0:T(8,128)(2,1)S(1)}, u32[]{:S(2)}, u32[]{:S(2)}) collective-permute-start(bf16[1,1,64,1472]{3,2,1,0:T(8,128)(2,1)S(1)} %maximum_bitcast_fusion), channel_id=1, source_target_pairs={{0,24},{4,28},{8,16},{12,20},{16,8},{20,12},{24,0},{28,4},{1,25},{... | collective-permute-start | bytes 565256 | tf_op jit(solution)/shard_map/ppermute | solution.py:919
  31.1 227.5 %all-gather.7.cloned.1.call-start = ((), (), s32[]{:S(2)}) async-start(), calls=%async_computation.3 | async-start | bytes 5013504 | tf_op jit(solution)/shard_map/all_gather | solution.py:1053
  36.0 425.4 %reduce-scatter.2.cloned.1.call-start = ((), (), s32[]{:S(2)}) async-start(), calls=%async_computation.1 | async-start | bytes 7520256 | tf_op jit(solution)/shard_map/reduce_scatter | solution.py:1149
  81.9 47.1 %collective-permute-start.15 = (bf16[4,784,256]{2,1,0:T(8,128)(2,1)}, bf16[4,784,256]{2,1,0:T(8,128)(2,1)S(1)}, u32[]{:S(2)}, u32[]{:S(2)}) collective-permute-start(bf16[4,784,256]{2,1,0:T(8,128)(2,1)} %key_value.1.refs_0_), channel_id=1, source_target_pairs={{0,2},{2,0},{1,3},{3,1},{4,6},{6,4},{5,7},{7,5},{8,10},{10,8},{9,1... | collective-permute-start | bytes 4816904 | tf_op jit(solution)/shard_map/ppermute | solution.py:919
  82.3 42.9 %collective-permute-start.8 = (bf16[2,3,32,1472]{3,2,1,0:T(8,128)(2,1)S(1)}, bf16[2,3,32,1472]{3,2,1,0:T(8,128)(2,1)S(1)}, u32[]{:S(2)}, u32[]{:S(2)}) collective-permute-start(bf16[2,3,32,1472]{3,2,1,0:T(8,128)(2,1)S(1)} %constant_dynamic-update-slice_fusion.4), channel_id=1, source_target_pairs={{0,16},{4,20},{8,24},{12,28},{16,0},{20,4},{24,8},{28,12},{1,17},{... | collective-permute-start | bytes 1695752 | tf_op jit(solution)/shard_map/ppermute | solution.py:919
  125.3 35.6 %collective-permute-start.14 = (bf16[4,3,32,1472]{3,2,1,0:T(8,128)(2,1)S(1)}, bf16[4,3,32,1472]{3,2,1,0:T(8,128)(2,1)S(1)}, u32[]{:S(2)}, u32[]{:S(2)}) collective-permute-start(bf16[4,3,32,1472]{3,2,1,0:T(8,128)(2,1)S(1)} %constant_dynamic-update-slice_fusion.10), channel_id=1, source_target_pairs={{0,4},{4,0},{8,12},{12,8},{16,20},{20,16},{24,28},{28,24},{1,5},{5... | collective-permute-start | bytes 3391496 | tf_op jit(solution)/shard_map/ppermute | solution.py:919
  163.3 64.7 %collective-permute-start.18 = (bf16[8,3,32,1472]{3,2,1,0:T(8,128)(2,1)S(1)}, bf16[8,3,32,1472]{3,2,1,0:T(8,128)(2,1)}, u32[]{:S(2)}, u32[]{:S(2)}) collective-permute-start(bf16[8,3,32,1472]{3,2,1,0:T(8,128)(2,1)S(1)} %constant_dynamic-update-slice_fusion.12.refs_0_.refs_2_), channel_id=1, source_target_pairs={{0,2},{2,0},{1,3},{3,1},{4,6},{6,4},{5,7},{7,5},{8,10},{10,8},{9,1... | collective-permute-start | bytes 6782984 | tf_op jit(solution)/shard_map/ppermute | solution.py:919
  288.6 73.1 %collective-permute-start.22 = (bf16[8,3,32,1472]{3,2,1,0:T(8,128)(2,1)}, bf16[8,3,32,1472]{3,2,1,0:T(8,128)(2,1)}, u32[]{:S(2)}, u32[]{:S(2)}) collective-permute-start(bf16[8,3,32,1472]{3,2,1,0:T(8,128)(2,1)} %get-tuple-element.440), channel_id=1, source_target_pairs={{0,4},{4,0},{8,12},{12,8},{16,20},{20,16},{24,28},{28,24},{1,5},{5... | collective-permute-start | bytes 6782984 | tf_op jit(solution)/shard_map/ppermute | solution.py:919
  290.1 71.6 %collective-permute-start.23 = (bf16[8,3,32,1472]{3,2,1,0:T(8,128)(2,1)}, bf16[8,3,32,1472]{3,2,1,0:T(8,128)(2,1)}, u32[]{:S(2)}, u32[]{:S(2)}) collective-permute-start(bf16[8,3,32,1472]{3,2,1,0:T(8,128)(2,1)} %get-tuple-element.433), channel_id=1, source_target_pairs={{0,2},{2,0},{1,3},{3,1},{4,6},{6,4},{5,7},{7,5},{8,10},{10,8},{9,1... | collective-permute-start | bytes 6782984 | tf_op jit(solution)/shard_map/ppermute | solution.py:919
  322.0 48.4 %collective-permute-start.21 = (bf16[1472,1024]{1,0:T(8,128)(2,1)}, bf16[1472,1024]{1,0:T(8,128)(2,1)S(1)}, u32[]{:S(2)}, u32[]{:S(2)}) collective-permute-start(bf16[1472,1024]{1,0:T(8,128)(2,1)} %ffn_back.3), channel_id=1, source_target_pairs={{0,1},{1,0},{2,3},{3,2},{4,5},{5,4},{6,7},{7,6},{8,9},{9,8},{10,11... | collective-permute-start | bytes 9043976 | tf_op jit(solution)/shard_map/ppermute | solution.py:919
  365.5 48.5 %collective-permute-start.28 = (bf16[4,3,32,1472]{3,2,1,0:T(8,128)(2,1)}, bf16[4,3,32,1472]{3,2,1,0:T(8,128)(2,1)}, u32[]{:S(2)}, u32[]{:S(2)}) collective-permute-start(bf16[4,3,32,1472]{3,2,1,0:T(8,128)(2,1)} %get-tuple-element.627), channel_id=1, source_target_pairs={{0,2},{2,0},{1,3},{3,1},{4,6},{6,4},{5,7},{7,5},{8,10},{10,8},{9,1... | collective-permute-start | bytes 3391496 | tf_op jit(solution)/shard_map/ppermute | solution.py:919
  369.8 44.2 %collective-permute-start.29 = (bf16[4,3,32,1472]{3,2,1,0:T(8,128)(2,1)}, bf16[4,3,32,1472]{3,2,1,0:T(8,128)(2,1)}, u32[]{:S(2)}, u32[]{:S(2)}) collective-permute-start(bf16[4,3,32,1472]{3,2,1,0:T(8,128)(2,1)} %get-tuple-element.625), channel_id=1, source_target_pairs={{0,4},{4,0},{8,12},{12,8},{16,20},{20,16},{24,28},{28,24},{1,5},{5... | collective-permute-start | bytes 3391496 | tf_op jit(solution)/shard_map/ppermute | solution.py:919
  417.9 66.6 %collective-permute-start.33 = (bf16[2,3,64,1472]{3,2,1,0:T(8,128)(2,1)}, bf16[2,3,64,1472]{3,2,1,0:T(8,128)(2,1)}, u32[]{:S(2)}, u32[]{:S(2)}) collective-permute-start(bf16[2,3,64,1472]{3,2,1,0:T(8,128)(2,1)} %pad_maximum_fusion.2), channel_id=1, source_target_pairs={{0,16},{4,20},{8,24},{12,28},{16,0},{20,4},{24,8},{28,12},{1,17},{... | collective-permute-start | bytes 3391496 | tf_op jit(solution)/shard_map/ppermute | solution.py:919
  420.9 65.9 %collective-permute-start.31 = (bf16[16,16,1472]{2,1,0:T(8,128)(2,1)}, bf16[16,16,1472]{2,1,0:T(8,128)(2,1)}, u32[]{:S(2)}, u32[]{:S(2)}) collective-permute-start(bf16[16,16,1472]{2,1,0:T(8,128)(2,1)} %bitcast.31), channel_id=1, source_target_pairs={{0,1},{1,0},{2,3},{3,2},{4,5},{5,4},{6,7},{7,6},{8,9},{9,8},{10,11... | collective-permute-start | bytes 2261000 | tf_op jit(solution)/shard_map/ppermute | solution.py:919
  433.1 53.7 %collective-permute-start.32 = (bf16[16,16,1472]{2,1,0:T(8,128)(2,1)}, bf16[16,16,1472]{2,1,0:T(8,128)(2,1)}, u32[]{:S(2)}, u32[]{:S(2)}) collective-permute-start(bf16[16,16,1472]{2,1,0:T(8,128)(2,1)} %bitcast.124), channel_id=1, source_target_pairs={{0,1},{1,0},{2,3},{3,2},{4,5},{5,4},{6,7},{7,6},{8,9},{9,8},{10,11... | collective-permute-start | bytes 2261000 | tf_op jit(solution)/shard_map/ppermute | solution.py:919
  433.5 60.2 %collective-permute-start.30 = (bf16[4,784,256]{2,1,0:T(8,128)(2,1)}, bf16[4,784,256]{2,1,0:T(8,128)(2,1)}, u32[]{:S(2)}, u32[]{:S(2)}) collective-permute-start(bf16[4,784,256]{2,1,0:T(8,128)(2,1)} %add.255), channel_id=1, source_target_pairs={{0,2},{2,0},{1,3},{3,1},{4,6},{6,4},{5,7},{7,5},{8,10},{10,8},{9,1... | collective-permute-start | bytes 4816904 | tf_op jit(solution)/shard_map/ppermute | solution.py:919
  488.1 22.7 %collective-permute-start.36 = (bf16[8,16,1472]{2,1,0:T(8,128)(2,1)S(1)}, bf16[8,16,1472]{2,1,0:T(8,128)(2,1)}, u32[]{:S(2)}, u32[]{:S(2)}) collective-permute-start(bf16[8,16,1472]{2,1,0:T(8,128)(2,1)S(1)} %get-tuple-element.643), channel_id=1, source_target_pairs={{0,4},{4,0},{8,12},{12,8},{16,20},{20,16},{24,28},{28,24},{1,5},{5... | collective-permute-start | bytes 1130504 | tf_op jit(solution)/shard_map/ppermute | solution.py:919
  491.5 19.3 %collective-permute-start.37 = (bf16[8,16,1472]{2,1,0:T(8,128)(2,1)}, bf16[8,16,1472]{2,1,0:T(8,128)(2,1)}, u32[]{:S(2)}, u32[]{:S(2)}) collective-permute-start(bf16[8,16,1472]{2,1,0:T(8,128)(2,1)} %get-tuple-element.641), channel_id=1, source_target_pairs={{0,4},{4,0},{8,12},{12,8},{16,20},{20,16},{24,28},{28,24},{1,5},{5... | collective-permute-start | bytes 1130504 | tf_op jit(solution)/shard_map/ppermute | solution.py:919
  493.6 51.9 %collective-permute-start.54 = (bf16[1,3,64,1472]{3,2,1,0:T(8,128)(2,1)}, bf16[1,3,64,1472]{3,2,1,0:T(8,128)(2,1)}, u32[]{:S(2)}, u32[]{:S(2)}) collective-permute-start(bf16[1,3,64,1472]{3,2,1,0:T(8,128)(2,1)} %get-tuple-element.629), channel_id=1, source_target_pairs={{0,8},{4,12},{8,0},{12,4},{16,24},{20,28},{24,16},{28,20},{1,9},{5... | collective-permute-start | bytes 1695752 | tf_op jit(solution)/shard_map/ppermute | solution.py:919
  514.8 28.0 %collective-permute-start.41 = (bf16[8,16,1472]{2,1,0:T(8,128)(2,1)}, bf16[8,16,1472]{2,1,0:T(8,128)(2,1)}, u32[]{:S(2)}, u32[]{:S(2)}) collective-permute-start(bf16[8,16,1472]{2,1,0:T(8,128)(2,1)} %get-tuple-element.639), channel_id=1, source_target_pairs={{0,2},{2,0},{1,3},{3,1},{4,6},{6,4},{5,7},{7,5},{8,10},{10,8},{9,1... | collective-permute-start | bytes 1130504 | tf_op jit(solution)/shard_map/ppermute | solution.py:919
  517.1 25.7 %collective-permute-start.42 = (bf16[8,16,1472]{2,1,0:T(8,128)(2,1)}, bf16[8,16,1472]{2,1,0:T(8,128)(2,1)}, u32[]{:S(2)}, u32[]{:S(2)}) collective-permute-start(bf16[8,16,1472]{2,1,0:T(8,128)(2,1)} %get-tuple-element.637), channel_id=1, source_target_pairs={{0,4},{4,0},{8,12},{12,8},{16,20},{20,16},{24,28},{28,24},{1,5},{5... | collective-permute-start | bytes 1130504 | tf_op jit(solution)/shard_map/ppermute | solution.py:919
  518.8 28.5 %collective-permute-start.39 = (bf16[4,16,1472]{2,1,0:T(8,128)(2,1)S(1)}, bf16[4,16,1472]{2,1,0:T(8,128)(2,1)}, u32[]{:S(2)}, u32[]{:S(2)}) collective-permute-start(bf16[4,16,1472]{2,1,0:T(8,128)(2,1)S(1)} %get-tuple-element.659), channel_id=1, source_target_pairs={{0,2},{2,0},{1,3},{3,1},{4,6},{6,4},{5,7},{7,5},{8,10},{10,8},{9,1... | collective-permute-start | bytes 565256 | tf_op jit(solution)/shard_map/ppermute | solution.py:919
  519.3 28.1 %collective-permute-start.40 = (bf16[4,16,1472]{2,1,0:T(8,128)(2,1)}, bf16[4,16,1472]{2,1,0:T(8,128)(2,1)}, u32[]{:S(2)}, u32[]{:S(2)}) collective-permute-start(bf16[4,16,1472]{2,1,0:T(8,128)(2,1)} %get-tuple-element.657), channel_id=1, source_target_pairs={{0,2},{2,0},{1,3},{3,1},{4,6},{6,4},{5,7},{7,5},{8,10},{10,8},{9,1... | collective-permute-start | bytes 565256 | tf_op jit(solution)/shard_map/ppermute | solution.py:919
  (67 other events, 555.4 us)
Sparse Core Ops, SparseCore 0:
  31.2 130.8 all-gather.4
  164.9 93.6 all-gather.6
  264.0 197.3 reduce-scatter.1
